TPU v7x, 32 devices: a whole 2x2x4 slice. The times are simulated.
32 devices in a mesh: seq: 8 (over z, y), head: 4 (over x, core).
Axes of the slice: x: 2, y: 2, z: 4, core: 2. Of those that a mesh axis runs over, the one named last changes fastest.
Arguments:
- block_input: bfloat16 [8, 512, 4096], P(None, 'seq'), may hold values from -6 to 6
- lengths: int32 [8], replicated, may hold values from 1 to 4096, as said below
- cache_keys: bfloat16 [8, 4096, 4096], P(None, 'seq', 'head'), may hold values from -6 to 6
- cache_values: bfloat16 [8, 4096, 4096], P(None, 'seq', 'head'), may hold values from -6 to 6
- w_query: bfloat16 [4096, 4096], P('seq', 'head'), may hold values from -1 to 1
- w_key: bfloat16 [4096, 4096], P('seq', 'head'), may hold values from -1 to 1
- w_value: bfloat16 [4096, 4096], P('seq', 'head'), may hold values from -0.09375 to 0.09375
- w_attn_out: bfloat16 [4096, 2048], P('head'), may hold values from -0.09375 to 0.09375
- norm_gain: float32 [2048], replicated, may hold values from 0.25 to 1.75
- w_in: bfloat16 [2048, 2, 4096], P(None, None, 'head'), may hold values from -0.125 to 0.125
- w_bc: bfloat16 [2048, 128], replicated, may hold values from -0.125 to 0.125
- w_dt: bfloat16 [2048, 64], P(None, 'head'), may hold values from -0.125 to 0.125
- dt_bias: float32 [64], P('head'), may hold values from -5 to 0
- a_log: float32 [64], P('head'), may hold values from -4 to 1
- d_skip: float32 [64], P('head'), may hold values from 0.5 to 1.5
- gated_gain: float32 [4096], P('head'), may hold values from 0.1 to 1.9
- w_out: bfloat16 [4096, 2048], P('head'), may hold values from -0.09375 to 0.09375
- ssm_init: float32 [8, 64, 4096], P(None, 'head'), may hold values from -6 to 6
Outputs:
- mixed: bfloat16 [8, 512, 2048], P(None, 'seq', 'head')
- new_keys: bfloat16 [8, 512, 4096], P(None, 'seq', 'head')
- new_values: bfloat16 [8, 512, 4096], P(None, 'seq', 'head')
- chain_states: float32 [8, 8, 64, 4096], P(None, 'seq', 'head')
- greatest_logit: float32 [8, 512, 32], P(None, 'seq', 'head')
Inputs may be any that keep to these rules, and one draw needn't show every extreme that they name: `lengths`: every request has at least one cached token, and one request's cache holds exactly 4096 tokens.
All inputs are finite; a program needn't handle non-finite values.
Results may differ from a plain program's by a relative error of at most 0.019.
Values may be sent and summed in bfloat16 or wider, within the bound.
No kernel may reach another device: no remote copies, remote signals or barrier semaphores. Data moves between devices by JAX's collectives and lax.ppermute only.
A program may use at most 256 MiB of HBM per device.

v0:
```python
import math

import jax
import jax.numpy as jnp
from jax import lax
from jax.sharding import PartitionSpec as P

D = 2048
HEAD_DIM = 128
MHEAD_DIM = 64
STATE = 64
D_INNER = 4096


def shifted(block, axis, distance):
    devices = range(lax.axis_size(axis))
    route = [(i - distance, i) for i in devices if i - distance in devices]
    return lax.ppermute(block, axis, route)


def rotate(values, positions):
    half_dim = values.shape[-1] // 2
    frequency = jnp.exp(
        jnp.arange(half_dim, dtype=jnp.float32) * (-2.0 * math.log(10000.0) / values.shape[-1])
    )
    angles = positions.astype(jnp.float32)[:, :, None, None] * frequency
    cosine = jnp.cos(angles)
    sine_part = jnp.sin(angles)
    front_half = values[..., :half_dim]
    back_half = values[..., half_dim:]
    return jnp.concatenate(
        [front_half * cosine - back_half * sine_part, back_half * cosine + front_half * sine_part],
        axis=-1,
    )


def shards(
    block_input,
    lengths,
    cache_keys,
    cache_values,
    w_query,
    w_key,
    w_value,
    w_attn_out,
    norm_gain,
    w_in,
    w_bc,
    w_dt,
    dt_bias,
    a_log,
    d_skip,
    gated_gain,
    w_out,
    ssm_init,
):
    requests = block_input.shape[0]
    tok_block = block_input.shape[1]
    seq_count = lax.axis_size("seq")
    seq_index = lax.axis_index("seq")
    head_count = lax.axis_size("head")
    head_index = lax.axis_index("head")
    local_att = w_query.shape[1]
    local_heads = local_att // HEAD_DIM
    cache_block = cache_keys.shape[1]
    group_len = tok_block * seq_count
    flat_input = block_input.reshape(requests * tok_block, block_input.shape[2])
    pieces = (
        lax.all_gather(w_query, "seq", axis=0, tiled=True),
        lax.all_gather(w_key, "seq", axis=0, tiled=True),
        lax.all_gather(w_value, "seq", axis=0, tiled=True),
    )
    projected = tuple(
        (jnp.dot(flat_input, row_block, preferred_element_type=jnp.float32) for row_block in pieces)
    )
    positions = (
        lengths[:, None] + seq_index * tok_block + jnp.arange(tok_block, dtype=jnp.int32)[None, :]
    )

    def heads_of(matrix):
        return matrix.reshape(requests, tok_block, local_heads, HEAD_DIM)

    queries = (
        rotate(heads_of(projected[0]), positions)
        .astype(jnp.bfloat16)
        .reshape(requests, tok_block, local_att)
    )
    new_keys = (
        rotate(heads_of(projected[1]), positions)
        .astype(jnp.bfloat16)
        .reshape(requests, tok_block, local_att)
    )
    new_values = projected[2].astype(jnp.bfloat16).reshape(requests, tok_block, local_att)
    all_queries = lax.all_gather(queries, "seq", axis=1, tiled=True)
    key_rows = jnp.concatenate([cache_keys, new_keys], axis=1).reshape(
        requests, cache_block + tok_block, local_heads, HEAD_DIM
    )
    value_rows = jnp.concatenate([cache_values, new_values], axis=1).reshape(
        requests, cache_block + tok_block, local_heads, HEAD_DIM
    )
    scores = jnp.einsum(
        "rthd,rkhd->rthk",
        all_queries.reshape(requests, group_len, local_heads, HEAD_DIM),
        key_rows,
        preferred_element_type=jnp.float32,
    ) * (1.0 / math.sqrt(HEAD_DIM))
    cache_live = (seq_index * cache_block + jnp.arange(cache_block, dtype=jnp.int32))[
        None, :
    ] < lengths[:, None]
    group_live = (seq_index * tok_block + jnp.arange(tok_block, dtype=jnp.int32))[
        None, :
    ] <= jnp.arange(group_len, dtype=jnp.int32)[:, None]
    live_mask = jnp.concatenate(
        [
            jnp.broadcast_to(cache_live[:, None, :], (requests, group_len, cache_block)),
            jnp.broadcast_to(group_live[None], (requests, group_len, tok_block)),
        ],
        axis=2,
    )[:, :, None, :]
    masked = jnp.where(live_mask, scores, -1e30)
    peaks = jnp.max(masked, axis=3)
    weights = jnp.where(live_mask, jnp.exp(masked - peaks[..., None]), 0.0)
    totals = jnp.sum(weights, axis=3)
    partial_value = jnp.einsum(
        "rthk,rkhd->rthd",
        weights.astype(jnp.bfloat16),
        value_rows,
        preferred_element_type=jnp.float32,
    ).reshape(requests, group_len, local_att)
    received = (
        lax.all_to_all(partial_value[None], "seq", split_axis=2, concat_axis=0, tiled=True),
        lax.all_to_all(peaks[None], "seq", split_axis=2, concat_axis=0, tiled=True),
        lax.all_to_all(totals[None], "seq", split_axis=2, concat_axis=0, tiled=True),
    )
    best_score = jnp.max(received[1], axis=0)
    rescale = jnp.exp(received[1] - best_score)
    denominator = jnp.sum(rescale * received[2], axis=0)
    numerator = jnp.sum(
        received[0].reshape(seq_count, requests, tok_block, local_heads, HEAD_DIM)
        * rescale[..., None],
        axis=0,
    )
    attended = numerator / denominator[..., None]
    attended = attended.reshape(requests * tok_block, local_att).astype(jnp.bfloat16)
    attn_terms = jnp.dot(attended, w_attn_out, preferred_element_type=jnp.float32).reshape(
        requests, tok_block, D
    )
    hidden = block_input[:, :, :D].astype(jnp.float32)
    normed = (
        hidden * lax.rsqrt(jnp.mean(hidden * hidden, axis=-1, keepdims=True) + 1e-05) * norm_gain
    ).astype(jnp.bfloat16)
    flat_normed = normed.reshape(requests * tok_block, D)
    local_inner = w_in.shape[2]
    local_mheads = local_inner // MHEAD_DIM
    gate_inner = jnp.dot(
        flat_normed, w_in.reshape(D, 2 * local_inner), preferred_element_type=jnp.float32
    ).reshape(requests, tok_block, 2, local_inner)
    gate_part = gate_inner[:, :, 0]
    inner_heads = jax.nn.silu(gate_inner[:, :, 1]).reshape(
        requests, tok_block, local_mheads, MHEAD_DIM
    )
    bc_part = jnp.dot(flat_normed, w_bc, preferred_element_type=jnp.float32).reshape(
        requests, tok_block, 2 * STATE
    )
    input_map = bc_part[..., :STATE]
    output_map = bc_part[..., STATE:]
    step_size = jax.nn.softplus(
        jnp.dot(flat_normed, w_dt, preferred_element_type=jnp.float32).reshape(
            requests, tok_block, local_mheads
        )
        + dt_bias
    )
    log_decay = -step_size * jnp.exp(a_log)
    cumulative = jnp.cumsum(log_decay, axis=1)
    causal = jnp.arange(tok_block)[None, :] <= jnp.arange(tok_block)[:, None]
    head_major = jnp.transpose(cumulative, (0, 2, 1))
    differences = head_major[:, :, :, None] - head_major[:, :, None, :]
    decays = jnp.where(causal, jnp.exp(jnp.where(causal, differences, 0.0)), 0.0)
    contact = jnp.einsum("rtn,run->rtu", output_map, input_map, precision=lax.Precision.HIGHEST)
    mixing = decays * contact[:, None] * jnp.transpose(step_size, (0, 2, 1))[:, :, None, :]
    intra_part = jnp.einsum("rhtu,ruhp->rthp", mixing, inner_heads, precision=lax.Precision.HIGHEST)
    tail_decay = jnp.exp(cumulative[:, -1:, :] - cumulative) * step_size
    local_state = jnp.einsum(
        "ruhp,run->rhpn",
        inner_heads * tail_decay[..., None],
        input_map,
        precision=lax.Precision.HIGHEST,
    ).reshape(requests, local_mheads, MHEAD_DIM * STATE)
    through = jnp.exp(cumulative[:, -1, :])[:, :, None]
    chain_base = jnp.where(seq_index == 0, ssm_init, 0.0)

    def relay_step(relay_turn, incoming):
        outgoing = through * incoming + local_state
        return chain_base + shifted(outgoing.astype(jnp.bfloat16), "seq", 1).astype(outgoing.dtype)

    incoming = lax.fori_loop(0, seq_count - 1, relay_step, chain_base)
    entry_state = incoming.reshape(requests, local_mheads, MHEAD_DIM, STATE)
    inter_part = (
        jnp.einsum("rhpn,rtn->rthp", entry_state, output_map, precision=lax.Precision.HIGHEST)
        * jnp.exp(cumulative)[..., None]
    )
    read_out = intra_part + inter_part + d_skip[:, None] * inner_heads
    chain_states = (through * incoming + local_state)[:, None]
    mixed_inner = read_out.reshape(requests, tok_block, local_inner) * jax.nn.silu(gate_part)
    squares = jnp.sum(mixed_inner * mixed_inner, axis=-1, keepdims=True)
    gated = (mixed_inner * gated_gain).astype(jnp.bfloat16)
    mamba_terms = jnp.dot(
        gated.reshape(requests * tok_block, local_inner), w_out, preferred_element_type=jnp.float32
    ).reshape(requests, tok_block, D)
    summed = (
        lax.psum_scatter(
            attn_terms.astype(jnp.bfloat16), "head", scatter_dimension=2, tiled=True
        ).astype(jnp.float32),
        lax.psum_scatter(
            mamba_terms.astype(jnp.bfloat16), "head", scatter_dimension=2, tiled=True
        ).astype(jnp.float32),
        lax.psum_scatter(
            jnp.broadcast_to(squares, (requests, tok_block, head_count)).astype(jnp.bfloat16),
            "head",
            scatter_dimension=2,
            tiled=True,
        ).astype(jnp.float32),
    )
    local_width = D // head_count
    residual = lax.dynamic_slice_in_dim(hidden, head_index * local_width, local_width, 2)
    mixed = (residual + summed[0] + summed[1] * lax.rsqrt(summed[2] / D_INNER + 1e-05)).astype(
        jnp.bfloat16
    )
    return (mixed, new_keys, new_values, chain_states, best_score)


def solution(mesh):
    placed = (
        P(None, "seq", None),
        P(),
        P(None, "seq", "head"),
        P(None, "seq", "head"),
        P("seq", "head"),
        P("seq", "head"),
        P("seq", "head"),
        P("head", None),
        P(),
        P(None, None, "head"),
        P(),
        P(None, "head"),
        P("head"),
        P("head"),
        P("head"),
        P("head"),
        P("head", None),
        P(None, "head", None),
    )
    return jax.shard_map(
        shards,
        mesh=mesh,
        in_specs=placed,
        out_specs=(
            P(None, "seq", "head"),
            P(None, "seq", "head"),
            P(None, "seq", "head"),
            P(None, "seq", "head", None),
            P(None, "seq", "head"),
        ),
        check_vma=False,
    )
```

profile of v0, /device:TPU:0, one launch (start us, length us, event | category | flops | bytes accessed | tf_op | source)
XLA Modules:
  0.0 1329.7 jit_solution(4023553336975505147)
XLA Ops:
  11.3 127.6 %all-gather.9.cloned.1.call-done = bf16[4096,1024]{1,0:T(8,128)(2,1)} async-done(((bf16[512,1024]{1,0:T(8,128)(2,1)}), bf16[4096,1024]{1,0:T(8,128)(2,1)}) %all-gather.9.cloned.1.call-update) | async-done | bytes 8388624 | tf_op jit(solution)/shard_map/all_gather | solution.py:69
  138.9 11.4 copy.96
  160.9 11.4 copy.93
  172.3 11.4 copy.95
  183.7 11.6 copy.90
  195.3 11.4 copy.91
  208.5 55.8 %all-gather.7.cloned.1.call-done = bf16[4096,1024]{1,0:T(8,128)(2,1)} async-done(((bf16[512,1024]{1,0:T(8,128)(2,1)}), bf16[4096,1024]{1,0:T(8,128)(2,1)}) %all-gather.7.cloned.1.call-update) | async-done | bytes 8388624 | tf_op jit(solution)/shard_map/all_gather | solution.py:70
  264.4 11.8 copy.94
  287.6 102.9 %all-gather.11.cloned.1.call-done = bf16[8,512,1024]{2,1,0:T(8,128)(2,1)} async-done(((bf16[8,64,1024]{2,1,0:T(8,128)(2,1)}), bf16[8,512,1024]{2,1,0:T(8,128)(2,1)}) %all-gather.11.cloned.1.call-update) | async-done | bytes 8388624 | tf_op jit(solution)/shard_map/all_gather | solution.py:94
  390.5 11.6 copy.98
  402.1 34.1 %fusion = (f32[8,512,8]{1,2,0:T(8,128)S(1)}, f32[8,8,576,512]{3,2,1,0:T(8,128)}) fusion(pred[8,512,576]{1,2,0:T(8,128)(4,1)S(1)} %pad_add_fusion, bf16[8,512,8,128]{1,3,2,0:T(8,128)(2,1)} %bitcast.194, bf16[8,64,8,128]{3,1,2,0:T(8,128)(2,1)} %maximum_convert_fusion, bf16[8,512,8,128]{3,1,2,0:T(8,128)(2,1)} %copy.95), kind=kOutput, calls=%fused_computation.4 | convolution fusion | flops 4907302912 | bytes 95813632 | tf_op jit(solution)/shard_map/rthd,rkhd->rthk/dot_general | solution.py:101
  436.2 25.6 %fusion.1 = f32[8,512,8]{1,2,0:T(8,128)S(1)} fusion(f32[8,8,576,512]{3,2,1,0:T(8,128)} %get-tuple-element.58, f32[8,512,8]{1,2,0:T(8,128)S(1)} %get-tuple-element.57, pred[8,512,576]{1,2,0:T(8,128)(4,1)S(1)} %pad_add_fusion), kind=kLoop, calls=%fused_computation.5 | loop fusion | flops 94339072 | bytes 78118912 | tf_op jit(solution)/shard_map/reduce_sum | solution.py:123
  470.5 46.7 %all-gather.5.cloned.1.call-done = bf16[4096,1024]{1,0:T(8,128)(2,1)} async-done(((bf16[512,1024]{1,0:T(8,128)(2,1)}), bf16[4096,1024]{1,0:T(8,128)(2,1)}) %all-gather.5.cloned.1.call-update) | async-done | bytes 8388624 | tf_op jit(solution)/shard_map/all_gather | solution.py:71
  536.6 39.9 %fusion.3 = f32[8,8,128,512]{3,2,1,0:T(8,128)} fusion(f32[8,8,576,512]{3,2,1,0:T(8,128)} %get-tuple-element.58, f32[8,512,8]{1,2,0:T(8,128)S(1)} %get-tuple-element.57, pred[8,512,576]{1,2,0:T(8,128)(4,1)S(1)} %pad_add_fusion, bf16[8,64,8,128]{3,1,2,0:T(8,128)(2,1)} %copy.92, bf16[8,512,8,128]{3,1,2,0:T(8,128)(2,1)} %copy.91), kind=kOutput, calls=%fused_computation.7 | convolution fusion | flops 4945084416 | bytes 104202240 | tf_op jit(solution)/shard_map/rthk,rkhd->rthd/dot_general | solution.py:124
  576.5 16.9 %copy.100 = f32[1,8,512,1024]{3,1,0,2:T(8,128)} copy(f32[1,8,512,1024]{2,3,1,0:T(8,128)} %bitcast.190) | data formatting | bytes 33554432 | tf_op jit(solution)/shard_map/broadcast_in_dim;reshape | solution.py:131
  615.2 10.2 copy.131
  625.3 12.3 copy.108
  670.2 499.5 %while.10 = (s32[]{:T(128)}, f32[8,16,4096]{2,1,0:T(8,128)S(1)}, f32[8,16,1]{1,0,2:T(8,128)S(1)}, f32[8,16,4096]{2,1,0:T(8,128)}, f32[8,16,4096]{2,1,0:T(8,128)}, /*index=5*/s32[]{:T(128)}) while((s32[]{:T(128)}, f32[8,16,4096]{2,1,0:T(8,128)S(1)}, f32[8,16,1]{1,0,2:T(8,128)S(1)}, f32[8,16,4096]{2,1,0:T(8,128)}, f32[8,16,4096]{2,1,0:T(8,128)}, ...), condition=%wide.region_9.10_spmd, body=%wide.region_8.9_spmd.sunk | while | flops 2621442 | bytes 18875016 | solution.py:196
  677.4 80.8 %collective-permute-done = bf16[8,16,4096]{2,1,0:T(8,128)(2,1)S(1)} collective-permute-done((bf16[8,16,4096]{2,1,0:T(8,128)(2,1)}, bf16[8,16,4096]{2,1,0:T(8,128)(2,1)S(1)}, u32[]{:S(2)}, u32[]{:S(2)}) %collective-permute-start) | collective-permute-done | bytes 1048608 | tf_op jit(solution)/shard_map/while/body/eval_jaxpr/ppermute | solution.py:18
  764.1 157.4 %collective-permute-start = (bf16[8,16,4096]{2,1,0:T(8,128)(2,1)}, bf16[8,16,4096]{2,1,0:T(8,128)(2,1)S(1)}, u32[]{:S(2)}, u32[]{:S(2)}) collective-permute-start(bf16[8,16,4096]{2,1,0:T(8,128)(2,1)} %add_convert_fusion.5), channel_id=1, source_target_pairs={{0,4},{4,8},{8,12},{12,16},{16,20},{20,24},{24,28},{1,5},{5,9},{9,... | collective-permute-start | bytes 3145736 | tf_op jit(solution)/shard_map/while/body/eval_jaxpr/ppermute | solution.py:18
  921.5 19.2 %collective-permute-done = bf16[8,16,4096]{2,1,0:T(8,128)(2,1)S(1)} collective-permute-done((bf16[8,16,4096]{2,1,0:T(8,128)(2,1)}, bf16[8,16,4096]{2,1,0:T(8,128)(2,1)S(1)}, u32[]{:S(2)}, u32[]{:S(2)}) %collective-permute-start) | collective-permute-done | bytes 1048608 | tf_op jit(solution)/shard_map/while/body/eval_jaxpr/ppermute | solution.py:18
  946.6 21.1 %collective-permute-start = (bf16[8,16,4096]{2,1,0:T(8,128)(2,1)}, bf16[8,16,4096]{2,1,0:T(8,128)(2,1)S(1)}, u32[]{:S(2)}, u32[]{:S(2)}) collective-permute-start(bf16[8,16,4096]{2,1,0:T(8,128)(2,1)} %add_convert_fusion.5), channel_id=1, source_target_pairs={{0,4},{4,8},{8,12},{12,16},{16,20},{20,24},{24,28},{1,5},{5,9},{9,... | collective-permute-start | bytes 3145736 | tf_op jit(solution)/shard_map/while/body/eval_jaxpr/ppermute | solution.py:18
  967.8 19.9 %collective-permute-done = bf16[8,16,4096]{2,1,0:T(8,128)(2,1)S(1)} collective-permute-done((bf16[8,16,4096]{2,1,0:T(8,128)(2,1)}, bf16[8,16,4096]{2,1,0:T(8,128)(2,1)S(1)}, u32[]{:S(2)}, u32[]{:S(2)}) %collective-permute-start) | collective-permute-done | bytes 1048608 | tf_op jit(solution)/shard_map/while/body/eval_jaxpr/ppermute | solution.py:18
  993.6 60.9 %collective-permute-start = (bf16[8,16,4096]{2,1,0:T(8,128)(2,1)}, bf16[8,16,4096]{2,1,0:T(8,128)(2,1)S(1)}, u32[]{:S(2)}, u32[]{:S(2)}) collective-permute-start(bf16[8,16,4096]{2,1,0:T(8,128)(2,1)} %add_convert_fusion.5), channel_id=1, source_target_pairs={{0,4},{4,8},{8,12},{12,16},{16,20},{20,24},{24,28},{1,5},{5,9},{9,... | collective-permute-start | bytes 3145736 | tf_op jit(solution)/shard_map/while/body/eval_jaxpr/ppermute | solution.py:18
  1054.5 21.1 %collective-permute-done = bf16[8,16,4096]{2,1,0:T(8,128)(2,1)S(1)} collective-permute-done((bf16[8,16,4096]{2,1,0:T(8,128)(2,1)}, bf16[8,16,4096]{2,1,0:T(8,128)(2,1)S(1)}, u32[]{:S(2)}, u32[]{:S(2)}) %collective-permute-start) | collective-permute-done | bytes 1048608 | tf_op jit(solution)/shard_map/while/body/eval_jaxpr/ppermute | solution.py:18
  1086.7 20.1 %collective-permute-done = bf16[8,16,4096]{2,1,0:T(8,128)(2,1)S(1)} collective-permute-done((bf16[8,16,4096]{2,1,0:T(8,128)(2,1)}, bf16[8,16,4096]{2,1,0:T(8,128)(2,1)S(1)}, u32[]{:S(2)}, u32[]{:S(2)}) %collective-permute-start) | collective-permute-done | bytes 1048608 | tf_op jit(solution)/shard_map/while/body/eval_jaxpr/ppermute | solution.py:18
  1118.0 19.2 %collective-permute-done = bf16[8,16,4096]{2,1,0:T(8,128)(2,1)S(1)} collective-permute-done((bf16[8,16,4096]{2,1,0:T(8,128)(2,1)}, bf16[8,16,4096]{2,1,0:T(8,128)(2,1)S(1)}, u32[]{:S(2)}, u32[]{:S(2)}) %collective-permute-start) | collective-permute-done | bytes 1048608 | tf_op jit(solution)/shard_map/while/body/eval_jaxpr/ppermute | solution.py:18
  1148.4 18.3 %collective-permute-done = bf16[8,16,4096]{2,1,0:T(8,128)(2,1)S(1)} collective-permute-done((bf16[8,16,4096]{2,1,0:T(8,128)(2,1)}, bf16[8,16,4096]{2,1,0:T(8,128)(2,1)S(1)}, u32[]{:S(2)}, u32[]{:S(2)}) %collective-permute-start) | collective-permute-done | bytes 1048608 | tf_op jit(solution)/shard_map/while/body/eval_jaxpr/ppermute | solution.py:18
  1173.5 10.4 fusion.24
  1232.0 18.0 %mul.275 = f32[8,1,8,64,1024]{4,3,0,2,1:T(8,128)} reshape(f32[8,8,64,8,128]{4,3,2,0,1:T(8,128)} %mul.274) | data formatting | bytes 33554432 | tf_op jit(solution)/shard_map/mul | solution.py:139
  1250.0 19.2 %copy.101 = f32[1,8,512,1024]{3,2,1,0:T(8,128)} copy(f32[1,8,512,1024]{3,1,0,2:T(8,128)} %all-to-all-done) | data formatting | bytes 33554432 | tf_op jit(solution)/shard_map/all_to_all | solution.py:131
  1296.9 23.0 %reduce-scatter.3.cloned.1.call-done = bf16[8,64,512]{2,1,0:T(8,128)(2,1)} async-done(((bf16[8,64,2048]{2,1,0:T(8,128)(2,1)}), bf16[8,64,512]{2,1,0:T(8,128)(2,1)}) %reduce-scatter.3.cloned.1.call-update) | async-done | bytes 524304 | tf_op jit(solution)/shard_map/reduce_scatter | solution.py:211
  (186 shorter events, 251.6 us)
Async XLA Ops:
  8.0 648.6 %copy-start = (bf16[2048,128]{1,0:T(8,128)(2,1)S(1)}, bf16[2048,128]{1,0:T(8,128)(2,1)}, u32[]{:S(2)}) copy-start(bf16[2048,128]{1,0:T(8,128)(2,1)} %param.30) | copy-start | bytes 1572868
  8.0 130.8 %all-gather.9.cloned.1.call-start = ((), (), s32[]{:S(2)}) async-start(), calls=%async_computation.7 | async-start | bytes 9437184 | tf_op jit(solution)/shard_map/all_gather | solution.py:69
  8.7 255.6 %all-gather.7.cloned.1.call-start = ((), (), s32[]{:S(2)}) async-start(), calls=%async_computation.6 | async-start | bytes 9437184 | tf_op jit(solution)/shard_map/all_gather | solution.py:70
  9.5 381.0 %all-gather.11.cloned.1.call-start = ((), (), s32[]{:S(2)}) async-start(), calls=%async_computation.8 | async-start | bytes 9437184 | tf_op jit(solution)/shard_map/all_gather | solution.py:94
  160.3 357.0 %all-gather.5.cloned.1.call-start = ((), (), s32[]{:S(2)}) async-start(), calls=%async_computation.5 | async-start | bytes 9437184 | tf_op jit(solution)/shard_map/all_gather | solution.py:71
  195.3 11.4 copy-start.21
  467.1 66.0 %all-to-all-start.2 = ((f32[8,1,4096]{2,1,0:T(1,128)}), f32[8,1,4096]{2,1,0:T(1,128)S(1)}, u32[]{:S(2)}, u32[]{:S(2)}) async-start(f32[8,1,4096]{2,1,0:T(1,128)} %reshape.246), calls=%async_computation.2 | async-start | bytes 262144 | tf_op jit(solution)/shard_map/all_to_all | solution.py:133
  533.2 60.3 %all-to-all-start.1 = ((f32[8,1,4096]{2,1,0:T(1,128)}), f32[8,1,4096]{2,1,0:T(1,128)S(1)}, u32[]{:S(2)}, u32[]{:S(2)}) async-start(f32[8,1,4096]{2,1,0:T(1,128)} %reshape.244), calls=%async_computation.1 | async-start | bytes 262144 | tf_op jit(solution)/shard_map/all_to_all | solution.py:132
  593.4 6.3 copy-start.26
  593.4 8.4 copy-start.23
  593.4 8.4 copy-start.24
  593.4 8.4 copy-start.27
  593.5 656.6 %all-to-all-start = ((f32[1,8,512,1024]{3,1,0,2:T(8,128)}), f32[1,8,512,1024]{3,1,0,2:T(8,128)}, u32[]{:S(2)}, u32[]{:S(2)}) async-start(f32[1,8,512,1024]{3,1,0,2:T(8,128)} %copy.100), calls=%async_computation | async-start | bytes 33554432 | tf_op jit(solution)/shard_map/all_to_all | solution.py:131
  599.5 697.4 %reduce-scatter.5.cloned.1.call-start = ((), (), s32[]{:S(2)}) async-start(), calls=%async_computation.10 | async-start | bytes 2621440 | tf_op jit(solution)/shard_map/reduce_scatter | solution.py:214
  601.8 11.7 copy-start.14
  673.5 84.7 %collective-permute-start = (bf16[8,16,4096]{2,1,0:T(8,128)(2,1)}, bf16[8,16,4096]{2,1,0:T(8,128)(2,1)S(1)}, u32[]{:S(2)}, u32[]{:S(2)}) collective-permute-start(bf16[8,16,4096]{2,1,0:T(8,128)(2,1)} %add_convert_fusion.5), channel_id=1, source_target_pairs={{0,4},{4,8},{8,12},{12,16},{16,20},{20,24},{24,28},{1,5},{5,9},{9,... | collective-permute-start | bytes 3145736 | tf_op jit(solution)/shard_map/while/body/eval_jaxpr/ppermute | solution.py:18
  764.1 176.6 %collective-permute-start = (bf16[8,16,4096]{2,1,0:T(8,128)(2,1)}, bf16[8,16,4096]{2,1,0:T(8,128)(2,1)S(1)}, u32[]{:S(2)}, u32[]{:S(2)}) collective-permute-start(bf16[8,16,4096]{2,1,0:T(8,128)(2,1)} %add_convert_fusion.5), channel_id=1, source_target_pairs={{0,4},{4,8},{8,12},{12,16},{16,20},{20,24},{24,28},{1,5},{5,9},{9,... | collective-permute-start | bytes 3145736 | tf_op jit(solution)/shard_map/while/body/eval_jaxpr/ppermute | solution.py:18
  946.6 41.1 %collective-permute-start = (bf16[8,16,4096]{2,1,0:T(8,128)(2,1)}, bf16[8,16,4096]{2,1,0:T(8,128)(2,1)S(1)}, u32[]{:S(2)}, u32[]{:S(2)}) collective-permute-start(bf16[8,16,4096]{2,1,0:T(8,128)(2,1)} %add_convert_fusion.5), channel_id=1, source_target_pairs={{0,4},{4,8},{8,12},{12,16},{16,20},{20,24},{24,28},{1,5},{5,9},{9,... | collective-permute-start | bytes 3145736 | tf_op jit(solution)/shard_map/while/body/eval_jaxpr/ppermute | solution.py:18
  993.6 82.0 %collective-permute-start = (bf16[8,16,4096]{2,1,0:T(8,128)(2,1)}, bf16[8,16,4096]{2,1,0:T(8,128)(2,1)S(1)}, u32[]{:S(2)}, u32[]{:S(2)}) collective-permute-start(bf16[8,16,4096]{2,1,0:T(8,128)(2,1)} %add_convert_fusion.5), channel_id=1, source_target_pairs={{0,4},{4,8},{8,12},{12,16},{16,20},{20,24},{24,28},{1,5},{5,9},{9,... | collective-permute-start | bytes 3145736 | tf_op jit(solution)/shard_map/while/body/eval_jaxpr/ppermute | solution.py:18
  1081.5 25.4 %collective-permute-start = (bf16[8,16,4096]{2,1,0:T(8,128)(2,1)}, bf16[8,16,4096]{2,1,0:T(8,128)(2,1)S(1)}, u32[]{:S(2)}, u32[]{:S(2)}) collective-permute-start(bf16[8,16,4096]{2,1,0:T(8,128)(2,1)} %add_convert_fusion.5), channel_id=1, source_target_pairs={{0,4},{4,8},{8,12},{12,16},{16,20},{20,24},{24,28},{1,5},{5,9},{9,... | collective-permute-start | bytes 3145736 | tf_op jit(solution)/shard_map/while/body/eval_jaxpr/ppermute | solution.py:18
  1112.8 24.5 %collective-permute-start = (bf16[8,16,4096]{2,1,0:T(8,128)(2,1)}, bf16[8,16,4096]{2,1,0:T(8,128)(2,1)S(1)}, u32[]{:S(2)}, u32[]{:S(2)}) collective-permute-start(bf16[8,16,4096]{2,1,0:T(8,128)(2,1)} %add_convert_fusion.5), channel_id=1, source_target_pairs={{0,4},{4,8},{8,12},{12,16},{16,20},{20,24},{24,28},{1,5},{5,9},{9,... | collective-permute-start | bytes 3145736 | tf_op jit(solution)/shard_map/while/body/eval_jaxpr/ppermute | solution.py:18
  1143.2 23.5 %collective-permute-start = (bf16[8,16,4096]{2,1,0:T(8,128)(2,1)}, bf16[8,16,4096]{2,1,0:T(8,128)(2,1)S(1)}, u32[]{:S(2)}, u32[]{:S(2)}) collective-permute-start(bf16[8,16,4096]{2,1,0:T(8,128)(2,1)} %add_convert_fusion.5), channel_id=1, source_target_pairs={{0,4},{4,8},{8,12},{12,16},{16,20},{20,24},{24,28},{1,5},{5,9},{9,... | collective-permute-start | bytes 3145736 | tf_op jit(solution)/shard_map/while/body/eval_jaxpr/ppermute | solution.py:18
  1173.4 10.5 copy-start.9
  1173.4 10.5 copy-start.11
  1173.4 10.5 copy-start.12
  1173.4 10.5 copy-start.19
  1173.4 10.5 copy-start.28
  1202.6 117.3 %reduce-scatter.3.cloned.1.call-start = ((), (), s32[]{:S(2)}) async-start(), calls=%async_computation.9 | async-start | bytes 2621440 | tf_op jit(solution)/shard_map/reduce_scatter | solution.py:211
  1214.6 7.5 copy-start.18
  1250.0 19.2 %copy-start.3 = (f32[8,1,8,64,1024]{4,3,0,2,1:T(8,128)S(1)}, f32[8,1,8,64,1024]{4,3,0,2,1:T(8,128)}, u32[]{:S(2)}) copy-start(f32[8,1,8,64,1024]{4,3,0,2,1:T(8,128)} %mul.275) | copy-start | bytes 50331652
  1269.3 8.6 copy-start.15
  1269.3 8.6 copy-start.22
  (20 other events, 43.4 us)
Sparse Core Ops, SparseCore 0:
  11.2 127.6 all-gather.8
  141.2 123.1 all-gather.6
  267.3 123.0 all-gather.10
  392.7 124.5 all-gather.4
Sparse Core Ops, SparseCore 1:
  1202.6 38.1 reduce-scatter.4
  1281.7 38.1 reduce-scatter.2
where the time goes:
time: 1340 us; the launch traced here: 1330 us
  waiting for transfers between devices  556 us (41%)
  starting transfers between devices  273 us (20%)
  local copies, waits for them, and re-layouts  232 us (17%)
  matrix products  148 us (11%)
  other arithmetic  98.3 us (7%)
  between operations  16 us (1%)
    ppermute x7, starting transfers between devices, shifted(): return lax.ppermute(block, axis, route)  259 us
    ppermute x7, waiting for transfers between devices, shifted(): return lax.ppermute(block, axis, route)  199 us
    all_gather x1, waiting for transfers between devices, shards(): lax.all_gather(w_query, 'seq', axis=0, tiled=True)  128 us
    all_gather x1, waiting for transfers between devices, shards(): all_queries = lax.all_gather(queries, 'seq', axis=1, tiled=True)  103 us
    all_gather x1, waiting for transfers between devices, shards(): lax.all_gather(w_key, 'seq', axis=0, tiled=True)  55.8 us
    unnamed x68, local copies, waits for them, and re-layouts  50.5 us
    all_gather x1, waiting for transfers between devices, shards(): lax.all_gather(w_value, 'seq', axis=0, tiled=True)  46.7 us
    dot_general x1, matrix products, shards(): jnp.einsum('rthk,rkhd->rthd', weights.astype(jnp.bfloat16), value_rows, p...  39.9 us
  transfers between devices with their start and end apart: 16, of which 12 were waited for; matrix products, arithmetic and copies ran while one was open for 35% of the time, Pallas kernels for 0%

commit v1 on v0

v1 whole, which is shorter than its diff:
```python
import functools
import math

import jax
import jax.numpy as jnp
from jax import lax
from jax.experimental import pallas as pl
from jax.experimental.pallas import tpu as pltpu
from jax.sharding import PartitionSpec as P

D = 2048
HEAD_DIM = 128
MHEAD_DIM = 64
STATE = 64
D_INNER = 4096
SCALE = 1.0 / math.sqrt(HEAD_DIM)
EXP2_SCALE = SCALE * math.log2(math.e)
DEAD = -1e30
GROUPS = 2


def ring_order(count):
    y_count = max(1, count // 4)
    z_count = count // y_count
    order = []
    for y in range(y_count):
        turn = range(z_count) if y % 2 == 0 else range(z_count - 1, -1, -1)
        order += [z * y_count + y for z in turn]
    return order


def ring_step(block, order, distance):
    count = len(order)
    route = [(order[i], order[(i + distance) % count]) for i in range(count)]
    return lax.ppermute(block, "seq", route)


def ring_gather(block, order):
    count = len(order)
    half = block.shape[0] // 2
    pieces = [(0, 0, block)]
    ahead = back = block
    for step in range(1, count // 2):
        ahead = ring_step(ahead, order, 1)
        back = ring_step(back, order, -1)
        pieces += [(step, 0, ahead), (-step, 0, back)]
    pieces.append((count // 2, 0, ring_step(ahead[:half], order, 1)))
    pieces.append((count // 2, half, ring_step(back[half:], order, -1)))
    return pieces


def ring_sum(parts, order):
    count = len(order)
    far = count // 2
    half = parts[0].shape[0] // 2
    add = lambda a, b: (a.astype(jnp.float32) + b.astype(jnp.float32)).astype(jnp.bfloat16)
    ahead = ring_step(parts[far][:half], order, 1)
    back = ring_step(parts[far][half:], order, -1)
    top, bottom = parts[far - 1], parts[-(far - 1)]
    ahead = jnp.concatenate([add(ahead, top[:half]), top[half:]], axis=0)
    back = jnp.concatenate([bottom[:half], add(back, bottom[half:])], axis=0)
    for step in range(far - 1, 0, -1):
        ahead = ring_step(ahead, order, 1)
        back = ring_step(back, order, -1)
        if step > 1:
            ahead = add(ahead, parts[step - 1])
            back = add(back, parts[-(step - 1)])
    return (
        ahead.astype(jnp.float32) + back.astype(jnp.float32) + parts[0].astype(jnp.float32)
    )


def after(value, *earlier):
    return lax.optimization_barrier((value,) + earlier)[0]


def rope_kernel(value_ref, cosine_ref, sine_ref, out_ref):
    cosine = cosine_ref[...]
    sine = sine_ref[...]
    for head in range(value_ref.shape[1] // HEAD_DIM):
        at = slice(head * HEAD_DIM, (head + 1) * HEAD_DIM)
        part = value_ref[:, at]
        turned = part * cosine + pltpu.roll(part, HEAD_DIM // 2, 1) * sine
        out_ref[:, at] = turned.astype(out_ref.dtype)


def rope(value, cosine, sine):
    rows, width = value.shape
    block = min(rows, 128)
    return pl.pallas_call(
        rope_kernel,
        grid=(rows // block,),
        in_specs=[
            pl.BlockSpec((block, width), lambda i: (i, 0)),
            pl.BlockSpec((block, HEAD_DIM), lambda i: (i, 0)),
            pl.BlockSpec((block, HEAD_DIM), lambda i: (i, 0)),
        ],
        out_specs=pl.BlockSpec((block, width), lambda i: (i, 0)),
        out_shape=jax.ShapeDtypeStruct((rows, width), jnp.bfloat16),
        cost_estimate=pl.CostEstimate(
            flops=4 * rows * width, bytes_accessed=6 * rows * width, transcendentals=0
        ),
        name="rope",
    )(value, cosine, sine)


def dot_nt(a, b):
    return lax.dot_general(a, b, (((1,), (1,)), ((), ())), preferred_element_type=jnp.float32)


def dot_tn(a, b):
    return lax.dot_general(a, b, (((0,), (0,)), ((), ())), preferred_element_type=jnp.float32)


def cache_kernel(slots, place_ref, live_ref, *refs):
    query_refs = refs[:slots]
    key_ref, value_ref, joined_ref, out_ref, peak_ref, total_ref = refs[slots:]
    tok_block = query_refs[0].shape[1]
    keys, width = key_ref.shape[1:]
    tokens = tok_block * slots
    for slot in range(slots):
        start = pl.multiple_of(place_ref[slot] * tok_block, tok_block)
        joined_ref[0, pl.ds(start, tok_block), :] = query_refs[slot][0]
    live = live_ref[pl.program_id(0)]
    bias = jnp.where(
        lax.broadcasted_iota(jnp.int32, (keys, 128), 0) < live, 0.0, DEAD
    ).astype(jnp.float32)
    bias = jnp.concatenate([bias] * (tokens // 128), axis=1)
    for head in range(width // HEAD_DIM):
        at = slice(head * HEAD_DIM, (head + 1) * HEAD_DIM)
        scores = dot_nt(key_ref[0, :, at], joined_ref[0, :, at]) + bias
        peak = jnp.max(scores, axis=0, keepdims=True)
        weights = jnp.exp2((scores - peak) * EXP2_SCALE)
        total_ref[0, head : head + 1, :] = jnp.sum(weights, axis=0, keepdims=True)
        peak_ref[0, head : head + 1, :] = peak
        out_ref[0, at, :] = dot_tn(value_ref[0, :, at], weights.astype(jnp.bfloat16)).astype(
            out_ref.dtype
        )


def cache_part(places, live, query_slots, keys, values):
    slots = len(query_slots)
    requests, tok_block, width = query_slots[0].shape
    tokens = tok_block * slots
    cache_block = keys.shape[1]
    heads = width // HEAD_DIM
    one = lambda rows: pl.BlockSpec((1, rows, width), lambda r, *_: (r, 0, 0))
    stat = pl.BlockSpec((1, heads, tokens), lambda r, *_: (r, 0, 0))
    return pl.pallas_call(
        functools.partial(cache_kernel, slots),
        grid_spec=pltpu.PrefetchScalarGridSpec(
            num_scalar_prefetch=2,
            grid=(requests,),
            in_specs=[one(tok_block)] * slots + [one(cache_block), one(cache_block)],
            out_specs=[
                one(tokens),
                pl.BlockSpec((1, width, tokens), lambda r, *_: (r, 0, 0)),
                stat,
                stat,
            ],
        ),
        out_shape=[
            jax.ShapeDtypeStruct((requests, tokens, width), jnp.bfloat16),
            jax.ShapeDtypeStruct((requests, width, tokens), jnp.bfloat16),
            jax.ShapeDtypeStruct((requests, heads, tokens), jnp.float32),
            jax.ShapeDtypeStruct((requests, heads, tokens), jnp.float32),
        ],
        compiler_params=pltpu.CompilerParams(vmem_limit_bytes=48 * 1024 * 1024),
        cost_estimate=pl.CostEstimate(
            flops=4 * requests * tokens * cache_block * width,
            bytes_accessed=2 * requests * width * (3 * tokens + 2 * cache_block),
            transcendentals=requests * tokens * cache_block * heads,
        ),
        name="cache_part",
    )(places, live, *query_slots, keys, values)


def group_scores(first, key, query):
    scores = dot_nt(key, query)
    shape = scores.shape
    live = first + lax.broadcasted_iota(jnp.int32, shape, 0) <= lax.broadcasted_iota(
        jnp.int32, shape, 1
    )
    return jnp.where(live, scores, DEAD)


def peak_kernel(first_ref, query_ref, key_ref, peak_ref, out_ref):
    for head in range(query_ref.shape[2] // HEAD_DIM):
        at = slice(head * HEAD_DIM, (head + 1) * HEAD_DIM)
        scores = group_scores(first_ref[0], key_ref[0, :, at], query_ref[0, :, at])
        out_ref[0, head : head + 1, :] = jnp.maximum(
            peak_ref[0, head : head + 1, :], jnp.max(scores, axis=0, keepdims=True)
        )


def group_peaks(first, queries, new_keys, peaks):
    requests, tokens, width = queries.shape
    tok_block = new_keys.shape[1]
    heads = width // HEAD_DIM
    one = lambda rows: pl.BlockSpec((1, rows, width), lambda r, *_: (r, 0, 0))
    stat = pl.BlockSpec((1, heads, tokens), lambda r, *_: (r, 0, 0))
    return pl.pallas_call(
        peak_kernel,
        grid_spec=pltpu.PrefetchScalarGridSpec(
            num_scalar_prefetch=1,
            grid=(requests,),
            in_specs=[one(tokens), one(tok_block), stat],
            out_specs=stat,
        ),
        out_shape=jax.ShapeDtypeStruct(peaks.shape, jnp.float32),
        compiler_params=pltpu.CompilerParams(vmem_limit_bytes=32 * 1024 * 1024),
        cost_estimate=pl.CostEstimate(
            flops=2 * requests * tokens * tok_block * width,
            bytes_accessed=2 * requests * width * tokens,
            transcendentals=0,
        ),
        name="group_peaks",
    )(first, queries, new_keys, peaks)


def finish_kernel(slots, first_ref, place_ref, *refs):
    query_ref, key_ref, value_ref, cache_ref, peak_ref, total_ref, best_ref = refs[:7]
    sum_ref, *part_refs = refs[7:-1]
    joined_ref = refs[-1]
    tok_block = key_ref.shape[1]
    for head in range(query_ref.shape[2] // HEAD_DIM):
        at = slice(head * HEAD_DIM, (head + 1) * HEAD_DIM)
        row = slice(head, head + 1)
        scores = group_scores(first_ref[0], key_ref[0, :, at], query_ref[0, :, at])
        best = best_ref[0, row, :]
        weights = jnp.exp2((scores - best) * EXP2_SCALE)
        rescale = jnp.exp2((peak_ref[0, row, :] - best) * EXP2_SCALE)
        sum_ref[0, row, :] = total_ref[0, row, :] * rescale + jnp.sum(
            weights, axis=0, keepdims=True
        )
        joined = cache_ref[0, at, :].astype(jnp.float32) * rescale + dot_tn(
            value_ref[0, :, at], weights.astype(jnp.bfloat16)
        )
        joined_ref[:, at] = joined.T.astype(jnp.bfloat16)
    for slot in range(slots):
        start = pl.multiple_of(place_ref[slot] * tok_block, tok_block)
        part_refs[slot][0] = joined_ref[pl.ds(start, tok_block), :]


def finish_part(begin, requests, first, places, queries, new_keys, new_values, cached, peaks, totals, best):
    tokens, width = queries.shape[1:]
    tok_block = new_keys.shape[1]
    slots = tokens // tok_block
    heads = width // HEAD_DIM
    one = lambda rows: pl.BlockSpec((1, rows, width), lambda r, *_: (r + begin, 0, 0))
    stat = pl.BlockSpec((1, heads, tokens), lambda r, *_: (r + begin, 0, 0))
    return pl.pallas_call(
        functools.partial(finish_kernel, slots),
        grid_spec=pltpu.PrefetchScalarGridSpec(
            num_scalar_prefetch=2,
            grid=(requests,),
            in_specs=[
                one(tokens),
                one(tok_block),
                one(tok_block),
                pl.BlockSpec((1, width, tokens), lambda r, *_: (r + begin, 0, 0)),
                stat,
                stat,
                stat,
            ],
            out_specs=[pl.BlockSpec((1, heads, tokens), lambda r, *_: (r, 0, 0))]
            + [pl.BlockSpec((1, tok_block, width), lambda r, *_: (r, 0, 0))] * slots,
            scratch_shapes=[pltpu.VMEM((tokens, width), jnp.bfloat16)],
        ),
        out_shape=[jax.ShapeDtypeStruct((requests, heads, tokens), jnp.float32)]
        + [jax.ShapeDtypeStruct((requests, tok_block, width), jnp.bfloat16)] * slots,
        compiler_params=pltpu.CompilerParams(vmem_limit_bytes=48 * 1024 * 1024),
        cost_estimate=pl.CostEstimate(
            flops=4 * requests * tokens * tok_block * width,
            bytes_accessed=6 * requests * width * tokens,
            transcendentals=requests * tokens * tok_block * heads,
        ),
        name="finish_part",
    )(first, places, queries, new_keys, new_values, cached, peaks, totals, best)


def head_sum(terms, head_count, head_index):
    if head_count != 4:
        return lax.psum_scatter(
            terms.astype(jnp.bfloat16), "head", scatter_dimension=1, tiled=True
        ).astype(jnp.float32)
    width = terms.shape[1] // 4
    chunk = lambda index: lax.dynamic_slice_in_dim(terms, index * width, width, 1)
    core, column = head_index % 2, head_index // 2
    near, far = 2 * column, 2 * (1 - column)
    got = lax.ppermute(
        jnp.concatenate([chunk(near + 1 - core), chunk(far + 1 - core)], axis=1).astype(
            jnp.bfloat16
        ),
        "head",
        [(h, h ^ 1) for h in range(4)],
    ).astype(jnp.float32)
    keep = chunk(near + core) + got[:, :width]
    give = chunk(far + core) + got[:, width:]
    return keep + lax.ppermute(
        give.astype(jnp.bfloat16), "head", [(h, h ^ 2) for h in range(4)]
    ).astype(jnp.float32)


def entry_states(through, local_state, base, seq_index, seq_count):
    factor = through[:, :, None]
    if seq_count != 8:
        entry = base
        for turn in range(seq_count - 1):
            leaving = (factor * entry + local_state).astype(jnp.bfloat16)
            entry = entry + lax.ppermute(leaving, "seq", [(turn, turn + 1)]).astype(jnp.float32)
        return entry
    swap = [(i, i ^ 1) for i in range(8)]
    other_state = lax.ppermute(local_state.astype(jnp.bfloat16), "seq", swap).astype(jnp.float32)
    other_factor = lax.ppermute(through, "seq", swap)[:, :, None]
    is_first = seq_index % 2 == 0
    first_state = jnp.where(is_first, local_state, other_state)
    second_state = jnp.where(is_first, other_state, local_state)
    first_factor = jnp.where(is_first, factor, other_factor)
    second_factor = jnp.where(is_first, other_factor, factor)
    pair_state = second_factor * first_state + second_state
    pair_factor = first_factor * second_factor
    entry = base
    for turn in range(3):
        leaving = (pair_factor * entry + pair_state).astype(jnp.bfloat16)
        route = [(2 * turn + y, 2 * turn + 2 + y) for y in range(2)]
        entry = entry + lax.ppermute(leaving, "seq", route).astype(jnp.float32)
    return jnp.where(is_first, entry, first_factor * entry + first_state)


def shards(
    block_input,
    lengths,
    cache_keys,
    cache_values,
    w_query,
    w_key,
    w_value,
    w_attn_out,
    norm_gain,
    w_in,
    w_bc,
    w_dt,
    dt_bias,
    a_log,
    d_skip,
    gated_gain,
    w_out,
    ssm_init,
):
    requests, tok_block, _ = block_input.shape
    seq_count = lax.axis_size("seq")
    seq_index = lax.axis_index("seq")
    head_count = lax.axis_size("head")
    head_index = lax.axis_index("head")
    local_att = w_query.shape[1]
    local_heads = local_att // HEAD_DIM
    cache_block = cache_keys.shape[1]
    rows = w_query.shape[0]
    tokens = requests * tok_block
    flat_input = block_input.reshape(tokens, block_input.shape[2])

    order = ring_order(seq_count)
    place = [order.index(i) for i in range(seq_count)]
    order_table = jnp.asarray(order, jnp.int32)
    ring_index = jnp.asarray(place, jnp.int32)[seq_index]
    origin = lambda offset: order_table[(ring_index - offset + seq_count) % seq_count]

    def project(pieces):
        total = None
        for offset, row, piece in pieces:
            start = origin(offset) * rows + row
            part = lax.dynamic_slice_in_dim(flat_input, start, piece.shape[0], 1)
            term = jnp.dot(part, piece, preferred_element_type=jnp.float32)
            total = term if total is None else total + term
        return total

    positions = (
        lengths[:, None] + seq_index * tok_block + jnp.arange(tok_block, dtype=jnp.int32)[None, :]
    ).reshape(tokens)
    half_dim = HEAD_DIM // 2
    frequency = jnp.exp(
        jnp.arange(half_dim, dtype=jnp.float32) * (-2.0 * math.log(10000.0) / HEAD_DIM)
    )
    angles = positions.astype(jnp.float32)[:, None] * frequency
    cosine = jnp.cos(angles)
    sine = jnp.sin(angles)
    cosine = jnp.concatenate([cosine, cosine], axis=1)
    sine = jnp.concatenate([-sine, sine], axis=1)

    query_pieces = ring_gather(w_query, order)
    key_pieces = ring_gather(after(w_key, query_pieces[-1][2]), order)
    value_pieces = ring_gather(after(w_value, key_pieces[-1][2]), order)
    queries = rope(project(query_pieces), cosine, sine).reshape(requests, tok_block, local_att)
    new_keys = rope(project(key_pieces), cosine, sine).reshape(requests, tok_block, local_att)
    new_values = project(value_pieces).astype(jnp.bfloat16).reshape(requests, tok_block, local_att)

    half = seq_count // 2
    query_ring = ring_gather(queries, order)
    offsets = [0] + [sign * step for step in range(1, half) for sign in (1, -1)] + [half]
    query_slots = [piece for _, _, piece in query_ring[:-2]]
    query_slots.append(jnp.concatenate([query_ring[-2][2], query_ring[-1][2]], axis=0))
    places = jnp.stack([origin(offset) for offset in offsets]).astype(jnp.int32)
    live = jnp.clip(lengths - seq_index * cache_block, 0, cache_block).astype(jnp.int32)
    first = (seq_index * tok_block).astype(jnp.int32).reshape(1)
    all_queries, cached, peaks, totals = cache_part(
        places, live, query_slots, cache_keys, cache_values
    )
    best = lax.pmax(group_peaks(first, all_queries, new_keys, peaks), "seq")

    own = lambda stat: lax.dynamic_slice_in_dim(stat, seq_index * tok_block, tok_block, 2)
    greatest_logit = jnp.transpose(own(best), (0, 2, 1)) * SCALE
    group = requests // GROUPS
    attended = []
    for begin in range(0, requests, group):
        sums, *parts = finish_part(
            begin, group, first, places, all_queries, new_keys, new_values, cached, peaks, totals, best
        )
        denominator = jnp.transpose(own(lax.psum(sums, "seq")), (0, 2, 1))
        terms = {-offset: part for offset, part in zip(offsets, parts)}
        terms[half] = terms[-half]
        numerator = ring_sum(terms, order).reshape(group, tok_block, local_heads, HEAD_DIM)
        attended.append((numerator / denominator[..., None]).astype(jnp.bfloat16))
    attended = jnp.concatenate(attended, axis=0).reshape(tokens, local_att)
    attn_terms = jnp.dot(attended, w_attn_out, preferred_element_type=jnp.float32)

    hidden = block_input[:, :, :D].astype(jnp.float32)
    normed = (
        hidden * lax.rsqrt(jnp.mean(hidden * hidden, axis=-1, keepdims=True) + 1e-05) * norm_gain
    ).astype(jnp.bfloat16)
    flat_normed = normed.reshape(tokens, D)
    local_inner = w_in.shape[2]
    local_mheads = local_inner // MHEAD_DIM
    gate_inner = jnp.dot(
        flat_normed, w_in.reshape(D, 2 * local_inner), preferred_element_type=jnp.float32
    ).reshape(requests, tok_block, 2, local_inner)
    gate_part = gate_inner[:, :, 0]
    inner_heads = jax.nn.silu(gate_inner[:, :, 1]).reshape(
        requests, tok_block, local_mheads, MHEAD_DIM
    )
    bc_part = jnp.dot(flat_normed, w_bc, preferred_element_type=jnp.float32).reshape(
        requests, tok_block, 2 * STATE
    )
    input_map = bc_part[..., :STATE]
    output_map = bc_part[..., STATE:]
    step_size = jax.nn.softplus(
        jnp.dot(flat_normed, w_dt, preferred_element_type=jnp.float32).reshape(
            requests, tok_block, local_mheads
        )
        + dt_bias
    )
    log_decay = -step_size * jnp.exp(a_log)
    cumulative = jnp.cumsum(log_decay, axis=1)
    causal = jnp.arange(tok_block)[None, :] <= jnp.arange(tok_block)[:, None]
    head_major = jnp.transpose(cumulative, (0, 2, 1))
    differences = head_major[:, :, :, None] - head_major[:, :, None, :]
    decays = jnp.where(causal, jnp.exp(jnp.where(causal, differences, 0.0)), 0.0)
    contact = jnp.einsum("rtn,run->rtu", output_map, input_map, precision=lax.Precision.HIGHEST)
    mixing = decays * contact[:, None] * jnp.transpose(step_size, (0, 2, 1))[:, :, None, :]
    intra_part = jnp.einsum("rhtu,ruhp->rthp", mixing, inner_heads, precision=lax.Precision.HIGHEST)
    tail_decay = jnp.exp(cumulative[:, -1:, :] - cumulative) * step_size
    local_state = jnp.einsum(
        "ruhp,run->rhpn",
        inner_heads * tail_decay[..., None],
        input_map,
        precision=lax.Precision.HIGHEST,
    ).reshape(requests, local_mheads, MHEAD_DIM * STATE)
    through = jnp.exp(cumulative[:, -1, :])
    base = jnp.where(seq_index == 0, ssm_init, 0.0)
    if seq_count == 8:
        base = jnp.where(seq_index < 2, ssm_init, 0.0)
    incoming = entry_states(through, local_state, base, seq_index, seq_count)
    entry_state = incoming.reshape(requests, local_mheads, MHEAD_DIM, STATE)
    inter_part = (
        jnp.einsum("rhpn,rtn->rthp", entry_state, output_map, precision=lax.Precision.HIGHEST)
        * jnp.exp(cumulative)[..., None]
    )
    read_out = intra_part + inter_part + d_skip[:, None] * inner_heads
    chain_states = (through[:, :, None] * incoming + local_state)[:, None]
    mixed_inner = read_out.reshape(requests, tok_block, local_inner) * jax.nn.silu(gate_part)
    squares = lax.psum(jnp.sum(mixed_inner * mixed_inner, axis=-1).reshape(1, tokens), "head")
    gated = (mixed_inner * gated_gain).astype(jnp.bfloat16)
    mamba_terms = jnp.dot(
        gated.reshape(tokens, local_inner), w_out, preferred_element_type=jnp.float32
    ) * lax.rsqrt(squares.reshape(tokens, 1) / D_INNER + 1e-05)

    summed = head_sum(attn_terms + mamba_terms, head_count, head_index)
    local_width = D // head_count
    residual = lax.dynamic_slice_in_dim(
        hidden.reshape(tokens, D), head_index * local_width, local_width, 1
    )
    mixed = (residual + summed).astype(jnp.bfloat16).reshape(requests, tok_block, local_width)
    return (mixed, new_keys, new_values, chain_states, greatest_logit)


def solution(mesh):
    placed = (
        P(None, "seq", None),
        P(),
        P(None, "seq", "head"),
        P(None, "seq", "head"),
        P("seq", "head"),
        P("seq", "head"),
        P("seq", "head"),
        P("head", None),
        P(),
        P(None, None, "head"),
        P(),
        P(None, "head"),
        P("head"),
        P("head"),
        P("head"),
        P("head"),
        P("head", None),
        P(None, "head", None),
    )
    return jax.shard_map(
        shards,
        mesh=mesh,
        in_specs=placed,
        out_specs=(
            P(None, "seq", "head"),
            P(None, "seq", "head"),
            P(None, "seq", "head"),
            P(None, "seq", "head", None),
            P(None, "seq", "head"),
        ),
        check_vma=False,
    )
```

time: 1340 us -> 717 us (0.54)
  waiting for transfers between devices: 556 us -> 248 us
  local copies, waits for them, and re-layouts: 232 us -> 81.4 us
  starting transfers between devices: 273 us -> 126 us
  Pallas kernels: 0 us -> 73.6 us
  matrix products: 148 us -> 92.8 us
  other arithmetic: 98.3 us -> 52.2 us
    all_gather x4 -> x0, waiting for transfers between devices: 333 us -> none  [the longest x1 128 us: shards(): lax.all_gather(w_query, 'seq', axis=0, tiled=True)]
    ppermute x7 -> x55, starting transfers between devices: 259 us -> 125 us  [the longest x48 116 us: ring_step(): return lax.ppermute(block, 'seq', route)]
    pallas_call x0 -> x6, Pallas kernels: none -> 73.6 us  [the longest x1 39.9 us: cache_part(): pl.pallas_call(functools.partial(cache_kernel, slots), grid_spec=pltpu.Pr...]
    dot_general x6 -> x28, matrix products: 106 us -> 46 us  [the longest x27 43.6 us: project(): term = jnp.dot(part, piece, preferred_element_type=jnp.float32)]
    reduce_sum x3 -> x0, other arithmetic: 35 us -> none  [the longest x1 25.6 us: shards(): totals = jnp.sum(weights, axis=3)]
    pmax x0 -> x1, waiting for transfers between devices: none -> 33.1 us  [shards(): best = lax.pmax(group_peaks(first, all_queries, new_keys, peaks), 'seq')]
    mul x2 -> x0, local copies, waits for them, and re-layouts: 27.9 us -> none  [shards(): received[0].reshape(seq_count, requests, tok_block, local_heads, HEAD_DIM)]
    unnamed x68 -> x141, local copies, waits for them, and re-layouts: 50.5 us -> 25.6 us
  transfers between devices with their start and end apart: 16 -> 57, of which waited for: 12 -> 27; matrix products, arithmetic and copies ran while one was open for 35% -> 28% of each run, Pallas kernels for 0% -> 9%
where the time goes in v1:
time: 717 us; the launch traced here: 705 us
  waiting for transfers between devices  248 us (35%)
  starting transfers between devices  126 us (18%)
  matrix products  92.8 us (13%)
  local copies, waits for them, and re-layouts  81.4 us (11%)
  Pallas kernels  73.6 us (10%)
  other arithmetic  52.2 us (7%)
  between operations  25.7 us (4%)
    ppermute x48, waiting for transfers between devices, ring_step(): return lax.ppermute(block, 'seq', route)  179 us
    ppermute x48, starting transfers between devices, ring_step(): return lax.ppermute(block, 'seq', route)  116 us
    dot_general x27, matrix products, project(): term = jnp.dot(part, piece, preferred_element_type=jnp.float32)  43.6 us
    pallas_call x1, Pallas kernels, cache_part(): pl.pallas_call(functools.partial(cache_kernel, slots), grid_spec=pltpu.Pr...  39.9 us
    pmax x1, waiting for transfers between devices, shards(): best = lax.pmax(group_peaks(first, all_queries, new_keys, peaks), 'seq')  33.1 us
    unnamed x141, local copies, waits for them, and re-layouts  25.6 us
    pallas_call x2, Pallas kernels, finish_part(): pl.pallas_call(functools.partial(finish_kernel, slots), grid_spec=pltpu.P...  20.7 us
  transfers between devices with their start and end apart: 57, of which 27 were waited for; matrix products, arithmetic and copies ran while one was open for 28% of the time, Pallas kernels for 9%

profile of v1, /device:TPU:0, one launch (start us, length us, event | category | flops | bytes accessed | tf_op | source)
XLA Modules:
  0.0 705.4 jit_solution(16775347983313542376)
XLA Ops:
  16.0 6.3 fusion.144
  22.5 10.3 %copy.58 = bf16[256,8,2,1024]{3,1,2,0:T(8,128)(2,1)} copy(bf16[256,8,2,1024]{3,2,1,0:T(2,128)(2,1)} %bitcast.210) | data formatting | bytes 16777216
  32.8 12.3 %copy.39 = bf16[2048,2048]{1,0:T(8,128)(2,1)} copy(bf16[2048,2048]{0,1:T(8,128)(2,1)} %bitcast.206) | data formatting | bytes 16777216 | tf_op jit(solution)/shard_map/dot_general | solution.py:434
  45.1 7.7 %fusion.11 = f32[8,64,2,1024]{3,1,2,0:T(8,128)S(1)} fusion(bf16[2,1024,2048,1]{2,1,0,3:T(8,128)(2,1)} %bitcast.211, f32[2048]{0:T(1024)S(1)} %copy-done.64, f32[8,64]{1,0:T(8,128)S(1)} %add_rsqrt_fusion, bf16[8,64,4096]{2,1,0:T(8,128)(2,1)} %param.20), kind=kOutput, calls=%fused_computation.19 | convolution fusion | flops 4299161600 | bytes 14690304 | tf_op jit(solution)/shard_map/dot_general | solution.py:434
  88.7 8.1 %collective-permute-done.48 = f32[8,16]{1,0:T(8,128)S(1)} collective-permute-done((f32[8,16]{1,0:T(8,128)S(1)}, f32[8,16]{1,0:T(8,128)S(1)}, u32[]{:S(2)}, u32[]{:S(2)}) %collective-permute-start.48) | collective-permute-done | bytes 544 | tf_op jit(solution)/shard_map/ppermute | solution.py:315
  121.9 11.7 %fusion.3 = f32[8,16,64,64]{3,2,1,0:T(8,128)} fusion(f32[8,16,64]{2,1,0:T(8,128)} %get-tuple-element.81, f32[8,64,64]{2,1,0:T(8,128)} %fusion.88, f32[8,16,64]{2,1,0:T(8,128)S(1)} %copy.43, pred[64,64]{1,0:T(8,128)(4,1)} %iota_compare_fusion, f32[8,64,16,64]{1,3,2,0:T(8,128)} %bitcast.214), kind=kOutput, calls=%fused_computation.6 | convolution fusion | flops 407371776 | bytes 4395008 | tf_op jit(solution)/shard_map/rhtu,ruhp->rthp/dot_general | solution.py:460
  138.5 18.7 %collective-permute-done.3 = bf16[512,1024]{1,0:T(8,128)(2,1)S(1)} collective-permute-done((bf16[512,1024]{1,0:T(8,128)(2,1)}, bf16[512,1024]{1,0:T(8,128)(2,1)S(1)}, u32[]{:S(2)}, u32[]{:S(2)}) %collective-permute-start.3) | collective-permute-done | bytes 1048608 | tf_op jit(solution)/shard_map/ppermute | solution.py:35
  165.0 15.5 %collective-permute-done.5 = bf16[512,1024]{1,0:T(8,128)(2,1)S(1)} collective-permute-done((bf16[512,1024]{1,0:T(8,128)(2,1)S(1)}, bf16[512,1024]{1,0:T(8,128)(2,1)S(1)}, u32[]{:S(2)}, u32[]{:S(2)}) %collective-permute-start.5) | collective-permute-done | bytes 1048608 | tf_op jit(solution)/shard_map/ppermute | solution.py:35
  182.1 19.7 %collective-permute-start.6 = (bf16[256,1024]{1,0:T(8,128)(2,1)S(1)}, bf16[256,1024]{1,0:T(8,128)(2,1)S(1)}, u32[]{:S(2)}, u32[]{:S(2)}) collective-permute-start(bf16[256,1024]{1,0:T(8,128)(2,1)S(1)} %slice.113), channel_id=1, source_target_pairs={{0,8},{8,16},{16,24},{24,28},{28,20},{20,12},{12,4},{4,0},{1,9},{9... | collective-permute-start | bytes 1572872 | tf_op jit(solution)/shard_map/ppermute | solution.py:35
  227.4 7.7 %collective-permute-done.17 = bf16[512,1024]{1,0:T(8,128)(2,1)} collective-permute-done((bf16[512,1024]{1,0:T(8,128)(2,1)}, bf16[512,1024]{1,0:T(8,128)(2,1)}, u32[]{:S(2)}, u32[]{:S(2)}) %collective-permute-start.17) | collective-permute-done | bytes 1048608 | tf_op jit(solution)/shard_map/ppermute | solution.py:35
  247.9 9.6 %collective-permute-done.9.refs_2_ = bf16[8,64,1024]{2,1,0:T(8,128)(2,1)S(1)} collective-permute-done((bf16[8,64,1024]{2,1,0:T(8,128)(2,1)}, bf16[8,64,1024]{2,1,0:T(8,128)(2,1)S(1)}, u32[]{:S(2)}, u32[]{:S(2)}) %collective-permute-start.9) | collective-permute-done | bytes 1048608 | tf_op jit(solution)/shard_map/ppermute | solution.py:35
  260.0 9.2 %collective-permute-done.16 = bf16[512,1024]{1,0:T(8,128)(2,1)} collective-permute-done((bf16[512,1024]{1,0:T(8,128)(2,1)}, bf16[512,1024]{1,0:T(8,128)(2,1)}, u32[]{:S(2)}, u32[]{:S(2)}) %collective-permute-start.16) | collective-permute-done | bytes 1048608 | tf_op jit(solution)/shard_map/ppermute | solution.py:35
  270.3 9.6 %collective-permute-done.19 = bf16[512,1024]{1,0:T(8,128)(2,1)} collective-permute-done((bf16[512,1024]{1,0:T(8,128)(2,1)}, bf16[512,1024]{1,0:T(8,128)(2,1)}, u32[]{:S(2)}, u32[]{:S(2)}) %collective-permute-start.19) | collective-permute-done | bytes 1048608 | tf_op jit(solution)/shard_map/ppermute | solution.py:35
  282.5 10.8 %multiply_reduce_fusion = (f32[8,64]{1,0:T(8,128)S(1)}, f32[8,64,16,64]{1,3,2,0:T(8,128)}) fusion(f32[8,64,16,64]{1,3,2,0:T(8,128)} %bitcast.217, f32[8,64,16,64]{1,3,2,0:T(8,128)} %bitcast.215, f32[16]{0:T(128)S(1)} %copy-done.67, f32[8,64,16]{1,2,0:T(8,128)S(1)} %copy.46, f32[8,16,64,64]{3,2,1,0:T(8,128)} %reshape.188, f32[8,64,128]{2,1,0:T(8,128)S(1)} %copy-done.46, ...), kind=kOutput, calls=%fused_computation.3 | convolution fusion | flops 410516992 | bytes 10782784 | tf_op jit(solution)/shard_map/rhpn,rtn->rthp/dot_general | solution.py:475
  303.8 6.2 psum.23
  323.9 17.1 %collective-permute-start.23 = (bf16[256,1024]{1,0:T(8,128)(2,1)S(1)}, bf16[256,1024]{1,0:T(8,128)(2,1)S(1)}, u32[]{:S(2)}, u32[]{:S(2)}) collective-permute-start(bf16[256,1024]{1,0:T(8,128)(2,1)S(1)} %slice.118), channel_id=1, source_target_pairs={{0,4},{8,0},{16,8},{24,16},{28,24},{20,28},{12,20},{4,12},{1,5},{9... | collective-permute-start | bytes 1572872 | tf_op jit(solution)/shard_map/ppermute | solution.py:35
  344.9 9.4 %collective-permute-done.23 = bf16[256,1024]{1,0:T(8,128)(2,1)S(1)} collective-permute-done((bf16[256,1024]{1,0:T(8,128)(2,1)S(1)}, bf16[256,1024]{1,0:T(8,128)(2,1)S(1)}, u32[]{:S(2)}, u32[]{:S(2)}) %collective-permute-start.23) | collective-permute-done | bytes 524320 | tf_op jit(solution)/shard_map/ppermute | solution.py:35
  354.4 17.4 %collective-permute-start.25 = (bf16[512,1024]{1,0:T(8,128)(2,1)S(1)}, bf16[512,1024]{1,0:T(8,128)(2,1)S(1)}, u32[]{:S(2)}, u32[]{:S(2)}) collective-permute-start(bf16[512,1024]{1,0:T(8,128)(2,1)S(1)} %copy-done.50), channel_id=1, source_target_pairs={{0,4},{8,0},{16,8},{24,16},{28,24},{20,28},{12,20},{4,12},{1,5},{9... | collective-permute-start | bytes 3145736 | tf_op jit(solution)/shard_map/ppermute | solution.py:35
  382.0 27.5 %collective-permute-done.22 = bf16[256,1024]{1,0:T(8,128)(2,1)S(1)} collective-permute-done((bf16[256,1024]{1,0:T(8,128)(2,1)S(1)}, bf16[256,1024]{1,0:T(8,128)(2,1)S(1)}, u32[]{:S(2)}, u32[]{:S(2)}) %collective-permute-start.22) | collective-permute-done | bytes 524320 | tf_op jit(solution)/shard_map/ppermute | solution.py:35
  417.6 10.7 %collective-permute-done.24 = bf16[512,1024]{1,0:T(8,128)(2,1)} collective-permute-done((bf16[512,1024]{1,0:T(8,128)(2,1)S(1)}, bf16[512,1024]{1,0:T(8,128)(2,1)}, u32[]{:S(2)}, u32[]{:S(2)}) %collective-permute-start.24) | collective-permute-done | bytes 1048608 | tf_op jit(solution)/shard_map/ppermute | solution.py:35
  428.3 39.9 %cache_part.1 = (bf16[8,512,1024]{2,1,0:T(8,128)(2,1)}, bf16[8,1024,512]{2,1,0:T(8,128)(2,1)}, f32[8,8,512]{2,1,0:T(8,128)S(1)}, f32[8,8,512]{2,1,0:T(8,128)S(1)}) custom-call(s32[8]{0:T(128)S(1)} %stack.3.place_ref, s32[8]{0:T(128)S(1)} %get-tuple-element.72.live_ref, bf16[8,64,1024]{2,1,0:T(8,128)(2,1)S(1)} %bitcast.178, ...), custom_call_target="tpu_custom_call" | custom-call | flops 8589934592 | bytes 41943040 | tf_op jit(solution)/shard_map/cache_part/pallas_call | solution.py:149
  498.1 13.5 %collective-permute-done.28 = bf16[512,1024]{1,0:T(8,128)(2,1)S(1)} collective-permute-done((bf16[512,1024]{1,0:T(8,128)(2,1)}, bf16[512,1024]{1,0:T(8,128)(2,1)S(1)}, u32[]{:S(2)}, u32[]{:S(2)}) %collective-permute-start.28) | collective-permute-done | bytes 1048608 | tf_op jit(solution)/shard_map/ppermute | solution.py:35
  514.3 7.8 %collective-permute-done.30 = bf16[256,1024]{1,0:T(8,128)(2,1)S(1)} collective-permute-done((bf16[256,1024]{1,0:T(8,128)(2,1)S(1)}, bf16[256,1024]{1,0:T(8,128)(2,1)S(1)}, u32[]{:S(2)}, u32[]{:S(2)}) %collective-permute-start.30) | collective-permute-done | bytes 524320 | tf_op jit(solution)/shard_map/ppermute | solution.py:35
  524.8 33.1 %all-reduce.4.cloned.1.call-done.refs_6_ = f32[8,8,512]{2,1,0:T(8,128)} async-done(((f32[8,8,512]{2,1,0:T(8,128)}), f32[8,8,512]{2,1,0:T(8,128)}) %all-reduce.4.cloned.1.call-update) | async-done | bytes 131088 | tf_op jit(solution)/shard_map/pmax | solution.py:409
  558.8 10.3 %finish_part.3 = (f32[4,8,512]{2,1,0:T(8,128)}, bf16[4,64,1024]{2,1,0:T(8,128)(2,1)S(1)}, bf16[4,64,1024]{2,1,0:T(8,128)(2,1)S(1)}, bf16[4,64,1024]{2,1,0:T(8,12...) custom-call(s32[1]{0:T(128)} %bitcast.1.first_ref, ...), custom_call_target="tpu_custom_call" | custom-call | flops 536870912 | bytes 12582912 | tf_op jit(solution)/shard_map/finish_part/pallas_call | solution.py:252
  573.0 10.3 %finish_part.2 = (f32[4,8,512]{2,1,0:T(8,128)}, bf16[4,64,1024]{2,1,0:T(8,128)(2,1)S(1)}, bf16[4,64,1024]{2,1,0:T(8,128)(2,1)S(1)}, bf16[4,64,1024]{2,1,0:T(8,12...) custom-call(s32[1]{0:T(128)} %bitcast.1.first_ref, ...), custom_call_target="tpu_custom_call" | custom-call | flops 536870912 | bytes 12582912 | tf_op jit(solution)/shard_map/finish_part/pallas_call | solution.py:252
  601.2 8.4 %collective-permute-done.45 = bf16[4,64,1024]{2,1,0:T(8,128)(2,1)S(1)} collective-permute-done((bf16[4,64,1024]{2,1,0:T(8,128)(2,1)S(1)}, bf16[4,64,1024]{2,1,0:T(8,128)(2,1)S(1)}, u32[]{:S(2)}, u32[]{:S(2)}) %collective-permute-start.45) | collective-permute-done | bytes 524320 | tf_op jit(solution)/shard_map/ppermute | solution.py:35
  612.4 8.7 %collective-permute-done.37 = bf16[4,64,1024]{2,1,0:T(8,128)(2,1)S(1)} collective-permute-done((bf16[4,64,1024]{2,1,0:T(8,128)(2,1)S(1)}, bf16[4,64,1024]{2,1,0:T(8,128)(2,1)S(1)}, u32[]{:S(2)}, u32[]{:S(2)}) %collective-permute-start.37) | collective-permute-done | bytes 524320 | tf_op jit(solution)/shard_map/ppermute | solution.py:35
  624.1 8.4 %collective-permute-done.46 = bf16[4,64,1024]{2,1,0:T(8,128)(2,1)S(1)} collective-permute-done((bf16[4,64,1024]{2,1,0:T(8,128)(2,1)S(1)}, bf16[4,64,1024]{2,1,0:T(8,128)(2,1)S(1)}, u32[]{:S(2)}, u32[]{:S(2)}) %collective-permute-start.46) | collective-permute-done | bytes 524320 | tf_op jit(solution)/shard_map/ppermute | solution.py:35
  636.3 7.9 %collective-permute-done.38 = bf16[4,64,1024]{2,1,0:T(8,128)(2,1)S(1)} collective-permute-done((bf16[4,64,1024]{2,1,0:T(8,128)(2,1)S(1)}, bf16[4,64,1024]{2,1,0:T(8,128)(2,1)S(1)}, u32[]{:S(2)}, u32[]{:S(2)}) %collective-permute-start.38) | collective-permute-done | bytes 524320 | tf_op jit(solution)/shard_map/ppermute | solution.py:35
  648.4 13.8 %all-reduce.6.cloned.1.call-done = (f32[4,8,512]{2,1,0:T(8,128)}, f32[4,8,512]{2,1,0:T(8,128)}) async-done(((f32[4,8,512]{2,1,0:T(8,128)}, f32[4,8,512]{2,1,0:T(8,128)}), (f32[4,8,512]{2,1,0:T(8,128)}, f32[4,8,512]{2,1,0:T(8,128)})) %all-reduce.6.cloned.1.call-update) | async-done | bytes 131088 | tf_op jit(solution)/shard_map/psum | solution.py:419
  685.3 10.5 %collective-permute-done.54 = bf16[512,512]{1,0:T(8,128)(2,1)S(1)} collective-permute-done((bf16[512,512]{1,0:T(8,128)(2,1)S(1)}, bf16[512,512]{1,0:T(8,128)(2,1)S(1)}, u32[]{:S(2)}, u32[]{:S(2)}) %collective-permute-start.54) | collective-permute-done | bytes 524320 | tf_op jit(solution)/shard_map/ppermute | solution.py:300
  (355 shorter events, 261.5 us)
Async XLA Ops:
  7.2 550.7 %all-reduce.4.cloned.1.call-start = ((), (), s32[]{:S(2)}) async-start(), calls=%async_computation | async-start | bytes 262144 | tf_op jit(solution)/shard_map/pmax | solution.py:409
  7.3 126.4 %collective-permute-start.1 = (bf16[512,1024]{1,0:T(8,128)(2,1)}, bf16[512,1024]{1,0:T(8,128)(2,1)}, u32[]{:S(2)}, u32[]{:S(2)}) collective-permute-start(bf16[512,1024]{1,0:T(8,128)(2,1)} %param.24), channel_id=1, source_target_pairs={{0,4},{8,0},{16,8},{24,16},{28,24},{20,28},{12,20},{4,12},{1,5},{9... | collective-permute-start | bytes 3145736 | tf_op jit(solution)/shard_map/ppermute | solution.py:35
  10.3 124.9 %collective-permute-start = (bf16[512,1024]{1,0:T(8,128)(2,1)}, bf16[512,1024]{1,0:T(8,128)(2,1)}, u32[]{:S(2)}, u32[]{:S(2)}) collective-permute-start(bf16[512,1024]{1,0:T(8,128)(2,1)} %param.24), channel_id=1, source_target_pairs={{0,8},{8,16},{16,24},{24,28},{28,20},{20,12},{12,4},{4,0},{1,9},{9... | collective-permute-start | bytes 3145736 | tf_op jit(solution)/shard_map/ppermute | solution.py:35
  100.6 35.1 %collective-permute-start.50 = (bf16[8,16,4096]{2,1,0:T(8,128)(2,1)}, bf16[8,16,4096]{2,1,0:T(8,128)(2,1)}, u32[]{:S(2)}, u32[]{:S(2)}) collective-permute-start(bf16[8,16,4096]{2,1,0:T(8,128)(2,1)} %add_convert_fusion.2), channel_id=1, source_target_pairs={{0,8},{4,12},{1,9},{5,13},{2,10},{6,14},{3,11},{7,15}} | collective-permute-start | bytes 3145736 | tf_op jit(solution)/shard_map/ppermute | solution.py:327
  137.8 64.1 %collective-permute-start.51 = (bf16[8,16,4096]{2,1,0:T(8,128)(2,1)S(1)}, bf16[8,16,4096]{2,1,0:T(8,128)(2,1)S(1)}, u32[]{:S(2)}, u32[]{:S(2)}) collective-permute-start(bf16[8,16,4096]{2,1,0:T(8,128)(2,1)S(1)} %add_convert_fusion.1), channel_id=1, source_target_pairs={{8,16},{12,20},{9,17},{13,21},{10,18},{14,22},{11,19},{15,23}} | collective-permute-start | bytes 3145736 | tf_op jit(solution)/shard_map/ppermute | solution.py:327
  180.5 27.3 %collective-permute-start.7 = (bf16[256,1024]{1,0:T(8,128)(2,1)S(1)}, bf16[256,1024]{1,0:T(8,128)(2,1)S(1)}, u32[]{:S(2)}, u32[]{:S(2)}) collective-permute-start(bf16[256,1024]{1,0:T(8,128)(2,1)S(1)} %slice.114), channel_id=1, source_target_pairs={{0,4},{8,0},{16,8},{24,16},{28,24},{20,28},{12,20},{4,12},{1,5},{9... | collective-permute-start | bytes 1572872 | tf_op jit(solution)/shard_map/ppermute | solution.py:35
  182.1 29.4 %collective-permute-start.6 = (bf16[256,1024]{1,0:T(8,128)(2,1)S(1)}, bf16[256,1024]{1,0:T(8,128)(2,1)S(1)}, u32[]{:S(2)}, u32[]{:S(2)}) collective-permute-start(bf16[256,1024]{1,0:T(8,128)(2,1)S(1)} %slice.113), channel_id=1, source_target_pairs={{0,8},{8,16},{16,24},{24,28},{28,20},{20,12},{12,4},{4,0},{1,9},{9... | collective-permute-start | bytes 1572872 | tf_op jit(solution)/shard_map/ppermute | solution.py:35
  205.4 32.1 %collective-permute-start.52 = (bf16[8,16,4096]{2,1,0:T(8,128)(2,1)}, bf16[8,16,4096]{2,1,0:T(8,128)(2,1)}, u32[]{:S(2)}, u32[]{:S(2)}) collective-permute-start(bf16[8,16,4096]{2,1,0:T(8,128)(2,1)} %add_convert_fusion), channel_id=1, source_target_pairs={{16,24},{20,28},{17,25},{21,29},{18,26},{22,30},{19,27},{23,31}} | collective-permute-start | bytes 3145736 | tf_op jit(solution)/shard_map/ppermute | solution.py:327
  207.8 27.2 %collective-permute-start.17 = (bf16[512,1024]{1,0:T(8,128)(2,1)}, bf16[512,1024]{1,0:T(8,128)(2,1)}, u32[]{:S(2)}, u32[]{:S(2)}) collective-permute-start(bf16[512,1024]{1,0:T(8,128)(2,1)} %param.25), channel_id=1, source_target_pairs={{0,4},{8,0},{16,8},{24,16},{28,24},{20,28},{12,20},{4,12},{1,5},{9... | collective-permute-start | bytes 3145736 | tf_op jit(solution)/shard_map/ppermute | solution.py:35
  219.8 27.8 %collective-permute-start.8 = (bf16[8,64,1024]{2,1,0:T(8,128)(2,1)}, bf16[8,64,1024]{2,1,0:T(8,128)(2,1)S(1)}, u32[]{:S(2)}, u32[]{:S(2)}) collective-permute-start(bf16[8,64,1024]{2,1,0:T(8,128)(2,1)} %bitcast.176), channel_id=1, source_target_pairs={{0,8},{8,16},{16,24},{24,28},{28,20},{20,12},{12,4},{4,0},{1,9},{9... | collective-permute-start | bytes 3145736 | tf_op jit(solution)/shard_map/ppermute | solution.py:35
  220.1 37.4 %collective-permute-start.9 = (bf16[8,64,1024]{2,1,0:T(8,128)(2,1)}, bf16[8,64,1024]{2,1,0:T(8,128)(2,1)S(1)}, u32[]{:S(2)}, u32[]{:S(2)}) collective-permute-start(bf16[8,64,1024]{2,1,0:T(8,128)(2,1)} %bitcast.177), channel_id=1, source_target_pairs={{0,4},{8,0},{16,8},{24,16},{28,24},{20,28},{12,20},{4,12},{1,5},{9... | collective-permute-start | bytes 3145736 | tf_op jit(solution)/shard_map/ppermute | solution.py:35
  222.4 46.8 %collective-permute-start.16 = (bf16[512,1024]{1,0:T(8,128)(2,1)}, bf16[512,1024]{1,0:T(8,128)(2,1)}, u32[]{:S(2)}, u32[]{:S(2)}) collective-permute-start(bf16[512,1024]{1,0:T(8,128)(2,1)} %param.25), channel_id=1, source_target_pairs={{0,8},{8,16},{16,24},{24,28},{28,20},{20,12},{12,4},{4,0},{1,9},{9... | collective-permute-start | bytes 3145736 | tf_op jit(solution)/shard_map/ppermute | solution.py:35
  235.0 44.9 %collective-permute-start.19 = (bf16[512,1024]{1,0:T(8,128)(2,1)}, bf16[512,1024]{1,0:T(8,128)(2,1)}, u32[]{:S(2)}, u32[]{:S(2)}) collective-permute-start(bf16[512,1024]{1,0:T(8,128)(2,1)} %collective-permute-done.17), channel_id=1, source_target_pairs={{0,4},{8,0},{16,8},{24,16},{28,24},{20,28},{12,20},{4,12},{1,5},{9... | collective-permute-start | bytes 3145736 | tf_op jit(solution)/shard_map/ppermute | solution.py:35
  247.6 66.4 %collective-permute-start.10 = (bf16[8,64,1024]{2,1,0:T(8,128)(2,1)S(1)}, bf16[8,64,1024]{2,1,0:T(8,128)(2,1)S(1)}, u32[]{:S(2)}, u32[]{:S(2)}) collective-permute-start(bf16[8,64,1024]{2,1,0:T(8,128)(2,1)S(1)} %collective-permute-done.8.refs_1_), channel_id=1, source_target_pairs={{0,8},{8,16},{16,24},{24,28},{28,20},{20,12},{12,4},{4,0},{1,9},{9... | collective-permute-start | bytes 3145736 | tf_op jit(solution)/shard_map/ppermute | solution.py:35
  257.5 58.4 %collective-permute-start.11 = (bf16[8,64,1024]{2,1,0:T(8,128)(2,1)S(1)}, bf16[8,64,1024]{2,1,0:T(8,128)(2,1)}, u32[]{:S(2)}, u32[]{:S(2)}) collective-permute-start(bf16[8,64,1024]{2,1,0:T(8,128)(2,1)S(1)} %collective-permute-done.9.refs_2_), channel_id=1, source_target_pairs={{0,4},{8,0},{16,8},{24,16},{28,24},{20,28},{12,20},{4,12},{1,5},{9... | collective-permute-start | bytes 3145736 | tf_op jit(solution)/shard_map/ppermute | solution.py:35
  269.2 47.4 %collective-permute-start.18 = (bf16[512,1024]{1,0:T(8,128)(2,1)}, bf16[512,1024]{1,0:T(8,128)(2,1)}, u32[]{:S(2)}, u32[]{:S(2)}) collective-permute-start(bf16[512,1024]{1,0:T(8,128)(2,1)} %collective-permute-done.16), channel_id=1, source_target_pairs={{0,8},{8,16},{16,24},{24,28},{28,20},{20,12},{12,4},{4,0},{1,9},{9... | collective-permute-start | bytes 3145736 | tf_op jit(solution)/shard_map/ppermute | solution.py:35
  280.0 42.9 %collective-permute-start.21 = (bf16[512,1024]{1,0:T(8,128)(2,1)}, bf16[512,1024]{1,0:T(8,128)(2,1)}, u32[]{:S(2)}, u32[]{:S(2)}) collective-permute-start(bf16[512,1024]{1,0:T(8,128)(2,1)} %collective-permute-done.19), channel_id=1, source_target_pairs={{0,4},{8,0},{16,8},{24,16},{28,24},{20,28},{12,20},{4,12},{1,5},{9... | collective-permute-start | bytes 3145736 | tf_op jit(solution)/shard_map/ppermute | solution.py:35
  314.1 62.2 %collective-permute-start.12 = (bf16[8,64,1024]{2,1,0:T(8,128)(2,1)S(1)}, bf16[8,64,1024]{2,1,0:T(8,128)(2,1)S(1)}, u32[]{:S(2)}, u32[]{:S(2)}) collective-permute-start(bf16[8,64,1024]{2,1,0:T(8,128)(2,1)S(1)} %collective-permute-done.10.refs_3_), channel_id=1, source_target_pairs={{0,8},{8,16},{16,24},{24,28},{28,20},{20,12},{12,4},{4,0},{1,9},{9... | collective-permute-start | bytes 3145736 | tf_op jit(solution)/shard_map/ppermute | solution.py:35
  315.9 57.8 %collective-permute-start.13 = (bf16[8,64,1024]{2,1,0:T(8,128)(2,1)}, bf16[8,64,1024]{2,1,0:T(8,128)(2,1)S(1)}, u32[]{:S(2)}, u32[]{:S(2)}) collective-permute-start(bf16[8,64,1024]{2,1,0:T(8,128)(2,1)} %collective-permute-done.11.refs_4_), channel_id=1, source_target_pairs={{0,4},{8,0},{16,8},{24,16},{28,24},{20,28},{12,20},{4,12},{1,5},{9... | collective-permute-start | bytes 3145736 | tf_op jit(solution)/shard_map/ppermute | solution.py:35
  316.6 60.7 %collective-permute-start.20 = (bf16[512,1024]{1,0:T(8,128)(2,1)}, bf16[512,1024]{1,0:T(8,128)(2,1)S(1)}, u32[]{:S(2)}, u32[]{:S(2)}) collective-permute-start(bf16[512,1024]{1,0:T(8,128)(2,1)} %collective-permute-done.18), channel_id=1, source_target_pairs={{0,8},{8,16},{16,24},{24,28},{28,20},{20,12},{12,4},{4,0},{1,9},{9... | collective-permute-start | bytes 3145736 | tf_op jit(solution)/shard_map/ppermute | solution.py:35
  323.9 30.5 %collective-permute-start.23 = (bf16[256,1024]{1,0:T(8,128)(2,1)S(1)}, bf16[256,1024]{1,0:T(8,128)(2,1)S(1)}, u32[]{:S(2)}, u32[]{:S(2)}) collective-permute-start(bf16[256,1024]{1,0:T(8,128)(2,1)S(1)} %slice.118), channel_id=1, source_target_pairs={{0,4},{8,0},{16,8},{24,16},{28,24},{20,28},{12,20},{4,12},{1,5},{9... | collective-permute-start | bytes 1572872 | tf_op jit(solution)/shard_map/ppermute | solution.py:35
  354.4 55.6 %collective-permute-start.25 = (bf16[512,1024]{1,0:T(8,128)(2,1)S(1)}, bf16[512,1024]{1,0:T(8,128)(2,1)S(1)}, u32[]{:S(2)}, u32[]{:S(2)}) collective-permute-start(bf16[512,1024]{1,0:T(8,128)(2,1)S(1)} %copy-done.50), channel_id=1, source_target_pairs={{0,4},{8,0},{16,8},{24,16},{28,24},{20,28},{12,20},{4,12},{1,5},{9... | collective-permute-start | bytes 3145736 | tf_op jit(solution)/shard_map/ppermute | solution.py:35
  373.7 42.7 %collective-permute-start.15 = (bf16[4,64,1024]{2,1,0:T(8,128)(2,1)S(1)}, bf16[4,64,1024]{2,1,0:T(8,128)(2,1)S(1)}, u32[]{:S(2)}, u32[]{:S(2)}) collective-permute-start(bf16[4,64,1024]{2,1,0:T(8,128)(2,1)S(1)} %slice.116), channel_id=1, source_target_pairs={{0,4},{8,0},{16,8},{24,16},{28,24},{20,28},{12,20},{4,12},{1,5},{9... | collective-permute-start | bytes 1572872 | tf_op jit(solution)/shard_map/ppermute | solution.py:35
  377.3 39.1 %collective-permute-start.14 = (bf16[4,64,1024]{2,1,0:T(8,128)(2,1)S(1)}, bf16[4,64,1024]{2,1,0:T(8,128)(2,1)S(1)}, u32[]{:S(2)}, u32[]{:S(2)}) collective-permute-start(bf16[4,64,1024]{2,1,0:T(8,128)(2,1)S(1)} %slice.115), channel_id=1, source_target_pairs={{0,8},{8,16},{16,24},{24,28},{28,20},{20,12},{12,4},{4,0},{1,9},{9... | collective-permute-start | bytes 1572872 | tf_op jit(solution)/shard_map/ppermute | solution.py:35
  377.4 32.1 %collective-permute-start.22 = (bf16[256,1024]{1,0:T(8,128)(2,1)S(1)}, bf16[256,1024]{1,0:T(8,128)(2,1)S(1)}, u32[]{:S(2)}, u32[]{:S(2)}) collective-permute-start(bf16[256,1024]{1,0:T(8,128)(2,1)S(1)} %slice.117), channel_id=1, source_target_pairs={{0,8},{8,16},{16,24},{24,28},{28,20},{20,12},{12,4},{4,0},{1,9},{9... | collective-permute-start | bytes 1572872 | tf_op jit(solution)/shard_map/ppermute | solution.py:35
  379.5 48.8 %collective-permute-start.24 = (bf16[512,1024]{1,0:T(8,128)(2,1)S(1)}, bf16[512,1024]{1,0:T(8,128)(2,1)}, u32[]{:S(2)}, u32[]{:S(2)}) collective-permute-start(bf16[512,1024]{1,0:T(8,128)(2,1)S(1)} %copy-done.50), channel_id=1, source_target_pairs={{0,8},{8,16},{16,24},{24,28},{28,20},{20,12},{12,4},{4,0},{1,9},{9... | collective-permute-start | bytes 3145736 | tf_op jit(solution)/shard_map/ppermute | solution.py:35
  410.0 58.2 %collective-permute-start.27 = (bf16[512,1024]{1,0:T(8,128)(2,1)S(1)}, bf16[512,1024]{1,0:T(8,128)(2,1)}, u32[]{:S(2)}, u32[]{:S(2)}) collective-permute-start(bf16[512,1024]{1,0:T(8,128)(2,1)S(1)} %collective-permute-done.25), channel_id=1, source_target_pairs={{0,4},{8,0},{16,8},{24,16},{28,24},{20,28},{12,20},{4,12},{1,5},{9... | collective-permute-start | bytes 3145736 | tf_op jit(solution)/shard_map/ppermute | solution.py:35
  428.3 59.3 %collective-permute-start.26 = (bf16[512,1024]{1,0:T(8,128)(2,1)}, bf16[512,1024]{1,0:T(8,128)(2,1)}, u32[]{:S(2)}, u32[]{:S(2)}) collective-permute-start(bf16[512,1024]{1,0:T(8,128)(2,1)} %collective-permute-done.24), channel_id=1, source_target_pairs={{0,8},{8,16},{16,24},{24,28},{28,20},{20,12},{12,4},{4,0},{1,9},{9... | collective-permute-start | bytes 3145736 | tf_op jit(solution)/shard_map/ppermute | solution.py:35
  468.1 25.9 %collective-permute-start.29 = (bf16[512,1024]{1,0:T(8,128)(2,1)}, bf16[512,1024]{1,0:T(8,128)(2,1)S(1)}, u32[]{:S(2)}, u32[]{:S(2)}) collective-permute-start(bf16[512,1024]{1,0:T(8,128)(2,1)} %collective-permute-done.27), channel_id=1, source_target_pairs={{0,4},{8,0},{16,8},{24,16},{28,24},{20,28},{12,20},{4,12},{1,5},{9... | collective-permute-start | bytes 3145736 | tf_op jit(solution)/shard_map/ppermute | solution.py:35
  487.1 175.0 %all-reduce.6.cloned.1.call-start = ((), (), s32[]{:S(2)}) async-start(), calls=%async_computation.1 | async-start | bytes 262144 | tf_op jit(solution)/shard_map/psum | solution.py:419
  632.8 31.2 %collective-permute-start.47 = (bf16[4,64,1024]{2,1,0:T(8,128)(2,1)S(1)}, bf16[4,64,1024]{2,1,0:T(8,128)(2,1)S(1)}, u32[]{:S(2)}, u32[]{:S(2)}) collective-permute-start(bf16[4,64,1024]{2,1,0:T(8,128)(2,1)S(1)} %add_convert_fusion.4), channel_id=1, source_target_pairs={{0,4},{8,0},{16,8},{24,16},{28,24},{20,28},{12,20},{4,12},{1,5},{9... | collective-permute-start | bytes 1572872 | tf_op jit(solution)/shard_map/ppermute | solution.py:35
  634.1 29.9 %collective-permute-start.43 = (bf16[4,64,1024]{2,1,0:T(8,128)(2,1)}, bf16[4,64,1024]{2,1,0:T(8,128)(2,1)S(1)}, u32[]{:S(2)}, u32[]{:S(2)}) collective-permute-start(bf16[4,64,1024]{2,1,0:T(8,128)(2,1)} %add_convert_fusion.6), channel_id=1, source_target_pairs={{0,8},{8,16},{16,24},{24,28},{28,20},{20,12},{12,4},{4,0},{1,9},{9... | collective-permute-start | bytes 1572872 | tf_op jit(solution)/shard_map/ppermute | solution.py:35
  (94 other events, 1286.2 us)
Sparse Core Ops, SparseCore 0:
  487.2 70.6 all-reduce.3
  591.0 71.1 all-reduce.5

commit v2 on v1

--- a/solution.py
+++ b/solution.py
@@ -35,18 +35,56 @@
     return lax.ppermute(block, "seq", route)
 
 
-def ring_gather(block, order):
-    count = len(order)
-    half = block.shape[0] // 2
-    pieces = [(0, 0, block)]
-    ahead = back = block
-    for step in range(1, count // 2):
-        ahead = ring_step(ahead, order, 1)
-        back = ring_step(back, order, -1)
-        pieces += [(step, 0, ahead), (-step, 0, back)]
-    pieces.append((count // 2, 0, ring_step(ahead[:half], order, 1)))
-    pieces.append((count // 2, half, ring_step(back[half:], order, -1)))
-    return pieces
+class Ring:
+    def __init__(self, block, order):
+        self.order = order
+        self.steps = len(order) // 2
+        self.done = 0
+        self.block = self.ahead = self.back = block
+        self.pieces = [(0, 0, block)]
+        self.landed = 1
+        self.used = 0
+        self.total = None
+
+    def step(self, clock):
+        self.landed = len(self.pieces)
+        if self.done == self.steps:
+            return []
+        self.done += 1
+        half = self.block.shape[0] // 2
+        last = self.done == self.steps
+        ahead = self.ahead[:half] if last else self.ahead
+        back = self.back[half:] if last else self.back
+        ahead, back = clock.hold(ahead, back)
+        self.ahead = ring_step(ahead, self.order, 1)
+        self.back = ring_step(back, self.order, -1)
+        if last:
+            self.pieces += [(self.steps, 0, self.ahead), (self.steps, half, self.back)]
+        else:
+            self.pieces += [(self.done, 0, self.ahead), (-self.done, 0, self.back)]
+        return [self.ahead, self.back]
+
+
+class Clock:
+    def __init__(self):
+        self.fence = ()
+
+    def hold(self, *values):
+        held = lax.optimization_barrier(tuple(values) + self.fence)[: len(values)]
+        return held[0] if len(values) == 1 else held
+
+    def turn(self, rings, work=None):
+        moved = [array for ring in rings for array in ring.step(self)]
+        done = work() if work is not None else ()
+        self.fence = tuple(moved) + tuple(done)
+
+
+def butterfly(value, axis, count, combine):
+    bit = 1
+    while bit < count:
+        value = combine(value, lax.ppermute(value, axis, [(i, i ^ bit) for i in range(count)]))
+        bit *= 2
+    return value
 
 
 def ring_sum(parts, order):
@@ -68,10 +106,6 @@
     return (
         ahead.astype(jnp.float32) + back.astype(jnp.float32) + parts[0].astype(jnp.float32)
     )
-
-
-def after(value, *earlier):
-    return lax.optimization_barrier((value,) + earlier)[0]
 
 
 def rope_kernel(value_ref, cosine_ref, sine_ref, out_ref):
@@ -138,22 +172,25 @@
         )
 
 
-def cache_part(places, live, query_slots, keys, values):
+def cache_part(begin, requests, places, live, query_slots, keys, values):
     slots = len(query_slots)
-    requests, tok_block, width = query_slots[0].shape
+    tok_block, width = query_slots[0].shape[1:]
     tokens = tok_block * slots
     cache_block = keys.shape[1]
     heads = width // HEAD_DIM
-    one = lambda rows: pl.BlockSpec((1, rows, width), lambda r, *_: (r, 0, 0))
+    one = lambda rows, start: pl.BlockSpec((1, rows, width), lambda r, *_: (r + start, 0, 0))
     stat = pl.BlockSpec((1, heads, tokens), lambda r, *_: (r, 0, 0))
     return pl.pallas_call(
         functools.partial(cache_kernel, slots),
         grid_spec=pltpu.PrefetchScalarGridSpec(
             num_scalar_prefetch=2,
             grid=(requests,),
-            in_specs=[one(tok_block)] * slots + [one(cache_block), one(cache_block)],
+            in_specs=[
+                one(tok_block, 0 if slot.shape[0] == requests else begin) for slot in query_slots
+            ]
+            + [one(cache_block, begin), one(cache_block, begin)],
             out_specs=[
-                one(tokens),
+                one(tokens, 0),
                 pl.BlockSpec((1, width, tokens), lambda r, *_: (r, 0, 0)),
                 stat,
                 stat,
@@ -193,18 +230,18 @@
         )
 
 
-def group_peaks(first, queries, new_keys, peaks):
+def group_peaks(begin, first, queries, new_keys, peaks):
     requests, tokens, width = queries.shape
     tok_block = new_keys.shape[1]
     heads = width // HEAD_DIM
-    one = lambda rows: pl.BlockSpec((1, rows, width), lambda r, *_: (r, 0, 0))
+    one = lambda rows, start: pl.BlockSpec((1, rows, width), lambda r, *_: (r + start, 0, 0))
     stat = pl.BlockSpec((1, heads, tokens), lambda r, *_: (r, 0, 0))
     return pl.pallas_call(
         peak_kernel,
         grid_spec=pltpu.PrefetchScalarGridSpec(
             num_scalar_prefetch=1,
             grid=(requests,),
-            in_specs=[one(tokens), one(tok_block), stat],
+            in_specs=[one(tokens, 0), one(tok_block, begin), stat],
             out_specs=stat,
         ),
         out_shape=jax.ShapeDtypeStruct(peaks.shape, jnp.float32),
@@ -242,29 +279,28 @@
         part_refs[slot][0] = joined_ref[pl.ds(start, tok_block), :]
 
 
-def finish_part(begin, requests, first, places, queries, new_keys, new_values, cached, peaks, totals, best):
-    tokens, width = queries.shape[1:]
+def finish_part(begin, first, places, queries, new_keys, new_values, cached, peaks, totals, best):
+    requests, tokens, width = queries.shape
     tok_block = new_keys.shape[1]
     slots = tokens // tok_block
     heads = width // HEAD_DIM
-    one = lambda rows: pl.BlockSpec((1, rows, width), lambda r, *_: (r + begin, 0, 0))
-    stat = pl.BlockSpec((1, heads, tokens), lambda r, *_: (r + begin, 0, 0))
+    one = lambda rows, start: pl.BlockSpec((1, rows, width), lambda r, *_: (r + start, 0, 0))
+    stat = lambda start: pl.BlockSpec((1, heads, tokens), lambda r, *_: (r + start, 0, 0))
     return pl.pallas_call(
         functools.partial(finish_kernel, slots),
         grid_spec=pltpu.PrefetchScalarGridSpec(
             num_scalar_prefetch=2,
             grid=(requests,),
             in_specs=[
-                one(tokens),
-                one(tok_block),
-                one(tok_block),
-                pl.BlockSpec((1, width, tokens), lambda r, *_: (r + begin, 0, 0)),
-                stat,
-                stat,
-                stat,
+                one(tokens, 0),
+                one(tok_block, begin),
+                one(tok_block, begin),
+                pl.BlockSpec((1, width, tokens), lambda r, *_: (r, 0, 0)),
+                stat(0),
+                stat(0),
+                stat(begin),
             ],
-            out_specs=[pl.BlockSpec((1, heads, tokens), lambda r, *_: (r, 0, 0))]
-            + [pl.BlockSpec((1, tok_block, width), lambda r, *_: (r, 0, 0))] * slots,
+            out_specs=[stat(0)] + [one(tok_block, 0)] * slots,
             scratch_shapes=[pltpu.VMEM((tokens, width), jnp.bfloat16)],
         ),
         out_shape=[jax.ShapeDtypeStruct((requests, heads, tokens), jnp.float32)]
@@ -302,30 +338,65 @@
     ).astype(jnp.float32)
 
 
-def entry_states(through, local_state, base, seq_index, seq_count):
-    factor = through[:, :, None]
-    if seq_count != 8:
-        entry = base
-        for turn in range(seq_count - 1):
-            leaving = (factor * entry + local_state).astype(jnp.bfloat16)
-            entry = entry + lax.ppermute(leaving, "seq", [(turn, turn + 1)]).astype(jnp.float32)
-        return entry
-    swap = [(i, i ^ 1) for i in range(8)]
-    other_state = lax.ppermute(local_state.astype(jnp.bfloat16), "seq", swap).astype(jnp.float32)
-    other_factor = lax.ppermute(through, "seq", swap)[:, :, None]
-    is_first = seq_index % 2 == 0
-    first_state = jnp.where(is_first, local_state, other_state)
-    second_state = jnp.where(is_first, other_state, local_state)
-    first_factor = jnp.where(is_first, factor, other_factor)
-    second_factor = jnp.where(is_first, other_factor, factor)
-    pair_state = second_factor * first_state + second_state
-    pair_factor = first_factor * second_factor
-    entry = base
-    for turn in range(3):
-        leaving = (pair_factor * entry + pair_state).astype(jnp.bfloat16)
-        route = [(2 * turn + y, 2 * turn + 2 + y) for y in range(2)]
-        entry = entry + lax.ppermute(leaving, "seq", route).astype(jnp.float32)
-    return jnp.where(is_first, entry, first_factor * entry + first_state)
+class Relay:
+    def __init__(self, through, local_state, initial, seq_index, seq_count):
+        self.factor = through[:, :, None]
+        self.local = local_state
+        self.seq_count = seq_count
+        self.paired = seq_count == 8
+        self.hops = seq_count - 1
+        if not self.paired:
+            self.entry = jnp.where(seq_index == 0, initial, 0.0)
+            self.hop = 0
+            return
+        self.hops = 3
+        self.hop = 0
+        self.swap = [(i, i ^ 1) for i in range(8)]
+        self.is_first = is_first = seq_index % 2 == 0
+        self.half = half = local_state.shape[1] // 2
+        mine = jnp.where(is_first, local_state[:, :half], local_state[:, half:])
+        other = jnp.where(is_first, local_state[:, half:], local_state[:, :half])
+        got = self.exchange(other)
+        other_factor = lax.ppermute(through, "seq", self.swap)[:, :, None]
+        first_state = jnp.where(is_first, mine, got)
+        second_state = jnp.where(is_first, got, mine)
+        side = lambda value: jnp.where(is_first, value[:, :half], value[:, half:])
+        first_factor = side(jnp.where(is_first, self.factor, other_factor))
+        second_factor = side(jnp.where(is_first, other_factor, self.factor))
+        self.first_state, self.first_factor = first_state, first_factor
+        self.pair_state = second_factor * first_state + second_state
+        self.pair_factor = first_factor * second_factor
+        self.entry = jnp.where(seq_index < 2, side(initial), 0.0)
+
+    def exchange(self, value):
+        return lax.ppermute(value.astype(jnp.bfloat16), "seq", self.swap).astype(jnp.float32)
+
+    def advance(self, clock):
+        factor, state = (
+            (self.pair_factor, self.pair_state) if self.paired else (self.factor, self.local)
+        )
+        entry = clock.hold(self.entry)
+        leaving = (factor * entry + state).astype(jnp.bfloat16)
+        if self.paired:
+            route = [(2 * self.hop + y, 2 * self.hop + 2 + y) for y in range(2)]
+        else:
+            route = [(self.hop, self.hop + 1)]
+        self.hop += 1
+        self.entry = entry + lax.ppermute(leaving, "seq", route).astype(jnp.float32)
+        return (self.entry,)
+
+    def result(self, clock):
+        while self.hop < self.hops:
+            self.advance(clock)
+        entry = clock.hold(self.entry)
+        if not self.paired:
+            return entry
+        second = self.first_factor * entry + self.first_state
+        got = self.exchange(jnp.where(self.is_first, second, entry))
+        mine = jnp.where(self.is_first, entry, second)
+        return jnp.concatenate(
+            [jnp.where(self.is_first, mine, got), jnp.where(self.is_first, got, mine)], axis=1
+        )
 
 
 def shards(
@@ -366,14 +437,15 @@
     ring_index = jnp.asarray(place, jnp.int32)[seq_index]
     origin = lambda offset: order_table[(ring_index - offset + seq_count) % seq_count]
 
-    def project(pieces):
-        total = None
-        for offset, row, piece in pieces:
+    def project(ring, whole=False):
+        landed = len(ring.pieces) if whole else ring.landed
+        for offset, row, piece in ring.pieces[ring.used : landed]:
             start = origin(offset) * rows + row
             part = lax.dynamic_slice_in_dim(flat_input, start, piece.shape[0], 1)
             term = jnp.dot(part, piece, preferred_element_type=jnp.float32)
-            total = term if total is None else total + term
-        return total
+            ring.total = term if ring.total is None else ring.total + term
+        ring.used = landed
+        return ring.total
 
     positions = (
         lengths[:, None] + seq_index * tok_block + jnp.arange(tok_block, dtype=jnp.int32)[None, :]
@@ -388,109 +460,235 @@
     cosine = jnp.concatenate([cosine, cosine], axis=1)
     sine = jnp.concatenate([-sine, sine], axis=1)
 
-    query_pieces = ring_gather(w_query, order)
-    key_pieces = ring_gather(after(w_key, query_pieces[-1][2]), order)
-    value_pieces = ring_gather(after(w_value, key_pieces[-1][2]), order)
-    queries = rope(project(query_pieces), cosine, sine).reshape(requests, tok_block, local_att)
-    new_keys = rope(project(key_pieces), cosine, sine).reshape(requests, tok_block, local_att)
-    new_values = project(value_pieces).astype(jnp.bfloat16).reshape(requests, tok_block, local_att)
-
+    clock = Clock()
     half = seq_count // 2
-    query_ring = ring_gather(queries, order)
+    group = requests // GROUPS
+    local_inner = w_in.shape[2]
+    local_mheads = local_inner // MHEAD_DIM
+    local_width = D // head_count
+    exact = functools.partial(jnp.einsum, precision=lax.Precision.HIGHEST)
+    mix = {}
+
+    def mix_steps():
+        hidden = clock.hold(flat_input)[:, :D].astype(jnp.float32)
+        scale = lax.rsqrt(jnp.mean(hidden * hidden, axis=-1, keepdims=True) + 1e-05)
+        normed = (hidden * scale * norm_gain).astype(jnp.bfloat16)
+        mix["normed"] = normed
+        bc_part = jnp.dot(normed, w_bc, preferred_element_type=jnp.float32).reshape(
+            requests, tok_block, 2 * STATE
+        )
+        mix["input_map"] = bc_part[..., :STATE]
+        mix["output_map"] = bc_part[..., STATE:]
+        step_size = jax.nn.softplus(
+            jnp.dot(normed, w_dt, preferred_element_type=jnp.float32).reshape(
+                requests, tok_block, local_mheads
+            )
+            + dt_bias
+        )
+        log_decay = -step_size * jnp.exp(a_log)
+        causal = jnp.arange(tok_block)[None, :] <= jnp.arange(tok_block)[:, None]
+        mix["causal"] = causal
+        mix["step_size"] = step_size
+        mix["cumulative"] = exact("tu,ruh->rth", causal.astype(jnp.float32), log_decay)
+        return (mix["normed"], bc_part, step_size, mix["cumulative"])
+
+    def mix_inner():
+        normed = clock.hold(mix["normed"])
+        gate_inner = jnp.dot(
+            normed, w_in.reshape(D, 2 * local_inner), preferred_element_type=jnp.float32
+        ).reshape(tokens, 2, local_inner)
+        mix["gate"] = jax.nn.silu(gate_inner[:, 0])
+        mix["inner"] = jax.nn.silu(gate_inner[:, 1]).reshape(
+            requests, tok_block, local_mheads, MHEAD_DIM
+        )
+        return (mix["gate"], mix["inner"])
+
+    def mix_local():
+        cumulative = clock.hold(mix["cumulative"])
+        tail_decay = jnp.exp(cumulative[:, -1:, :] - cumulative) * mix["step_size"]
+        mix["local"] = exact(
+            "ruhp,run->rhpn", mix["inner"] * tail_decay[..., None], mix["input_map"]
+        ).reshape(requests, local_mheads, MHEAD_DIM * STATE)
+        mix["through"] = jnp.exp(cumulative[:, -1, :])
+        return (mix["local"],)
+
+    def mix_intra():
+        cumulative, causal = clock.hold(mix["cumulative"]), mix["causal"]
+        head_major = jnp.transpose(cumulative, (0, 2, 1))
+        differences = head_major[:, :, :, None] - head_major[:, :, None, :]
+        decays = jnp.where(causal, jnp.exp(jnp.where(causal, differences, 0.0)), 0.0)
+        contact = exact("rtn,run->rtu", mix["output_map"], mix["input_map"])
+        mixing = (
+            decays * contact[:, None] * jnp.transpose(mix["step_size"], (0, 2, 1))[:, :, None, :]
+        )
+        mix["read"] = (
+            exact("rhtu,ruhp->rthp", mixing, mix["inner"]) + d_skip[:, None] * mix["inner"]
+        )
+        return (mix["read"],)
+
+    def mix_out():
+        incoming = clock.hold(mix["entry"])
+        entry_state = incoming.reshape(requests, local_mheads, MHEAD_DIM, STATE)
+        inter_part = (
+            exact("rhpn,rtn->rthp", entry_state, mix["output_map"])
+            * jnp.exp(mix["cumulative"])[..., None]
+        )
+        mix["chain"] = (mix["through"][:, :, None] * incoming + mix["local"])[:, None]
+        inner = (mix["read"] + inter_part).reshape(tokens, local_inner) * mix["gate"]
+        squares = butterfly(
+            jnp.sum(inner * inner, axis=-1, keepdims=True).reshape(1, tokens),
+            "head",
+            head_count,
+            jnp.add,
+        )
+        gated = (inner * gated_gain).astype(jnp.bfloat16)
+        mix["terms"] = jnp.dot(gated, w_out, preferred_element_type=jnp.float32) * lax.rsqrt(
+            squares.reshape(tokens, 1) / D_INNER + 1e-05
+        )
+        return (mix["terms"], mix["chain"])
+
+    query_ring = Ring(w_query, order)
+    relay = None
+    works = [mix_steps, mix_inner, mix_local]
+    while query_ring.done < query_ring.steps - 1:
+        clock.turn([query_ring], works.pop(0) if works else None)
+    while works:
+        clock.turn([], works.pop(0))
+
+    def start_relay():
+        nonlocal relay
+        query_total = project(query_ring)
+        relay = Relay(mix["through"], clock.hold(mix["local"]), ssm_init, seq_index, seq_count)
+        return (relay.pair_state, query_total) if relay.paired else (query_total,)
+
+    clock.turn([query_ring], start_relay)
+
+    key_ring = Ring(w_key, order)
+
+    def make_queries():
+        moved = relay.advance(clock)
+        total = project(query_ring, whole=True)
+        queries = rope(total, cosine, sine).reshape(requests, tok_block, local_att)
+        return (queries,) + tuple(moved)
+
+    clock.turn([key_ring], make_queries)
+    queries = clock.fence[2]
+
+    slot_ring = Ring(queries, order)
+
+    def relay_turn():
+        moved = relay.advance(clock)
+        clock_moved = mix_intra()
+        return tuple(moved) + tuple(clock_moved)
+
+    def relay_end():
+        mix["entry"] = relay.result(clock)
+        return (mix["entry"],)
+
+    def key_terms():
+        return (project(key_ring),)
+
+    works = [relay_turn, relay_end, mix_out, key_terms]
+    while slot_ring.done < slot_ring.steps:
+        clock.turn([slot_ring, key_ring], works.pop(0) if works else None)
+    while works:
+        clock.turn([key_ring], works.pop(0))
+
     offsets = [0] + [sign * step for step in range(1, half) for sign in (1, -1)] + [half]
-    query_slots = [piece for _, _, piece in query_ring[:-2]]
-    query_slots.append(jnp.concatenate([query_ring[-2][2], query_ring[-1][2]], axis=0))
     places = jnp.stack([origin(offset) for offset in offsets]).astype(jnp.int32)
     live = jnp.clip(lengths - seq_index * cache_block, 0, cache_block).astype(jnp.int32)
     first = (seq_index * tok_block).astype(jnp.int32).reshape(1)
-    all_queries, cached, peaks, totals = cache_part(
-        places, live, query_slots, cache_keys, cache_values
+    value_ring = Ring(w_value, order)
+    cached = []
+    state = {}
+
+    def meet_cache(index):
+        full = [piece for _, _, piece in slot_ring.pieces[:-2]]
+        slots = full + [slot_ring.pieces[-2 + index][2]]
+        slots[0] = clock.hold(slots[0])
+        begin = index * group
+        cached.append(
+            cache_part(
+                begin,
+                group,
+                places,
+                live[begin : begin + group],
+                slots,
+                cache_keys,
+                cache_values,
+            )
+        )
+        return tuple(cached[-1])
+
+    def cache_first():
+        total = project(key_ring, whole=True)
+        state["keys"] = rope(total, cosine, sine).reshape(requests, tok_block, local_att)
+        return meet_cache(0) + (state["keys"],)
+
+    def cache_second():
+        done = meet_cache(1)
+        state["peaks"] = jnp.concatenate(
+            [
+                group_peaks(index * group, first, part[0], state["keys"], part[2])
+                for index, part in enumerate(cached)
+            ],
+            axis=0,
+        )
+        return done + (state["peaks"],)
+
+    def join_peaks():
+        state["best"] = butterfly(clock.hold(state["peaks"]), "seq", seq_count, jnp.maximum)
+        return (state["best"], project(value_ring))
+
+    works = [cache_first, cache_second, join_peaks]
+    while value_ring.done < value_ring.steps:
+        clock.turn([value_ring], works.pop(0) if works else None)
+    while works:
+        clock.turn([], works.pop(0))
+    new_keys = state["keys"]
+    best = clock.hold(state["best"])
+    new_values = (
+        project(value_ring, whole=True)
+        .astype(jnp.bfloat16)
+        .reshape(requests, tok_block, local_att)
     )
-    best = lax.pmax(group_peaks(first, all_queries, new_keys, peaks), "seq")
 
     own = lambda stat: lax.dynamic_slice_in_dim(stat, seq_index * tok_block, tok_block, 2)
     greatest_logit = jnp.transpose(own(best), (0, 2, 1)) * SCALE
-    group = requests // GROUPS
-    attended = []
-    for begin in range(0, requests, group):
+    residual = lax.dynamic_slice_in_dim(
+        flat_input, head_index * local_width, local_width, 1
+    ).astype(jnp.float32)
+    mixed = []
+    for index, (joined, out, peaks, totals) in enumerate(cached):
+        begin = index * group
         sums, *parts = finish_part(
-            begin, group, first, places, all_queries, new_keys, new_values, cached, peaks, totals, best
-        )
-        denominator = jnp.transpose(own(lax.psum(sums, "seq")), (0, 2, 1))
+            begin, first, places, joined, new_keys, new_values, out, peaks, totals, best
+        )
+        sums = butterfly(sums, "seq", seq_count, jnp.add)
+        denominator = jnp.transpose(own(sums), (0, 2, 1))
         terms = {-offset: part for offset, part in zip(offsets, parts)}
         terms[half] = terms[-half]
         numerator = ring_sum(terms, order).reshape(group, tok_block, local_heads, HEAD_DIM)
-        attended.append((numerator / denominator[..., None]).astype(jnp.bfloat16))
-    attended = jnp.concatenate(attended, axis=0).reshape(tokens, local_att)
-    attn_terms = jnp.dot(attended, w_attn_out, preferred_element_type=jnp.float32)
-
-    hidden = block_input[:, :, :D].astype(jnp.float32)
-    normed = (
-        hidden * lax.rsqrt(jnp.mean(hidden * hidden, axis=-1, keepdims=True) + 1e-05) * norm_gain
-    ).astype(jnp.bfloat16)
-    flat_normed = normed.reshape(tokens, D)
-    local_inner = w_in.shape[2]
-    local_mheads = local_inner // MHEAD_DIM
-    gate_inner = jnp.dot(
-        flat_normed, w_in.reshape(D, 2 * local_inner), preferred_element_type=jnp.float32
-    ).reshape(requests, tok_block, 2, local_inner)
-    gate_part = gate_inner[:, :, 0]
-    inner_heads = jax.nn.silu(gate_inner[:, :, 1]).reshape(
-        requests, tok_block, local_mheads, MHEAD_DIM
+        attended = (
+            (numerator / denominator[..., None])
+            .astype(jnp.bfloat16)
+            .reshape(group * tok_block, local_att)
+        )
+        at = slice(begin * tok_block, (begin + group) * tok_block)
+        attn_terms = jnp.dot(attended, w_attn_out, preferred_element_type=jnp.float32)
+        summed = head_sum(attn_terms + mix["terms"][at], head_count, head_index)
+        mixed.append(
+            (residual[at] + summed)
+            .astype(jnp.bfloat16)
+            .reshape(group, tok_block, local_width)
+        )
+    return (
+        jnp.concatenate(mixed, axis=0),
+        new_keys,
+        new_values,
+        mix["chain"],
+        greatest_logit,
     )
-    bc_part = jnp.dot(flat_normed, w_bc, preferred_element_type=jnp.float32).reshape(
-        requests, tok_block, 2 * STATE
-    )
-    input_map = bc_part[..., :STATE]
-    output_map = bc_part[..., STATE:]
-    step_size = jax.nn.softplus(
-        jnp.dot(flat_normed, w_dt, preferred_element_type=jnp.float32).reshape(
-            requests, tok_block, local_mheads
-        )
-        + dt_bias
-    )
-    log_decay = -step_size * jnp.exp(a_log)
-    cumulative = jnp.cumsum(log_decay, axis=1)
-    causal = jnp.arange(tok_block)[None, :] <= jnp.arange(tok_block)[:, None]
-    head_major = jnp.transpose(cumulative, (0, 2, 1))
-    differences = head_major[:, :, :, None] - head_major[:, :, None, :]
-    decays = jnp.where(causal, jnp.exp(jnp.where(causal, differences, 0.0)), 0.0)
-    contact = jnp.einsum("rtn,run->rtu", output_map, input_map, precision=lax.Precision.HIGHEST)
-    mixing = decays * contact[:, None] * jnp.transpose(step_size, (0, 2, 1))[:, :, None, :]
-    intra_part = jnp.einsum("rhtu,ruhp->rthp", mixing, inner_heads, precision=lax.Precision.HIGHEST)
-    tail_decay = jnp.exp(cumulative[:, -1:, :] - cumulative) * step_size
-    local_state = jnp.einsum(
-        "ruhp,run->rhpn",
-        inner_heads * tail_decay[..., None],
-        input_map,
-        precision=lax.Precision.HIGHEST,
-    ).reshape(requests, local_mheads, MHEAD_DIM * STATE)
-    through = jnp.exp(cumulative[:, -1, :])
-    base = jnp.where(seq_index == 0, ssm_init, 0.0)
-    if seq_count == 8:
-        base = jnp.where(seq_index < 2, ssm_init, 0.0)
-    incoming = entry_states(through, local_state, base, seq_index, seq_count)
-    entry_state = incoming.reshape(requests, local_mheads, MHEAD_DIM, STATE)
-    inter_part = (
-        jnp.einsum("rhpn,rtn->rthp", entry_state, output_map, precision=lax.Precision.HIGHEST)
-        * jnp.exp(cumulative)[..., None]
-    )
-    read_out = intra_part + inter_part + d_skip[:, None] * inner_heads
-    chain_states = (through[:, :, None] * incoming + local_state)[:, None]
-    mixed_inner = read_out.reshape(requests, tok_block, local_inner) * jax.nn.silu(gate_part)
-    squares = lax.psum(jnp.sum(mixed_inner * mixed_inner, axis=-1).reshape(1, tokens), "head")
-    gated = (mixed_inner * gated_gain).astype(jnp.bfloat16)
-    mamba_terms = jnp.dot(
-        gated.reshape(tokens, local_inner), w_out, preferred_element_type=jnp.float32
-    ) * lax.rsqrt(squares.reshape(tokens, 1) / D_INNER + 1e-05)
-
-    summed = head_sum(attn_terms + mamba_terms, head_count, head_index)
-    local_width = D // head_count
-    residual = lax.dynamic_slice_in_dim(
-        hidden.reshape(tokens, D), head_index * local_width, local_width, 1
-    )
-    mixed = (residual + summed).astype(jnp.bfloat16).reshape(requests, tok_block, local_width)
-    return (mixed, new_keys, new_values, chain_states, greatest_logit)
 
 
 def solution(mesh):

time: 717 us -> 644 us (0.90)
  waiting for transfers between devices: 248 us -> 206 us
  starting transfers between devices: 126 us -> 91.5 us
  matrix products: 92.8 us -> 112 us
  local copies, waits for them, and re-layouts: 81.4 us -> 98.4 us
  other arithmetic: 52.2 us -> 37.5 us
  between operations: 25.7 us -> 13.1 us
    ppermute x5 -> x17, waiting for transfers between devices: 8.12 us -> 109 us  [the longest x2 54.2 us: exchange(): lax.ppermute(value.astype(jnp.bfloat16), 'seq', self.swap)]
    ppermute x48, waiting for transfers between devices: 179 us -> 88.2 us  [ring_step(): return lax.ppermute(block, 'seq', route)]
    ppermute x48, starting transfers between devices: 116 us -> 64.4 us  [ring_step(): return lax.ppermute(block, 'seq', route)]
    pmax x1 -> x0, waiting for transfers between devices: 33.1 us -> none  [shards(): best = lax.pmax(group_peaks(first, all_queries, new_keys, peaks), 'seq')]
    dot_general x27, matrix products: 43.6 us -> 66.9 us  [project(): term = jnp.dot(part, piece, preferred_element_type=jnp.float32)]
    ppermute x5 -> x17, starting transfers between devices: 7.5 us -> 24.9 us  [the longest x11 13.8 us: butterfly(): lax.ppermute(value, axis, [(i, i ^ bit) for i in range(count)])]
    psum x1 -> x0, waiting for transfers between devices: 13.8 us -> none  [shards(): denominator = jnp.transpose(own(lax.psum(sums, 'seq')), (0, 2, 1))]
    squeeze x3 -> x4, local copies, waits for them, and re-layouts: 6.65 us -> 18.3 us  [the longest x2 10.2 us: mix_inner(): gate_inner[:, 1]]
  transfers between devices with their start and end apart: 57 -> 69, of which waited for: 27 -> 32; matrix products, arithmetic and copies ran while one was open for 28% -> 35% of each run, Pallas kernels for 9% -> 10%
where the time goes in v2:
time: 644 us; the launch traced here: 634 us
  waiting for transfers between devices  206 us (32%)
  matrix products  112 us (17%)
  local copies, waits for them, and re-layouts  98.4 us (15%)
  starting transfers between devices  91.5 us (14%)
  Pallas kernels  75.6 us (12%)
  other arithmetic  37.5 us (6%)
  between operations  13.1 us (2%)
    ppermute x48, waiting for transfers between devices, ring_step(): return lax.ppermute(block, 'seq', route)  88.2 us
    dot_general x27, matrix products, project(): term = jnp.dot(part, piece, preferred_element_type=jnp.float32)  66.9 us
    ppermute x48, starting transfers between devices, ring_step(): return lax.ppermute(block, 'seq', route)  64.4 us
    ppermute x2, waiting for transfers between devices, exchange(): lax.ppermute(value.astype(jnp.bfloat16), 'seq', self.swap)  54.2 us
    pallas_call x2, Pallas kernels, cache_part(): pl.pallas_call(functools.partial(cache_kernel, slots), grid_spec=pltpu.Pr...  43.3 us
    ppermute x11, waiting for transfers between devices, butterfly(): lax.ppermute(value, axis, [(i, i ^ bit) for i in range(count)])  32.7 us
    unnamed x159, local copies, waits for them, and re-layouts  24.7 us
    pallas_call x2, Pallas kernels, finish_part(): pl.pallas_call(functools.partial(finish_kernel, slots), grid_spec=pltpu.P...  20.1 us
  transfers between devices with their start and end apart: 69, of which 32 were waited for; matrix products, arithmetic and copies ran while one was open for 35% of the time, Pallas kernels for 10%

profile of v2, /device:TPU:0, one launch (start us, length us, event | category | flops | bytes accessed | tf_op | source)
XLA Modules:
  0.0 634.3 jit_solution(17219933350187170689)
XLA Ops:
  23.8 10.3 %copy.45 = bf16[256,8,2,1024]{3,1,2,0:T(8,128)(2,1)} copy(bf16[256,8,2,1024]{3,2,1,0:T(2,128)(2,1)} %bitcast.196) | data formatting | bytes 16777216
  34.1 12.3 %copy.35 = bf16[2048,2048]{1,0:T(8,128)(2,1)} copy(bf16[2048,2048]{0,1:T(8,128)(2,1)} %bitcast.192) | data formatting | bytes 16777216 | tf_op jit(solution)/shard_map/dot_general | solution.py:497
  62.6 7.0 %fusion.17 = f32[512,2,1024]{2,0,1:T(8,128)S(1)} fusion(bf16[2,1024,2048]{2,1,0:T(8,128)(2,1)} %bitcast.197, bf16[512,2048]{1,0:T(8,128)(2,1)S(1)} %fusion.2), kind=kOutput, calls=%fused_computation.27 | convolution fusion | flops 4294967296 | bytes 14680064 | tf_op jit(solution)/shard_map/dot_general | solution.py:497
  72.2 4.5 squeeze.7
  76.8 5.6 copy.37
  85.0 5.6 copy.40
  100.0 6.2 fusion.10
  133.2 13.6 %collective-permute-done.9 = bf16[8,8,4096]{2,1,0:T(8,128)(2,1)S(1)} collective-permute-done((bf16[8,8,4096]{2,1,0:T(8,128)(2,1)S(1)}, bf16[8,8,4096]{2,1,0:T(8,128)(2,1)S(1)}, u32[]{:S(2)}, u32[]{:S(2)}) %collective-permute-start.9) | collective-permute-done | bytes 524320 | tf_op jit(solution)/shard_map/ppermute | solution.py:372
  161.5 18.0 %collective-permute-done.12 = bf16[8,8,4096]{2,1,0:T(8,128)(2,1)} collective-permute-done((bf16[8,8,4096]{2,1,0:T(8,128)(2,1)S(1)}, bf16[8,8,4096]{2,1,0:T(8,128)(2,1)}, u32[]{:S(2)}, u32[]{:S(2)}) %collective-permute-start.12) | collective-permute-done | bytes 524320 | tf_op jit(solution)/shard_map/ppermute | solution.py:385
  187.5 10.2 %bitcast_add_fusion = f32[8,64,16,64]{1,3,2,0:T(8,128)} fusion(f32[16]{0:T(128)S(1)} %copy-done.78, f32[8,16,64]{2,1,0:T(8,128)S(1)} %copy-done.72, f32[8,64,64]{2,1,0:T(8,128)S(1)} %copy-done.70, f32[8,16,64]{2,1,0:T(8,128)S(1)} %bitcast.205, pred[64,64]{1,0:T(8,128)(4,1)S(1)} %copy-done.73, f32[8,64,16,64]{1,3,2,0:T(8,128)S(1)} %copy-done.65), kind=kOutput, calls=%fused_computation.5 | convolution fusion | flops 410517504 | bytes 4395072 | tf_op jit(solution)/shard_map/rhtu,ruhp->rthp/dot_general | solution.py:525
  197.9 10.4 %collective-permute-done.13.refs_1_ = bf16[8,64,1024]{2,1,0:T(8,128)(2,1)S(1)} collective-permute-done((bf16[8,64,1024]{2,1,0:T(8,128)(2,1)}, bf16[8,64,1024]{2,1,0:T(8,128)(2,1)S(1)}, u32[]{:S(2)}, u32[]{:S(2)}) %collective-permute-start.13) | collective-permute-done | bytes 1048608 | tf_op jit(solution)/shard_map/ppermute | solution.py:35
  209.6 15.8 %collective-permute-done.15 = bf16[512,1024]{1,0:T(8,128)(2,1)S(1)} collective-permute-done((bf16[512,1024]{1,0:T(8,128)(2,1)}, bf16[512,1024]{1,0:T(8,128)(2,1)S(1)}, u32[]{:S(2)}, u32[]{:S(2)}) %collective-permute-start.15) | collective-permute-done | bytes 1048608 | tf_op jit(solution)/shard_map/ppermute | solution.py:35
  234.8 9.6 %collective-permute-start.18 = (bf16[8,64,1024]{2,1,0:T(8,128)(2,1)S(1)}, bf16[8,64,1024]{2,1,0:T(8,128)(2,1)S(1)}, u32[]{:S(2)}, u32[]{:S(2)}) collective-permute-start(bf16[8,64,1024]{2,1,0:T(8,128)(2,1)S(1)} %collective-permute-done.13.refs_1_), channel_id=1, source_target_pairs={{0,8},{8,16},{16,24},{24,28},{28,20},{20,12},{12,4},{4,0},{1,9},{9... | collective-permute-start | bytes 3145736 | tf_op jit(solution)/shard_map/ppermute | solution.py:35
  256.0 40.6 %collective-permute-done.23 = bf16[8,8,4096]{2,1,0:T(8,128)(2,1)S(1)} collective-permute-done((bf16[8,8,4096]{2,1,0:T(8,128)(2,1)S(1)}, bf16[8,8,4096]{2,1,0:T(8,128)(2,1)S(1)}, u32[]{:S(2)}, u32[]{:S(2)}) %collective-permute-start.23) | collective-permute-done | bytes 524320 | tf_op jit(solution)/shard_map/ppermute | solution.py:372
  298.5 5.2 reshape.174
  316.4 8.0 %multiply_reduce_fusion = (f32[8,64]{1,0:T(8,128)S(1)}, f32[8,64,16,64]{1,3,2,0:T(8,128)}) fusion(f32[8,64,16,64]{1,3,2,0:T(8,128)S(1)} %copy-done.63, f32[8,64,16,64]{1,3,2,0:T(8,128)} %bitcast_add_fusion, f32[8,64,16]{1,2,0:T(8,128)S(1)} %get-tuple-element.183, f32[8,16,64,64]{3,2,1,0:T(8,128)S(1)} %copy-done.61, f32[8,64,128]{2,1,0:T(8,128)S(1)} %bitcast.202), kind=kOutput, calls=%fused_computation.6 | convolution fusion | flops 407371264 | bytes 8685568 | tf_op jit(solution)/shard_map/rhpn,rtn->rthp/dot_general | solution.py:533
  332.3 5.6 copy.38
  337.9 4.9 reshape.175
  342.9 8.0 %convolution_multiply_fusion = f32[512,2048]{1,0:T(8,128)} fusion(bf16[1024,2048]{1,0:T(8,128)(2,1)} %param.36, f32[512]{0:T(512)S(1)} %bitcast.206, f32[512,1024]{1,0:T(8,128)} %reshape.175, f32[1024]{0:T(1024)S(1)} %copy-done.76, f32[512,2,1024]{2,0,1:T(8,128)} %copy-done.62), kind=kOutput, calls=%fused_computation.18 | convolution fusion | flops 2152202240 | bytes 12589056 | tf_op jit(solution)/shard_map/dot_general | solution.py:545
  361.5 8.1 %collective-permute-done.30.refs_7_ = bf16[4,64,1024]{2,1,0:T(8,128)(2,1)S(1)} collective-permute-done((bf16[4,64,1024]{2,1,0:T(8,128)(2,1)S(1)}, bf16[4,64,1024]{2,1,0:T(8,128)(2,1)S(1)}, u32[]{:S(2)}, u32[]{:S(2)}) %collective-permute-start.30) | collective-permute-done | bytes 524320 | tf_op jit(solution)/shard_map/ppermute | solution.py:35
  374.3 5.3 stack.3.place_ref
  387.3 21.7 %cache_part.2 = (bf16[4,512,1024]{2,1,0:T(8,128)(2,1)}, bf16[4,1024,512]{2,1,0:T(8,128)(2,1)}, f32[4,8,512]{2,1,0:T(8,128)S(1)}, f32[4,8,512]{2,1,0:T(8,128)S(1)}) custom-call(s32[8]{0:T(128)S(1)} %stack.3.place_ref, s32[4]{0:T(128)S(1)} %get-tuple-element.171.live_ref, bf16[8,64,1024]{2,1,0:T(8,128)(2,1)S(1)} %bitcast.160, ...), custom_call_target="tpu_custom_call" | custom-call | flops 4294967296 | bytes 20971520 | tf_op jit(solution)/shard_map/cache_part/pallas_call | solution.py:183
  417.4 21.6 %cache_part.3 = (bf16[4,512,1024]{2,1,0:T(8,128)(2,1)}, bf16[4,1024,512]{2,1,0:T(8,128)(2,1)}, f32[4,8,512]{2,1,0:T(8,128)S(1)}, f32[4,8,512]{2,1,0:T(8,128)S(1)}) custom-call(s32[8]{0:T(128)S(1)} %stack.3.place_ref, s32[4]{0:T(128)S(1)} %get-tuple-element.172.live_ref, bf16[8,64,1024]{2,1,0:T(8,128)(2,1)S(1)} %bitcast.161, ...), custom_call_target="tpu_custom_call" | custom-call | flops 4294967296 | bytes 20971520 | tf_op jit(solution)/shard_map/cache_part/pallas_call | solution.py:183
  449.6 22.4 %collective-permute-done.38 = f32[8,8,512]{2,1,0:T(8,128)S(1)} collective-permute-done((f32[8,8,512]{2,1,0:T(8,128)S(1)}, f32[8,8,512]{2,1,0:T(8,128)S(1)}, u32[]{:S(2)}, u32[]{:S(2)}) %collective-permute-start.38) | collective-permute-done | bytes 131104 | tf_op jit(solution)/shard_map/ppermute | solution.py:85
  489.4 5.6 collective-permute-done.41
  497.6 10.0 %finish_part.2 = (f32[4,8,512]{2,1,0:T(8,128)S(1)}, bf16[4,64,1024]{2,1,0:T(8,128)(2,1)S(1)}, bf16[4,64,1024]{2,1,0:T(8,128)(2,1)S(1)}, bf16[4,64,1024]{2,1,0:T(...) custom-call(s32[1]{0:T(128)} %bitcast.1.first_ref, ...), custom_call_target="tpu_custom_call" | custom-call | flops 536870912 | bytes 12582912 | tf_op jit(solution)/shard_map/finish_part/pallas_call | solution.py:289
  513.4 10.1 %finish_part.3 = (f32[4,8,512]{2,1,0:T(8,128)S(1)}, bf16[4,64,1024]{2,1,0:T(8,128)(2,1)S(1)}, bf16[4,64,1024]{2,1,0:T(8,128)(2,1)S(1)}, bf16[4,64,1024]{2,1,0:T(...) custom-call(s32[1]{0:T(128)} %bitcast.1.first_ref, ...), custom_call_target="tpu_custom_call" | custom-call | flops 536870912 | bytes 12582912 | tf_op jit(solution)/shard_map/finish_part/pallas_call | solution.py:289
  557.3 7.2 %collective-permute-done.48 = bf16[4,64,1024]{2,1,0:T(8,128)(2,1)S(1)} collective-permute-done((bf16[4,64,1024]{2,1,0:T(8,128)(2,1)S(1)}, bf16[4,64,1024]{2,1,0:T(8,128)(2,1)S(1)}, u32[]{:S(2)}, u32[]{:S(2)}) %collective-permute-start.48) | collective-permute-done | bytes 524320 | tf_op jit(solution)/shard_map/ppermute | solution.py:35
  568.0 7.7 %collective-permute-done.61 = bf16[4,64,1024]{2,1,0:T(8,128)(2,1)S(1)} collective-permute-done((bf16[4,64,1024]{2,1,0:T(8,128)(2,1)S(1)}, bf16[4,64,1024]{2,1,0:T(8,128)(2,1)S(1)}, u32[]{:S(2)}, u32[]{:S(2)}) %collective-permute-start.61) | collective-permute-done | bytes 524320 | tf_op jit(solution)/shard_map/ppermute | solution.py:35
  579.3 7.7 %collective-permute-done.49 = bf16[4,64,1024]{2,1,0:T(8,128)(2,1)S(1)} collective-permute-done((bf16[4,64,1024]{2,1,0:T(8,128)(2,1)S(1)}, bf16[4,64,1024]{2,1,0:T(8,128)(2,1)S(1)}, u32[]{:S(2)}, u32[]{:S(2)}) %collective-permute-start.49) | collective-permute-done | bytes 524320 | tf_op jit(solution)/shard_map/ppermute | solution.py:35
  590.5 7.3 %collective-permute-done.62 = bf16[4,64,1024]{2,1,0:T(8,128)(2,1)S(1)} collective-permute-done((bf16[4,64,1024]{2,1,0:T(8,128)(2,1)S(1)}, bf16[4,64,1024]{2,1,0:T(8,128)(2,1)S(1)}, u32[]{:S(2)}, u32[]{:S(2)}) %collective-permute-start.62) | collective-permute-done | bytes 524320 | tf_op jit(solution)/shard_map/ppermute | solution.py:35
  626.2 5.2 collective-permute-done.68
  (420 shorter events, 279.8 us)
Async XLA Ops:
  0.7 59.7 %collective-permute-start = (bf16[512,1024]{1,0:T(8,128)(2,1)}, bf16[512,1024]{1,0:T(8,128)(2,1)}, u32[]{:S(2)}, u32[]{:S(2)}) collective-permute-start(bf16[512,1024]{1,0:T(8,128)(2,1)} %param.24), channel_id=1, source_target_pairs={{0,8},{8,16},{16,24},{24,28},{28,20},{20,12},{12,4},{4,0},{1,9},{9... | collective-permute-start | bytes 3145736 | tf_op jit(solution)/shard_map/ppermute | solution.py:35
  3.7 56.6 %collective-permute-start.1 = (bf16[512,1024]{1,0:T(8,128)(2,1)}, bf16[512,1024]{1,0:T(8,128)(2,1)}, u32[]{:S(2)}, u32[]{:S(2)}) collective-permute-start(bf16[512,1024]{1,0:T(8,128)(2,1)} %param.24), channel_id=1, source_target_pairs={{0,4},{8,0},{16,8},{24,16},{28,24},{20,28},{12,20},{4,12},{1,5},{9... | collective-permute-start | bytes 3145736 | tf_op jit(solution)/shard_map/ppermute | solution.py:35
  60.4 37.2 %collective-permute-start.2 = (bf16[512,1024]{1,0:T(8,128)(2,1)}, bf16[512,1024]{1,0:T(8,128)(2,1)}, u32[]{:S(2)}, u32[]{:S(2)}) collective-permute-start(bf16[512,1024]{1,0:T(8,128)(2,1)} %collective-permute-done), channel_id=1, source_target_pairs={{0,8},{8,16},{16,24},{24,28},{28,20},{20,12},{12,4},{4,0},{1,9},{9... | collective-permute-start | bytes 3145736 | tf_op jit(solution)/shard_map/ppermute | solution.py:35
  62.4 35.2 %collective-permute-start.3 = (bf16[512,1024]{1,0:T(8,128)(2,1)}, bf16[512,1024]{1,0:T(8,128)(2,1)}, u32[]{:S(2)}, u32[]{:S(2)}) collective-permute-start(bf16[512,1024]{1,0:T(8,128)(2,1)} %collective-permute-done.1), channel_id=1, source_target_pairs={{0,4},{8,0},{16,8},{24,16},{28,24},{20,28},{12,20},{4,12},{1,5},{9... | collective-permute-start | bytes 3145736 | tf_op jit(solution)/shard_map/ppermute | solution.py:35
  97.9 24.6 %collective-permute-start.4 = (bf16[512,1024]{1,0:T(8,128)(2,1)}, bf16[512,1024]{1,0:T(8,128)(2,1)}, u32[]{:S(2)}, u32[]{:S(2)}) collective-permute-start(bf16[512,1024]{1,0:T(8,128)(2,1)} %collective-permute-done.2), channel_id=1, source_target_pairs={{0,8},{8,16},{16,24},{24,28},{28,20},{20,12},{12,4},{4,0},{1,9},{9... | collective-permute-start | bytes 3145736 | tf_op jit(solution)/shard_map/ppermute | solution.py:35
  100.0 23.7 %collective-permute-start.5 = (bf16[512,1024]{1,0:T(8,128)(2,1)}, bf16[512,1024]{1,0:T(8,128)(2,1)S(1)}, u32[]{:S(2)}, u32[]{:S(2)}) collective-permute-start(bf16[512,1024]{1,0:T(8,128)(2,1)} %collective-permute-done.3), channel_id=1, source_target_pairs={{0,4},{8,0},{16,8},{24,16},{28,24},{20,28},{12,20},{4,12},{1,5},{9... | collective-permute-start | bytes 3145736 | tf_op jit(solution)/shard_map/ppermute | solution.py:35
  123.7 24.4 %collective-permute-start.6 = (bf16[256,1024]{1,0:T(8,128)(2,1)S(1)}, bf16[256,1024]{1,0:T(8,128)(2,1)S(1)}, u32[]{:S(2)}, u32[]{:S(2)}) collective-permute-start(bf16[256,1024]{1,0:T(8,128)(2,1)S(1)} %slice.183), channel_id=1, source_target_pairs={{0,8},{8,16},{16,24},{24,28},{28,20},{20,12},{12,4},{4,0},{1,9},{9... | collective-permute-start | bytes 1572872 | tf_op jit(solution)/shard_map/ppermute | solution.py:35
  125.3 22.8 %collective-permute-start.7 = (bf16[256,1024]{1,0:T(8,128)(2,1)S(1)}, bf16[256,1024]{1,0:T(8,128)(2,1)S(1)}, u32[]{:S(2)}, u32[]{:S(2)}) collective-permute-start(bf16[256,1024]{1,0:T(8,128)(2,1)S(1)} %slice.184), channel_id=1, source_target_pairs={{0,4},{8,0},{16,8},{24,16},{28,24},{20,28},{12,20},{4,12},{1,5},{9... | collective-permute-start | bytes 1572872 | tf_op jit(solution)/shard_map/ppermute | solution.py:35
  148.1 32.5 %collective-permute-start.10 = (bf16[512,1024]{1,0:T(8,128)(2,1)}, bf16[512,1024]{1,0:T(8,128)(2,1)}, u32[]{:S(2)}, u32[]{:S(2)}) collective-permute-start(bf16[512,1024]{1,0:T(8,128)(2,1)} %param.25), channel_id=1, source_target_pairs={{0,8},{8,16},{16,24},{24,28},{28,20},{20,12},{12,4},{4,0},{1,9},{9... | collective-permute-start | bytes 3145736 | tf_op jit(solution)/shard_map/ppermute | solution.py:35
  148.1 32.5 %collective-permute-start.11 = (bf16[512,1024]{1,0:T(8,128)(2,1)}, bf16[512,1024]{1,0:T(8,128)(2,1)}, u32[]{:S(2)}, u32[]{:S(2)}) collective-permute-start(bf16[512,1024]{1,0:T(8,128)(2,1)} %param.25), channel_id=1, source_target_pairs={{0,4},{8,0},{16,8},{24,16},{28,24},{20,28},{12,20},{4,12},{1,5},{9... | collective-permute-start | bytes 3145736 | tf_op jit(solution)/shard_map/ppermute | solution.py:35
  150.4 29.1 %collective-permute-start.12 = (bf16[8,8,4096]{2,1,0:T(8,128)(2,1)S(1)}, bf16[8,8,4096]{2,1,0:T(8,128)(2,1)}, u32[]{:S(2)}, u32[]{:S(2)}) collective-permute-start(bf16[8,8,4096]{2,1,0:T(8,128)(2,1)S(1)} %add_convert_fusion.11), channel_id=1, source_target_pairs={{0,8},{4,12},{1,9},{5,13},{2,10},{6,14},{3,11},{7,15}} | collective-permute-start | bytes 1572872 | tf_op jit(solution)/shard_map/ppermute | solution.py:385
  180.7 27.6 %collective-permute-start.13 = (bf16[8,64,1024]{2,1,0:T(8,128)(2,1)}, bf16[8,64,1024]{2,1,0:T(8,128)(2,1)S(1)}, u32[]{:S(2)}, u32[]{:S(2)}) collective-permute-start(bf16[8,64,1024]{2,1,0:T(8,128)(2,1)} %bitcast.158), channel_id=1, source_target_pairs={{0,8},{8,16},{16,24},{24,28},{28,20},{20,12},{12,4},{4,0},{1,9},{9... | collective-permute-start | bytes 3145736 | tf_op jit(solution)/shard_map/ppermute | solution.py:35
  183.3 26.3 %collective-permute-start.14 = (bf16[8,64,1024]{2,1,0:T(8,128)(2,1)}, bf16[8,64,1024]{2,1,0:T(8,128)(2,1)S(1)}, u32[]{:S(2)}, u32[]{:S(2)}) collective-permute-start(bf16[8,64,1024]{2,1,0:T(8,128)(2,1)} %bitcast.159), channel_id=1, source_target_pairs={{0,4},{8,0},{16,8},{24,16},{28,24},{20,28},{12,20},{4,12},{1,5},{9... | collective-permute-start | bytes 3145736 | tf_op jit(solution)/shard_map/ppermute | solution.py:35
  184.0 41.4 %collective-permute-start.15 = (bf16[512,1024]{1,0:T(8,128)(2,1)}, bf16[512,1024]{1,0:T(8,128)(2,1)S(1)}, u32[]{:S(2)}, u32[]{:S(2)}) collective-permute-start(bf16[512,1024]{1,0:T(8,128)(2,1)} %collective-permute-done.10), channel_id=1, source_target_pairs={{0,8},{8,16},{16,24},{24,28},{28,20},{20,12},{12,4},{4,0},{1,9},{9... | collective-permute-start | bytes 3145736 | tf_op jit(solution)/shard_map/ppermute | solution.py:35
  185.3 41.9 %collective-permute-start.16 = (bf16[512,1024]{1,0:T(8,128)(2,1)}, bf16[512,1024]{1,0:T(8,128)(2,1)S(1)}, u32[]{:S(2)}, u32[]{:S(2)}) collective-permute-start(bf16[512,1024]{1,0:T(8,128)(2,1)} %collective-permute-done.11), channel_id=1, source_target_pairs={{0,4},{8,0},{16,8},{24,16},{28,24},{20,28},{12,20},{4,12},{1,5},{9... | collective-permute-start | bytes 3145736 | tf_op jit(solution)/shard_map/ppermute | solution.py:35
  234.8 63.6 %collective-permute-start.18 = (bf16[8,64,1024]{2,1,0:T(8,128)(2,1)S(1)}, bf16[8,64,1024]{2,1,0:T(8,128)(2,1)S(1)}, u32[]{:S(2)}, u32[]{:S(2)}) collective-permute-start(bf16[8,64,1024]{2,1,0:T(8,128)(2,1)S(1)} %collective-permute-done.13.refs_1_), channel_id=1, source_target_pairs={{0,8},{8,16},{16,24},{24,28},{28,20},{20,12},{12,4},{4,0},{1,9},{9... | collective-permute-start | bytes 3145736 | tf_op jit(solution)/shard_map/ppermute | solution.py:35
  244.5 54.0 %collective-permute-start.19 = (bf16[8,64,1024]{2,1,0:T(8,128)(2,1)S(1)}, bf16[8,64,1024]{2,1,0:T(8,128)(2,1)S(1)}, u32[]{:S(2)}, u32[]{:S(2)}) collective-permute-start(bf16[8,64,1024]{2,1,0:T(8,128)(2,1)S(1)} %collective-permute-done.14.refs_2_), channel_id=1, source_target_pairs={{0,4},{8,0},{16,8},{24,16},{28,24},{20,28},{12,20},{4,12},{1,5},{9... | collective-permute-start | bytes 3145736 | tf_op jit(solution)/shard_map/ppermute | solution.py:35
  244.5 54.0 %collective-permute-start.20 = (bf16[512,1024]{1,0:T(8,128)(2,1)S(1)}, bf16[512,1024]{1,0:T(8,128)(2,1)}, u32[]{:S(2)}, u32[]{:S(2)}) collective-permute-start(bf16[512,1024]{1,0:T(8,128)(2,1)S(1)} %collective-permute-done.15), channel_id=1, source_target_pairs={{0,8},{8,16},{16,24},{24,28},{28,20},{20,12},{12,4},{4,0},{1,9},{9... | collective-permute-start | bytes 3145736 | tf_op jit(solution)/shard_map/ppermute | solution.py:35
  247.6 50.9 %collective-permute-start.21 = (bf16[512,1024]{1,0:T(8,128)(2,1)S(1)}, bf16[512,1024]{1,0:T(8,128)(2,1)}, u32[]{:S(2)}, u32[]{:S(2)}) collective-permute-start(bf16[512,1024]{1,0:T(8,128)(2,1)S(1)} %collective-permute-done.16), channel_id=1, source_target_pairs={{0,4},{8,0},{16,8},{24,16},{28,24},{20,28},{12,20},{4,12},{1,5},{9... | collective-permute-start | bytes 3145736 | tf_op jit(solution)/shard_map/ppermute | solution.py:35
  248.6 47.9 %collective-permute-start.23 = (bf16[8,8,4096]{2,1,0:T(8,128)(2,1)S(1)}, bf16[8,8,4096]{2,1,0:T(8,128)(2,1)S(1)}, u32[]{:S(2)}, u32[]{:S(2)}) collective-permute-start(bf16[8,8,4096]{2,1,0:T(8,128)(2,1)S(1)} %select_convert_fusion), channel_id=1, source_target_pairs={{0,4},{4,0},{8,12},{12,8},{16,20},{20,16},{24,28},{28,24},{1,5},{5... | collective-permute-start | bytes 1572872 | tf_op jit(solution)/shard_map/ppermute | solution.py:372
  307.7 45.0 %collective-permute-start.24 = (bf16[8,64,1024]{2,1,0:T(8,128)(2,1)S(1)}, bf16[8,64,1024]{2,1,0:T(8,128)(2,1)}, u32[]{:S(2)}, u32[]{:S(2)}) collective-permute-start(bf16[8,64,1024]{2,1,0:T(8,128)(2,1)S(1)} %collective-permute-done.18.refs_3_), channel_id=1, source_target_pairs={{0,8},{8,16},{16,24},{24,28},{28,20},{20,12},{12,4},{4,0},{1,9},{9... | collective-permute-start | bytes 3145736 | tf_op jit(solution)/shard_map/ppermute | solution.py:35
  307.7 46.0 %collective-permute-start.25 = (bf16[8,64,1024]{2,1,0:T(8,128)(2,1)S(1)}, bf16[8,64,1024]{2,1,0:T(8,128)(2,1)}, u32[]{:S(2)}, u32[]{:S(2)}) collective-permute-start(bf16[8,64,1024]{2,1,0:T(8,128)(2,1)S(1)} %collective-permute-done.19.refs_4_), channel_id=1, source_target_pairs={{0,4},{8,0},{16,8},{24,16},{28,24},{20,28},{12,20},{4,12},{1,5},{9... | collective-permute-start | bytes 3145736 | tf_op jit(solution)/shard_map/ppermute | solution.py:35
  314.0 36.9 %collective-permute-start.26 = (bf16[256,1024]{1,0:T(8,128)(2,1)}, bf16[256,1024]{1,0:T(8,128)(2,1)}, u32[]{:S(2)}, u32[]{:S(2)}) collective-permute-start(bf16[256,1024]{1,0:T(8,128)(2,1)} %slice.189), channel_id=1, source_target_pairs={{0,8},{8,16},{16,24},{24,28},{28,20},{20,12},{12,4},{4,0},{1,9},{9... | collective-permute-start | bytes 1572872 | tf_op jit(solution)/shard_map/ppermute | solution.py:35
  314.0 40.9 %collective-permute-start.27 = (bf16[256,1024]{1,0:T(8,128)(2,1)}, bf16[256,1024]{1,0:T(8,128)(2,1)}, u32[]{:S(2)}, u32[]{:S(2)}) collective-permute-start(bf16[256,1024]{1,0:T(8,128)(2,1)} %slice.190), channel_id=1, source_target_pairs={{0,4},{8,0},{16,8},{24,16},{28,24},{20,28},{12,20},{4,12},{1,5},{9... | collective-permute-start | bytes 1572872 | tf_op jit(solution)/shard_map/ppermute | solution.py:35
  372.1 36.9 %collective-permute-start.32 = (bf16[512,1024]{1,0:T(8,128)(2,1)}, bf16[512,1024]{1,0:T(8,128)(2,1)}, u32[]{:S(2)}, u32[]{:S(2)}) collective-permute-start(bf16[512,1024]{1,0:T(8,128)(2,1)} %param.26), channel_id=1, source_target_pairs={{0,8},{8,16},{16,24},{24,28},{28,20},{20,12},{12,4},{4,0},{1,9},{9... | collective-permute-start | bytes 3145736 | tf_op jit(solution)/shard_map/ppermute | solution.py:35
  374.1 34.9 %collective-permute-start.33 = (bf16[512,1024]{1,0:T(8,128)(2,1)}, bf16[512,1024]{1,0:T(8,128)(2,1)}, u32[]{:S(2)}, u32[]{:S(2)}) collective-permute-start(bf16[512,1024]{1,0:T(8,128)(2,1)} %param.26), channel_id=1, source_target_pairs={{0,4},{8,0},{16,8},{24,16},{28,24},{20,28},{12,20},{4,12},{1,5},{9... | collective-permute-start | bytes 3145736 | tf_op jit(solution)/shard_map/ppermute | solution.py:35
  409.0 36.2 %collective-permute-start.34 = (bf16[512,1024]{1,0:T(8,128)(2,1)}, bf16[512,1024]{1,0:T(8,128)(2,1)}, u32[]{:S(2)}, u32[]{:S(2)}) collective-permute-start(bf16[512,1024]{1,0:T(8,128)(2,1)} %collective-permute-done.32), channel_id=1, source_target_pairs={{0,8},{8,16},{16,24},{24,28},{28,20},{20,12},{12,4},{4,0},{1,9},{9... | collective-permute-start | bytes 3145736 | tf_op jit(solution)/shard_map/ppermute | solution.py:35
  411.1 34.2 %collective-permute-start.35 = (bf16[512,1024]{1,0:T(8,128)(2,1)}, bf16[512,1024]{1,0:T(8,128)(2,1)}, u32[]{:S(2)}, u32[]{:S(2)}) collective-permute-start(bf16[512,1024]{1,0:T(8,128)(2,1)} %collective-permute-done.33), channel_id=1, source_target_pairs={{0,4},{8,0},{16,8},{24,16},{28,24},{20,28},{12,20},{4,12},{1,5},{9... | collective-permute-start | bytes 3145736 | tf_op jit(solution)/shard_map/ppermute | solution.py:35
  445.3 39.9 %collective-permute-start.36 = (bf16[512,1024]{1,0:T(8,128)(2,1)}, bf16[512,1024]{1,0:T(8,128)(2,1)S(1)}, u32[]{:S(2)}, u32[]{:S(2)}) collective-permute-start(bf16[512,1024]{1,0:T(8,128)(2,1)} %collective-permute-done.34), channel_id=1, source_target_pairs={{0,8},{8,16},{16,24},{24,28},{28,20},{20,12},{12,4},{4,0},{1,9},{9... | collective-permute-start | bytes 3145736 | tf_op jit(solution)/shard_map/ppermute | solution.py:35
  447.3 37.9 %collective-permute-start.37 = (bf16[512,1024]{1,0:T(8,128)(2,1)}, bf16[512,1024]{1,0:T(8,128)(2,1)S(1)}, u32[]{:S(2)}, u32[]{:S(2)}) collective-permute-start(bf16[512,1024]{1,0:T(8,128)(2,1)} %collective-permute-done.35), channel_id=1, source_target_pairs={{0,4},{8,0},{16,8},{24,16},{28,24},{20,28},{12,20},{4,12},{1,5},{9... | collective-permute-start | bytes 3145736 | tf_op jit(solution)/shard_map/ppermute | solution.py:35
  447.6 24.4 %collective-permute-start.38 = (f32[8,8,512]{2,1,0:T(8,128)S(1)}, f32[8,8,512]{2,1,0:T(8,128)S(1)}, u32[]{:S(2)}, u32[]{:S(2)}) collective-permute-start(f32[8,8,512]{2,1,0:T(8,128)S(1)} %pad_maximum_fusion.10), channel_id=1, source_target_pairs={{0,4},{4,0},{8,12},{12,8},{16,20},{20,16},{24,28},{28,24},{1,5},{5... | collective-permute-start | bytes 393224 | tf_op jit(solution)/shard_map/ppermute | solution.py:85
  564.7 22.3 %collective-permute-start.49 = (bf16[4,64,1024]{2,1,0:T(8,128)(2,1)S(1)}, bf16[4,64,1024]{2,1,0:T(8,128)(2,1)S(1)}, u32[]{:S(2)}, u32[]{:S(2)}) collective-permute-start(bf16[4,64,1024]{2,1,0:T(8,128)(2,1)S(1)} %add_convert_fusion.6), channel_id=1, source_target_pairs={{0,4},{8,0},{16,8},{24,16},{28,24},{20,28},{12,20},{4,12},{1,5},{9... | collective-permute-start | bytes 1572872 | tf_op jit(solution)/shard_map/ppermute | solution.py:35
  (116 other events, 1718.9 us)

commit v3 on v2

v3 whole, which is shorter than its diff:
```python
import functools
import math

import jax
import jax.numpy as jnp
from jax import lax
from jax.experimental import pallas as pl
from jax.experimental.pallas import tpu as pltpu
from jax.sharding import PartitionSpec as P

D = 2048
HEAD_DIM = 128
MHEAD_DIM = 64
STATE = 64
D_INNER = 4096
SCALE = 1.0 / math.sqrt(HEAD_DIM)
EXP2_SCALE = SCALE * math.log2(math.e)
DEAD = -1e30
GROUPS = 2


def ring_order(count):
    y_count = max(1, count // 4)
    z_count = count // y_count
    order = []
    for y in range(y_count):
        turn = range(z_count) if y % 2 == 0 else range(z_count - 1, -1, -1)
        order += [z * y_count + y for z in turn]
    return order


def ring_step(block, order, distance):
    count = len(order)
    route = [(order[i], order[(i + distance) % count]) for i in range(count)]
    return lax.ppermute(block, "seq", route)


class Ring:
    def __init__(self, block, order, first_row=0):
        self.order = order
        self.steps = len(order) // 2
        self.done = 0
        self.first_row = first_row
        self.block = self.ahead = self.back = block
        self.pieces = [(0, first_row, block)]

    def step(self, clock):
        self.done += 1
        half = self.block.shape[0] // 2
        last = self.done == self.steps
        ahead = self.ahead[:half] if last else self.ahead
        back = self.back[half:] if last else self.back
        ahead, back = clock.hold(ahead, back)
        self.ahead = ring_step(ahead, self.order, 1)
        self.back = ring_step(back, self.order, -1)
        at = self.first_row
        if last:
            self.pieces += [(self.steps, at, self.ahead), (self.steps, at + half, self.back)]
        else:
            self.pieces += [(self.done, at, self.ahead), (-self.done, at, self.back)]
        return [self.ahead, self.back]


class Clock:
    def __init__(self):
        self.fence = ()
        self.late = ()

    def hold(self, *values):
        held = lax.optimization_barrier(tuple(values) + self.fence)[: len(values)]
        return held[0] if len(values) == 1 else held

    def turn(self, ring=None, work=None):
        moved = tuple(ring.step(self)) if ring is not None else ()
        done, deferred = work() if work is not None else ((), ())
        self.fence = self.late + tuple(done)
        self.late = moved + tuple(deferred)


def butterfly(value, axis, count, combine):
    bit = 1
    while bit < count:
        value = combine(value, lax.ppermute(value, axis, [(i, i ^ bit) for i in range(count)]))
        bit *= 2
    return value


def ring_sum(parts, order):
    far = len(order) // 2
    add = lambda a, b: (a.astype(jnp.float32) + b.astype(jnp.float32)).astype(jnp.bfloat16)
    ahead = ring_step(parts[far][0], order, 1)
    back = ring_step(parts[far][1], order, -1)
    ahead = jnp.concatenate([add(ahead, parts[far - 1][0]), parts[far - 1][1]], axis=0)
    back = jnp.concatenate([parts[1 - far][0], add(back, parts[1 - far][1])], axis=0)
    whole = lambda offset: jnp.concatenate(parts[offset], axis=0)
    for step in range(far - 1, 0, -1):
        ahead = ring_step(ahead, order, 1)
        back = ring_step(back, order, -1)
        if step > 1:
            ahead = add(ahead, whole(step - 1))
            back = add(back, whole(1 - step))
    return ahead.astype(jnp.float32) + back.astype(jnp.float32) + whole(0).astype(jnp.float32)


def project_kernel(count, turned, places_ref, *refs):
    input_refs, weight_refs = refs[:count], refs[count : 2 * count]
    cosine_ref, sine_ref, out_ref = refs[2 * count :]
    total = None
    for input_ref, weight_ref in zip(input_refs, weight_refs):
        term = jnp.dot(input_ref[...], weight_ref[...], preferred_element_type=jnp.float32)
        total = term if total is None else total + term
    if not turned:
        out_ref[...] = total.astype(out_ref.dtype)
        return
    cosine = cosine_ref[...]
    sine = sine_ref[...]
    for head in range(out_ref.shape[1] // HEAD_DIM):
        at = slice(head * HEAD_DIM, (head + 1) * HEAD_DIM)
        part = total[:, at]
        rolled = pltpu.roll(part, HEAD_DIM // 2, 1)
        out_ref[:, at] = (part * cosine + rolled * sine).astype(out_ref.dtype)


def project(places, offsets, rows, value, pieces, cosine, sine, turned):
    tokens = value.shape[0]
    width = pieces[0][2].shape[1]
    block = min(width, 256)
    input_specs, weight_specs = [], []
    for offset, row, piece in pieces:
        depth = piece.shape[0]

        def place(j, places_ref, slot=offsets.index(offset), scale=rows // depth, at=row // depth):
            return (0, places_ref[slot] * scale + at)

        input_specs.append(pl.BlockSpec((tokens, depth), place))
        weight_specs.append(pl.BlockSpec((depth, block), lambda j, *_: (0, j)))
    angle = pl.BlockSpec((tokens, HEAD_DIM), lambda j, *_: (0, 0))
    return pl.pallas_call(
        functools.partial(project_kernel, len(pieces), turned),
        grid_spec=pltpu.PrefetchScalarGridSpec(
            num_scalar_prefetch=1,
            grid=(width // block,),
            in_specs=input_specs + weight_specs + [angle, angle],
            out_specs=pl.BlockSpec((tokens, block), lambda j, *_: (0, j)),
        ),
        out_shape=jax.ShapeDtypeStruct((tokens, width), jnp.bfloat16),
        compiler_params=pltpu.CompilerParams(vmem_limit_bytes=40 * 1024 * 1024),
        cost_estimate=pl.CostEstimate(
            flops=2 * tokens * value.shape[1] * width,
            bytes_accessed=2 * (tokens + width) * value.shape[1],
            transcendentals=0,
        ),
        name="project",
    )(places, *[value] * len(pieces), *[piece for _, _, piece in pieces], cosine, sine)


def silu(value):
    return value / (1.0 + jnp.exp(-value))


def exact_dot(a, b):
    return jnp.dot(a, b, precision=lax.Precision.HIGHEST, preferred_element_type=jnp.float32)


def spread(heads, block):
    shape = (heads, heads * block)
    column = lax.broadcasted_iota(jnp.int32, shape, 1) // block
    return (column == lax.broadcasted_iota(jnp.int32, shape, 0)).astype(jnp.float32)


def enter_kernel(input_ref, gain_ref, bc_ref, dt_ref, bias_ref, weight_ref, act_ref, map_ref, size_ref, normed_ref):
    @pl.when(pl.program_id(0) == 0)
    def _():
        rows = input_ref.shape[0]
        chunk = min(rows, 64)
        for start in range(0, rows, chunk):
            at = slice(start, start + chunk)
            hidden = input_ref[at, :].astype(jnp.float32)
            scale = lax.rsqrt(jnp.mean(hidden * hidden, axis=-1, keepdims=True) + 1e-05)
            normed_ref[at, :] = (hidden * scale * gain_ref[...]).astype(jnp.bfloat16)
        normed = normed_ref[...]
        map_ref[...] = jnp.dot(normed, bc_ref[...], preferred_element_type=jnp.float32)
        size = jnp.dot(normed, dt_ref[...], preferred_element_type=jnp.float32) + bias_ref[...]
        size_ref[...] = jnp.maximum(size, 0.0) + jnp.log1p(jnp.exp(-jnp.abs(size)))

    act_ref[...] = silu(
        jnp.dot(normed_ref[...], weight_ref[...], preferred_element_type=jnp.float32)
    )


def enter_mixer(flat_input, norm_gain, w_bc, w_dt, dt_bias, weight):
    tokens = flat_input.shape[0]
    width = weight.shape[1]
    block = min(width, 512)
    heads = w_dt.shape[1]
    whole = lambda *shape: pl.BlockSpec(shape, lambda j: (0, 0))
    return pl.pallas_call(
        enter_kernel,
        grid=(width // block,),
        in_specs=[
            whole(tokens, D),
            whole(1, D),
            whole(D, 2 * STATE),
            whole(D, heads),
            whole(1, heads),
            pl.BlockSpec((D, block), lambda j: (0, j)),
        ],
        out_specs=[
            pl.BlockSpec((tokens, block), lambda j: (0, j)),
            whole(tokens, 2 * STATE),
            whole(tokens, heads),
        ],
        out_shape=[
            jax.ShapeDtypeStruct((tokens, width), jnp.float32),
            jax.ShapeDtypeStruct((tokens, 2 * STATE), jnp.float32),
            jax.ShapeDtypeStruct((tokens, heads), jnp.float32),
        ],
        scratch_shapes=[pltpu.VMEM((tokens, D), jnp.bfloat16)],
        compiler_params=pltpu.CompilerParams(vmem_limit_bytes=40 * 1024 * 1024),
        cost_estimate=pl.CostEstimate(
            flops=2 * tokens * D * width,
            bytes_accessed=2 * D * (width + tokens) + 4 * tokens * width,
            transcendentals=tokens * width,
        ),
        name="enter_mixer",
    )(flat_input, norm_gain.reshape(1, D), w_bc, w_dt, dt_bias.reshape(1, heads), weight)


def inside_kernel(inner_ref, map_ref, decay_ref, size_ref, decay_row_ref, size_row_ref, skip_ref, read_ref, local_ref, through_ref):
    tokens, heads = decay_ref.shape[1:]
    inner = inner_ref[...]
    input_map = map_ref[:, :STATE]
    output_map = map_ref[:, STATE:]
    decay = decay_ref[0]
    by_head = spread(heads, MHEAD_DIM)
    wide = (tokens, heads * tokens)
    contact = dot_nt(
        output_map.astype(jnp.bfloat16),
        jnp.concatenate([input_map.astype(jnp.bfloat16)] * heads, axis=0),
    )
    source = lax.rem(lax.broadcasted_iota(jnp.int32, wide, 1), tokens)
    causal = source <= lax.broadcasted_iota(jnp.int32, wide, 0)
    difference = exact_dot(decay, spread(heads, tokens)) - decay_row_ref[0]
    mixing = jnp.exp(jnp.where(causal, difference, DEAD)) * contact * size_row_ref[0]
    mixing = mixing.astype(jnp.bfloat16)
    inner_low = inner.astype(jnp.bfloat16)
    together = min(heads, 256 // MHEAD_DIM)
    shape = (together * tokens, together * MHEAD_DIM)
    own = (
        lax.broadcasted_iota(jnp.int32, shape, 0) // tokens
        == lax.broadcasted_iota(jnp.int32, shape, 1) // MHEAD_DIM
    )
    for begin in range(0, heads, together):
        at = slice(begin * MHEAD_DIM, (begin + together) * MHEAD_DIM)
        stacked = jnp.concatenate([inner_low[:, at]] * together, axis=0)
        stacked = jnp.where(own, stacked, jnp.zeros_like(stacked))
        read_ref[:, at] = (
            jnp.dot(
                mixing[:, begin * tokens : (begin + together) * tokens],
                stacked,
                preferred_element_type=jnp.float32,
            )
            + skip_ref[:, at] * inner[:, at]
        )
    last = decay[tokens - 1 :, :]
    tail = exact_dot(jnp.exp(last - decay) * size_ref[0], by_head)
    local_ref[0] = dot_tn(input_map.astype(jnp.bfloat16), (inner * tail).astype(jnp.bfloat16))
    through_ref[0] = exact_dot(jnp.exp(jnp.broadcast_to(last, (8, heads))), by_head)[:1]


def inside_block(requests, act, maps, decay, size, decay_row, size_row, skip):
    tokens, heads = decay.shape[1:]
    inner = act.shape[1] // 2
    one = lambda *shape: pl.BlockSpec((1,) + shape, lambda r: (r, 0, 0))
    return pl.pallas_call(
        inside_kernel,
        grid=(requests,),
        in_specs=[
            pl.BlockSpec((tokens, inner), lambda r: (r, 1)),
            pl.BlockSpec((tokens, 2 * STATE), lambda r: (r, 0)),
            one(tokens, heads),
            one(tokens, heads),
            one(1, heads * tokens),
            one(1, heads * tokens),
            pl.BlockSpec((1, inner), lambda r: (0, 0)),
        ],
        out_specs=[
            pl.BlockSpec((tokens, inner), lambda r: (r, 0)),
            one(STATE, inner),
            one(1, inner),
        ],
        out_shape=[
            jax.ShapeDtypeStruct((requests * tokens, inner), jnp.float32),
            jax.ShapeDtypeStruct((requests, STATE, inner), jnp.float32),
            jax.ShapeDtypeStruct((requests, 1, inner), jnp.float32),
        ],
        compiler_params=pltpu.CompilerParams(vmem_limit_bytes=40 * 1024 * 1024),
        cost_estimate=pl.CostEstimate(
            flops=12 * requests * tokens * tokens * inner,
            bytes_accessed=16 * requests * tokens * inner,
            transcendentals=requests * tokens * tokens * heads,
        ),
        name="inside_block",
    )(act, maps, decay, size, decay_row, size_row, skip)


def leave_kernel(entry_ref, map_ref, decay_ref, read_ref, gate_ref, gain_ref, local_ref, through_ref, gated_ref, square_ref, chain_ref):
    heads = decay_ref.shape[2]
    entry = entry_ref[0]
    grown = exact_dot(jnp.exp(decay_ref[0]), spread(heads, MHEAD_DIM))
    inter = jnp.dot(
        map_ref[:, STATE:].astype(jnp.bfloat16),
        entry.astype(jnp.bfloat16),
        preferred_element_type=jnp.float32,
    )
    mixed = (read_ref[...] + inter * grown) * gate_ref[...]
    squares = jnp.sum(mixed * mixed, axis=1, keepdims=True)
    square_ref[...] = jnp.broadcast_to(squares, square_ref.shape)
    gated_ref[...] = (mixed * gain_ref[...]).astype(jnp.bfloat16)
    chain_ref[0] = through_ref[0] * entry + local_ref[0]


def leave_mixer(entry, maps, decay, read, act, gain, local, through):
    requests, tokens, heads = decay.shape
    inner = read.shape[1]
    one = lambda *shape: pl.BlockSpec((1,) + shape, lambda r: (r, 0, 0))
    flat = lambda width: pl.BlockSpec((tokens, width), lambda r: (r, 0))
    return pl.pallas_call(
        leave_kernel,
        grid=(requests,),
        in_specs=[
            one(STATE, inner),
            flat(2 * STATE),
            one(tokens, heads),
            flat(inner),
            flat(inner),
            pl.BlockSpec((1, inner), lambda r: (0, 0)),
            one(STATE, inner),
            one(1, inner),
        ],
        out_specs=[flat(inner), flat(128), one(STATE, inner)],
        out_shape=[
            jax.ShapeDtypeStruct((requests * tokens, inner), jnp.bfloat16),
            jax.ShapeDtypeStruct((requests * tokens, 128), jnp.float32),
            jax.ShapeDtypeStruct((requests, STATE, inner), jnp.float32),
        ],
        compiler_params=pltpu.CompilerParams(vmem_limit_bytes=40 * 1024 * 1024),
        cost_estimate=pl.CostEstimate(
            flops=2 * requests * tokens * STATE * inner,
            bytes_accessed=24 * requests * tokens * inner,
            transcendentals=requests * tokens * heads,
        ),
        name="leave_mixer",
    )(entry, maps, decay, read, act, gain, local, through)


def dot_nt(a, b):
    return lax.dot_general(a, b, (((1,), (1,)), ((), ())), preferred_element_type=jnp.float32)


def dot_tn(a, b):
    return lax.dot_general(a, b, (((0,), (0,)), ((), ())), preferred_element_type=jnp.float32)


def cache_kernel(slots, place_ref, live_ref, *refs):
    query_refs = refs[:slots]
    key_ref, value_ref, joined_ref, out_ref, peak_ref, total_ref = refs[slots:]
    tok_block = query_refs[0].shape[1]
    keys, width = key_ref.shape[1:]
    tokens = tok_block * slots
    for slot in range(slots):
        start = pl.multiple_of(place_ref[slot] * tok_block, tok_block)
        joined_ref[0, pl.ds(start, tok_block), :] = query_refs[slot][0]
    live = live_ref[pl.program_id(0)]
    bias = jnp.where(
        lax.broadcasted_iota(jnp.int32, (keys, 128), 0) < live, 0.0, DEAD
    ).astype(jnp.float32)
    bias = jnp.concatenate([bias] * (tokens // 128), axis=1)
    for head in range(width // HEAD_DIM):
        at = slice(head * HEAD_DIM, (head + 1) * HEAD_DIM)
        scores = dot_nt(key_ref[0, :, at], joined_ref[0, :, at]) + bias
        peak = jnp.max(scores, axis=0, keepdims=True)
        weights = jnp.exp2((scores - peak) * EXP2_SCALE)
        total_ref[0, head : head + 1, :] = jnp.sum(weights, axis=0, keepdims=True)
        peak_ref[0, head : head + 1, :] = peak
        out_ref[0, at, :] = dot_tn(value_ref[0, :, at], weights.astype(jnp.bfloat16)).astype(
            out_ref.dtype
        )


def cache_part(begin, at, requests, places, live, query_slots, keys, values):
    slots = len(query_slots)
    tok_block, width = query_slots[0].shape[1:]
    tokens = tok_block * slots
    cache_block = keys.shape[1]
    heads = width // HEAD_DIM
    one = lambda rows, start: pl.BlockSpec((1, rows, width), lambda r, *_: (r + start, 0, 0))
    stat = pl.BlockSpec((1, heads, tokens), lambda r, *_: (r, 0, 0))
    return pl.pallas_call(
        functools.partial(cache_kernel, slots),
        grid_spec=pltpu.PrefetchScalarGridSpec(
            num_scalar_prefetch=2,
            grid=(requests,),
            in_specs=[
                one(tok_block, 0 if slot.shape[0] == requests else at) for slot in query_slots
            ]
            + [one(cache_block, begin), one(cache_block, begin)],
            out_specs=[
                one(tokens, 0),
                pl.BlockSpec((1, width, tokens), lambda r, *_: (r, 0, 0)),
                stat,
                stat,
            ],
        ),
        out_shape=[
            jax.ShapeDtypeStruct((requests, tokens, width), jnp.bfloat16),
            jax.ShapeDtypeStruct((requests, width, tokens), jnp.bfloat16),
            jax.ShapeDtypeStruct((requests, heads, tokens), jnp.float32),
            jax.ShapeDtypeStruct((requests, heads, tokens), jnp.float32),
        ],
        compiler_params=pltpu.CompilerParams(vmem_limit_bytes=48 * 1024 * 1024),
        cost_estimate=pl.CostEstimate(
            flops=4 * requests * tokens * cache_block * width,
            bytes_accessed=2 * requests * width * (3 * tokens + 2 * cache_block),
            transcendentals=requests * tokens * cache_block * heads,
        ),
        name="cache_part",
    )(places, live, *query_slots, keys, values)


def group_scores(first, key, query):
    scores = dot_nt(key, query)
    shape = scores.shape
    live = first + lax.broadcasted_iota(jnp.int32, shape, 0) <= lax.broadcasted_iota(
        jnp.int32, shape, 1
    )
    return jnp.where(live, scores, DEAD)


def peak_kernel(first_ref, query_ref, key_ref, peak_ref, out_ref):
    for head in range(query_ref.shape[2] // HEAD_DIM):
        at = slice(head * HEAD_DIM, (head + 1) * HEAD_DIM)
        scores = group_scores(first_ref[0], key_ref[0, :, at], query_ref[0, :, at])
        out_ref[0, head : head + 1, :] = jnp.maximum(
            peak_ref[0, head : head + 1, :], jnp.max(scores, axis=0, keepdims=True)
        )


def group_peaks(begin, first, queries, new_keys, peaks):
    requests, tokens, width = queries.shape
    tok_block = new_keys.shape[1]
    heads = width // HEAD_DIM
    one = lambda rows, start: pl.BlockSpec((1, rows, width), lambda r, *_: (r + start, 0, 0))
    stat = pl.BlockSpec((1, heads, tokens), lambda r, *_: (r, 0, 0))
    return pl.pallas_call(
        peak_kernel,
        grid_spec=pltpu.PrefetchScalarGridSpec(
            num_scalar_prefetch=1,
            grid=(requests,),
            in_specs=[one(tokens, 0), one(tok_block, begin), stat],
            out_specs=stat,
        ),
        out_shape=jax.ShapeDtypeStruct(peaks.shape, jnp.float32),
        compiler_params=pltpu.CompilerParams(vmem_limit_bytes=32 * 1024 * 1024),
        cost_estimate=pl.CostEstimate(
            flops=2 * requests * tokens * tok_block * width,
            bytes_accessed=2 * requests * width * tokens,
            transcendentals=0,
        ),
        name="group_peaks",
    )(first, queries, new_keys, peaks)


def finish_kernel(slots, first_ref, place_ref, *refs):
    query_ref, key_ref, value_ref, cache_ref, peak_ref, total_ref, best_ref = refs[:7]
    sum_ref, *part_refs = refs[7:-1]
    joined_ref = refs[-1]
    tok_block = key_ref.shape[1]
    for head in range(query_ref.shape[2] // HEAD_DIM):
        at = slice(head * HEAD_DIM, (head + 1) * HEAD_DIM)
        row = slice(head, head + 1)
        scores = group_scores(first_ref[0], key_ref[0, :, at], query_ref[0, :, at])
        best = best_ref[0, row, :]
        weights = jnp.exp2((scores - best) * EXP2_SCALE)
        rescale = jnp.exp2((peak_ref[0, row, :] - best) * EXP2_SCALE)
        sum_ref[0, row, :] = total_ref[0, row, :] * rescale + jnp.sum(
            weights, axis=0, keepdims=True
        )
        joined = cache_ref[0, at, :].astype(jnp.float32) * rescale + dot_tn(
            value_ref[0, :, at], weights.astype(jnp.bfloat16)
        )
        joined_ref[:, at] = joined.T.astype(jnp.bfloat16)
    for slot in range(slots):
        start = pl.multiple_of(place_ref[slot] * tok_block, tok_block)
        part_refs[slot][0] = joined_ref[pl.ds(start, tok_block), :]


def finish_part(begin, first, places, queries, new_keys, new_values, cached, peaks, totals, best):
    requests, tokens, width = queries.shape
    tok_block = new_keys.shape[1]
    slots = tokens // tok_block
    heads = width // HEAD_DIM
    one = lambda rows, start: pl.BlockSpec((1, rows, width), lambda r, *_: (r + start, 0, 0))
    stat = lambda start: pl.BlockSpec((1, heads, tokens), lambda r, *_: (r + start, 0, 0))
    return pl.pallas_call(
        functools.partial(finish_kernel, slots),
        grid_spec=pltpu.PrefetchScalarGridSpec(
            num_scalar_prefetch=2,
            grid=(requests,),
            in_specs=[
                one(tokens, 0),
                one(tok_block, begin),
                one(tok_block, begin),
                pl.BlockSpec((1, width, tokens), lambda r, *_: (r, 0, 0)),
                stat(0),
                stat(0),
                stat(begin),
            ],
            out_specs=[stat(0)] + [one(tok_block, 0)] * slots,
            scratch_shapes=[pltpu.VMEM((tokens, width), jnp.bfloat16)],
        ),
        out_shape=[jax.ShapeDtypeStruct((requests, heads, tokens), jnp.float32)]
        + [jax.ShapeDtypeStruct((requests, tok_block, width), jnp.bfloat16)] * slots,
        compiler_params=pltpu.CompilerParams(vmem_limit_bytes=48 * 1024 * 1024),
        cost_estimate=pl.CostEstimate(
            flops=4 * requests * tokens * tok_block * width,
            bytes_accessed=6 * requests * width * tokens,
            transcendentals=requests * tokens * tok_block * heads,
        ),
        name="finish_part",
    )(first, places, queries, new_keys, new_values, cached, peaks, totals, best)


def head_sum(terms, head_count, head_index):
    if head_count != 4:
        return lax.psum_scatter(
            terms.astype(jnp.bfloat16), "head", scatter_dimension=1, tiled=True
        ).astype(jnp.float32)
    width = terms.shape[1] // 4
    chunk = lambda index: lax.dynamic_slice_in_dim(terms, index * width, width, 1)
    core, column = head_index % 2, head_index // 2
    near, far = 2 * column, 2 * (1 - column)
    got = lax.ppermute(
        jnp.concatenate([chunk(near + 1 - core), chunk(far + 1 - core)], axis=1).astype(
            jnp.bfloat16
        ),
        "head",
        [(h, h ^ 1) for h in range(4)],
    ).astype(jnp.float32)
    keep = chunk(near + core) + got[:, :width]
    give = chunk(far + core) + got[:, width:]
    return keep + lax.ppermute(
        give.astype(jnp.bfloat16), "head", [(h, h ^ 2) for h in range(4)]
    ).astype(jnp.float32)


class Relay:
    def __init__(self, through, local, initial, seq_index, seq_count):
        self.factor, self.local = through, local
        self.paired = seq_count == 8
        self.hop = 0
        if not self.paired:
            self.hops = seq_count - 1
            self.entry = jnp.where(seq_index == 0, initial, 0.0)
            return
        self.hops = 3
        self.swap = [(i, i ^ 1) for i in range(8)]
        self.is_first = is_first = seq_index % 2 == 0
        half = local.shape[2] // 2
        side = lambda value: jnp.where(is_first, value[..., :half], value[..., half:])
        mine = side(local)
        got = self.exchange(jnp.where(is_first, local[..., half:], local[..., :half]))
        other_factor = side(lax.ppermute(through, "seq", self.swap))
        factor = side(through)
        self.first_state = jnp.where(is_first, mine, got)
        second_state = jnp.where(is_first, got, mine)
        self.first_factor = jnp.where(is_first, factor, other_factor)
        second_factor = jnp.where(is_first, other_factor, factor)
        self.pair_state = second_factor * self.first_state + second_state
        self.pair_factor = self.first_factor * second_factor
        self.entry = jnp.where(seq_index < 2, side(initial), 0.0)

    def exchange(self, value):
        return lax.ppermute(value.astype(jnp.bfloat16), "seq", self.swap).astype(jnp.float32)

    def advance(self, clock):
        if self.hop == self.hops:
            return
        factor, state = (
            (self.pair_factor, self.pair_state) if self.paired else (self.factor, self.local)
        )
        entry = clock.hold(self.entry)
        leaving = (factor * entry + state).astype(jnp.bfloat16)
        if self.paired:
            route = [(2 * self.hop + y, 2 * self.hop + 2 + y) for y in range(2)]
        else:
            route = [(self.hop, self.hop + 1)]
        self.hop += 1
        self.entry = entry + lax.ppermute(leaving, "seq", route).astype(jnp.float32)

    def result(self, clock):
        while self.hop < self.hops:
            self.advance(clock)
        entry = clock.hold(self.entry)
        if not self.paired:
            return entry
        second = self.first_factor * entry + self.first_state
        got = self.exchange(jnp.where(self.is_first, second, entry))
        mine = jnp.where(self.is_first, entry, second)
        return jnp.concatenate(
            [jnp.where(self.is_first, mine, got), jnp.where(self.is_first, got, mine)], axis=2
        )


def shards(
    block_input,
    lengths,
    cache_keys,
    cache_values,
    w_query,
    w_key,
    w_value,
    w_attn_out,
    norm_gain,
    w_in,
    w_bc,
    w_dt,
    dt_bias,
    a_log,
    d_skip,
    gated_gain,
    w_out,
    ssm_init,
):
    requests, tok_block, _ = block_input.shape
    seq_count = lax.axis_size("seq")
    seq_index = lax.axis_index("seq")
    head_count = lax.axis_size("head")
    head_index = lax.axis_index("head")
    local_att = w_query.shape[1]
    local_heads = local_att // HEAD_DIM
    cache_block = cache_keys.shape[1]
    rows = w_query.shape[0]
    tokens = requests * tok_block
    flat_input = block_input.reshape(tokens, block_input.shape[2])

    order = ring_order(seq_count)
    half = seq_count // 2
    offsets = [0] + [sign * step for step in range(1, half) for sign in (1, -1)] + [half]
    places = jnp.asarray(
        [
            [order[(order.index(i) - offset) % seq_count] for offset in offsets]
            for i in range(seq_count)
        ],
        jnp.int32,
    )[seq_index]

    positions = (
        lengths[:, None] + seq_index * tok_block + jnp.arange(tok_block, dtype=jnp.int32)[None, :]
    ).reshape(tokens)
    half_dim = HEAD_DIM // 2
    frequency = jnp.exp(
        jnp.arange(half_dim, dtype=jnp.float32) * (-2.0 * math.log(10000.0) / HEAD_DIM)
    )
    angles = positions.astype(jnp.float32)[:, None] * frequency
    cosine = jnp.cos(angles)
    sine = jnp.sin(angles)
    cosine = jnp.concatenate([cosine, cosine], axis=1)
    sine = jnp.concatenate([-sine, sine], axis=1)

    clock = Clock()
    group = requests // GROUPS
    part_size = group // 2
    local_inner = w_in.shape[2]
    local_mheads = local_inner // MHEAD_DIM
    local_width = D // head_count
    made = {}

    def weight_rings(weight):
        top = weight.shape[0] // 2
        return [Ring(weight[:top], order), Ring(weight[top:], order, top)]

    def product(rings, turned):
        pieces = []
        for ring in rings:
            pieces += ring.pieces
            if pieces[-1][2].shape[0] < 128:
                (offset, row, upper), (_, _, lower) = pieces[-2:]
                pieces[-2:] = [(offset, row, jnp.concatenate([upper, lower], axis=0))]
        return project(
            places, offsets, rows, flat_input, pieces, cosine, sine, turned
        ).reshape(requests, tok_block, local_att)

    def order_weight():
        made["w_in"] = w_in.reshape(D, 2 * local_inner)
        return (made["w_in"],), ()

    def enter():
        made["act"], made["maps"], size = enter_mixer(
            clock.hold(flat_input), norm_gain, w_bc, w_dt, dt_bias, made["w_in"]
        )
        size = size.reshape(requests, tok_block, local_mheads)
        log_decay = -size * jnp.exp(a_log)
        causal = jnp.arange(tok_block)[None, :] <= jnp.arange(tok_block)[:, None]
        decay = jnp.einsum(
            "tu,ruh->rth", causal.astype(jnp.float32), log_decay, precision=lax.Precision.HIGHEST
        )
        by_row = lambda value: jnp.transpose(value, (0, 2, 1)).reshape(
            requests, 1, local_mheads * tok_block
        )
        made["size"], made["decay"] = size, decay
        made["size_row"], made["decay_row"] = by_row(size), by_row(decay)
        return (made["act"], made["size_row"], made["decay_row"]), ()

    def inside():
        made["read"], made["local"], made["through"] = inside_block(
            requests,
            clock.hold(made["act"]),
            made["maps"],
            made["decay"],
            made["size"],
            made["decay_row"],
            made["size_row"],
            jnp.repeat(d_skip, MHEAD_DIM).reshape(1, local_inner),
        )
        return (made["read"], made["local"]), ()

    def initial_state():
        first_state = clock.hold(ssm_init).reshape(requests, local_mheads, MHEAD_DIM, STATE)
        made["initial"] = jnp.transpose(first_state, (0, 3, 1, 2)).reshape(
            requests, STATE, local_inner
        )
        return (made["initial"],), ()

    def start_relay():
        made["relay"] = relay = Relay(
            made["through"], clock.hold(made["local"]), made["initial"], seq_index, seq_count
        )
        return (), ((relay.pair_state,) if relay.paired else ())

    def hop():
        made["relay"].advance(clock)
        return (), (made["relay"].entry,)

    def end_relay():
        made["entry"] = made["relay"].result(clock)
        return (), (made["entry"],)

    def leave():
        gated, squares, chain = leave_mixer(
            clock.hold(made["entry"]),
            made["maps"],
            made["decay"],
            made["read"],
            made["act"],
            gated_gain.reshape(1, local_inner),
            made["local"],
            made["through"],
        )
        made["gated"] = gated
        made["squares"] = butterfly(
            squares[:, :1].reshape(1, tokens), "head", head_count, jnp.add
        )
        made["chain"] = chain
        return (gated,), (made["squares"],)

    def leave_terms():
        made["terms"] = jnp.dot(
            clock.hold(made["gated"]), w_out, preferred_element_type=jnp.float32
        ) * lax.rsqrt(made["squares"].reshape(tokens, 1) / D_INNER + 1e-05)
        return (made["terms"],), ()

    def leave_chain():
        chain = clock.hold(made["chain"]).reshape(requests, STATE, local_mheads, MHEAD_DIM)
        made["chain"] = jnp.transpose(chain, (0, 2, 3, 1)).reshape(
            requests, 1, local_mheads, MHEAD_DIM * STATE
        )
        return (made["chain"],), ()

    query_rings = weight_rings(w_query)
    key_rings = weight_rings(w_key)
    value_rings = weight_rings(w_value)
    slot_rings = []
    live = jnp.clip(lengths - seq_index * cache_block, 0, cache_block).astype(jnp.int32)
    first = (seq_index * tok_block).astype(jnp.int32).reshape(1)
    cached = []

    def make_queries():
        queries = product(query_rings, True)
        slot_rings.extend(
            Ring(queries[begin : begin + group], order) for begin in range(0, requests, group)
        )
        return (queries,), ()

    def make_keys():
        made["keys"] = product(key_rings, True)
        return (made["keys"],), ()

    def meet_cache(index):
        def work():
            ring = slot_rings[index // 2]
            at = (index % 2) * part_size
            begin = index * part_size
            slots = [piece for _, _, piece in ring.pieces[:-2]]
            slots.append(ring.pieces[-2 + index % 2][2])
            slots[0] = clock.hold(slots[0])
            cached.append(
                cache_part(
                    begin,
                    at,
                    part_size,
                    places,
                    live[begin : begin + part_size],
                    slots,
                    cache_keys,
                    cache_values,
                )
            )
            return tuple(cached[-1]), ()

        return work

    def make_peaks():
        keys = clock.hold(made["keys"])
        made["peaks"] = jnp.concatenate(
            [
                group_peaks(index * part_size, first, part[0], keys, part[2])
                for index, part in enumerate(cached)
            ],
            axis=0,
        )
        return (made["peaks"],), ()

    def join_peaks():
        made["best"] = butterfly(clock.hold(made["peaks"]), "seq", seq_count, jnp.maximum)
        return (), ()

    def steps(rings, begin, end):
        return [ring for _ in range(begin, end) for ring in rings]

    def run(sends, works):
        for index in range(max(len(sends), len(works))):
            clock.turn(
                sends[index] if index < len(sends) else None,
                works[index] if index < len(works) else None,
            )

    run(
        steps(query_rings, 0, half),
        [order_weight, None, enter, inside, initial_state, start_relay, None, hop],
    )
    run(steps(key_rings, 0, 1), [make_queries])
    run(
        steps(slot_rings, 0, half),
        [None, hop, None, None, hop, None, None, end_relay],
    )
    run(
        steps(key_rings, 1, half) + steps(value_rings, 0, half),
        [meet_cache(0), meet_cache(1), meet_cache(2), meet_cache(3), leave, leave_terms]
        + [make_keys, make_peaks, join_peaks, None, None, leave_chain],
    )

    new_keys = made["keys"]
    best = made["best"]
    new_values = product(value_rings, False)

    own = lambda stat: lax.dynamic_slice_in_dim(stat, seq_index * tok_block, tok_block, 2)
    greatest_logit = jnp.transpose(own(best), (0, 2, 1)) * SCALE
    residual = lax.dynamic_slice_in_dim(
        flat_input, head_index * local_width, local_width, 1
    ).astype(jnp.float32)
    mixed = []
    for index in range(GROUPS):
        begin = index * group
        sums, parts = [], []
        for inner_index in range(2):
            joined, out, peaks, totals = cached[2 * index + inner_index]
            some_sums, *some_parts = finish_part(
                begin + inner_index * part_size,
                first,
                places,
                joined,
                new_keys,
                new_values,
                out,
                peaks,
                totals,
                best,
            )
            sums.append(some_sums)
            parts.append(some_parts)
        sums = butterfly(jnp.concatenate(sums, axis=0), "seq", seq_count, jnp.add)
        denominator = jnp.transpose(own(sums), (0, 2, 1))
        terms = {-offset: pair for offset, pair in zip(offsets, zip(*parts))}
        terms[half] = terms[-half]
        numerator = ring_sum(terms, order).reshape(group, tok_block, local_heads, HEAD_DIM)
        attended = (
            (numerator / denominator[..., None])
            .astype(jnp.bfloat16)
            .reshape(group * tok_block, local_att)
        )
        at = slice(begin * tok_block, (begin + group) * tok_block)
        attn_terms = jnp.dot(attended, w_attn_out, preferred_element_type=jnp.float32)
        summed = head_sum(attn_terms + made["terms"][at], head_count, head_index)
        mixed.append(
            (residual[at] + summed)
            .astype(jnp.bfloat16)
            .reshape(group, tok_block, local_width)
        )
    return (
        jnp.concatenate(mixed, axis=0),
        new_keys,
        new_values,
        made["chain"],
        greatest_logit,
    )


def solution(mesh):
    placed = (
        P(None, "seq", None),
        P(),
        P(None, "seq", "head"),
        P(None, "seq", "head"),
        P("seq", "head"),
        P("seq", "head"),
        P("seq", "head"),
        P("head", None),
        P(),
        P(None, None, "head"),
        P(),
        P(None, "head"),
        P("head"),
        P("head"),
        P("head"),
        P("head"),
        P("head", None),
        P(None, "head", None),
    )
    return jax.shard_map(
        shards,
        mesh=mesh,
        in_specs=placed,
        out_specs=(
            P(None, "seq", "head"),
            P(None, "seq", "head"),
            P(None, "seq", "head"),
            P(None, "seq", "head", None),
            P(None, "seq", "head"),
        ),
        check_vma=False,
    )
```

time: 644 us -> 617 us (0.958)
  matrix products: 112 us -> 7.19 us
  Pallas kernels: 75.6 us -> 127 us
  starting transfers between devices: 91.5 us -> 132 us
  waiting for transfers between devices: 206 us -> 195 us
  between operations: 13.1 us -> 2.55 us
    dot_general x36 -> x2, matrix products: 109 us -> 4.67 us  [the longest x1 4.31 us: leave_terms(): jnp.dot(clock.hold(made['gated']), w_out, preferred_element_type=jnp.floa...]
    ppermute x48 -> x80, waiting for transfers between devices: 88.2 us -> 144 us  [ring_step(): return lax.ppermute(block, 'seq', route)]
    ppermute x2, waiting for transfers between devices: 54.2 us -> 7.97 us  [exchange(): lax.ppermute(value.astype(jnp.bfloat16), 'seq', self.swap)]
    ppermute x48 -> x80, starting transfers between devices: 64.4 us -> 110 us  [ring_step(): return lax.ppermute(block, 'seq', route)]
    pallas_call x2 -> x6, Pallas kernels: 8.03 us -> 49 us  [the longest x3 28.1 us: project(): pl.pallas_call(functools.partial(project_kernel, len(pieces), turned), gr...]
    unnamed x159 -> x290, local copies, waits for them, and re-layouts: 24.7 us -> 59.9 us
    ppermute x3, waiting for transfers between devices: 18 us -> 0.01 us  [advance(): self.entry = entry + lax.ppermute(leaving, 'seq', route).astype(jnp.float32)]
    squeeze x4 -> x1, local copies, waits for them, and re-layouts: 18.3 us -> 0.78 us  [shards(): jnp.asarray([[order[(order.index(i) - offset) % seq_count] for offset in...]
  transfers between devices with their start and end apart: 69 -> 101, of which waited for: 32 -> 49; matrix products, arithmetic and copies ran while one was open for 35% -> 15% of each run, Pallas kernels for 10% -> 15%
where the time goes in v3:
time: 617 us; the launch traced here: 605 us
  waiting for transfers between devices  195 us (32%)
  starting transfers between devices  132 us (21%)
  Pallas kernels  127 us (21%)
  local copies, waits for them, and re-layouts  101 us (16%)
  other arithmetic  40.6 us (7%)
  matrix products  7.19 us (1%)
    ppermute x80, waiting for transfers between devices, ring_step(): return lax.ppermute(block, 'seq', route)  144 us
    ppermute x80, starting transfers between devices, ring_step(): return lax.ppermute(block, 'seq', route)  110 us
    unnamed x290, local copies, waits for them, and re-layouts  59.9 us
    pallas_call x4, Pallas kernels, cache_part(): pl.pallas_call(functools.partial(cache_kernel, slots), grid_spec=pltpu.Pr...  49 us
    ppermute x11, waiting for transfers between devices, butterfly(): lax.ppermute(value, axis, [(i, i ^ bit) for i in range(count)])  36.4 us
    pallas_call x3, Pallas kernels, project(): pl.pallas_call(functools.partial(project_kernel, len(pieces), turned), gr...  28.1 us
    pallas_call x4, Pallas kernels, finish_part(): pl.pallas_call(functools.partial(finish_kernel, slots), grid_spec=pltpu.P...  24.7 us
  transfers between devices with their start and end apart: 101, of which 49 were waited for; matrix products, arithmetic and copies ran while one was open for 15% of the time, Pallas kernels for 15%

profile of v3, /device:TPU:0, one launch (start us, length us, event | category | flops | bytes accessed | tf_op | source)
XLA Modules:
  0.0 605.5 jit_solution(3506586130841945664)
XLA Ops:
  5.0 10.3 %copy.52 = bf16[256,8,2,1024]{3,1,2,0:T(8,128)(2,1)} copy(bf16[256,8,2,1024]{3,2,1,0:T(2,128)(2,1)} %bitcast.153) | data formatting | bytes 16777216
  22.7 9.3 %enter_mixer.1 = (f32[512,2048]{1,0:T(8,128)S(1)}, f32[512,128]{1,0:T(8,128)S(1)}, f32[512,16]{1,0:T(8,128)S(1)}) custom-call(bf16[512,4096]{1,0:T(8,128)(2,1)S(1)} %bitcast.66, f32[1,2048]{1,0:T(1,128)S(1)} %bitcast.149, bf16[2048,128]{1,0:T(8,128)(2,1)S(1)} %copy-done.117, bf16[2048,16]{1,0:T(8,128)(2,1)S(1)} %copy.40.dt_ref, f32[1,16]{1,0:T(1,128)S(1)} %bitcast.150, ...), custom_call_target="tpu_custom_call" | custom-call | flops 4294967296 | bytes 14680064 | tf_op jit(solution)/shard_map/enter_mixer/pallas_call | solution.py:197
  39.4 7.6 %inside_block.1 = (f32[512,1024]{1,0:T(8,128)S(1)}, f32[8,64,1024]{2,1,0:T(8,128)S(1)}, f32[8,1,1024]{2,1,0:T(1,128)S(1)}) custom-call(f32[512,2048]{1,0:T(8,128)S(1)} %copy-done.7, f32[512,128]{1,0:T(8,128)S(1)} %get-tuple-element.157.map_ref, f32[8,64,16]{2,1,0:T(8,128)S(1)} %bitcast.143, f32[8,64,16]{2,1,0:T(8,128)S(1)} %bitcast.147, ...), custom_call_target="tpu_custom_call" | custom-call | flops 402653184 | bytes 8388608 | tf_op jit(solution)/shard_map/inside_block/pallas_call | solution.py:275
  54.4 5.6 copy.44
  71.9 8.0 %collective-permute-done.15 = bf16[8,64,512]{2,1,0:T(8,128)(2,1)S(1)} collective-permute-done((bf16[8,64,512]{2,1,0:T(8,128)(2,1)S(1)}, bf16[8,64,512]{2,1,0:T(8,128)(2,1)S(1)}, u32[]{:S(2)}, u32[]{:S(2)}) %collective-permute-start.15) | collective-permute-done | bytes 524320 | tf_op jit(solution)/shard_map/ppermute | solution.py:584
  81.1 10.0 %collective-permute-done.12.refs_32_ = bf16[256,1024]{1,0:T(8,128)(2,1)S(1)} collective-permute-done((bf16[256,1024]{1,0:T(8,128)(2,1)}, bf16[256,1024]{1,0:T(8,128)(2,1)S(1)}, u32[]{:S(2)}, u32[]{:S(2)}) %collective-permute-start.12) | collective-permute-done | bytes 524320 | tf_op jit(solution)/shard_map/ppermute | solution.py:35
  117.6 9.1 %project.3 = bf16[512,1024]{1,0:T(8,128)(2,1)S(1)} custom-call(s32[8]{0:T(128)S(1)} %fusion.22.places_ref.place_ref, bf16[512,4096]{1,0:T(8,128)(2,1)S(1)} %bitcast.67, bf16[512,4096]{1,0:T(8,128)(2,1)S(1)} %bitcast.68, bf16[512,4096]{1,0:T(8,128)(2,1)S(1)} %bitcast.69, bf16[512,4096]{1,0:T(8,128)(2,1)S(1)} %bitcast.70, bf16[512,4096]{1,0:T(8,128)(2,1)S(1)} %bitcast.71, ...), custom_call_target="tpu_custom_call" | custom-call | flops 4294967296 | bytes 12582912 | tf_op jit(solution)/shard_map/project/pallas_call | solution.py:138
  129.0 9.2 %collective-permute-done.27.refs_28_ = bf16[256,1024]{1,0:T(8,128)(2,1)} collective-permute-done((bf16[256,1024]{1,0:T(8,128)(2,1)S(1)}, bf16[256,1024]{1,0:T(8,128)(2,1)}, u32[]{:S(2)}, u32[]{:S(2)}) %collective-permute-start.27) | collective-permute-done | bytes 524320 | tf_op jit(solution)/shard_map/ppermute | solution.py:35
  151.5 9.0 %collective-permute-done.35.refs_1_ = bf16[4,64,1024]{2,1,0:T(8,128)(2,1)S(1)} collective-permute-done((bf16[4,64,1024]{2,1,0:T(8,128)(2,1)S(1)}, bf16[4,64,1024]{2,1,0:T(8,128)(2,1)S(1)}, u32[]{:S(2)}, u32[]{:S(2)}) %collective-permute-start.35) | collective-permute-done | bytes 524320 | tf_op jit(solution)/shard_map/ppermute | solution.py:35
  160.5 10.6 %collective-permute-start.37 = (bf16[4,64,1024]{2,1,0:T(8,128)(2,1)S(1)}, bf16[4,64,1024]{2,1,0:T(8,128)(2,1)S(1)}, u32[]{:S(2)}, u32[]{:S(2)}) collective-permute-start(bf16[4,64,1024]{2,1,0:T(8,128)(2,1)S(1)} %collective-permute-done.35.refs_1_), channel_id=1, source_target_pairs={{0,8},{8,16},{16,24},{24,28},{28,20},{20,12},{12,4},{4,0},{1,9},{9... | collective-permute-start | bytes 1572872 | tf_op jit(solution)/shard_map/ppermute | solution.py:35
  172.7 7.3 %collective-permute-done.37.refs_3_ = bf16[4,64,1024]{2,1,0:T(8,128)(2,1)S(1)} collective-permute-done((bf16[4,64,1024]{2,1,0:T(8,128)(2,1)S(1)}, bf16[4,64,1024]{2,1,0:T(8,128)(2,1)S(1)}, u32[]{:S(2)}, u32[]{:S(2)}) %collective-permute-start.37) | collective-permute-done | bytes 524320 | tf_op jit(solution)/shard_map/ppermute | solution.py:35
  180.9 10.0 %collective-permute-start.39 = (bf16[4,64,1024]{2,1,0:T(8,128)(2,1)S(1)}, bf16[4,64,1024]{2,1,0:T(8,128)(2,1)S(1)}, u32[]{:S(2)}, u32[]{:S(2)}) collective-permute-start(bf16[4,64,1024]{2,1,0:T(8,128)(2,1)S(1)} %collective-permute-done.37.refs_3_), channel_id=1, source_target_pairs={{0,8},{8,16},{16,24},{24,28},{28,20},{20,12},{12,4},{4,0},{1,9},{9... | collective-permute-start | bytes 1572872 | tf_op jit(solution)/shard_map/ppermute | solution.py:35
  205.5 6.4 %collective-permute-done.25.refs_6_ = bf16[4,64,1024]{2,1,0:T(8,128)(2,1)S(1)} collective-permute-done((bf16[4,64,1024]{2,1,0:T(8,128)(2,1)S(1)}, bf16[4,64,1024]{2,1,0:T(8,128)(2,1)S(1)}, u32[]{:S(2)}, u32[]{:S(2)}) %collective-permute-start.25) | collective-permute-done | bytes 524320 | tf_op jit(solution)/shard_map/ppermute | solution.py:35
  214.6 5.3 collective-permute-done.31.refs_7_
  219.9 5.7 collective-permute-done.32.refs_7_
  231.5 12.2 %cache_part.4 = (bf16[2,512,1024]{2,1,0:T(8,128)(2,1)S(1)}, bf16[2,1024,512]{2,1,0:T(8,128)(2,1)}, f32[2,8,512]{2,1,0:T(8,128)S(1)}, f32[2,8,512]{2,1,0:T(8,128)S(1)}) custom-call(s32[8]{0:T(128)S(1)} %fusion.22.places_ref.place_ref, s32[2]{0:T(128)S(1)} %get-tuple-element.320.live_ref, bf16[4,64,1024]{2,1,0:T(8,128)(2,1)S(1)} %bitcast.141, ...), custom_call_target="tpu_custom_call" | custom-call | flops 2147483648 | bytes 10485760 | tf_op jit(solution)/shard_map/cache_part/pallas_call | solution.py:399
  251.9 12.2 %cache_part.5 = (bf16[2,512,1024]{2,1,0:T(8,128)(2,1)S(1)}, bf16[2,1024,512]{2,1,0:T(8,128)(2,1)}, f32[2,8,512]{2,1,0:T(8,128)S(1)}, f32[2,8,512]{2,1,0:T(8,128)S(1)}) custom-call(s32[8]{0:T(128)S(1)} %fusion.22.places_ref.place_ref, s32[2]{0:T(128)S(1)} %get-tuple-element.319.live_ref, bf16[4,64,1024]{2,1,0:T(8,128)(2,1)S(1)} %bitcast.142, ...), custom_call_target="tpu_custom_call" | custom-call | flops 2147483648 | bytes 10485760 | tf_op jit(solution)/shard_map/cache_part/pallas_call | solution.py:399
  269.7 12.2 %cache_part.6 = (bf16[2,512,1024]{2,1,0:T(8,128)(2,1)S(1)}, bf16[2,1024,512]{2,1,0:T(8,128)(2,1)}, f32[2,8,512]{2,1,0:T(8,128)S(1)}, f32[2,8,512]{2,1,0:T(8,128)S(1)}) custom-call(s32[8]{0:T(128)S(1)} %fusion.22.places_ref.place_ref, s32[2]{0:T(128)S(1)} %get-tuple-element.318.live_ref, bf16[4,64,1024]{2,1,0:T(8,128)(2,1)S(1)} %bitcast.137, ...), custom_call_target="tpu_custom_call" | custom-call | flops 2147483648 | bytes 10485760 | tf_op jit(solution)/shard_map/cache_part/pallas_call | solution.py:399
  291.2 12.4 %cache_part.7 = (bf16[2,512,1024]{2,1,0:T(8,128)(2,1)S(1)}, bf16[2,1024,512]{2,1,0:T(8,128)(2,1)}, f32[2,8,512]{2,1,0:T(8,128)S(1)}, f32[2,8,512]{2,1,0:T(8,128)S(1)}) custom-call(s32[8]{0:T(128)S(1)} %fusion.22.places_ref.place_ref, s32[2]{0:T(128)S(1)} %get-tuple-element.317.live_ref, bf16[4,64,1024]{2,1,0:T(8,128)(2,1)S(1)} %bitcast.138, ...), custom_call_target="tpu_custom_call" | custom-call | flops 2147483648 | bytes 10485760 | tf_op jit(solution)/shard_map/cache_part/pallas_call | solution.py:399
  336.9 9.7 %project.4 = bf16[512,1024]{1,0:T(8,128)(2,1)} custom-call(s32[8]{0:T(128)S(1)} %fusion.22.places_ref.place_ref, bf16[512,4096]{1,0:T(8,128)(2,1)S(1)} %bitcast.93, bf16[512,4096]{1,0:T(8,128)(2,1)S(1)} %bitcast.86, bf16[512,4096]{1,0:T(8,128)(2,1)S(1)} %bitcast.87, bf16[512,4096]{1,0:T(8,128)(2,1)S(1)} %bitcast.88, bf16[512,4096]{1,0:T(8,128)(2,1)S(1)} %bitcast.89, ...), custom_call_target="tpu_custom_call" | custom-call | flops 4294967296 | bytes 12582912 | tf_op jit(solution)/shard_map/project/pallas_call | solution.py:138
  365.9 6.6 %collective-permute-done.58.refs_21_ = bf16[256,1024]{1,0:T(8,128)(2,1)} collective-permute-done((bf16[256,1024]{1,0:T(8,128)(2,1)S(1)}, bf16[256,1024]{1,0:T(8,128)(2,1)}, u32[]{:S(2)}, u32[]{:S(2)}) %collective-permute-start.58) | collective-permute-done | bytes 524320 | tf_op jit(solution)/shard_map/ppermute | solution.py:35
  375.6 8.1 %collective-permute-done.64.refs_30_ = bf16[256,1024]{1,0:T(8,128)(2,1)} collective-permute-done((bf16[256,1024]{1,0:T(8,128)(2,1)S(1)}, bf16[256,1024]{1,0:T(8,128)(2,1)}, u32[]{:S(2)}, u32[]{:S(2)}) %collective-permute-start.64) | collective-permute-done | bytes 524320 | tf_op jit(solution)/shard_map/ppermute | solution.py:35
  387.1 18.9 %collective-permute-done.72 = f32[8,8,512]{2,1,0:T(8,128)S(1)} collective-permute-done((f32[8,8,512]{2,1,0:T(8,128)S(1)}, f32[8,8,512]{2,1,0:T(8,128)S(1)}, u32[]{:S(2)}, u32[]{:S(2)}) %collective-permute-start.72) | collective-permute-done | bytes 131104 | tf_op jit(solution)/shard_map/ppermute | solution.py:83
  408.7 5.5 copy.45
  430.3 10.2 %collective-permute-done.74 = f32[8,8,512]{2,1,0:T(8,128)S(1)} collective-permute-done((f32[8,8,512]{2,1,0:T(8,128)S(1)}, f32[8,8,512]{2,1,0:T(8,128)S(1)}, u32[]{:S(2)}, u32[]{:S(2)}) %collective-permute-start.74) | collective-permute-done | bytes 131104 | tf_op jit(solution)/shard_map/ppermute | solution.py:83
  442.8 9.3 %project.5 = bf16[512,1024]{1,0:T(8,128)(2,1)} custom-call(s32[8]{0:T(128)S(1)} %fusion.22.places_ref.place_ref, bf16[512,4096]{1,0:T(8,128)(2,1)S(1)} %bitcast.104, bf16[512,4096]{1,0:T(8,128)(2,1)S(1)} %bitcast.103, bf16[512,4096]{1,0:T(8,128)(2,1)S(1)} %bitcast.105, bf16[512,4096]{1,0:T(8,128)(2,1)S(1)} %bitcast.106, bf16[512,4096]{1,0:T(8,128)(2,1)S(1)} %bitcast.107, ...), custom_call_target="tpu_custom_call" | custom-call | flops 4294967296 | bytes 12582912 | tf_op jit(solution)/shard_map/project/pallas_call | solution.py:138
  453.4 6.0 finish_part.6
  462.3 6.7 %finish_part.7 = (f32[2,8,512]{2,1,0:T(8,128)S(1)}, bf16[2,64,1024]{2,1,0:T(8,128)(2,1)S(1)}, bf16[2,64,1024]{2,1,0:T(8,128)(2,1)S(1)}, bf16[2,64,1024]{2,1,0:T(...) custom-call(s32[1]{0:T(128)} %bitcast.1.first_ref, ...), custom_call_target="tpu_custom_call" | custom-call | flops 268435456 | bytes 6291456 | tf_op jit(solution)/shard_map/finish_part/pallas_call | solution.py:505
  471.8 6.0 finish_part.4
  480.7 6.0 finish_part.5
  518.4 7.4 %collective-permute-done.93 = bf16[4,64,1024]{2,1,0:T(8,128)(2,1)S(1)} collective-permute-done((bf16[4,64,1024]{2,1,0:T(8,128)(2,1)S(1)}, bf16[4,64,1024]{2,1,0:T(8,128)(2,1)S(1)}, u32[]{:S(2)}, u32[]{:S(2)}) %collective-permute-start.93) | collective-permute-done | bytes 524320 | tf_op jit(solution)/shard_map/ppermute | solution.py:35
  531.0 5.9 collective-permute-done.80
  (587 shorter events, 324.3 us)
Async XLA Ops:
  18.5 31.3 %collective-permute-start.2 = (bf16[256,1024]{1,0:T(8,128)(2,1)}, bf16[256,1024]{1,0:T(8,128)(2,1)}, u32[]{:S(2)}, u32[]{:S(2)}) collective-permute-start(bf16[256,1024]{1,0:T(8,128)(2,1)} %collective-permute-done.refs_19_), channel_id=1, source_target_pairs={{0,8},{8,16},{16,24},{24,28},{28,20},{20,12},{12,4},{4,0},{1,9},{9... | collective-permute-start | bytes 1572872 | tf_op jit(solution)/shard_map/ppermute | solution.py:35
  20.1 29.7 %collective-permute-start.3 = (bf16[256,1024]{1,0:T(8,128)(2,1)}, bf16[256,1024]{1,0:T(8,128)(2,1)}, u32[]{:S(2)}, u32[]{:S(2)}) collective-permute-start(bf16[256,1024]{1,0:T(8,128)(2,1)} %collective-permute-done.1.refs_20_), channel_id=1, source_target_pairs={{0,4},{8,0},{16,8},{24,16},{28,24},{20,28},{12,20},{4,12},{1,5},{9... | collective-permute-start | bytes 1572872 | tf_op jit(solution)/shard_map/ppermute | solution.py:35
  34.8 30.1 %collective-permute-start.10 = (bf16[256,1024]{1,0:T(8,128)(2,1)}, bf16[256,1024]{1,0:T(8,128)(2,1)}, u32[]{:S(2)}, u32[]{:S(2)}) collective-permute-start(bf16[256,1024]{1,0:T(8,128)(2,1)} %collective-permute-done.4.refs_28_), channel_id=1, source_target_pairs={{0,8},{8,16},{16,24},{24,28},{28,20},{20,12},{12,4},{4,0},{1,9},{9... | collective-permute-start | bytes 1572872 | tf_op jit(solution)/shard_map/ppermute | solution.py:35
  36.4 28.4 %collective-permute-start.11 = (bf16[256,1024]{1,0:T(8,128)(2,1)}, bf16[256,1024]{1,0:T(8,128)(2,1)}, u32[]{:S(2)}, u32[]{:S(2)}) collective-permute-start(bf16[256,1024]{1,0:T(8,128)(2,1)} %collective-permute-done.5.refs_29_), channel_id=1, source_target_pairs={{0,4},{8,0},{16,8},{24,16},{28,24},{20,28},{12,20},{4,12},{1,5},{9... | collective-permute-start | bytes 1572872 | tf_op jit(solution)/shard_map/ppermute | solution.py:35
  65.7 25.4 %collective-permute-start.12 = (bf16[256,1024]{1,0:T(8,128)(2,1)}, bf16[256,1024]{1,0:T(8,128)(2,1)S(1)}, u32[]{:S(2)}, u32[]{:S(2)}) collective-permute-start(bf16[256,1024]{1,0:T(8,128)(2,1)} %collective-permute-done.10.refs_30_), channel_id=1, source_target_pairs={{0,8},{8,16},{16,24},{24,28},{28,20},{20,12},{12,4},{4,0},{1,9},{9... | collective-permute-start | bytes 1572872 | tf_op jit(solution)/shard_map/ppermute | solution.py:35
  67.4 23.7 %collective-permute-start.13 = (bf16[256,1024]{1,0:T(8,128)(2,1)}, bf16[256,1024]{1,0:T(8,128)(2,1)}, u32[]{:S(2)}, u32[]{:S(2)}) collective-permute-start(bf16[256,1024]{1,0:T(8,128)(2,1)} %collective-permute-done.11.refs_31_), channel_id=1, source_target_pairs={{0,4},{8,0},{16,8},{24,16},{28,24},{20,28},{12,20},{4,12},{1,5},{9... | collective-permute-start | bytes 1572872 | tf_op jit(solution)/shard_map/ppermute | solution.py:35
  67.8 30.9 %collective-permute-start.6 = (bf16[256,1024]{1,0:T(8,128)(2,1)}, bf16[256,1024]{1,0:T(8,128)(2,1)}, u32[]{:S(2)}, u32[]{:S(2)}) collective-permute-start(bf16[256,1024]{1,0:T(8,128)(2,1)} %collective-permute-done.2.refs_21_), channel_id=1, source_target_pairs={{0,8},{8,16},{16,24},{24,28},{28,20},{20,12},{12,4},{4,0},{1,9},{9... | collective-permute-start | bytes 1572872 | tf_op jit(solution)/shard_map/ppermute | solution.py:35
  69.4 30.3 %collective-permute-start.7 = (bf16[256,1024]{1,0:T(8,128)(2,1)}, bf16[256,1024]{1,0:T(8,128)(2,1)}, u32[]{:S(2)}, u32[]{:S(2)}) collective-permute-start(bf16[256,1024]{1,0:T(8,128)(2,1)} %collective-permute-done.3.refs_22_), channel_id=1, source_target_pairs={{0,4},{8,0},{16,8},{24,16},{28,24},{20,28},{12,20},{4,12},{1,5},{9... | collective-permute-start | bytes 1572872 | tf_op jit(solution)/shard_map/ppermute | solution.py:35
  115.6 22.6 %collective-permute-start.27 = (bf16[256,1024]{1,0:T(8,128)(2,1)S(1)}, bf16[256,1024]{1,0:T(8,128)(2,1)}, u32[]{:S(2)}, u32[]{:S(2)}) collective-permute-start(bf16[256,1024]{1,0:T(8,128)(2,1)S(1)} %get-tuple-element.183.refs_27_), channel_id=1, source_target_pairs={{0,8},{8,16},{16,24},{24,28},{28,20},{20,12},{12,4},{4,0},{1,9},{9... | collective-permute-start | bytes 1572872 | tf_op jit(solution)/shard_map/ppermute | solution.py:35
  126.9 22.4 %collective-permute-start.20 = (bf16[4,64,1024]{2,1,0:T(8,128)(2,1)S(1)}, bf16[4,64,1024]{2,1,0:T(8,128)(2,1)S(1)}, u32[]{:S(2)}, u32[]{:S(2)}) collective-permute-start(bf16[4,64,1024]{2,1,0:T(8,128)(2,1)S(1)} %bitcast.139), channel_id=1, source_target_pairs={{0,8},{8,16},{16,24},{24,28},{28,20},{20,12},{12,4},{4,0},{1,9},{9... | collective-permute-start | bytes 1572872 | tf_op jit(solution)/shard_map/ppermute | solution.py:35
  149.3 22.5 %collective-permute-start.22 = (bf16[4,64,1024]{2,1,0:T(8,128)(2,1)S(1)}, bf16[4,64,1024]{2,1,0:T(8,128)(2,1)S(1)}, u32[]{:S(2)}, u32[]{:S(2)}) collective-permute-start(bf16[4,64,1024]{2,1,0:T(8,128)(2,1)S(1)} %collective-permute-done.20.refs_1_), channel_id=1, source_target_pairs={{0,8},{8,16},{16,24},{24,28},{28,20},{20,12},{12,4},{4,0},{1,9},{9... | collective-permute-start | bytes 1572872 | tf_op jit(solution)/shard_map/ppermute | solution.py:35
  202.9 40.8 %collective-permute-start.43 = (bf16[8,64,512]{2,1,0:T(8,128)(2,1)}, bf16[8,64,512]{2,1,0:T(8,128)(2,1)}, u32[]{:S(2)}, u32[]{:S(2)}) collective-permute-start(bf16[8,64,512]{2,1,0:T(8,128)(2,1)} %select_convert_fusion), channel_id=1, source_target_pairs={{0,4},{4,0},{8,12},{12,8},{16,20},{20,16},{24,28},{28,24},{1,5},{5... | collective-permute-start | bytes 1572872 | tf_op jit(solution)/shard_map/ppermute | solution.py:584
  225.7 39.8 %collective-permute-start.33 = (bf16[256,1024]{1,0:T(8,128)(2,1)}, bf16[256,1024]{1,0:T(8,128)(2,1)}, u32[]{:S(2)}, u32[]{:S(2)}) collective-permute-start(bf16[256,1024]{1,0:T(8,128)(2,1)} %collective-permute-done.18.refs_19_), channel_id=1, source_target_pairs={{0,8},{8,16},{16,24},{24,28},{28,20},{20,12},{12,4},{4,0},{1,9},{9... | collective-permute-start | bytes 1572872 | tf_op jit(solution)/shard_map/ppermute | solution.py:35
  225.7 39.8 %collective-permute-start.34 = (bf16[256,1024]{1,0:T(8,128)(2,1)}, bf16[256,1024]{1,0:T(8,128)(2,1)}, u32[]{:S(2)}, u32[]{:S(2)}) collective-permute-start(bf16[256,1024]{1,0:T(8,128)(2,1)} %collective-permute-done.19.refs_20_), channel_id=1, source_target_pairs={{0,4},{8,0},{16,8},{24,16},{28,24},{20,28},{12,20},{4,12},{1,5},{9... | collective-permute-start | bytes 1572872 | tf_op jit(solution)/shard_map/ppermute | solution.py:35
  248.2 35.6 %collective-permute-start.46 = (bf16[256,1024]{1,0:T(8,128)(2,1)}, bf16[256,1024]{1,0:T(8,128)(2,1)}, u32[]{:S(2)}, u32[]{:S(2)}) collective-permute-start(bf16[256,1024]{1,0:T(8,128)(2,1)} %collective-permute-done.27.refs_28_), channel_id=1, source_target_pairs={{0,8},{8,16},{16,24},{24,28},{28,20},{20,12},{12,4},{4,0},{1,9},{9... | collective-permute-start | bytes 1572872 | tf_op jit(solution)/shard_map/ppermute | solution.py:35
  251.9 32.0 %collective-permute-start.47 = (bf16[256,1024]{1,0:T(8,128)(2,1)}, bf16[256,1024]{1,0:T(8,128)(2,1)}, u32[]{:S(2)}, u32[]{:S(2)}) collective-permute-start(bf16[256,1024]{1,0:T(8,128)(2,1)} %collective-permute-done.28.refs_29_), channel_id=1, source_target_pairs={{0,4},{8,0},{16,8},{24,16},{28,24},{20,28},{12,20},{4,12},{1,5},{9... | collective-permute-start | bytes 1572872 | tf_op jit(solution)/shard_map/ppermute | solution.py:35
  265.4 38.2 %collective-permute-start.44 = (bf16[256,1024]{1,0:T(8,128)(2,1)}, bf16[256,1024]{1,0:T(8,128)(2,1)}, u32[]{:S(2)}, u32[]{:S(2)}) collective-permute-start(bf16[256,1024]{1,0:T(8,128)(2,1)} %collective-permute-done.33.refs_21_), channel_id=1, source_target_pairs={{0,8},{8,16},{16,24},{24,28},{28,20},{20,12},{12,4},{4,0},{1,9},{9... | collective-permute-start | bytes 1572872 | tf_op jit(solution)/shard_map/ppermute | solution.py:35
  267.5 36.1 %collective-permute-start.45 = (bf16[256,1024]{1,0:T(8,128)(2,1)}, bf16[256,1024]{1,0:T(8,128)(2,1)}, u32[]{:S(2)}, u32[]{:S(2)}) collective-permute-start(bf16[256,1024]{1,0:T(8,128)(2,1)} %collective-permute-done.34.refs_22_), channel_id=1, source_target_pairs={{0,4},{8,0},{16,8},{24,16},{28,24},{20,28},{12,20},{4,12},{1,5},{9... | collective-permute-start | bytes 1572872 | tf_op jit(solution)/shard_map/ppermute | solution.py:35
  331.2 23.9 %collective-permute-start.56 = (bf16[256,1024]{1,0:T(8,128)(2,1)S(1)}, bf16[256,1024]{1,0:T(8,128)(2,1)S(1)}, u32[]{:S(2)}, u32[]{:S(2)}) collective-permute-start(bf16[256,1024]{1,0:T(8,128)(2,1)S(1)} %get-tuple-element.234.refs_18_), channel_id=1, source_target_pairs={{0,8},{8,16},{16,24},{24,28},{28,20},{20,12},{12,4},{4,0},{1,9},{9... | collective-permute-start | bytes 1572872 | tf_op jit(solution)/shard_map/ppermute | solution.py:35
  333.3 21.9 %collective-permute-start.57 = (bf16[256,1024]{1,0:T(8,128)(2,1)S(1)}, bf16[256,1024]{1,0:T(8,128)(2,1)S(1)}, u32[]{:S(2)}, u32[]{:S(2)}) collective-permute-start(bf16[256,1024]{1,0:T(8,128)(2,1)S(1)} %get-tuple-element.234.refs_18_), channel_id=1, source_target_pairs={{0,4},{8,0},{16,8},{24,16},{28,24},{20,28},{12,20},{4,12},{1,5},{9... | collective-permute-start | bytes 1572872 | tf_op jit(solution)/shard_map/ppermute | solution.py:35
  373.6 45.5 %collective-permute-start.60 = (bf16[256,1024]{1,0:T(8,128)(2,1)}, bf16[256,1024]{1,0:T(8,128)(2,1)S(1)}, u32[]{:S(2)}, u32[]{:S(2)}) collective-permute-start(bf16[256,1024]{1,0:T(8,128)(2,1)} %collective-permute-done.58.refs_21_), channel_id=1, source_target_pairs={{0,8},{8,16},{16,24},{24,28},{28,20},{20,12},{12,4},{4,0},{1,9},{9... | collective-permute-start | bytes 1572872 | tf_op jit(solution)/shard_map/ppermute | solution.py:35
  375.0 44.1 %collective-permute-start.61 = (bf16[256,1024]{1,0:T(8,128)(2,1)}, bf16[256,1024]{1,0:T(8,128)(2,1)S(1)}, u32[]{:S(2)}, u32[]{:S(2)}) collective-permute-start(bf16[256,1024]{1,0:T(8,128)(2,1)} %collective-permute-done.59.refs_22_), channel_id=1, source_target_pairs={{0,4},{8,0},{16,8},{24,16},{28,24},{20,28},{12,20},{4,12},{1,5},{9... | collective-permute-start | bytes 1572872 | tf_op jit(solution)/shard_map/ppermute | solution.py:35
  384.8 36.4 %collective-permute-start.68 = (bf16[256,1024]{1,0:T(8,128)(2,1)}, bf16[256,1024]{1,0:T(8,128)(2,1)}, u32[]{:S(2)}, u32[]{:S(2)}) collective-permute-start(bf16[256,1024]{1,0:T(8,128)(2,1)} %collective-permute-done.64.refs_30_), channel_id=1, source_target_pairs={{0,8},{8,16},{16,24},{24,28},{28,20},{20,12},{12,4},{4,0},{1,9},{9... | collective-permute-start | bytes 1572872 | tf_op jit(solution)/shard_map/ppermute | solution.py:35
  386.3 36.0 %collective-permute-start.69 = (bf16[256,1024]{1,0:T(8,128)(2,1)}, bf16[256,1024]{1,0:T(8,128)(2,1)}, u32[]{:S(2)}, u32[]{:S(2)}) collective-permute-start(bf16[256,1024]{1,0:T(8,128)(2,1)} %collective-permute-done.65.refs_31_), channel_id=1, source_target_pairs={{0,4},{8,0},{16,8},{24,16},{28,24},{20,28},{12,20},{4,12},{1,5},{9... | collective-permute-start | bytes 1572872 | tf_op jit(solution)/shard_map/ppermute | solution.py:35
  505.0 49.3 %collective-permute-start.85 = (f32[4,8,512]{2,1,0:T(8,128)S(1)}, f32[4,8,512]{2,1,0:T(8,128)S(1)}, u32[]{:S(2)}, u32[]{:S(2)}) collective-permute-start(f32[4,8,512]{2,1,0:T(8,128)S(1)} %add.245), channel_id=1, source_target_pairs={{0,16},{4,20},{8,24},{12,28},{16,0},{20,4},{24,8},{28,12},{1,17},{... | collective-permute-start | bytes 196616 | tf_op jit(solution)/shard_map/ppermute | solution.py:83
  513.3 23.7 %collective-permute-start.80 = (bf16[4,64,1024]{2,1,0:T(8,128)(2,1)S(1)}, bf16[4,64,1024]{2,1,0:T(8,128)(2,1)S(1)}, u32[]{:S(2)}, u32[]{:S(2)}) collective-permute-start(bf16[4,64,1024]{2,1,0:T(8,128)(2,1)S(1)} %pad_maximum_fusion.2), channel_id=1, source_target_pairs={{0,4},{8,0},{16,8},{24,16},{28,24},{20,28},{12,20},{4,12},{1,5},{9... | collective-permute-start | bytes 1572872 | tf_op jit(solution)/shard_map/ppermute | solution.py:35
  515.9 23.6 %collective-permute-start.76 = (bf16[4,64,1024]{2,1,0:T(8,128)(2,1)S(1)}, bf16[4,64,1024]{2,1,0:T(8,128)(2,1)S(1)}, u32[]{:S(2)}, u32[]{:S(2)}) collective-permute-start(bf16[4,64,1024]{2,1,0:T(8,128)(2,1)S(1)} %pad_maximum_fusion.1), channel_id=1, source_target_pairs={{0,8},{8,16},{16,24},{24,28},{28,20},{20,12},{12,4},{4,0},{1,9},{9... | collective-permute-start | bytes 1572872 | tf_op jit(solution)/shard_map/ppermute | solution.py:35
  525.9 22.3 %collective-permute-start.94 = (bf16[4,64,1024]{2,1,0:T(8,128)(2,1)S(1)}, bf16[4,64,1024]{2,1,0:T(8,128)(2,1)S(1)}, u32[]{:S(2)}, u32[]{:S(2)}) collective-permute-start(bf16[4,64,1024]{2,1,0:T(8,128)(2,1)S(1)} %add_convert_fusion.1), channel_id=1, source_target_pairs={{0,4},{8,0},{16,8},{24,16},{28,24},{20,28},{12,20},{4,12},{1,5},{9... | collective-permute-start | bytes 1572872 | tf_op jit(solution)/shard_map/ppermute | solution.py:35
  528.5 22.3 %collective-permute-start.90 = (bf16[4,64,1024]{2,1,0:T(8,128)(2,1)S(1)}, bf16[4,64,1024]{2,1,0:T(8,128)(2,1)S(1)}, u32[]{:S(2)}, u32[]{:S(2)}) collective-permute-start(bf16[4,64,1024]{2,1,0:T(8,128)(2,1)S(1)} %add_convert_fusion.3), channel_id=1, source_target_pairs={{0,8},{8,16},{16,24},{24,28},{28,20},{20,12},{12,4},{4,0},{1,9},{9... | collective-permute-start | bytes 1572872 | tf_op jit(solution)/shard_map/ppermute | solution.py:35
  538.0 21.5 %collective-permute-start.81 = (bf16[4,64,1024]{2,1,0:T(8,128)(2,1)}, bf16[4,64,1024]{2,1,0:T(8,128)(2,1)}, u32[]{:S(2)}, u32[]{:S(2)}) collective-permute-start(bf16[4,64,1024]{2,1,0:T(8,128)(2,1)} %add_convert_fusion.5), channel_id=1, source_target_pairs={{0,4},{8,0},{16,8},{24,16},{28,24},{20,28},{12,20},{4,12},{1,5},{9... | collective-permute-start | bytes 1572872 | tf_op jit(solution)/shard_map/ppermute | solution.py:35
  540.6 21.6 %collective-permute-start.77 = (bf16[4,64,1024]{2,1,0:T(8,128)(2,1)}, bf16[4,64,1024]{2,1,0:T(8,128)(2,1)}, u32[]{:S(2)}, u32[]{:S(2)}) collective-permute-start(bf16[4,64,1024]{2,1,0:T(8,128)(2,1)} %add_convert_fusion.7), channel_id=1, source_target_pairs={{0,8},{8,16},{16,24},{24,28},{28,20},{20,12},{12,4},{4,0},{1,9},{9... | collective-permute-start | bytes 1572872 | tf_op jit(solution)/shard_map/ppermute | solution.py:35
  551.8 21.6 %collective-permute-start.91 = (bf16[4,64,1024]{2,1,0:T(8,128)(2,1)}, bf16[4,64,1024]{2,1,0:T(8,128)(2,1)S(1)}, u32[]{:S(2)}, u32[]{:S(2)}) collective-permute-start(bf16[4,64,1024]{2,1,0:T(8,128)(2,1)} %add_convert_fusion.2), channel_id=1, source_target_pairs={{0,8},{8,16},{16,24},{24,28},{28,20},{20,12},{12,4},{4,0},{1,9},{9... | collective-permute-start | bytes 1572872 | tf_op jit(solution)/shard_map/ppermute | solution.py:35
  (211 other events, 3070.6 us)

commit v4 on v3

--- a/solution.py
+++ b/solution.py
@@ -17,6 +17,7 @@
 EXP2_SCALE = SCALE * math.log2(math.e)
 DEAD = -1e30
 GROUPS = 2
+VMEM_BYTES = 56 * 1024 * 1024
 
 
 def ring_order(count):
@@ -87,19 +88,22 @@
 
 def ring_sum(parts, order):
     far = len(order) // 2
+    half = parts[0].shape[0] // 2
     add = lambda a, b: (a.astype(jnp.float32) + b.astype(jnp.float32)).astype(jnp.bfloat16)
-    ahead = ring_step(parts[far][0], order, 1)
-    back = ring_step(parts[far][1], order, -1)
-    ahead = jnp.concatenate([add(ahead, parts[far - 1][0]), parts[far - 1][1]], axis=0)
-    back = jnp.concatenate([parts[1 - far][0], add(back, parts[1 - far][1])], axis=0)
-    whole = lambda offset: jnp.concatenate(parts[offset], axis=0)
+    ahead = ring_step(parts[far][:half], order, 1)
+    back = ring_step(parts[far][half:], order, -1)
+    top, bottom = parts[far - 1], parts[1 - far]
+    ahead = jnp.concatenate([add(ahead, top[:half]), top[half:]], axis=0)
+    back = jnp.concatenate([bottom[:half], add(back, bottom[half:])], axis=0)
     for step in range(far - 1, 0, -1):
         ahead = ring_step(ahead, order, 1)
         back = ring_step(back, order, -1)
         if step > 1:
-            ahead = add(ahead, whole(step - 1))
-            back = add(back, whole(1 - step))
-    return ahead.astype(jnp.float32) + back.astype(jnp.float32) + whole(0).astype(jnp.float32)
+            ahead = add(ahead, parts[step - 1])
+            back = add(back, parts[1 - step])
+    return (
+        ahead.astype(jnp.float32) + back.astype(jnp.float32) + parts[0].astype(jnp.float32)
+    )
 
 
 def project_kernel(count, turned, places_ref, *refs):
@@ -144,7 +148,7 @@
             out_specs=pl.BlockSpec((tokens, block), lambda j, *_: (0, j)),
         ),
         out_shape=jax.ShapeDtypeStruct((tokens, width), jnp.bfloat16),
-        compiler_params=pltpu.CompilerParams(vmem_limit_bytes=40 * 1024 * 1024),
+        compiler_params=pltpu.CompilerParams(vmem_limit_bytes=VMEM_BYTES),
         cost_estimate=pl.CostEstimate(
             flops=2 * tokens * value.shape[1] * width,
             bytes_accessed=2 * (tokens + width) * value.shape[1],
@@ -216,7 +220,7 @@
             jax.ShapeDtypeStruct((tokens, heads), jnp.float32),
         ],
         scratch_shapes=[pltpu.VMEM((tokens, D), jnp.bfloat16)],
-        compiler_params=pltpu.CompilerParams(vmem_limit_bytes=40 * 1024 * 1024),
+        compiler_params=pltpu.CompilerParams(vmem_limit_bytes=VMEM_BYTES),
         cost_estimate=pl.CostEstimate(
             flops=2 * tokens * D * width,
             bytes_accessed=2 * D * (width + tokens) + 4 * tokens * width,
@@ -294,7 +298,7 @@
             jax.ShapeDtypeStruct((requests, STATE, inner), jnp.float32),
             jax.ShapeDtypeStruct((requests, 1, inner), jnp.float32),
         ],
-        compiler_params=pltpu.CompilerParams(vmem_limit_bytes=40 * 1024 * 1024),
+        compiler_params=pltpu.CompilerParams(vmem_limit_bytes=VMEM_BYTES),
         cost_estimate=pl.CostEstimate(
             flops=12 * requests * tokens * tokens * inner,
             bytes_accessed=16 * requests * tokens * inner,
@@ -344,7 +348,7 @@
             jax.ShapeDtypeStruct((requests * tokens, 128), jnp.float32),
             jax.ShapeDtypeStruct((requests, STATE, inner), jnp.float32),
         ],
-        compiler_params=pltpu.CompilerParams(vmem_limit_bytes=40 * 1024 * 1024),
+        compiler_params=pltpu.CompilerParams(vmem_limit_bytes=VMEM_BYTES),
         cost_estimate=pl.CostEstimate(
             flops=2 * requests * tokens * STATE * inner,
             bytes_accessed=24 * requests * tokens * inner,
@@ -388,9 +392,9 @@
         )
 
 
-def cache_part(begin, at, requests, places, live, query_slots, keys, values):
+def cache_part(begin, places, live, query_slots, keys, values):
     slots = len(query_slots)
-    tok_block, width = query_slots[0].shape[1:]
+    requests, tok_block, width = query_slots[0].shape
     tokens = tok_block * slots
     cache_block = keys.shape[1]
     heads = width // HEAD_DIM
@@ -401,10 +405,7 @@
         grid_spec=pltpu.PrefetchScalarGridSpec(
             num_scalar_prefetch=2,
             grid=(requests,),
-            in_specs=[
-                one(tok_block, 0 if slot.shape[0] == requests else at) for slot in query_slots
-            ]
-            + [one(cache_block, begin), one(cache_block, begin)],
+            in_specs=[one(tok_block, 0)] * slots + [one(cache_block, begin)] * 2,
             out_specs=[
                 one(tokens, 0),
                 pl.BlockSpec((1, width, tokens), lambda r, *_: (r, 0, 0)),
@@ -418,7 +419,7 @@
             jax.ShapeDtypeStruct((requests, heads, tokens), jnp.float32),
             jax.ShapeDtypeStruct((requests, heads, tokens), jnp.float32),
         ],
-        compiler_params=pltpu.CompilerParams(vmem_limit_bytes=48 * 1024 * 1024),
+        compiler_params=pltpu.CompilerParams(vmem_limit_bytes=VMEM_BYTES),
         cost_estimate=pl.CostEstimate(
             flops=4 * requests * tokens * cache_block * width,
             bytes_accessed=2 * requests * width * (3 * tokens + 2 * cache_block),
@@ -461,7 +462,7 @@
             out_specs=stat,
         ),
         out_shape=jax.ShapeDtypeStruct(peaks.shape, jnp.float32),
-        compiler_params=pltpu.CompilerParams(vmem_limit_bytes=32 * 1024 * 1024),
+        compiler_params=pltpu.CompilerParams(vmem_limit_bytes=VMEM_BYTES),
         cost_estimate=pl.CostEstimate(
             flops=2 * requests * tokens * tok_block * width,
             bytes_accessed=2 * requests * width * tokens,
@@ -521,7 +522,7 @@
         ),
         out_shape=[jax.ShapeDtypeStruct((requests, heads, tokens), jnp.float32)]
         + [jax.ShapeDtypeStruct((requests, tok_block, width), jnp.bfloat16)] * slots,
-        compiler_params=pltpu.CompilerParams(vmem_limit_bytes=48 * 1024 * 1024),
+        compiler_params=pltpu.CompilerParams(vmem_limit_bytes=VMEM_BYTES),
         cost_estimate=pl.CostEstimate(
             flops=4 * requests * tokens * tok_block * width,
             bytes_accessed=6 * requests * width * tokens,
@@ -670,23 +671,16 @@
 
     clock = Clock()
     group = requests // GROUPS
-    part_size = group // 2
     local_inner = w_in.shape[2]
     local_mheads = local_inner // MHEAD_DIM
     local_width = D // head_count
     made = {}
 
-    def weight_rings(weight):
-        top = weight.shape[0] // 2
-        return [Ring(weight[:top], order), Ring(weight[top:], order, top)]
-
-    def product(rings, turned):
-        pieces = []
-        for ring in rings:
-            pieces += ring.pieces
-            if pieces[-1][2].shape[0] < 128:
-                (offset, row, upper), (_, _, lower) = pieces[-2:]
-                pieces[-2:] = [(offset, row, jnp.concatenate([upper, lower], axis=0))]
+    def product(ring, turned):
+        pieces = list(ring.pieces)
+        if pieces[-1][2].shape[0] < 128:
+            (offset, row, upper), (_, _, lower) = pieces[-2:]
+            pieces[-2:] = [(offset, row, jnp.concatenate([upper, lower], axis=0))]
         return project(
             places, offsets, rows, flat_input, pieces, cosine, sine, turned
         ).reshape(requests, tok_block, local_att)
@@ -777,43 +771,33 @@
         )
         return (made["chain"],), ()
 
-    query_rings = weight_rings(w_query)
-    key_rings = weight_rings(w_key)
-    value_rings = weight_rings(w_value)
+    query_ring, key_ring, value_ring = (Ring(w, order) for w in (w_query, w_key, w_value))
     slot_rings = []
     live = jnp.clip(lengths - seq_index * cache_block, 0, cache_block).astype(jnp.int32)
     first = (seq_index * tok_block).astype(jnp.int32).reshape(1)
     cached = []
 
     def make_queries():
-        queries = product(query_rings, True)
+        queries = product(query_ring, True)
         slot_rings.extend(
             Ring(queries[begin : begin + group], order) for begin in range(0, requests, group)
         )
         return (queries,), ()
 
     def make_keys():
-        made["keys"] = product(key_rings, True)
+        made["keys"] = product(key_ring, True)
         return (made["keys"],), ()
 
     def meet_cache(index):
         def work():
-            ring = slot_rings[index // 2]
-            at = (index % 2) * part_size
-            begin = index * part_size
+            ring = slot_rings[index]
+            begin = index * group
             slots = [piece for _, _, piece in ring.pieces[:-2]]
-            slots.append(ring.pieces[-2 + index % 2][2])
+            slots.append(jnp.concatenate([ring.pieces[-2][2], ring.pieces[-1][2]], axis=0))
             slots[0] = clock.hold(slots[0])
             cached.append(
                 cache_part(
-                    begin,
-                    at,
-                    part_size,
-                    places,
-                    live[begin : begin + part_size],
-                    slots,
-                    cache_keys,
-                    cache_values,
+                    begin, places, live[begin : begin + group], slots, cache_keys, cache_values
                 )
             )
             return tuple(cached[-1]), ()
@@ -824,7 +808,7 @@
         keys = clock.hold(made["keys"])
         made["peaks"] = jnp.concatenate(
             [
-                group_peaks(index * part_size, first, part[0], keys, part[2])
+                group_peaks(index * group, first, part[0], keys, part[2])
                 for index, part in enumerate(cached)
             ],
             axis=0,
@@ -846,23 +830,22 @@
             )
 
     run(
-        steps(query_rings, 0, half),
-        [order_weight, None, enter, inside, initial_state, start_relay, None, hop],
-    )
-    run(steps(key_rings, 0, 1), [make_queries])
+        steps([query_ring, key_ring], 0, half),
+        [order_weight, enter, inside, initial_state, start_relay, hop, hop, hop],
+    )
+    run(steps([value_ring], 0, 1), [make_queries])
     run(
         steps(slot_rings, 0, half),
-        [None, hop, None, None, hop, None, None, end_relay],
+        [end_relay, make_keys, leave, leave_terms, leave_chain],
     )
     run(
-        steps(key_rings, 1, half) + steps(value_rings, 0, half),
-        [meet_cache(0), meet_cache(1), meet_cache(2), meet_cache(3), leave, leave_terms]
-        + [make_keys, make_peaks, join_peaks, None, None, leave_chain],
+        steps([value_ring], 1, half),
+        [meet_cache(0), meet_cache(1), make_peaks, join_peaks],
     )
 
     new_keys = made["keys"]
     best = made["best"]
-    new_values = product(value_rings, False)
+    new_values = product(value_ring, False)
 
     own = lambda stat: lax.dynamic_slice_in_dim(stat, seq_index * tok_block, tok_block, 2)
     greatest_logit = jnp.transpose(own(best), (0, 2, 1)) * SCALE
@@ -872,26 +855,13 @@
     mixed = []
     for index in range(GROUPS):
         begin = index * group
-        sums, parts = [], []
-        for inner_index in range(2):
-            joined, out, peaks, totals = cached[2 * index + inner_index]
-            some_sums, *some_parts = finish_part(
-                begin + inner_index * part_size,
-                first,
-                places,
-                joined,
-                new_keys,
-                new_values,
-                out,
-                peaks,
-                totals,
-                best,
-            )
-            sums.append(some_sums)
-            parts.append(some_parts)
-        sums = butterfly(jnp.concatenate(sums, axis=0), "seq", seq_count, jnp.add)
+        joined, out, peaks, totals = cached[index]
+        sums, *parts = finish_part(
+            begin, first, places, joined, new_keys, new_values, out, peaks, totals, best
+        )
+        sums = butterfly(sums, "seq", seq_count, jnp.add)
         denominator = jnp.transpose(own(sums), (0, 2, 1))
-        terms = {-offset: pair for offset, pair in zip(offsets, zip(*parts))}
+        terms = {-offset: part for offset, part in zip(offsets, parts)}
         terms[half] = terms[-half]
         numerator = ring_sum(terms, order).reshape(group, tok_block, local_heads, HEAD_DIM)
         attended = (

time: 617 us -> 560 us (0.908)
  starting transfers between devices: 132 us -> 88.5 us
  local copies, waits for them, and re-layouts: 101 us -> 59.8 us
  waiting for transfers between devices: 195 us -> 216 us
  Pallas kernels: 127 us -> 138 us
    unnamed x290 -> x116, local copies, waits for them, and re-layouts: 59.9 us -> 17 us
    ppermute x80 -> x56, starting transfers between devices: 110 us -> 67.6 us  [ring_step(): return lax.ppermute(block, 'seq', route)]
    ppermute x3, waiting for transfers between devices: 0.01 us -> 19.4 us  [advance(): self.entry = entry + lax.ppermute(leaving, 'seq', route).astype(jnp.float32)]
    ppermute x1, waiting for transfers between devices: 0.01 us -> 18.9 us  [__init__(): other_factor = side(lax.ppermute(through, 'seq', self.swap))]
    ppermute x11, waiting for transfers between devices: 36.4 us -> 23.9 us  [butterfly(): lax.ppermute(value, axis, [(i, i ^ bit) for i in range(count)])]
    ppermute x80 -> x56, waiting for transfers between devices: 144 us -> 132 us  [ring_step(): return lax.ppermute(block, 'seq', route)]
    ppermute x2, waiting for transfers between devices: 7.97 us -> 15.9 us  [exchange(): lax.ppermute(value.astype(jnp.bfloat16), 'seq', self.swap)]
    pallas_call x4 -> x2, Pallas kernels: 49 us -> 43.6 us  [cache_part(): pl.pallas_call(functools.partial(cache_kernel, slots), grid_spec=pltpu.Pr...]
  transfers between devices with their start and end apart: 101 -> 77, of which waited for: 49 -> 40; matrix products, arithmetic and copies ran while one was open for 15% -> 17% of each run, Pallas kernels for 15% -> 21%
where the time goes in v4:
time: 560 us; the launch traced here: 549 us
  waiting for transfers between devices  216 us (39%)
  Pallas kernels  138 us (25%)
  starting transfers between devices  88.5 us (16%)
  local copies, waits for them, and re-layouts  59.8 us (11%)
  other arithmetic  35.3 us (6%)
  matrix products  9.75 us (2%)
    ppermute x56, waiting for transfers between devices, ring_step(): return lax.ppermute(block, 'seq', route)  132 us
    ppermute x56, starting transfers between devices, ring_step(): return lax.ppermute(block, 'seq', route)  67.6 us
    pallas_call x2, Pallas kernels, cache_part(): pl.pallas_call(functools.partial(cache_kernel, slots), grid_spec=pltpu.Pr...  43.6 us
    pallas_call x3, Pallas kernels, project(): pl.pallas_call(functools.partial(project_kernel, len(pieces), turned), gr...  31.3 us
    ppermute x11, waiting for transfers between devices, butterfly(): lax.ppermute(value, axis, [(i, i ^ bit) for i in range(count)])  23.9 us
    pallas_call x2, Pallas kernels, finish_part(): pl.pallas_call(functools.partial(finish_kernel, slots), grid_spec=pltpu.P...  22.6 us
    ppermute x3, waiting for transfers between devices, advance(): self.entry = entry + lax.ppermute(leaving, 'seq', route).astype(jnp.float32)  19.4 us
    ppermute x1, waiting for transfers between devices, __init__(): other_factor = side(lax.ppermute(through, 'seq', self.swap))  18.9 us
  transfers between devices with their start and end apart: 77, of which 40 were waited for; matrix products, arithmetic and copies ran while one was open for 17% of the time, Pallas kernels for 21%

profile of v4, /device:TPU:0, one launch (start us, length us, event | category | flops | bytes accessed | tf_op | source)
XLA Modules:
  0.0 549.2 jit_solution(9374974908891647388)
XLA Ops:
  3.7 10.4 %copy.52 = bf16[256,8,2,1024]{3,1,2,0:T(8,128)(2,1)} copy(bf16[256,8,2,1024]{3,2,1,0:T(2,128)(2,1)} %bitcast.105) | data formatting | bytes 16777216
  17.2 11.6 %enter_mixer.1 = (f32[512,2048]{1,0:T(8,128)}, f32[512,128]{1,0:T(8,128)}, f32[512,16]{1,0:T(8,128)}) custom-call(bf16[512,4096]{1,0:T(8,128)(2,1)} %bitcast.66, f32[1,2048]{1,0:T(1,128)} %bitcast.128, bf16[2048,128]{1,0:T(8,128)(2,1)} %bc_ref.1, bf16[2048,16]{1,0:T(8,128)(2,1)} %copy.40.dt_ref, f32[1,16]{1,0:T(1,128)} %bitcast.129, bf16[2048,2048]{1,0:T(8,128)(2,1)} %bitcast.106), custom_call_target="tpu_custom_call" | custom-call | flops 4294967296 | bytes 14680064 | tf_op jit(solution)/shard_map/enter_mixer/pallas_call | solution.py:201
  36.4 9.6 %inside_block.1 = (f32[512,1024]{1,0:T(8,128)}, f32[8,64,1024]{2,1,0:T(8,128)}, f32[8,1,1024]{2,1,0:T(1,128)}) custom-call(f32[512,2048]{1,0:T(8,128)} %get-tuple-element.104.inner_ref.gate_ref, f32[512,128]{1,0:T(8,128)} %get-tuple-element.105.map_ref, f32[8,64,16]{2,1,0:T(8,128)} %bitcast.109, f32[8,64,16]{2,1,0:T(8,128)} %bitcast.113, ...), custom_call_target="tpu_custom_call" | custom-call | flops 402653184 | bytes 8388608 | tf_op jit(solution)/shard_map/inside_block/pallas_call | solution.py:279
  57.6 5.6 %copy.44 = f32[8,16,64,64]{2,1,3,0:T(8,128)} copy(f32[8,16,64,64]{3,2,1,0:T(8,128)} %reshape.131) | data formatting | bytes 4194304 | tf_op jit(solution)/shard_map/reshape | solution.py:723
  77.0 18.9 %collective-permute-done.8 = f32[8,1,1024]{2,1,0:T(1,128)S(1)} collective-permute-done((f32[8,1,1024]{2,1,0:T(1,128)S(1)}, f32[8,1,1024]{2,1,0:T(1,128)S(1)}, u32[]{:S(2)}, u32[]{:S(2)}) %collective-permute-start.8) | collective-permute-done | bytes 32800 | tf_op jit(solution)/shard_map/ppermute | solution.py:574
  98.3 8.9 %collective-permute-done.9 = bf16[8,64,512]{2,1,0:T(8,128)(2,1)S(1)} collective-permute-done((bf16[8,64,512]{2,1,0:T(8,128)(2,1)S(1)}, bf16[8,64,512]{2,1,0:T(8,128)(2,1)S(1)}, u32[]{:S(2)}, u32[]{:S(2)}) %collective-permute-start.9) | collective-permute-done | bytes 524320 | tf_op jit(solution)/shard_map/ppermute | solution.py:585
  113.4 19.4 %collective-permute-done.16 = bf16[8,64,512]{2,1,0:T(8,128)(2,1)} collective-permute-done((bf16[8,64,512]{2,1,0:T(8,128)(2,1)}, bf16[8,64,512]{2,1,0:T(8,128)(2,1)}, u32[]{:S(2)}, u32[]{:S(2)}) %collective-permute-start.16) | collective-permute-done | bytes 524320 | tf_op jit(solution)/shard_map/ppermute | solution.py:600
  145.8 9.4 %collective-permute-done.14.refs_14_ = bf16[512,1024]{1,0:T(8,128)(2,1)S(1)} collective-permute-done((bf16[512,1024]{1,0:T(8,128)(2,1)}, bf16[512,1024]{1,0:T(8,128)(2,1)S(1)}, u32[]{:S(2)}, u32[]{:S(2)}) %collective-permute-start.14) | collective-permute-done | bytes 1048608 | tf_op jit(solution)/shard_map/ppermute | solution.py:36
  167.5 10.6 %project.3 = bf16[512,1024]{1,0:T(8,128)(2,1)} custom-call(s32[8]{0:T(128)} %fusion.22.places_ref.place_ref, bf16[512,4096]{1,0:T(8,128)(2,1)} %bitcast.67, bf16[512,4096]{1,0:T(8,128)(2,1)} %bitcast.68, bf16[512,4096]{1,0:T(8,128)(2,1)} %bitcast.69, bf16[512,4096]{1,0:T(8,128)(2,1)} %bitcast.70, bf16[512,4096]{1,0:T(8,128)(2,1)} %bitcast.71, ...), custom_call_target="tpu_custom_call" | custom-call | flops 4294967296 | bytes 12582912 | tf_op jit(solution)/shard_map/project/pallas_call | solution.py:142
  185.9 10.4 %project.4 = bf16[512,1024]{1,0:T(8,128)(2,1)} custom-call(s32[8]{0:T(128)} %fusion.22.places_ref.place_ref, bf16[512,4096]{1,0:T(8,128)(2,1)} %bitcast.80, bf16[512,4096]{1,0:T(8,128)(2,1)} %bitcast.77, bf16[512,4096]{1,0:T(8,128)(2,1)} %bitcast.78, bf16[512,4096]{1,0:T(8,128)(2,1)} %bitcast.79, bf16[512,4096]{1,0:T(8,128)(2,1)} %bitcast.76, ...), custom_call_target="tpu_custom_call" | custom-call | flops 4294967296 | bytes 12582912 | tf_op jit(solution)/shard_map/project/pallas_call | solution.py:142
  196.4 8.4 %collective-permute-done.28.refs_10_ = bf16[512,1024]{1,0:T(8,128)(2,1)} collective-permute-done((bf16[512,1024]{1,0:T(8,128)(2,1)S(1)}, bf16[512,1024]{1,0:T(8,128)(2,1)}, u32[]{:S(2)}, u32[]{:S(2)}) %collective-permute-start.28) | collective-permute-done | bytes 1048608 | tf_op jit(solution)/shard_map/ppermute | solution.py:36
  208.8 7.0 %collective-permute-done.23 = bf16[8,64,512]{2,1,0:T(8,128)(2,1)S(1)} collective-permute-done((bf16[8,64,512]{2,1,0:T(8,128)(2,1)S(1)}, bf16[8,64,512]{2,1,0:T(8,128)(2,1)S(1)}, u32[]{:S(2)}, u32[]{:S(2)}) %collective-permute-start.23) | collective-permute-done | bytes 524320 | tf_op jit(solution)/shard_map/ppermute | solution.py:585
  217.7 9.1 %collective-permute-done.21.refs_1_ = bf16[4,64,1024]{2,1,0:T(8,128)(2,1)} collective-permute-done((bf16[4,64,1024]{2,1,0:T(8,128)(2,1)S(1)}, bf16[4,64,1024]{2,1,0:T(8,128)(2,1)}, u32[]{:S(2)}, u32[]{:S(2)}) %collective-permute-start.21) | collective-permute-done | bytes 524320 | tf_op jit(solution)/shard_map/ppermute | solution.py:36
  226.8 9.1 %leave_mixer.1 = (bf16[512,1024]{1,0:T(8,128)(2,1)}, f32[512,128]{1,0:T(8,128)}, f32[8,64,1024]{2,1,0:T(8,128)}) custom-call(f32[8,64,1024]{2,1,0:T(8,128)} %pad_maximum_fusion.entry_ref, f32[512,128]{1,0:T(8,128)} %get-tuple-element.105.map_ref, f32[8,64,16]{2,1,0:T(8,128)} %bitcast.110, f32[512,1024]{1,0:T(8,128)} %get-tuple-element.106.read_ref, ...), custom_call_target="tpu_custom_call" | custom-call | flops 67108864 | bytes 12582912 | tf_op jit(solution)/shard_map/leave_mixer/pallas_call | solution.py:332
  242.2 5.7 %convolution_multiply_fusion = f32[512,2048]{1,0:T(8,128)} fusion(bf16[512,1024]{1,0:T(8,128)(2,1)} %get-tuple-element.136, bf16[1024,2048]{1,0:T(8,128)(2,1)S(1)} %copy-done.54, f32[512]{0:T(512)S(1)} %bitcast.127), kind=kOutput, calls=%fused_computation | convolution fusion | flops 2148532224 | bytes 9439232 | tf_op jit(solution)/shard_map/dot_general | solution.py:762
  247.9 6.4 %collective-permute-done.24.refs_3_ = bf16[4,64,1024]{2,1,0:T(8,128)(2,1)S(1)} collective-permute-done((bf16[4,64,1024]{2,1,0:T(8,128)(2,1)}, bf16[4,64,1024]{2,1,0:T(8,128)(2,1)S(1)}, u32[]{:S(2)}, u32[]{:S(2)}) %collective-permute-start.24) | collective-permute-done | bytes 524320 | tf_op jit(solution)/shard_map/ppermute | solution.py:36
  259.1 10.3 %collective-permute-done.32.refs_5_ = bf16[4,64,1024]{2,1,0:T(8,128)(2,1)S(1)} collective-permute-done((bf16[4,64,1024]{2,1,0:T(8,128)(2,1)S(1)}, bf16[4,64,1024]{2,1,0:T(8,128)(2,1)S(1)}, u32[]{:S(2)}, u32[]{:S(2)}) %collective-permute-start.32) | collective-permute-done | bytes 524320 | tf_op jit(solution)/shard_map/ppermute | solution.py:36
  274.0 10.4 %collective-permute-done.34 = bf16[2,64,1024]{2,1,0:T(8,128)(2,1)S(1)} collective-permute-done((bf16[2,64,1024]{2,1,0:T(8,128)(2,1)S(1)}, bf16[2,64,1024]{2,1,0:T(8,128)(2,1)S(1)}, u32[]{:S(2)}, u32[]{:S(2)}) %collective-permute-start.34) | collective-permute-done | bytes 262176 | tf_op jit(solution)/shard_map/ppermute | solution.py:36
  292.2 5.6 %copy.45 = f32[8,16,64,64]{3,2,1,0:T(8,128)} copy(f32[8,16,64,64]{2,1,3,0:T(8,128)} %bitcast.101) | data formatting | bytes 4194304 | tf_op jit(solution)/shard_map/transpose | solution.py:769
  306.2 15.3 %collective-permute-done.40.refs_5_ = bf16[4,64,1024]{2,1,0:T(8,128)(2,1)S(1)} collective-permute-done((bf16[4,64,1024]{2,1,0:T(8,128)(2,1)}, bf16[4,64,1024]{2,1,0:T(8,128)(2,1)S(1)}, u32[]{:S(2)}, u32[]{:S(2)}) %collective-permute-start.40) | collective-permute-done | bytes 524320 | tf_op jit(solution)/shard_map/ppermute | solution.py:36
  324.9 21.8 %cache_part.2 = (bf16[4,512,1024]{2,1,0:T(8,128)(2,1)}, bf16[4,1024,512]{2,1,0:T(8,128)(2,1)}, f32[4,8,512]{2,1,0:T(8,128)}, f32[4,8,512]{2,1,0:T(8,128)}) custom-call(s32[8]{0:T(128)} %fusion.22.places_ref.place_ref, s32[4]{0:T(128)} %get-tuple-element.212.live_ref, bf16[4,64,1024]{2,1,0:T(8,128)(2,1)} %bitcast.119, ...), custom_call_target="tpu_custom_call" | custom-call | flops 4294967296 | bytes 20971520 | tf_op jit(solution)/shard_map/cache_part/pallas_call | solution.py:403
  349.6 21.8 %cache_part.3 = (bf16[4,512,1024]{2,1,0:T(8,128)(2,1)}, bf16[4,1024,512]{2,1,0:T(8,128)(2,1)}, f32[4,8,512]{2,1,0:T(8,128)}, f32[4,8,512]{2,1,0:T(8,128)}) custom-call(s32[8]{0:T(128)} %fusion.22.places_ref.place_ref, s32[4]{0:T(128)} %get-tuple-element.213.live_ref, bf16[4,64,1024]{2,1,0:T(8,128)(2,1)} %bitcast.116, ...), custom_call_target="tpu_custom_call" | custom-call | flops 4294967296 | bytes 20971520 | tf_op jit(solution)/shard_map/cache_part/pallas_call | solution.py:403
  396.0 6.3 %collective-permute-done.50 = f32[8,8,512]{2,1,0:T(8,128)S(1)} collective-permute-done((f32[8,8,512]{2,1,0:T(8,128)S(1)}, f32[8,8,512]{2,1,0:T(8,128)S(1)}, u32[]{:S(2)}, u32[]{:S(2)}) %collective-permute-start.50) | collective-permute-done | bytes 131104 | tf_op jit(solution)/shard_map/ppermute | solution.py:84
  404.7 10.2 %project.5 = bf16[512,1024]{1,0:T(8,128)(2,1)} custom-call(s32[8]{0:T(128)} %fusion.22.places_ref.place_ref, bf16[512,4096]{1,0:T(8,128)(2,1)} %bitcast.85, bf16[512,4096]{1,0:T(8,128)(2,1)} %bitcast.86, bf16[512,4096]{1,0:T(8,128)(2,1)} %bitcast.87, bf16[512,4096]{1,0:T(8,128)(2,1)} %bitcast.88, bf16[512,4096]{1,0:T(8,128)(2,1)} %bitcast.89, ...), custom_call_target="tpu_custom_call" | custom-call | flops 4294967296 | bytes 12582912 | tf_op jit(solution)/shard_map/project/pallas_call | solution.py:142
  414.9 11.2 %finish_part.3 = (f32[4,8,512]{2,1,0:T(8,128)}, bf16[4,64,1024]{2,1,0:T(8,128)(2,1)}, bf16[4,64,1024]{2,1,0:T(8,128)(2,1)}, bf16[4,64,1024]{2,1,0:T(8,128)(2,1)}...) custom-call(s32[1]{0:T(128)} %bitcast.1.first_ref, ...), custom_call_target="tpu_custom_call" | custom-call | flops 536870912 | bytes 12582912 | tf_op jit(solution)/shard_map/finish_part/pallas_call | solution.py:506
  427.2 11.4 %finish_part.2 = (f32[4,8,512]{2,1,0:T(8,128)}, bf16[4,64,1024]{2,1,0:T(8,128)(2,1)}, bf16[4,64,1024]{2,1,0:T(8,128)(2,1)}, bf16[4,64,1024]{2,1,0:T(8,128)(2,1)}...) custom-call(s32[1]{0:T(128)} %bitcast.1.first_ref, ...), custom_call_target="tpu_custom_call" | custom-call | flops 536870912 | bytes 12582912 | tf_op jit(solution)/shard_map/finish_part/pallas_call | solution.py:506
  454.1 6.8 %collective-permute-done.61 = f32[4,8,512]{2,1,0:T(8,128)S(1)} collective-permute-done((f32[4,8,512]{2,1,0:T(8,128)S(1)}, f32[4,8,512]{2,1,0:T(8,128)S(1)}, u32[]{:S(2)}, u32[]{:S(2)}) %collective-permute-start.61) | collective-permute-done | bytes 65568 | tf_op jit(solution)/shard_map/ppermute | solution.py:84
  471.1 6.8 %collective-permute-done.69 = bf16[4,64,1024]{2,1,0:T(8,128)(2,1)S(1)} collective-permute-done((bf16[4,64,1024]{2,1,0:T(8,128)(2,1)S(1)}, bf16[4,64,1024]{2,1,0:T(8,128)(2,1)S(1)}, u32[]{:S(2)}, u32[]{:S(2)}) %collective-permute-start.69) | collective-permute-done | bytes 524320 | tf_op jit(solution)/shard_map/ppermute | solution.py:36
  481.8 7.3 %collective-permute-done.56 = bf16[4,64,1024]{2,1,0:T(8,128)(2,1)S(1)} collective-permute-done((bf16[4,64,1024]{2,1,0:T(8,128)(2,1)S(1)}, bf16[4,64,1024]{2,1,0:T(8,128)(2,1)S(1)}, u32[]{:S(2)}, u32[]{:S(2)}) %collective-permute-start.56) | collective-permute-done | bytes 524320 | tf_op jit(solution)/shard_map/ppermute | solution.py:36
  493.0 7.3 %collective-permute-done.70 = bf16[4,64,1024]{2,1,0:T(8,128)(2,1)S(1)} collective-permute-done((bf16[4,64,1024]{2,1,0:T(8,128)(2,1)S(1)}, bf16[4,64,1024]{2,1,0:T(8,128)(2,1)S(1)}, u32[]{:S(2)}, u32[]{:S(2)}) %collective-permute-start.70) | collective-permute-done | bytes 524320 | tf_op jit(solution)/shard_map/ppermute | solution.py:36
  504.2 6.6 %collective-permute-done.57 = bf16[4,64,1024]{2,1,0:T(8,128)(2,1)S(1)} collective-permute-done((bf16[4,64,1024]{2,1,0:T(8,128)(2,1)S(1)}, bf16[4,64,1024]{2,1,0:T(8,128)(2,1)S(1)}, u32[]{:S(2)}, u32[]{:S(2)}) %collective-permute-start.57) | collective-permute-done | bytes 524320 | tf_op jit(solution)/shard_map/ppermute | solution.py:36
  540.8 5.6 %collective-permute-done.76 = bf16[256,512]{1,0:T(8,128)(2,1)} collective-permute-done((bf16[256,512]{1,0:T(8,128)(2,1)}, bf16[256,512]{1,0:T(8,128)(2,1)}, u32[]{:S(2)}, u32[]{:S(2)}) %collective-permute-start.76) | collective-permute-done | bytes 262176 | tf_op jit(solution)/shard_map/ppermute | solution.py:553
  (355 shorter events, 221.9 us)
Async XLA Ops:
  0.6 32.2 %collective-permute-start = (bf16[512,1024]{1,0:T(8,128)(2,1)}, bf16[512,1024]{1,0:T(8,128)(2,1)}, u32[]{:S(2)}, u32[]{:S(2)}) collective-permute-start(bf16[512,1024]{1,0:T(8,128)(2,1)} %refs_9_.5), channel_id=1, source_target_pairs={{0,8},{8,16},{16,24},{24,28},{28,20},{20,12},{12,4},{4,0},{1,9},{9... | collective-permute-start | bytes 3145736 | tf_op jit(solution)/shard_map/ppermute | solution.py:36
  3.7 29.1 %collective-permute-start.1 = (bf16[512,1024]{1,0:T(8,128)(2,1)}, bf16[512,1024]{1,0:T(8,128)(2,1)}, u32[]{:S(2)}, u32[]{:S(2)}) collective-permute-start(bf16[512,1024]{1,0:T(8,128)(2,1)} %refs_9_.5), channel_id=1, source_target_pairs={{0,4},{8,0},{16,8},{24,16},{28,24},{20,28},{12,20},{4,12},{1,5},{9... | collective-permute-start | bytes 3145736 | tf_op jit(solution)/shard_map/ppermute | solution.py:36
  14.1 36.3 %collective-permute-start.4 = (bf16[512,1024]{1,0:T(8,128)(2,1)S(1)}, bf16[512,1024]{1,0:T(8,128)(2,1)}, u32[]{:S(2)}, u32[]{:S(2)}) collective-permute-start(bf16[512,1024]{1,0:T(8,128)(2,1)S(1)} %copy-done.21), channel_id=1, source_target_pairs={{0,8},{8,16},{16,24},{24,28},{28,20},{20,12},{12,4},{4,0},{1,9},{9... | collective-permute-start | bytes 3145736 | tf_op jit(solution)/shard_map/ppermute | solution.py:36
  16.1 36.4 %collective-permute-start.5 = (bf16[512,1024]{1,0:T(8,128)(2,1)S(1)}, bf16[512,1024]{1,0:T(8,128)(2,1)}, u32[]{:S(2)}, u32[]{:S(2)}) collective-permute-start(bf16[512,1024]{1,0:T(8,128)(2,1)S(1)} %copy-done.21), channel_id=1, source_target_pairs={{0,4},{8,0},{16,8},{24,16},{28,24},{20,28},{12,20},{4,12},{1,5},{9... | collective-permute-start | bytes 3145736 | tf_op jit(solution)/shard_map/ppermute | solution.py:36
  32.8 40.1 %collective-permute-start.2 = (bf16[512,1024]{1,0:T(8,128)(2,1)}, bf16[512,1024]{1,0:T(8,128)(2,1)}, u32[]{:S(2)}, u32[]{:S(2)}) collective-permute-start(bf16[512,1024]{1,0:T(8,128)(2,1)} %collective-permute-done.refs_10_), channel_id=1, source_target_pairs={{0,8},{8,16},{16,24},{24,28},{28,20},{20,12},{12,4},{4,0},{1,9},{9... | collective-permute-start | bytes 3145736 | tf_op jit(solution)/shard_map/ppermute | solution.py:36
  34.8 40.2 %collective-permute-start.3 = (bf16[512,1024]{1,0:T(8,128)(2,1)}, bf16[512,1024]{1,0:T(8,128)(2,1)}, u32[]{:S(2)}, u32[]{:S(2)}) collective-permute-start(bf16[512,1024]{1,0:T(8,128)(2,1)} %collective-permute-done.1.refs_11_), channel_id=1, source_target_pairs={{0,4},{8,0},{16,8},{24,16},{28,24},{20,28},{12,20},{4,12},{1,5},{9... | collective-permute-start | bytes 3145736 | tf_op jit(solution)/shard_map/ppermute | solution.py:36
  52.6 43.4 %collective-permute-start.12 = (bf16[512,1024]{1,0:T(8,128)(2,1)}, bf16[512,1024]{1,0:T(8,128)(2,1)S(1)}, u32[]{:S(2)}, u32[]{:S(2)}) collective-permute-start(bf16[512,1024]{1,0:T(8,128)(2,1)} %collective-permute-done.4.refs_10_), channel_id=1, source_target_pairs={{0,8},{8,16},{16,24},{24,28},{28,20},{20,12},{12,4},{4,0},{1,9},{9... | collective-permute-start | bytes 3145736 | tf_op jit(solution)/shard_map/ppermute | solution.py:36
  54.2 41.9 %collective-permute-start.13 = (bf16[512,1024]{1,0:T(8,128)(2,1)}, bf16[512,1024]{1,0:T(8,128)(2,1)}, u32[]{:S(2)}, u32[]{:S(2)}) collective-permute-start(bf16[512,1024]{1,0:T(8,128)(2,1)} %collective-permute-done.5.refs_11_), channel_id=1, source_target_pairs={{0,4},{8,0},{16,8},{24,16},{28,24},{20,28},{12,20},{4,12},{1,5},{9... | collective-permute-start | bytes 3145736 | tf_op jit(solution)/shard_map/ppermute | solution.py:36
  68.3 27.7 %collective-permute-start.8 = (f32[8,1,1024]{2,1,0:T(1,128)S(1)}, f32[8,1,1024]{2,1,0:T(1,128)S(1)}, u32[]{:S(2)}, u32[]{:S(2)}) collective-permute-start(f32[8,1,1024]{2,1,0:T(1,128)S(1)} %copy-done.49), channel_id=1, source_target_pairs={{0,4},{4,0},{8,12},{12,8},{16,20},{20,16},{24,28},{28,24},{1,5},{5... | collective-permute-start | bytes 98312 | tf_op jit(solution)/shard_map/ppermute | solution.py:574
  75.2 32.0 %collective-permute-start.9 = (bf16[8,64,512]{2,1,0:T(8,128)(2,1)S(1)}, bf16[8,64,512]{2,1,0:T(8,128)(2,1)S(1)}, u32[]{:S(2)}, u32[]{:S(2)}) collective-permute-start(bf16[8,64,512]{2,1,0:T(8,128)(2,1)S(1)} %select_convert_fusion.1), channel_id=1, source_target_pairs={{0,4},{4,0},{8,12},{12,8},{16,20},{20,16},{24,28},{28,24},{1,5},{5... | collective-permute-start | bytes 1572872 | tf_op jit(solution)/shard_map/ppermute | solution.py:585
  96.1 38.3 %collective-permute-start.6 = (bf16[512,1024]{1,0:T(8,128)(2,1)}, bf16[512,1024]{1,0:T(8,128)(2,1)}, u32[]{:S(2)}, u32[]{:S(2)}) collective-permute-start(bf16[512,1024]{1,0:T(8,128)(2,1)} %collective-permute-done.2.refs_12_), channel_id=1, source_target_pairs={{0,8},{8,16},{16,24},{24,28},{28,20},{20,12},{12,4},{4,0},{1,9},{9... | collective-permute-start | bytes 3145736 | tf_op jit(solution)/shard_map/ppermute | solution.py:36
  97.6 36.7 %collective-permute-start.7 = (bf16[512,1024]{1,0:T(8,128)(2,1)}, bf16[512,1024]{1,0:T(8,128)(2,1)}, u32[]{:S(2)}, u32[]{:S(2)}) collective-permute-start(bf16[512,1024]{1,0:T(8,128)(2,1)} %collective-permute-done.3.refs_13_), channel_id=1, source_target_pairs={{0,4},{8,0},{16,8},{24,16},{28,24},{20,28},{12,20},{4,12},{1,5},{9... | collective-permute-start | bytes 3145736 | tf_op jit(solution)/shard_map/ppermute | solution.py:36
  108.9 23.9 %collective-permute-start.16 = (bf16[8,64,512]{2,1,0:T(8,128)(2,1)}, bf16[8,64,512]{2,1,0:T(8,128)(2,1)}, u32[]{:S(2)}, u32[]{:S(2)}) collective-permute-start(bf16[8,64,512]{2,1,0:T(8,128)(2,1)} %get-tuple-element.187), channel_id=1, source_target_pairs={{0,8},{4,12},{1,9},{5,13},{2,10},{6,14},{3,11},{7,15}} | collective-permute-start | bytes 1572872 | tf_op jit(solution)/shard_map/ppermute | solution.py:600
  111.2 44.0 %collective-permute-start.14 = (bf16[512,1024]{1,0:T(8,128)(2,1)}, bf16[512,1024]{1,0:T(8,128)(2,1)S(1)}, u32[]{:S(2)}, u32[]{:S(2)}) collective-permute-start(bf16[512,1024]{1,0:T(8,128)(2,1)} %copy-done.23), channel_id=1, source_target_pairs={{0,8},{8,16},{16,24},{24,28},{28,20},{20,12},{12,4},{4,0},{1,9},{9... | collective-permute-start | bytes 3145736 | tf_op jit(solution)/shard_map/ppermute | solution.py:36
  111.2 44.0 %collective-permute-start.15 = (bf16[512,1024]{1,0:T(8,128)(2,1)}, bf16[512,1024]{1,0:T(8,128)(2,1)}, u32[]{:S(2)}, u32[]{:S(2)}) collective-permute-start(bf16[512,1024]{1,0:T(8,128)(2,1)} %collective-permute-done.13.refs_13_), channel_id=1, source_target_pairs={{0,4},{8,0},{16,8},{24,16},{28,24},{20,28},{12,20},{4,12},{1,5},{9... | collective-permute-start | bytes 3145736 | tf_op jit(solution)/shard_map/ppermute | solution.py:36
  141.4 25.0 %collective-permute-start.10 = (bf16[256,1024]{1,0:T(8,128)(2,1)S(1)}, bf16[256,1024]{1,0:T(8,128)(2,1)S(1)}, u32[]{:S(2)}, u32[]{:S(2)}) collective-permute-start(bf16[256,1024]{1,0:T(8,128)(2,1)S(1)} %slice.183), channel_id=1, source_target_pairs={{0,8},{8,16},{16,24},{24,28},{28,20},{20,12},{12,4},{4,0},{1,9},{9... | collective-permute-start | bytes 1572872 | tf_op jit(solution)/shard_map/ppermute | solution.py:36
  156.4 24.2 %collective-permute-start.20 = (bf16[8,64,512]{2,1,0:T(8,128)(2,1)}, bf16[8,64,512]{2,1,0:T(8,128)(2,1)S(1)}, u32[]{:S(2)}, u32[]{:S(2)}) collective-permute-start(bf16[8,64,512]{2,1,0:T(8,128)(2,1)} %add_convert_fusion.8), channel_id=1, source_target_pairs={{16,24},{20,28},{17,25},{21,29},{18,26},{22,30},{19,27},{23,31}} | collective-permute-start | bytes 1572872 | tf_op jit(solution)/shard_map/ppermute | solution.py:600
  178.1 26.7 %collective-permute-start.28 = (bf16[512,1024]{1,0:T(8,128)(2,1)S(1)}, bf16[512,1024]{1,0:T(8,128)(2,1)}, u32[]{:S(2)}, u32[]{:S(2)}) collective-permute-start(bf16[512,1024]{1,0:T(8,128)(2,1)S(1)} %copy-done.22), channel_id=1, source_target_pairs={{0,8},{8,16},{16,24},{24,28},{28,20},{20,12},{12,4},{4,0},{1,9},{9... | collective-permute-start | bytes 3145736 | tf_op jit(solution)/shard_map/ppermute | solution.py:36
  180.6 26.2 %collective-permute-start.29 = (bf16[512,1024]{1,0:T(8,128)(2,1)S(1)}, bf16[512,1024]{1,0:T(8,128)(2,1)}, u32[]{:S(2)}, u32[]{:S(2)}) collective-permute-start(bf16[512,1024]{1,0:T(8,128)(2,1)S(1)} %copy-done.22), channel_id=1, source_target_pairs={{0,4},{8,0},{16,8},{24,16},{28,24},{20,28},{12,20},{4,12},{1,5},{9... | collective-permute-start | bytes 3145736 | tf_op jit(solution)/shard_map/ppermute | solution.py:36
  181.2 34.7 %collective-permute-start.23 = (bf16[8,64,512]{2,1,0:T(8,128)(2,1)S(1)}, bf16[8,64,512]{2,1,0:T(8,128)(2,1)S(1)}, u32[]{:S(2)}, u32[]{:S(2)}) collective-permute-start(bf16[8,64,512]{2,1,0:T(8,128)(2,1)S(1)} %select_convert_fusion), channel_id=1, source_target_pairs={{0,4},{4,0},{8,12},{12,8},{16,20},{20,16},{24,28},{28,24},{1,5},{5... | collective-permute-start | bytes 1572872 | tf_op jit(solution)/shard_map/ppermute | solution.py:585
  183.8 43.0 %collective-permute-start.21 = (bf16[4,64,1024]{2,1,0:T(8,128)(2,1)S(1)}, bf16[4,64,1024]{2,1,0:T(8,128)(2,1)}, u32[]{:S(2)}, u32[]{:S(2)}) collective-permute-start(bf16[4,64,1024]{2,1,0:T(8,128)(2,1)S(1)} %bitcast.117), channel_id=1, source_target_pairs={{0,8},{8,16},{16,24},{24,28},{28,20},{20,12},{12,4},{4,0},{1,9},{9... | collective-permute-start | bytes 1572872 | tf_op jit(solution)/shard_map/ppermute | solution.py:36
  185.9 41.0 %collective-permute-start.22 = (bf16[4,64,1024]{2,1,0:T(8,128)(2,1)S(1)}, bf16[4,64,1024]{2,1,0:T(8,128)(2,1)}, u32[]{:S(2)}, u32[]{:S(2)}) collective-permute-start(bf16[4,64,1024]{2,1,0:T(8,128)(2,1)S(1)} %bitcast.118), channel_id=1, source_target_pairs={{0,4},{8,0},{16,8},{24,16},{28,24},{20,28},{12,20},{4,12},{1,5},{9... | collective-permute-start | bytes 1572872 | tf_op jit(solution)/shard_map/ppermute | solution.py:36
  206.8 35.3 %collective-permute-start.30 = (bf16[4,64,1024]{2,1,0:T(8,128)(2,1)S(1)}, bf16[4,64,1024]{2,1,0:T(8,128)(2,1)}, u32[]{:S(2)}, u32[]{:S(2)}) collective-permute-start(bf16[4,64,1024]{2,1,0:T(8,128)(2,1)S(1)} %bitcast.114), channel_id=1, source_target_pairs={{0,8},{8,16},{16,24},{24,28},{28,20},{20,12},{12,4},{4,0},{1,9},{9... | collective-permute-start | bytes 1572872 | tf_op jit(solution)/shard_map/ppermute | solution.py:36
  208.4 33.8 %collective-permute-start.31 = (bf16[4,64,1024]{2,1,0:T(8,128)(2,1)S(1)}, bf16[4,64,1024]{2,1,0:T(8,128)(2,1)}, u32[]{:S(2)}, u32[]{:S(2)}) collective-permute-start(bf16[4,64,1024]{2,1,0:T(8,128)(2,1)S(1)} %bitcast.115), channel_id=1, source_target_pairs={{0,4},{8,0},{16,8},{24,16},{28,24},{20,28},{12,20},{4,12},{1,5},{9... | collective-permute-start | bytes 1572872 | tf_op jit(solution)/shard_map/ppermute | solution.py:36
  257.0 45.6 %collective-permute-start.38 = (bf16[4,64,1024]{2,1,0:T(8,128)(2,1)}, bf16[4,64,1024]{2,1,0:T(8,128)(2,1)}, u32[]{:S(2)}, u32[]{:S(2)}) collective-permute-start(bf16[4,64,1024]{2,1,0:T(8,128)(2,1)} %collective-permute-done.30.refs_1_), channel_id=1, source_target_pairs={{0,8},{8,16},{16,24},{24,28},{28,20},{20,12},{12,4},{4,0},{1,9},{9... | collective-permute-start | bytes 1572872 | tf_op jit(solution)/shard_map/ppermute | solution.py:36
  259.1 43.6 %collective-permute-start.39 = (bf16[4,64,1024]{2,1,0:T(8,128)(2,1)}, bf16[4,64,1024]{2,1,0:T(8,128)(2,1)}, u32[]{:S(2)}, u32[]{:S(2)}) collective-permute-start(bf16[4,64,1024]{2,1,0:T(8,128)(2,1)} %collective-permute-done.31.refs_2_), channel_id=1, source_target_pairs={{0,4},{8,0},{16,8},{24,16},{28,24},{20,28},{12,20},{4,12},{1,5},{9... | collective-permute-start | bytes 1572872 | tf_op jit(solution)/shard_map/ppermute | solution.py:36
  287.2 59.5 %collective-permute-start.36 = (bf16[512,1024]{1,0:T(8,128)(2,1)}, bf16[512,1024]{1,0:T(8,128)(2,1)}, u32[]{:S(2)}, u32[]{:S(2)}) collective-permute-start(bf16[512,1024]{1,0:T(8,128)(2,1)} %collective-permute-done.28.refs_10_), channel_id=1, source_target_pairs={{0,8},{8,16},{16,24},{24,28},{28,20},{20,12},{12,4},{4,0},{1,9},{9... | collective-permute-start | bytes 3145736 | tf_op jit(solution)/shard_map/ppermute | solution.py:36
  288.6 58.1 %collective-permute-start.37 = (bf16[512,1024]{1,0:T(8,128)(2,1)}, bf16[512,1024]{1,0:T(8,128)(2,1)}, u32[]{:S(2)}, u32[]{:S(2)}) collective-permute-start(bf16[512,1024]{1,0:T(8,128)(2,1)} %collective-permute-done.29.refs_11_), channel_id=1, source_target_pairs={{0,4},{8,0},{16,8},{24,16},{28,24},{20,28},{12,20},{4,12},{1,5},{9... | collective-permute-start | bytes 3145736 | tf_op jit(solution)/shard_map/ppermute | solution.py:36
  346.7 29.7 %collective-permute-start.44 = (bf16[512,1024]{1,0:T(8,128)(2,1)}, bf16[512,1024]{1,0:T(8,128)(2,1)S(1)}, u32[]{:S(2)}, u32[]{:S(2)}) collective-permute-start(bf16[512,1024]{1,0:T(8,128)(2,1)} %collective-permute-done.36.refs_12_), channel_id=1, source_target_pairs={{0,8},{8,16},{16,24},{24,28},{28,20},{20,12},{12,4},{4,0},{1,9},{9... | collective-permute-start | bytes 3145736 | tf_op jit(solution)/shard_map/ppermute | solution.py:36
  347.7 28.7 %collective-permute-start.45 = (bf16[512,1024]{1,0:T(8,128)(2,1)}, bf16[512,1024]{1,0:T(8,128)(2,1)S(1)}, u32[]{:S(2)}, u32[]{:S(2)}) collective-permute-start(bf16[512,1024]{1,0:T(8,128)(2,1)} %collective-permute-done.37.refs_13_), channel_id=1, source_target_pairs={{0,4},{8,0},{16,8},{24,16},{28,24},{20,28},{12,20},{4,12},{1,5},{9... | collective-permute-start | bytes 3145736 | tf_op jit(solution)/shard_map/ppermute | solution.py:36
  376.5 26.5 %collective-permute-start.46 = (bf16[256,1024]{1,0:T(8,128)(2,1)S(1)}, bf16[256,1024]{1,0:T(8,128)(2,1)S(1)}, u32[]{:S(2)}, u32[]{:S(2)}) collective-permute-start(bf16[256,1024]{1,0:T(8,128)(2,1)S(1)} %slice.197), channel_id=1, source_target_pairs={{0,8},{8,16},{16,24},{24,28},{28,20},{20,12},{12,4},{4,0},{1,9},{9... | collective-permute-start | bytes 1572872 | tf_op jit(solution)/shard_map/ppermute | solution.py:36
  377.5 25.5 %collective-permute-start.47 = (bf16[256,1024]{1,0:T(8,128)(2,1)S(1)}, bf16[256,1024]{1,0:T(8,128)(2,1)S(1)}, u32[]{:S(2)}, u32[]{:S(2)}) collective-permute-start(bf16[256,1024]{1,0:T(8,128)(2,1)S(1)} %slice.198), channel_id=1, source_target_pairs={{0,4},{8,0},{16,8},{24,16},{28,24},{20,28},{12,20},{4,12},{1,5},{9... | collective-permute-start | bytes 1572872 | tf_op jit(solution)/shard_map/ppermute | solution.py:36
  (101 other events, 1531.6 us)

commit v5 on v4

--- a/solution.py
+++ b/solution.py
@@ -108,8 +108,8 @@
 
 def project_kernel(count, turned, places_ref, *refs):
     input_refs, weight_refs = refs[:count], refs[count : 2 * count]
-    cosine_ref, sine_ref, out_ref = refs[2 * count :]
-    total = None
+    cosine_ref, sine_ref, *base_ref, out_ref = refs[2 * count :]
+    total = base_ref[0][...] if base_ref else None
     for input_ref, weight_ref in zip(input_refs, weight_refs):
         term = jnp.dot(input_ref[...], weight_ref[...], preferred_element_type=jnp.float32)
         total = term if total is None else total + term
@@ -125,7 +125,7 @@
         out_ref[:, at] = (part * cosine + rolled * sine).astype(out_ref.dtype)
 
 
-def project(places, offsets, rows, value, pieces, cosine, sine, turned):
+def project(places, offsets, rows, value, pieces, cosine, sine, turned, base=(), kind=jnp.bfloat16):
     tokens = value.shape[0]
     width = pieces[0][2].shape[1]
     block = min(width, 256)
@@ -144,18 +144,21 @@
         grid_spec=pltpu.PrefetchScalarGridSpec(
             num_scalar_prefetch=1,
             grid=(width // block,),
-            in_specs=input_specs + weight_specs + [angle, angle],
+            in_specs=input_specs
+            + weight_specs
+            + [angle, angle]
+            + [pl.BlockSpec((tokens, block), lambda j, *_: (0, j))] * len(base),
             out_specs=pl.BlockSpec((tokens, block), lambda j, *_: (0, j)),
         ),
-        out_shape=jax.ShapeDtypeStruct((tokens, width), jnp.bfloat16),
+        out_shape=jax.ShapeDtypeStruct((tokens, width), kind),
         compiler_params=pltpu.CompilerParams(vmem_limit_bytes=VMEM_BYTES),
         cost_estimate=pl.CostEstimate(
-            flops=2 * tokens * value.shape[1] * width,
+            flops=2 * tokens * sum(piece.shape[0] for _, _, piece in pieces) * width,
             bytes_accessed=2 * (tokens + width) * value.shape[1],
             transcendentals=0,
         ),
         name="project",
-    )(places, *[value] * len(pieces), *[piece for _, _, piece in pieces], cosine, sine)
+    )(places, *[value] * len(pieces), *[piece for _, _, piece in pieces], cosine, sine, *base)
 
 
 def silu(value):
@@ -366,9 +369,18 @@
     return lax.dot_general(a, b, (((0,), (0,)), ((), ())), preferred_element_type=jnp.float32)
 
 
-def cache_kernel(slots, place_ref, live_ref, *refs):
+def group_scores(first, key, query):
+    scores = dot_nt(key, query)
+    shape = scores.shape
+    live = first + lax.broadcasted_iota(jnp.int32, shape, 0) <= lax.broadcasted_iota(
+        jnp.int32, shape, 1
+    )
+    return jnp.where(live, scores, DEAD)
+
+
+def cache_kernel(slots, first_ref, place_ref, live_ref, *refs):
     query_refs = refs[:slots]
-    key_ref, value_ref, joined_ref, out_ref, peak_ref, total_ref = refs[slots:]
+    key_ref, value_ref, group_ref, joined_ref, out_ref, peak_ref, total_ref = refs[slots:]
     tok_block = query_refs[0].shape[1]
     keys, width = key_ref.shape[1:]
     tokens = tok_block * slots
@@ -382,8 +394,14 @@
     bias = jnp.concatenate([bias] * (tokens // 128), axis=1)
     for head in range(width // HEAD_DIM):
         at = slice(head * HEAD_DIM, (head + 1) * HEAD_DIM)
-        scores = dot_nt(key_ref[0, :, at], joined_ref[0, :, at]) + bias
-        peak = jnp.max(scores, axis=0, keepdims=True)
+        query = joined_ref[0, :, at]
+        scores = dot_nt(key_ref[0, :, at], query) + bias
+        peak = jnp.maximum(
+            jnp.max(scores, axis=0, keepdims=True),
+            jnp.max(
+                group_scores(first_ref[0], group_ref[0, :, at], query), axis=0, keepdims=True
+            ),
+        )
         weights = jnp.exp2((scores - peak) * EXP2_SCALE)
         total_ref[0, head : head + 1, :] = jnp.sum(weights, axis=0, keepdims=True)
         peak_ref[0, head : head + 1, :] = peak
@@ -392,7 +410,7 @@
         )
 
 
-def cache_part(begin, places, live, query_slots, keys, values):
+def cache_part(begin, first, places, live, query_slots, keys, values, new_keys):
     slots = len(query_slots)
     requests, tok_block, width = query_slots[0].shape
     tokens = tok_block * slots
@@ -403,9 +421,11 @@
     return pl.pallas_call(
         functools.partial(cache_kernel, slots),
         grid_spec=pltpu.PrefetchScalarGridSpec(
-            num_scalar_prefetch=2,
+            num_scalar_prefetch=3,
             grid=(requests,),
-            in_specs=[one(tok_block, 0)] * slots + [one(cache_block, begin)] * 2,
+            in_specs=[one(tok_block, 0)] * slots
+            + [one(cache_block, begin)] * 2
+            + [one(tok_block, begin)],
             out_specs=[
                 one(tokens, 0),
                 pl.BlockSpec((1, width, tokens), lambda r, *_: (r, 0, 0)),
@@ -426,50 +446,7 @@
             transcendentals=requests * tokens * cache_block * heads,
         ),
         name="cache_part",
-    )(places, live, *query_slots, keys, values)
-
-
-def group_scores(first, key, query):
-    scores = dot_nt(key, query)
-    shape = scores.shape
-    live = first + lax.broadcasted_iota(jnp.int32, shape, 0) <= lax.broadcasted_iota(
-        jnp.int32, shape, 1
-    )
-    return jnp.where(live, scores, DEAD)
-
-
-def peak_kernel(first_ref, query_ref, key_ref, peak_ref, out_ref):
-    for head in range(query_ref.shape[2] // HEAD_DIM):
-        at = slice(head * HEAD_DIM, (head + 1) * HEAD_DIM)
-        scores = group_scores(first_ref[0], key_ref[0, :, at], query_ref[0, :, at])
-        out_ref[0, head : head + 1, :] = jnp.maximum(
-            peak_ref[0, head : head + 1, :], jnp.max(scores, axis=0, keepdims=True)
-        )
-
-
-def group_peaks(begin, first, queries, new_keys, peaks):
-    requests, tokens, width = queries.shape
-    tok_block = new_keys.shape[1]
-    heads = width // HEAD_DIM
-    one = lambda rows, start: pl.BlockSpec((1, rows, width), lambda r, *_: (r + start, 0, 0))
-    stat = pl.BlockSpec((1, heads, tokens), lambda r, *_: (r, 0, 0))
-    return pl.pallas_call(
-        peak_kernel,
-        grid_spec=pltpu.PrefetchScalarGridSpec(
-            num_scalar_prefetch=1,
-            grid=(requests,),
-            in_specs=[one(tokens, 0), one(tok_block, begin), stat],
-            out_specs=stat,
-        ),
-        out_shape=jax.ShapeDtypeStruct(peaks.shape, jnp.float32),
-        compiler_params=pltpu.CompilerParams(vmem_limit_bytes=VMEM_BYTES),
-        cost_estimate=pl.CostEstimate(
-            flops=2 * requests * tokens * tok_block * width,
-            bytes_accessed=2 * requests * width * tokens,
-            transcendentals=0,
-        ),
-        name="group_peaks",
-    )(first, queries, new_keys, peaks)
+    )(first, places, live, *query_slots, keys, values, new_keys)
 
 
 def finish_kernel(slots, first_ref, place_ref, *refs):
@@ -490,7 +467,7 @@
         joined = cache_ref[0, at, :].astype(jnp.float32) * rescale + dot_tn(
             value_ref[0, :, at], weights.astype(jnp.bfloat16)
         )
-        joined_ref[:, at] = joined.T.astype(jnp.bfloat16)
+        joined_ref[:, at] = joined.astype(jnp.bfloat16).T
     for slot in range(slots):
         start = pl.multiple_of(place_ref[slot] * tok_block, tok_block)
         part_refs[slot][0] = joined_ref[pl.ds(start, tok_block), :]
@@ -676,14 +653,16 @@
     local_width = D // head_count
     made = {}
 
-    def product(ring, turned):
-        pieces = list(ring.pieces)
+    def product(pieces, turned, base=(), kind=jnp.bfloat16):
+        pieces = list(pieces)
         if pieces[-1][2].shape[0] < 128:
             (offset, row, upper), (_, _, lower) = pieces[-2:]
             pieces[-2:] = [(offset, row, jnp.concatenate([upper, lower], axis=0))]
         return project(
-            places, offsets, rows, flat_input, pieces, cosine, sine, turned
-        ).reshape(requests, tok_block, local_att)
+            places, offsets, rows, flat_input, pieces, cosine, sine, turned, base, kind
+        )
+
+    by_request = lambda value: value.reshape(requests, tok_block, local_att)
 
     def order_weight():
         made["w_in"] = w_in.reshape(D, 2 * local_inner)
@@ -778,14 +757,14 @@
     cached = []
 
     def make_queries():
-        queries = product(query_ring, True)
+        queries = by_request(product(query_ring.pieces, True))
         slot_rings.extend(
             Ring(queries[begin : begin + group], order) for begin in range(0, requests, group)
         )
         return (queries,), ()
 
     def make_keys():
-        made["keys"] = product(key_ring, True)
+        made["keys"] = by_request(product(key_ring.pieces, True))
         return (made["keys"],), ()
 
     def meet_cache(index):
@@ -797,27 +776,32 @@
             slots[0] = clock.hold(slots[0])
             cached.append(
                 cache_part(
-                    begin, places, live[begin : begin + group], slots, cache_keys, cache_values
+                    begin,
+                    first,
+                    places,
+                    live[begin : begin + group],
+                    slots,
+                    cache_keys,
+                    cache_values,
+                    made["keys"],
                 )
             )
             return tuple(cached[-1]), ()
 
         return work
 
-    def make_peaks():
-        keys = clock.hold(made["keys"])
-        made["peaks"] = jnp.concatenate(
-            [
-                group_peaks(index * group, first, part[0], keys, part[2])
-                for index, part in enumerate(cached)
-            ],
-            axis=0,
-        )
-        return (made["peaks"],), ()
-
     def join_peaks():
-        made["best"] = butterfly(clock.hold(made["peaks"]), "seq", seq_count, jnp.maximum)
-        return (), ()
+        peaks = jnp.concatenate([clock.hold(part[2]) for part in cached], axis=0)
+        made["best"] = butterfly(peaks, "seq", seq_count, jnp.maximum)
+        return leave_chain()[0], (made["best"],)
+
+    def make_values():
+        made["values"] = product(
+            [(0, 0, clock.hold(value_ring.block))] + value_ring.pieces[1:-2],
+            False,
+            kind=jnp.float32,
+        )
+        return (made["values"],), ()
 
     def steps(rings, begin, end):
         return [ring for _ in range(begin, end) for ring in rings]
@@ -829,23 +813,21 @@
                 works[index] if index < len(works) else None,
             )
 
-    run(
-        steps([query_ring, key_ring], 0, half),
-        [order_weight, enter, inside, initial_state, start_relay, hop, hop, hop],
-    )
-    run(steps([value_ring], 0, 1), [make_queries])
+    both = steps([query_ring, key_ring], 0, half - 2) + [query_ring] * 2 + [key_ring] * 2
+    works = [order_weight, enter, inside, initial_state, start_relay, hop, hop]
+    run(both, works + [None] * (len(both) - 1 - len(works)) + [make_queries])
     run(
         steps(slot_rings, 0, half),
-        [end_relay, make_keys, leave, leave_terms, leave_chain],
+        [hop, make_keys, end_relay, None, leave, None, leave_terms],
     )
     run(
-        steps([value_ring], 1, half),
-        [meet_cache(0), meet_cache(1), make_peaks, join_peaks],
+        steps([value_ring], 0, half),
+        [meet_cache(0), meet_cache(1)] + [None] * (half - 4) + [join_peaks, make_values],
     )
 
     new_keys = made["keys"]
     best = made["best"]
-    new_values = product(value_ring, False)
+    new_values = by_request(product(value_ring.pieces[-2:], False, base=(made["values"],)))
 
     own = lambda stat: lax.dynamic_slice_in_dim(stat, seq_index * tok_block, tok_block, 2)
     greatest_logit = jnp.transpose(own(best), (0, 2, 1)) * SCALE

time: 560 us -> 570 us (1.018)
  starting transfers between devices: 88.5 us -> 107 us
    ppermute x11, waiting for transfers between devices: 23.9 us -> 48.1 us  [butterfly(): lax.ppermute(value, axis, [(i, i ^ bit) for i in range(count)])]
    ppermute x3, waiting for transfers between devices: 19.4 us -> 0.01 us  [advance(): self.entry = entry + lax.ppermute(leaving, 'seq', route).astype(jnp.float32)]
    ppermute x56, starting transfers between devices: 67.6 us -> 85.3 us  [ring_step(): return lax.ppermute(block, 'seq', route)]
    pallas_call x2 -> x0, Pallas kernels: 9.83 us -> none  [group_peaks(): pl.pallas_call(peak_kernel, grid_spec=pltpu.PrefetchScalarGridSpec(num_sc...]
    ppermute x2, waiting for transfers between devices: 15.9 us -> 8.9 us  [exchange(): lax.ppermute(value.astype(jnp.bfloat16), 'seq', self.swap)]
    pallas_call x3 -> x4, Pallas kernels: 31.3 us -> 36 us  [project(): pl.pallas_call(functools.partial(project_kernel, len(pieces), turned), gr...]
    unnamed x116 -> x127, local copies, waits for them, and re-layouts: 17 us -> 17.8 us
  transfers between devices with their start and end apart: 77 -> 77, of which waited for: 40 -> 43; matrix products, arithmetic and copies ran while one was open for 17% -> 16% of each run, Pallas kernels for 21% -> 21%
where the time goes in v5:
time: 570 us; the launch traced here: 560 us
  waiting for transfers between devices  213 us (37%)
  Pallas kernels  133 us (23%)
  starting transfers between devices  107 us (19%)
  local copies, waits for them, and re-layouts  61.4 us (11%)
  other arithmetic  31.7 us (6%)
  matrix products  10.9 us (2%)
    ppermute x56, waiting for transfers between devices, ring_step(): return lax.ppermute(block, 'seq', route)  130 us
    ppermute x56, starting transfers between devices, ring_step(): return lax.ppermute(block, 'seq', route)  85.3 us
    ppermute x11, waiting for transfers between devices, butterfly(): lax.ppermute(value, axis, [(i, i ^ bit) for i in range(count)])  48.1 us
    pallas_call x2, Pallas kernels, cache_part(): pl.pallas_call(functools.partial(cache_kernel, slots), grid_spec=pltpu.Pr...  44.1 us
    pallas_call x4, Pallas kernels, project(): pl.pallas_call(functools.partial(project_kernel, len(pieces), turned), gr...  36 us
    pallas_call x2, Pallas kernels, finish_part(): pl.pallas_call(functools.partial(finish_kernel, slots), grid_spec=pltpu.P...  22.7 us
    ppermute x1, waiting for transfers between devices, __init__(): other_factor = side(lax.ppermute(through, 'seq', self.swap))  18.9 us
    unnamed x127, local copies, waits for them, and re-layouts  17.8 us
  transfers between devices with their start and end apart: 77, of which 43 were waited for; matrix products, arithmetic and copies ran while one was open for 16% of the time, Pallas kernels for 21%

profile of v5, /device:TPU:0, one launch (start us, length us, event | category | flops | bytes accessed | tf_op | source)
XLA Modules:
  0.0 559.9 jit_solution(8298766001992457620)
XLA Ops:
  3.7 10.4 %copy.52 = bf16[256,8,2,1024]{3,1,2,0:T(8,128)(2,1)} copy(bf16[256,8,2,1024]{3,2,1,0:T(2,128)(2,1)} %bitcast.105) | data formatting | bytes 16777216
  17.2 11.7 %enter_mixer.1 = (f32[512,2048]{1,0:T(8,128)}, f32[512,128]{1,0:T(8,128)}, f32[512,16]{1,0:T(8,128)}) custom-call(bf16[512,4096]{1,0:T(8,128)(2,1)} %bitcast.66, f32[1,2048]{1,0:T(1,128)} %bitcast.128, bf16[2048,128]{1,0:T(8,128)(2,1)} %bc_ref.1, bf16[2048,16]{1,0:T(8,128)(2,1)} %copy.40.dt_ref, f32[1,16]{1,0:T(1,128)} %bitcast.129, bf16[2048,2048]{1,0:T(8,128)(2,1)} %bitcast.106), custom_call_target="tpu_custom_call" | custom-call | flops 4294967296 | bytes 14680064 | tf_op jit(solution)/shard_map/enter_mixer/pallas_call | solution.py:204
  36.4 9.6 %inside_block.1 = (f32[512,1024]{1,0:T(8,128)}, f32[8,64,1024]{2,1,0:T(8,128)}, f32[8,1,1024]{2,1,0:T(1,128)}) custom-call(f32[512,2048]{1,0:T(8,128)} %get-tuple-element.105.inner_ref.gate_ref, f32[512,128]{1,0:T(8,128)} %get-tuple-element.106.map_ref, f32[8,64,16]{2,1,0:T(8,128)} %bitcast.109, f32[8,64,16]{2,1,0:T(8,128)} %bitcast.113, ...), custom_call_target="tpu_custom_call" | custom-call | flops 402653184 | bytes 8388608 | tf_op jit(solution)/shard_map/inside_block/pallas_call | solution.py:282
  57.7 5.6 %copy.44 = f32[8,16,64,64]{2,1,3,0:T(8,128)} copy(f32[8,16,64,64]{3,2,1,0:T(8,128)} %reshape.131) | data formatting | bytes 4194304 | tf_op jit(solution)/shard_map/reshape | solution.py:702
  77.0 18.9 %collective-permute-done.12 = f32[8,1,1024]{2,1,0:T(1,128)S(1)} collective-permute-done((f32[8,1,1024]{2,1,0:T(1,128)S(1)}, f32[8,1,1024]{2,1,0:T(1,128)S(1)}, u32[]{:S(2)}, u32[]{:S(2)}) %collective-permute-start.12) | collective-permute-done | bytes 32800 | tf_op jit(solution)/shard_map/ppermute | solution.py:551
  98.3 8.9 %collective-permute-done.13 = bf16[8,64,512]{2,1,0:T(8,128)(2,1)S(1)} collective-permute-done((bf16[8,64,512]{2,1,0:T(8,128)(2,1)S(1)}, bf16[8,64,512]{2,1,0:T(8,128)(2,1)S(1)}, u32[]{:S(2)}, u32[]{:S(2)}) %collective-permute-start.13) | collective-permute-done | bytes 524320 | tf_op jit(solution)/shard_map/ppermute | solution.py:562
  113.0 15.9 %collective-permute-done.6.refs_14_ = bf16[512,1024]{1,0:T(8,128)(2,1)} collective-permute-done((bf16[512,1024]{1,0:T(8,128)(2,1)}, bf16[512,1024]{1,0:T(8,128)(2,1)}, u32[]{:S(2)}, u32[]{:S(2)}) %collective-permute-start.6) | collective-permute-done | bytes 1048608 | tf_op jit(solution)/shard_map/ppermute | solution.py:36
  138.6 7.4 %collective-permute-done.10.refs_16_ = bf16[256,1024]{1,0:T(8,128)(2,1)S(1)} collective-permute-done((bf16[256,1024]{1,0:T(8,128)(2,1)S(1)}, bf16[256,1024]{1,0:T(8,128)(2,1)S(1)}, u32[]{:S(2)}, u32[]{:S(2)}) %collective-permute-start.10) | collective-permute-done | bytes 524320 | tf_op jit(solution)/shard_map/ppermute | solution.py:36
  147.0 10.4 %project.4 = bf16[512,1024]{1,0:T(8,128)(2,1)} custom-call(s32[8]{0:T(128)} %fusion.22.places_ref.place_ref, bf16[512,4096]{1,0:T(8,128)(2,1)} %bitcast.67, bf16[512,4096]{1,0:T(8,128)(2,1)} %bitcast.68, bf16[512,4096]{1,0:T(8,128)(2,1)} %bitcast.69, bf16[512,4096]{1,0:T(8,128)(2,1)} %bitcast.70, bf16[512,4096]{1,0:T(8,128)(2,1)} %bitcast.71, ...), custom_call_target="tpu_custom_call" | custom-call | flops 4294967296 | bytes 12582912 | tf_op jit(solution)/shard_map/project/pallas_call | solution.py:142
  157.6 9.1 %collective-permute-done.14.refs_14_ = bf16[512,1024]{1,0:T(8,128)(2,1)S(1)} collective-permute-done((bf16[512,1024]{1,0:T(8,128)(2,1)}, bf16[512,1024]{1,0:T(8,128)(2,1)S(1)}, u32[]{:S(2)}, u32[]{:S(2)}) %collective-permute-start.14) | collective-permute-done | bytes 1048608 | tf_op jit(solution)/shard_map/ppermute | solution.py:36
  188.6 10.4 %project.5 = bf16[512,1024]{1,0:T(8,128)(2,1)} custom-call(s32[8]{0:T(128)} %fusion.22.places_ref.place_ref, bf16[512,4096]{1,0:T(8,128)(2,1)} %bitcast.80, bf16[512,4096]{1,0:T(8,128)(2,1)} %bitcast.77, bf16[512,4096]{1,0:T(8,128)(2,1)} %bitcast.78, bf16[512,4096]{1,0:T(8,128)(2,1)} %bitcast.79, bf16[512,4096]{1,0:T(8,128)(2,1)} %bitcast.76, ...), custom_call_target="tpu_custom_call" | custom-call | flops 4294967296 | bytes 12582912 | tf_op jit(solution)/shard_map/project/pallas_call | solution.py:142
  207.7 9.8 %collective-permute-start.34 = (bf16[4,64,1024]{2,1,0:T(8,128)(2,1)S(1)}, bf16[4,64,1024]{2,1,0:T(8,128)(2,1)S(1)}, u32[]{:S(2)}, u32[]{:S(2)}) collective-permute-start(bf16[4,64,1024]{2,1,0:T(8,128)(2,1)S(1)} %bitcast.114), channel_id=1, source_target_pairs={{0,8},{8,16},{16,24},{24,28},{28,20},{20,12},{12,4},{4,0},{1,9},{9... | collective-permute-start | bytes 1572872 | tf_op jit(solution)/shard_map/ppermute | solution.py:36
  219.4 9.3 %collective-permute-done.23.refs_3_ = bf16[4,64,1024]{2,1,0:T(8,128)(2,1)S(1)} collective-permute-done((bf16[4,64,1024]{2,1,0:T(8,128)(2,1)S(1)}, bf16[4,64,1024]{2,1,0:T(8,128)(2,1)S(1)}, u32[]{:S(2)}, u32[]{:S(2)}) %collective-permute-start.23) | collective-permute-done | bytes 524320 | tf_op jit(solution)/shard_map/ppermute | solution.py:36
  232.4 7.6 %collective-permute-done.34.refs_1_ = bf16[4,64,1024]{2,1,0:T(8,128)(2,1)S(1)} collective-permute-done((bf16[4,64,1024]{2,1,0:T(8,128)(2,1)S(1)}, bf16[4,64,1024]{2,1,0:T(8,128)(2,1)S(1)}, u32[]{:S(2)}, u32[]{:S(2)}) %collective-permute-start.34) | collective-permute-done | bytes 524320 | tf_op jit(solution)/shard_map/ppermute | solution.py:36
  243.6 8.9 %leave_mixer.1 = (bf16[512,1024]{1,0:T(8,128)(2,1)}, f32[512,128]{1,0:T(8,128)}, f32[8,64,1024]{2,1,0:T(8,128)}) custom-call(f32[8,64,1024]{2,1,0:T(8,128)} %pad_maximum_fusion.entry_ref, f32[512,128]{1,0:T(8,128)} %get-tuple-element.106.map_ref, f32[8,64,16]{2,1,0:T(8,128)} %bitcast.110, f32[512,1024]{1,0:T(8,128)} %get-tuple-element.107.read_ref, ...), custom_call_target="tpu_custom_call" | custom-call | flops 67108864 | bytes 12582912 | tf_op jit(solution)/shard_map/leave_mixer/pallas_call | solution.py:335
  261.2 9.7 %collective-permute-start.38 = (bf16[4,64,1024]{2,1,0:T(8,128)(2,1)S(1)}, bf16[4,64,1024]{2,1,0:T(8,128)(2,1)S(1)}, u32[]{:S(2)}, u32[]{:S(2)}) collective-permute-start(bf16[4,64,1024]{2,1,0:T(8,128)(2,1)S(1)} %collective-permute-done.36.refs_3_), channel_id=1, source_target_pairs={{0,8},{8,16},{16,24},{24,28},{28,20},{20,12},{12,4},{4,0},{1,9},{9... | collective-permute-start | bytes 1572872 | tf_op jit(solution)/shard_map/ppermute | solution.py:36
  271.0 6.6 %collective-permute-done.31 = bf16[2,64,1024]{2,1,0:T(8,128)(2,1)S(1)} collective-permute-done((bf16[2,64,1024]{2,1,0:T(8,128)(2,1)S(1)}, bf16[2,64,1024]{2,1,0:T(8,128)(2,1)S(1)}, u32[]{:S(2)}, u32[]{:S(2)}) %collective-permute-start.31) | collective-permute-done | bytes 262176 | tf_op jit(solution)/shard_map/ppermute | solution.py:36
  279.6 6.9 %convolution_multiply_fusion = f32[512,2048]{1,0:T(8,128)} fusion(bf16[512,1024]{1,0:T(8,128)(2,1)} %get-tuple-element.147, bf16[1024,2048]{1,0:T(8,128)(2,1)} %param.35, f32[512]{0:T(512)S(1)} %bitcast.127), kind=kOutput, calls=%fused_computation | convolution fusion | flops 2148532224 | bytes 9439232 | tf_op jit(solution)/shard_map/dot_general | solution.py:741
  291.1 22.0 %cache_part.2 = (bf16[4,512,1024]{2,1,0:T(8,128)(2,1)}, bf16[4,1024,512]{2,1,0:T(8,128)(2,1)}, f32[4,8,512]{2,1,0:T(8,128)}, f32[4,8,512]{2,1,0:T(8,128)}) custom-call(s32[1]{0:T(128)} %bitcast.1.first_ref, s32[8]{0:T(128)} %fusion.22.places_ref.place_ref, s32[4]{0:T(128)} %get-tuple-element.214.live_ref, bf16[4,64,1024]{2,1,0:T(8,128)(2,1)} %bitcast.119, ...), custom_call_target="tpu_custom_call" | custom-call | flops 4294967296 | bytes 20971520 | tf_op jit(solution)/shard_map/cache_part/pallas_call | solution.py:421
  318.3 22.1 %cache_part.3 = (bf16[4,512,1024]{2,1,0:T(8,128)(2,1)}, bf16[4,1024,512]{2,1,0:T(8,128)(2,1)}, f32[4,8,512]{2,1,0:T(8,128)}, f32[4,8,512]{2,1,0:T(8,128)}) custom-call(s32[1]{0:T(128)} %bitcast.1.first_ref, s32[8]{0:T(128)} %fusion.22.places_ref.place_ref, s32[4]{0:T(128)} %get-tuple-element.215.live_ref, bf16[4,64,1024]{2,1,0:T(8,128)(2,1)} %bitcast.116, ...), custom_call_target="tpu_custom_call" | custom-call | flops 4294967296 | bytes 20971520 | tf_op jit(solution)/shard_map/cache_part/pallas_call | solution.py:421
  344.0 22.6 %collective-permute-done.48 = f32[8,8,512]{2,1,0:T(8,128)S(1)} collective-permute-done((f32[8,8,512]{2,1,0:T(8,128)S(1)}, f32[8,8,512]{2,1,0:T(8,128)S(1)}, u32[]{:S(2)}, u32[]{:S(2)}) %collective-permute-start.48) | collective-permute-done | bytes 131104 | tf_op jit(solution)/shard_map/ppermute | solution.py:84
  371.2 5.5 copy.45
  389.0 13.4 %collective-permute-done.50 = f32[8,8,512]{2,1,0:T(8,128)S(1)} collective-permute-done((f32[8,8,512]{2,1,0:T(8,128)S(1)}, f32[8,8,512]{2,1,0:T(8,128)S(1)}, u32[]{:S(2)}, u32[]{:S(2)}) %collective-permute-start.50) | collective-permute-done | bytes 131104 | tf_op jit(solution)/shard_map/ppermute | solution.py:84
  403.1 9.7 %project.6.refs_6_ = f32[512,1024]{1,0:T(8,128)} custom-call(s32[8]{0:T(128)} %fusion.22.places_ref.place_ref, bf16[512,4096]{1,0:T(8,128)(2,1)} %bitcast.85, bf16[512,4096]{1,0:T(8,128)(2,1)} %bitcast.86, bf16[512,4096]{1,0:T(8,128)(2,1)} %bitcast.87, bf16[512,4096]{1,0:T(8,128)(2,1)} %bitcast.88, bf16[512,4096]{1,0:T(8,128)(2,1)} %bitcast.89, ...), custom_call_target="tpu_custom_call" | custom-call | flops 3758096384 | bytes 12582912 | tf_op jit(solution)/shard_map/project/pallas_call | solution.py:142
  419.9 11.3 %finish_part.2 = (f32[4,8,512]{2,1,0:T(8,128)}, bf16[4,64,1024]{2,1,0:T(8,128)(2,1)}, bf16[4,64,1024]{2,1,0:T(8,128)(2,1)}, bf16[4,64,1024]{2,1,0:T(8,128)(2,1)}...) custom-call(s32[1]{0:T(128)} %bitcast.1.first_ref, ...), custom_call_target="tpu_custom_call" | custom-call | flops 536870912 | bytes 12582912 | tf_op jit(solution)/shard_map/finish_part/pallas_call | solution.py:483
  431.4 11.4 %finish_part.3 = (f32[4,8,512]{2,1,0:T(8,128)}, bf16[4,64,1024]{2,1,0:T(8,128)(2,1)}, bf16[4,64,1024]{2,1,0:T(8,128)(2,1)}, bf16[4,64,1024]{2,1,0:T(8,128)(2,1)}...) custom-call(s32[1]{0:T(128)} %bitcast.1.first_ref, ...), custom_call_target="tpu_custom_call" | custom-call | flops 536870912 | bytes 12582912 | tf_op jit(solution)/shard_map/finish_part/pallas_call | solution.py:483
  459.4 5.7 %collective-permute-done.74 = f32[4,8,512]{2,1,0:T(8,128)S(1)} collective-permute-done((f32[4,8,512]{2,1,0:T(8,128)S(1)}, f32[4,8,512]{2,1,0:T(8,128)S(1)}, u32[]{:S(2)}, u32[]{:S(2)}) %collective-permute-start.74) | collective-permute-done | bytes 65568 | tf_op jit(solution)/shard_map/ppermute | solution.py:84
  474.2 7.1 %collective-permute-done.52 = bf16[4,64,1024]{2,1,0:T(8,128)(2,1)S(1)} collective-permute-done((bf16[4,64,1024]{2,1,0:T(8,128)(2,1)S(1)}, bf16[4,64,1024]{2,1,0:T(8,128)(2,1)S(1)}, u32[]{:S(2)}, u32[]{:S(2)}) %collective-permute-start.52) | collective-permute-done | bytes 524320 | tf_op jit(solution)/shard_map/ppermute | solution.py:36
  484.8 7.7 %collective-permute-done.65 = bf16[4,64,1024]{2,1,0:T(8,128)(2,1)S(1)} collective-permute-done((bf16[4,64,1024]{2,1,0:T(8,128)(2,1)S(1)}, bf16[4,64,1024]{2,1,0:T(8,128)(2,1)S(1)}, u32[]{:S(2)}, u32[]{:S(2)}) %collective-permute-start.65) | collective-permute-done | bytes 524320 | tf_op jit(solution)/shard_map/ppermute | solution.py:36
  496.1 7.7 %collective-permute-done.53 = bf16[4,64,1024]{2,1,0:T(8,128)(2,1)S(1)} collective-permute-done((bf16[4,64,1024]{2,1,0:T(8,128)(2,1)S(1)}, bf16[4,64,1024]{2,1,0:T(8,128)(2,1)S(1)}, u32[]{:S(2)}, u32[]{:S(2)}) %collective-permute-start.53) | collective-permute-done | bytes 524320 | tf_op jit(solution)/shard_map/ppermute | solution.py:36
  507.3 7.7 %collective-permute-done.66 = bf16[4,64,1024]{2,1,0:T(8,128)(2,1)S(1)} collective-permute-done((bf16[4,64,1024]{2,1,0:T(8,128)(2,1)S(1)}, bf16[4,64,1024]{2,1,0:T(8,128)(2,1)S(1)}, u32[]{:S(2)}, u32[]{:S(2)}) %collective-permute-start.66) | collective-permute-done | bytes 524320 | tf_op jit(solution)/shard_map/ppermute | solution.py:36
  518.8 5.9 %collective-permute-done.54 = bf16[4,64,1024]{2,1,0:T(8,128)(2,1)S(1)} collective-permute-done((bf16[4,64,1024]{2,1,0:T(8,128)(2,1)S(1)}, bf16[4,64,1024]{2,1,0:T(8,128)(2,1)S(1)}, u32[]{:S(2)}, u32[]{:S(2)}) %collective-permute-start.54) | collective-permute-done | bytes 524320 | tf_op jit(solution)/shard_map/ppermute | solution.py:36
  (365 shorter events, 220.6 us)
Async XLA Ops:
  0.6 32.2 %collective-permute-start = (bf16[512,1024]{1,0:T(8,128)(2,1)}, bf16[512,1024]{1,0:T(8,128)(2,1)}, u32[]{:S(2)}, u32[]{:S(2)}) collective-permute-start(bf16[512,1024]{1,0:T(8,128)(2,1)} %refs_9_.4), channel_id=1, source_target_pairs={{0,8},{8,16},{16,24},{24,28},{28,20},{20,12},{12,4},{4,0},{1,9},{9... | collective-permute-start | bytes 3145736 | tf_op jit(solution)/shard_map/ppermute | solution.py:36
  3.7 29.1 %collective-permute-start.1 = (bf16[512,1024]{1,0:T(8,128)(2,1)}, bf16[512,1024]{1,0:T(8,128)(2,1)}, u32[]{:S(2)}, u32[]{:S(2)}) collective-permute-start(bf16[512,1024]{1,0:T(8,128)(2,1)} %refs_9_.4), channel_id=1, source_target_pairs={{0,4},{8,0},{16,8},{24,16},{28,24},{20,28},{12,20},{4,12},{1,5},{9... | collective-permute-start | bytes 3145736 | tf_op jit(solution)/shard_map/ppermute | solution.py:36
  14.1 36.3 %collective-permute-start.4 = (bf16[512,1024]{1,0:T(8,128)(2,1)S(1)}, bf16[512,1024]{1,0:T(8,128)(2,1)}, u32[]{:S(2)}, u32[]{:S(2)}) collective-permute-start(bf16[512,1024]{1,0:T(8,128)(2,1)S(1)} %copy-done.21), channel_id=1, source_target_pairs={{0,8},{8,16},{16,24},{24,28},{28,20},{20,12},{12,4},{4,0},{1,9},{9... | collective-permute-start | bytes 3145736 | tf_op jit(solution)/shard_map/ppermute | solution.py:36
  16.1 36.5 %collective-permute-start.5 = (bf16[512,1024]{1,0:T(8,128)(2,1)S(1)}, bf16[512,1024]{1,0:T(8,128)(2,1)}, u32[]{:S(2)}, u32[]{:S(2)}) collective-permute-start(bf16[512,1024]{1,0:T(8,128)(2,1)S(1)} %copy-done.21), channel_id=1, source_target_pairs={{0,4},{8,0},{16,8},{24,16},{28,24},{20,28},{12,20},{4,12},{1,5},{9... | collective-permute-start | bytes 3145736 | tf_op jit(solution)/shard_map/ppermute | solution.py:36
  32.8 40.1 %collective-permute-start.2 = (bf16[512,1024]{1,0:T(8,128)(2,1)}, bf16[512,1024]{1,0:T(8,128)(2,1)}, u32[]{:S(2)}, u32[]{:S(2)}) collective-permute-start(bf16[512,1024]{1,0:T(8,128)(2,1)} %collective-permute-done.refs_10_), channel_id=1, source_target_pairs={{0,8},{8,16},{16,24},{24,28},{28,20},{20,12},{12,4},{4,0},{1,9},{9... | collective-permute-start | bytes 3145736 | tf_op jit(solution)/shard_map/ppermute | solution.py:36
  34.8 40.2 %collective-permute-start.3 = (bf16[512,1024]{1,0:T(8,128)(2,1)}, bf16[512,1024]{1,0:T(8,128)(2,1)}, u32[]{:S(2)}, u32[]{:S(2)}) collective-permute-start(bf16[512,1024]{1,0:T(8,128)(2,1)} %collective-permute-done.1.refs_11_), channel_id=1, source_target_pairs={{0,4},{8,0},{16,8},{24,16},{28,24},{20,28},{12,20},{4,12},{1,5},{9... | collective-permute-start | bytes 3145736 | tf_op jit(solution)/shard_map/ppermute | solution.py:36
  52.6 45.7 %collective-permute-start.8 = (bf16[512,1024]{1,0:T(8,128)(2,1)}, bf16[512,1024]{1,0:T(8,128)(2,1)S(1)}, u32[]{:S(2)}, u32[]{:S(2)}) collective-permute-start(bf16[512,1024]{1,0:T(8,128)(2,1)} %collective-permute-done.4.refs_10_), channel_id=1, source_target_pairs={{0,8},{8,16},{16,24},{24,28},{28,20},{20,12},{12,4},{4,0},{1,9},{9... | collective-permute-start | bytes 3145736 | tf_op jit(solution)/shard_map/ppermute | solution.py:36
  54.2 44.1 %collective-permute-start.9 = (bf16[512,1024]{1,0:T(8,128)(2,1)}, bf16[512,1024]{1,0:T(8,128)(2,1)}, u32[]{:S(2)}, u32[]{:S(2)}) collective-permute-start(bf16[512,1024]{1,0:T(8,128)(2,1)} %collective-permute-done.5.refs_11_), channel_id=1, source_target_pairs={{0,4},{8,0},{16,8},{24,16},{28,24},{20,28},{12,20},{4,12},{1,5},{9... | collective-permute-start | bytes 3145736 | tf_op jit(solution)/shard_map/ppermute | solution.py:36
  68.3 27.6 %collective-permute-start.12 = (f32[8,1,1024]{2,1,0:T(1,128)S(1)}, f32[8,1,1024]{2,1,0:T(1,128)S(1)}, u32[]{:S(2)}, u32[]{:S(2)}) collective-permute-start(f32[8,1,1024]{2,1,0:T(1,128)S(1)} %copy-done.55), channel_id=1, source_target_pairs={{0,4},{4,0},{8,12},{12,8},{16,20},{20,16},{24,28},{28,24},{1,5},{5... | collective-permute-start | bytes 98312 | tf_op jit(solution)/shard_map/ppermute | solution.py:551
  75.1 32.1 %collective-permute-start.13 = (bf16[8,64,512]{2,1,0:T(8,128)(2,1)S(1)}, bf16[8,64,512]{2,1,0:T(8,128)(2,1)S(1)}, u32[]{:S(2)}, u32[]{:S(2)}) collective-permute-start(bf16[8,64,512]{2,1,0:T(8,128)(2,1)S(1)} %select_convert_fusion.1), channel_id=1, source_target_pairs={{0,4},{4,0},{8,12},{12,8},{16,20},{20,16},{24,28},{28,24},{1,5},{5... | collective-permute-start | bytes 1572872 | tf_op jit(solution)/shard_map/ppermute | solution.py:562
  96.0 32.9 %collective-permute-start.6 = (bf16[512,1024]{1,0:T(8,128)(2,1)}, bf16[512,1024]{1,0:T(8,128)(2,1)}, u32[]{:S(2)}, u32[]{:S(2)}) collective-permute-start(bf16[512,1024]{1,0:T(8,128)(2,1)} %collective-permute-done.2.refs_12_), channel_id=1, source_target_pairs={{0,8},{8,16},{16,24},{24,28},{28,20},{20,12},{12,4},{4,0},{1,9},{9... | collective-permute-start | bytes 3145736 | tf_op jit(solution)/shard_map/ppermute | solution.py:36
  96.1 33.9 %collective-permute-start.7 = (bf16[512,1024]{1,0:T(8,128)(2,1)}, bf16[512,1024]{1,0:T(8,128)(2,1)}, u32[]{:S(2)}, u32[]{:S(2)}) collective-permute-start(bf16[512,1024]{1,0:T(8,128)(2,1)} %collective-permute-done.3.refs_13_), channel_id=1, source_target_pairs={{0,4},{8,0},{16,8},{24,16},{28,24},{20,28},{12,20},{4,12},{1,5},{9... | collective-permute-start | bytes 3145736 | tf_op jit(solution)/shard_map/ppermute | solution.py:36
  108.9 26.3 %collective-permute-start.16 = (bf16[8,64,512]{2,1,0:T(8,128)(2,1)}, bf16[8,64,512]{2,1,0:T(8,128)(2,1)S(1)}, u32[]{:S(2)}, u32[]{:S(2)}) collective-permute-start(bf16[8,64,512]{2,1,0:T(8,128)(2,1)} %get-tuple-element.189), channel_id=1, source_target_pairs={{0,8},{4,12},{1,9},{5,13},{2,10},{6,14},{3,11},{7,15}} | collective-permute-start | bytes 1572872 | tf_op jit(solution)/shard_map/ppermute | solution.py:577
  133.2 33.6 %collective-permute-start.14 = (bf16[512,1024]{1,0:T(8,128)(2,1)}, bf16[512,1024]{1,0:T(8,128)(2,1)S(1)}, u32[]{:S(2)}, u32[]{:S(2)}) collective-permute-start(bf16[512,1024]{1,0:T(8,128)(2,1)} %copy-done.22), channel_id=1, source_target_pairs={{0,8},{8,16},{16,24},{24,28},{28,20},{20,12},{12,4},{4,0},{1,9},{9... | collective-permute-start | bytes 3145736 | tf_op jit(solution)/shard_map/ppermute | solution.py:36
  133.3 33.6 %collective-permute-start.15 = (bf16[512,1024]{1,0:T(8,128)(2,1)}, bf16[512,1024]{1,0:T(8,128)(2,1)S(1)}, u32[]{:S(2)}, u32[]{:S(2)}) collective-permute-start(bf16[512,1024]{1,0:T(8,128)(2,1)} %collective-permute-done.9.refs_13_), channel_id=1, source_target_pairs={{0,4},{8,0},{16,8},{24,16},{28,24},{20,28},{12,20},{4,12},{1,5},{9... | collective-permute-start | bytes 3145736 | tf_op jit(solution)/shard_map/ppermute | solution.py:36
  170.4 28.7 %collective-permute-start.18 = (bf16[4,64,1024]{2,1,0:T(8,128)(2,1)S(1)}, bf16[4,64,1024]{2,1,0:T(8,128)(2,1)S(1)}, u32[]{:S(2)}, u32[]{:S(2)}) collective-permute-start(bf16[4,64,1024]{2,1,0:T(8,128)(2,1)S(1)} %bitcast.117), channel_id=1, source_target_pairs={{0,8},{8,16},{16,24},{24,28},{28,20},{20,12},{12,4},{4,0},{1,9},{9... | collective-permute-start | bytes 1572872 | tf_op jit(solution)/shard_map/ppermute | solution.py:36
  175.1 24.0 %collective-permute-start.19 = (bf16[4,64,1024]{2,1,0:T(8,128)(2,1)S(1)}, bf16[4,64,1024]{2,1,0:T(8,128)(2,1)S(1)}, u32[]{:S(2)}, u32[]{:S(2)}) collective-permute-start(bf16[4,64,1024]{2,1,0:T(8,128)(2,1)S(1)} %bitcast.118), channel_id=1, source_target_pairs={{0,4},{8,0},{16,8},{24,16},{28,24},{20,28},{12,20},{4,12},{1,5},{9... | collective-permute-start | bytes 1572872 | tf_op jit(solution)/shard_map/ppermute | solution.py:36
  204.6 24.1 %collective-permute-start.23 = (bf16[4,64,1024]{2,1,0:T(8,128)(2,1)S(1)}, bf16[4,64,1024]{2,1,0:T(8,128)(2,1)S(1)}, u32[]{:S(2)}, u32[]{:S(2)}) collective-permute-start(bf16[4,64,1024]{2,1,0:T(8,128)(2,1)S(1)} %collective-permute-done.18.refs_1_), channel_id=1, source_target_pairs={{0,8},{8,16},{16,24},{24,28},{28,20},{20,12},{12,4},{4,0},{1,9},{9... | collective-permute-start | bytes 1572872 | tf_op jit(solution)/shard_map/ppermute | solution.py:36
  207.7 32.2 %collective-permute-start.34 = (bf16[4,64,1024]{2,1,0:T(8,128)(2,1)S(1)}, bf16[4,64,1024]{2,1,0:T(8,128)(2,1)S(1)}, u32[]{:S(2)}, u32[]{:S(2)}) collective-permute-start(bf16[4,64,1024]{2,1,0:T(8,128)(2,1)S(1)} %bitcast.114), channel_id=1, source_target_pairs={{0,8},{8,16},{16,24},{24,28},{28,20},{20,12},{12,4},{4,0},{1,9},{9... | collective-permute-start | bytes 1572872 | tf_op jit(solution)/shard_map/ppermute | solution.py:36
  217.5 24.1 %collective-permute-start.35 = (bf16[4,64,1024]{2,1,0:T(8,128)(2,1)S(1)}, bf16[4,64,1024]{2,1,0:T(8,128)(2,1)S(1)}, u32[]{:S(2)}, u32[]{:S(2)}) collective-permute-start(bf16[4,64,1024]{2,1,0:T(8,128)(2,1)S(1)} %bitcast.115), channel_id=1, source_target_pairs={{0,4},{8,0},{16,8},{24,16},{28,24},{20,28},{12,20},{4,12},{1,5},{9... | collective-permute-start | bytes 1572872 | tf_op jit(solution)/shard_map/ppermute | solution.py:36
  230.4 28.1 %collective-permute-start.26 = (bf16[4,64,1024]{2,1,0:T(8,128)(2,1)S(1)}, bf16[4,64,1024]{2,1,0:T(8,128)(2,1)S(1)}, u32[]{:S(2)}, u32[]{:S(2)}) collective-permute-start(bf16[4,64,1024]{2,1,0:T(8,128)(2,1)S(1)} %collective-permute-done.23.refs_3_), channel_id=1, source_target_pairs={{0,8},{8,16},{16,24},{24,28},{28,20},{20,12},{12,4},{4,0},{1,9},{9... | collective-permute-start | bytes 1572872 | tf_op jit(solution)/shard_map/ppermute | solution.py:36
  231.8 26.7 %collective-permute-start.27 = (bf16[4,64,1024]{2,1,0:T(8,128)(2,1)S(1)}, bf16[4,64,1024]{2,1,0:T(8,128)(2,1)S(1)}, u32[]{:S(2)}, u32[]{:S(2)}) collective-permute-start(bf16[4,64,1024]{2,1,0:T(8,128)(2,1)S(1)} %collective-permute-done.24.refs_4_), channel_id=1, source_target_pairs={{0,4},{8,0},{16,8},{24,16},{28,24},{20,28},{12,20},{4,12},{1,5},{9... | collective-permute-start | bytes 1572872 | tf_op jit(solution)/shard_map/ppermute | solution.py:36
  261.2 26.1 %collective-permute-start.38 = (bf16[4,64,1024]{2,1,0:T(8,128)(2,1)S(1)}, bf16[4,64,1024]{2,1,0:T(8,128)(2,1)S(1)}, u32[]{:S(2)}, u32[]{:S(2)}) collective-permute-start(bf16[4,64,1024]{2,1,0:T(8,128)(2,1)S(1)} %collective-permute-done.36.refs_3_), channel_id=1, source_target_pairs={{0,8},{8,16},{16,24},{24,28},{28,20},{20,12},{12,4},{4,0},{1,9},{9... | collective-permute-start | bytes 1572872 | tf_op jit(solution)/shard_map/ppermute | solution.py:36
  277.5 37.3 %collective-permute-start.32 = (bf16[512,1024]{1,0:T(8,128)(2,1)S(1)}, bf16[512,1024]{1,0:T(8,128)(2,1)S(1)}, u32[]{:S(2)}, u32[]{:S(2)}) collective-permute-start(bf16[512,1024]{1,0:T(8,128)(2,1)S(1)} %copy-done.23), channel_id=1, source_target_pairs={{0,8},{8,16},{16,24},{24,28},{28,20},{20,12},{12,4},{4,0},{1,9},{9... | collective-permute-start | bytes 3145736 | tf_op jit(solution)/shard_map/ppermute | solution.py:36
  279.6 35.3 %collective-permute-start.33 = (bf16[512,1024]{1,0:T(8,128)(2,1)S(1)}, bf16[512,1024]{1,0:T(8,128)(2,1)S(1)}, u32[]{:S(2)}, u32[]{:S(2)}) collective-permute-start(bf16[512,1024]{1,0:T(8,128)(2,1)S(1)} %copy-done.23), channel_id=1, source_target_pairs={{0,4},{8,0},{16,8},{24,16},{28,24},{20,28},{12,20},{4,12},{1,5},{9... | collective-permute-start | bytes 3145736 | tf_op jit(solution)/shard_map/ppermute | solution.py:36
  288.8 24.3 %collective-permute-start.40 = (bf16[2,64,1024]{2,1,0:T(8,128)(2,1)S(1)}, bf16[2,64,1024]{2,1,0:T(8,128)(2,1)S(1)}, u32[]{:S(2)}, u32[]{:S(2)}) collective-permute-start(bf16[2,64,1024]{2,1,0:T(8,128)(2,1)S(1)} %slice.195), channel_id=1, source_target_pairs={{0,8},{8,16},{16,24},{24,28},{28,20},{20,12},{12,4},{4,0},{1,9},{9... | collective-permute-start | bytes 786440 | tf_op jit(solution)/shard_map/ppermute | solution.py:36
  290.9 23.9 %collective-permute-start.41 = (bf16[2,64,1024]{2,1,0:T(8,128)(2,1)S(1)}, bf16[2,64,1024]{2,1,0:T(8,128)(2,1)S(1)}, u32[]{:S(2)}, u32[]{:S(2)}) collective-permute-start(bf16[2,64,1024]{2,1,0:T(8,128)(2,1)S(1)} %slice.196), channel_id=1, source_target_pairs={{0,4},{8,0},{16,8},{24,16},{28,24},{20,28},{12,20},{4,12},{1,5},{9... | collective-permute-start | bytes 786440 | tf_op jit(solution)/shard_map/ppermute | solution.py:36
  314.9 25.5 %collective-permute-start.42 = (bf16[512,1024]{1,0:T(8,128)(2,1)S(1)}, bf16[512,1024]{1,0:T(8,128)(2,1)S(1)}, u32[]{:S(2)}, u32[]{:S(2)}) collective-permute-start(bf16[512,1024]{1,0:T(8,128)(2,1)S(1)} %collective-permute-done.32.refs_8_), channel_id=1, source_target_pairs={{0,8},{8,16},{16,24},{24,28},{28,20},{20,12},{12,4},{4,0},{1,9},{9... | collective-permute-start | bytes 3145736 | tf_op jit(solution)/shard_map/ppermute | solution.py:36
  340.9 40.7 %collective-permute-start.44 = (bf16[512,1024]{1,0:T(8,128)(2,1)S(1)}, bf16[512,1024]{1,0:T(8,128)(2,1)S(1)}, u32[]{:S(2)}, u32[]{:S(2)}) collective-permute-start(bf16[512,1024]{1,0:T(8,128)(2,1)S(1)} %collective-permute-done.42.refs_10_), channel_id=1, source_target_pairs={{0,8},{8,16},{16,24},{24,28},{28,20},{20,12},{12,4},{4,0},{1,9},{9... | collective-permute-start | bytes 3145736 | tf_op jit(solution)/shard_map/ppermute | solution.py:36
  342.6 39.0 %collective-permute-start.45 = (bf16[512,1024]{1,0:T(8,128)(2,1)}, bf16[512,1024]{1,0:T(8,128)(2,1)S(1)}, u32[]{:S(2)}, u32[]{:S(2)}) collective-permute-start(bf16[512,1024]{1,0:T(8,128)(2,1)} %collective-permute-done.43.refs_11_), channel_id=1, source_target_pairs={{0,4},{8,0},{16,8},{24,16},{28,24},{20,28},{12,20},{4,12},{1,5},{9... | collective-permute-start | bytes 3145736 | tf_op jit(solution)/shard_map/ppermute | solution.py:36
  381.6 31.2 %collective-permute-start.46 = (bf16[256,1024]{1,0:T(8,128)(2,1)S(1)}, bf16[256,1024]{1,0:T(8,128)(2,1)S(1)}, u32[]{:S(2)}, u32[]{:S(2)}) collective-permute-start(bf16[256,1024]{1,0:T(8,128)(2,1)S(1)} %slice.197), channel_id=1, source_target_pairs={{0,8},{8,16},{16,24},{24,28},{28,20},{20,12},{12,4},{4,0},{1,9},{9... | collective-permute-start | bytes 1572872 | tf_op jit(solution)/shard_map/ppermute | solution.py:36
  383.9 28.9 %collective-permute-start.47 = (bf16[256,1024]{1,0:T(8,128)(2,1)S(1)}, bf16[256,1024]{1,0:T(8,128)(2,1)S(1)}, u32[]{:S(2)}, u32[]{:S(2)}) collective-permute-start(bf16[256,1024]{1,0:T(8,128)(2,1)S(1)} %slice.198), channel_id=1, source_target_pairs={{0,4},{8,0},{16,8},{24,16},{28,24},{20,28},{12,20},{4,12},{1,5},{9... | collective-permute-start | bytes 1572872 | tf_op jit(solution)/shard_map/ppermute | solution.py:36
  (106 other events, 1816.2 us)

commit v6 on v5

--- a/solution.py
+++ b/solution.py
@@ -78,32 +78,53 @@
         self.late = moved + tuple(deferred)
 
 
-def butterfly(value, axis, count, combine):
-    bit = 1
-    while bit < count:
-        value = combine(value, lax.ppermute(value, axis, [(i, i ^ bit) for i in range(count)]))
-        bit *= 2
-    return value
-
-
-def ring_sum(parts, order):
-    far = len(order) // 2
-    half = parts[0].shape[0] // 2
-    add = lambda a, b: (a.astype(jnp.float32) + b.astype(jnp.float32)).astype(jnp.bfloat16)
-    ahead = ring_step(parts[far][:half], order, 1)
-    back = ring_step(parts[far][half:], order, -1)
-    top, bottom = parts[far - 1], parts[1 - far]
-    ahead = jnp.concatenate([add(ahead, top[:half]), top[half:]], axis=0)
-    back = jnp.concatenate([bottom[:half], add(back, bottom[half:])], axis=0)
-    for step in range(far - 1, 0, -1):
-        ahead = ring_step(ahead, order, 1)
-        back = ring_step(back, order, -1)
-        if step > 1:
-            ahead = add(ahead, parts[step - 1])
-            back = add(back, parts[1 - step])
-    return (
-        ahead.astype(jnp.float32) + back.astype(jnp.float32) + parts[0].astype(jnp.float32)
-    )
+class Exchange:
+    def __init__(self, value, axis, count, combine):
+        self.value, self.axis, self.count, self.combine = value, axis, count, combine
+        self.bit = 1
+
+    def step(self):
+        if self.bit < self.count:
+            route = [(i, i ^ self.bit) for i in range(self.count)]
+            got = lax.ppermute(self.value, self.axis, route)
+            self.value = self.combine(self.value, got)
+            self.bit *= 2
+        return (self.value,)
+
+    def result(self):
+        while self.bit < self.count:
+            self.step()
+        return self.value
+
+
+class RingSum:
+    def __init__(self, parts, order):
+        self.parts, self.order = parts, order
+        self.left = len(order) // 2
+        self.half = parts[0].shape[0] // 2
+        self.ahead = self.back = None
+
+    def add(self, a, b):
+        return (a.astype(jnp.float32) + b.astype(jnp.float32)).astype(jnp.bfloat16)
+
+    def step(self, clock):
+        half, left, far = self.half, self.left, len(self.order) // 2
+        top, bottom = self.parts[left], self.parts[-left]
+        if left == far:
+            ahead, back = top[:half], bottom[half:]
+        elif left == far - 1:
+            ahead = jnp.concatenate([self.add(self.ahead, top[:half]), top[half:]], axis=0)
+            back = jnp.concatenate([bottom[:half], self.add(self.back, bottom[half:])], axis=0)
+        else:
+            ahead, back = self.add(self.ahead, top), self.add(self.back, bottom)
+        ahead, back = clock.hold(ahead, back)
+        self.ahead = ring_step(ahead, self.order, 1)
+        self.back = ring_step(back, self.order, -1)
+        self.left -= 1
+        return [self.ahead, self.back]
+
+    def total(self):
+        return sum(value.astype(jnp.float32) for value in (self.ahead, self.back, self.parts[0]))
 
 
 def project_kernel(count, turned, places_ref, *refs):
@@ -664,9 +685,13 @@
 
     by_request = lambda value: value.reshape(requests, tok_block, local_att)
 
-    def order_weight():
+    def prepare():
         made["w_in"] = w_in.reshape(D, 2 * local_inner)
-        return (made["w_in"],), ()
+        first_state = ssm_init.reshape(requests, local_mheads, MHEAD_DIM, STATE)
+        made["initial"] = jnp.transpose(first_state, (0, 3, 1, 2)).reshape(
+            requests, STATE, local_inner
+        )
+        return (made["w_in"], made["initial"]), ()
 
     def enter():
         made["act"], made["maps"], size = enter_mixer(
@@ -698,13 +723,6 @@
         )
         return (made["read"], made["local"]), ()
 
-    def initial_state():
-        first_state = clock.hold(ssm_init).reshape(requests, local_mheads, MHEAD_DIM, STATE)
-        made["initial"] = jnp.transpose(first_state, (0, 3, 1, 2)).reshape(
-            requests, STATE, local_inner
-        )
-        return (made["initial"],), ()
-
     def start_relay():
         made["relay"] = relay = Relay(
             made["through"], clock.hold(made["local"]), made["initial"], seq_index, seq_count
@@ -731,9 +749,9 @@
             made["through"],
         )
         made["gated"] = gated
-        made["squares"] = butterfly(
+        made["squares"] = Exchange(
             squares[:, :1].reshape(1, tokens), "head", head_count, jnp.add
-        )
+        ).result()
         made["chain"] = chain
         return (gated,), (made["squares"],)
 
@@ -792,10 +810,12 @@
 
     def join_peaks():
         peaks = jnp.concatenate([clock.hold(part[2]) for part in cached], axis=0)
-        made["best"] = butterfly(peaks, "seq", seq_count, jnp.maximum)
-        return leave_chain()[0], (made["best"],)
+        made["best"] = Exchange(peaks, "seq", seq_count, jnp.maximum)
+        made["best"].step()
+        return leave_chain()
 
     def make_values():
+        made["best"].step()
         made["values"] = product(
             [(0, 0, clock.hold(value_ring.block))] + value_ring.pieces[1:-2],
             False,
@@ -814,11 +834,11 @@
             )
 
     both = steps([query_ring, key_ring], 0, half - 2) + [query_ring] * 2 + [key_ring] * 2
-    works = [order_weight, enter, inside, initial_state, start_relay, hop, hop]
+    works = [prepare, enter, inside, start_relay, hop, hop, hop]
     run(both, works + [None] * (len(both) - 1 - len(works)) + [make_queries])
     run(
         steps(slot_rings, 0, half),
-        [hop, make_keys, end_relay, None, leave, None, leave_terms],
+        [end_relay, make_keys, leave, None, leave_terms],
     )
     run(
         steps([value_ring], 0, half),
@@ -826,7 +846,7 @@
     )
 
     new_keys = made["keys"]
-    best = made["best"]
+    best = made["best"].result()
     new_values = by_request(product(value_ring.pieces[-2:], False, base=(made["values"],)))
 
     own = lambda stat: lax.dynamic_slice_in_dim(stat, seq_index * tok_block, tok_block, 2)
@@ -834,18 +854,45 @@
     residual = lax.dynamic_slice_in_dim(
         flat_input, head_index * local_width, local_width, 1
     ).astype(jnp.float32)
-    mixed = []
+    sums, ring_sums, mixed = [], [], []
+
+    def finish(index):
+        def work():
+            joined, out, peaks, totals = cached[index]
+            some_sums, *parts = finish_part(
+                index * group,
+                first,
+                places,
+                clock.hold(joined),
+                new_keys,
+                new_values,
+                out,
+                peaks,
+                totals,
+                best,
+            )
+            sums.append(some_sums)
+            terms = {-offset: part for offset, part in zip(offsets, parts)}
+            terms[half] = terms[-half]
+            ring_sums.append(RingSum(terms, order))
+            return (some_sums, *parts), ()
+
+        return work
+
+    def add_sums():
+        if "sums" not in made:
+            made["sums"] = Exchange(jnp.concatenate(sums, axis=0), "seq", seq_count, jnp.add)
+        made["sums"].step()
+        return (), ()
+
+    run([], [finish(0)])
+    run([ring_sums[0]], [finish(1)])
+    run(steps(ring_sums[::-1], 0, half)[:-1], [add_sums, None, add_sums, None, add_sums])
+    denominators = jnp.transpose(own(made["sums"].result()), (0, 2, 1))
     for index in range(GROUPS):
         begin = index * group
-        joined, out, peaks, totals = cached[index]
-        sums, *parts = finish_part(
-            begin, first, places, joined, new_keys, new_values, out, peaks, totals, best
-        )
-        sums = butterfly(sums, "seq", seq_count, jnp.add)
-        denominator = jnp.transpose(own(sums), (0, 2, 1))
-        terms = {-offset: part for offset, part in zip(offsets, parts)}
-        terms[half] = terms[-half]
-        numerator = ring_sum(terms, order).reshape(group, tok_block, local_heads, HEAD_DIM)
+        denominator = denominators[begin : begin + group]
+        numerator = ring_sums[index].total().reshape(group, tok_block, local_heads, HEAD_DIM)
         attended = (
             (numerator / denominator[..., None])
             .astype(jnp.bfloat16)

time: 570 us -> 584 us (1.025)
  waiting for transfers between devices: 213 us -> 225 us
  starting transfers between devices: 107 us -> 96.4 us
  other arithmetic: 31.7 us -> 37.7 us
    ppermute x3, waiting for transfers between devices: 0.01 us -> 15 us  [advance(): self.entry = entry + lax.ppermute(leaving, 'seq', route).astype(jnp.float32)]
    ppermute x1, waiting for transfers between devices: 18.9 us -> 9.72 us  [__init__(): other_factor = side(lax.ppermute(through, 'seq', self.swap))]
    ppermute x56, starting transfers between devices: 85.3 us -> 78.4 us  [ring_step(): return lax.ppermute(block, 'seq', route)]
    ppermute x11 -> x8, waiting for transfers between devices: 48.1 us -> 53.6 us  [step(): got = lax.ppermute(self.value, self.axis, route)]
    unnamed x127 -> x124, local copies, waits for them, and re-layouts: 17.8 us -> 18.6 us
  transfers between devices with their start and end apart: 77 -> 74, of which waited for: 43 -> 36; matrix products, arithmetic and copies ran while one was open for 16% -> 18% of each run, Pallas kernels for 21% -> 20%
where the time goes in v6:
time: 584 us; the launch traced here: 573 us
  waiting for transfers between devices  225 us (39%)
  Pallas kernels  133 us (23%)
  starting transfers between devices  96.4 us (17%)
  local copies, waits for them, and re-layouts  67.1 us (11%)
  other arithmetic  37.7 us (6%)
  matrix products  10.7 us (2%)
    ppermute x56, waiting for transfers between devices, ring_step(): return lax.ppermute(block, 'seq', route)  131 us
    ppermute x56, starting transfers between devices, ring_step(): return lax.ppermute(block, 'seq', route)  78.4 us
    ppermute x8, waiting for transfers between devices, step(): got = lax.ppermute(self.value, self.axis, route)  53.6 us
    pallas_call x2, Pallas kernels, cache_part(): pl.pallas_call(functools.partial(cache_kernel, slots), grid_spec=pltpu.Pr...  44.1 us
    pallas_call x4, Pallas kernels, project(): pl.pallas_call(functools.partial(project_kernel, len(pieces), turned), gr...  36.2 us
    pallas_call x2, Pallas kernels, finish_part(): pl.pallas_call(functools.partial(finish_kernel, slots), grid_spec=pltpu.P...  22.5 us
    unnamed x124, local copies, waits for them, and re-layouts  18.6 us
    ppermute x3, waiting for transfers between devices, advance(): self.entry = entry + lax.ppermute(leaving, 'seq', route).astype(jnp.float32)  15 us
  transfers between devices with their start and end apart: 74, of which 36 were waited for; matrix products, arithmetic and copies ran while one was open for 18% of the time, Pallas kernels for 20%

profile of v6, /device:TPU:0, one launch (start us, length us, event | category | flops | bytes accessed | tf_op | source)
XLA Modules:
  0.0 572.7 jit_solution(3253747596232944212)
XLA Ops:
  8.3 5.6 copy.40
  18.8 10.4 %copy.52 = bf16[256,8,2,1024]{3,1,2,0:T(8,128)(2,1)} copy(bf16[256,8,2,1024]{3,2,1,0:T(2,128)(2,1)} %bitcast.103) | data formatting | bytes 16777216
  32.3 11.7 %enter_mixer.1 = (f32[512,2048]{1,0:T(8,128)}, f32[512,128]{1,0:T(8,128)}, f32[512,16]{1,0:T(8,128)}) custom-call(bf16[512,4096]{1,0:T(8,128)(2,1)} %bitcast.64, f32[1,2048]{1,0:T(1,128)} %bitcast.126, bf16[2048,128]{1,0:T(8,128)(2,1)} %bc_ref.1, bf16[2048,16]{1,0:T(8,128)(2,1)} %copy.41.dt_ref, f32[1,16]{1,0:T(1,128)} %bitcast.127, bf16[2048,2048]{1,0:T(8,128)(2,1)} %bitcast.104), custom_call_target="tpu_custom_call" | custom-call | flops 4294967296 | bytes 14680064 | tf_op jit(solution)/shard_map/enter_mixer/pallas_call | solution.py:225
  51.4 9.6 %inside_block.1 = (f32[512,1024]{1,0:T(8,128)}, f32[8,64,1024]{2,1,0:T(8,128)}, f32[8,1,1024]{2,1,0:T(1,128)}) custom-call(f32[512,2048]{1,0:T(8,128)} %get-tuple-element.124.inner_ref.gate_ref, f32[512,128]{1,0:T(8,128)} %get-tuple-element.125.map_ref, f32[8,64,16]{2,1,0:T(8,128)} %bitcast.107, f32[8,64,16]{2,1,0:T(8,128)} %bitcast.111, ...), custom_call_target="tpu_custom_call" | custom-call | flops 402653184 | bytes 8388608 | tf_op jit(solution)/shard_map/inside_block/pallas_call | solution.py:303
  68.7 9.7 %collective-permute-done.10 = f32[8,1,1024]{2,1,0:T(1,128)S(1)} collective-permute-done((f32[8,1,1024]{2,1,0:T(1,128)}, f32[8,1,1024]{2,1,0:T(1,128)S(1)}, u32[]{:S(2)}, u32[]{:S(2)}) %collective-permute-start.10) | collective-permute-done | bytes 32800 | tf_op jit(solution)/shard_map/ppermute | solution.py:572
  80.6 9.1 %collective-permute-done.11 = bf16[8,64,512]{2,1,0:T(8,128)(2,1)S(1)} collective-permute-done((bf16[8,64,512]{2,1,0:T(8,128)(2,1)S(1)}, bf16[8,64,512]{2,1,0:T(8,128)(2,1)S(1)}, u32[]{:S(2)}, u32[]{:S(2)}) %collective-permute-start.11) | collective-permute-done | bytes 524320 | tf_op jit(solution)/shard_map/ppermute | solution.py:583
  96.1 15.0 %collective-permute-done.14 = bf16[8,64,512]{2,1,0:T(8,128)(2,1)} collective-permute-done((bf16[8,64,512]{2,1,0:T(8,128)(2,1)}, bf16[8,64,512]{2,1,0:T(8,128)(2,1)}, u32[]{:S(2)}, u32[]{:S(2)}) %collective-permute-start.14) | collective-permute-done | bytes 524320 | tf_op jit(solution)/shard_map/ppermute | solution.py:598
  117.6 15.6 %collective-permute-done.4.refs_14_ = bf16[512,1024]{1,0:T(8,128)(2,1)S(1)} collective-permute-done((bf16[512,1024]{1,0:T(8,128)(2,1)}, bf16[512,1024]{1,0:T(8,128)(2,1)S(1)}, u32[]{:S(2)}, u32[]{:S(2)}) %collective-permute-start.4) | collective-permute-done | bytes 1048608 | tf_op jit(solution)/shard_map/ppermute | solution.py:36
  142.0 7.6 %collective-permute-done.12.refs_16_ = bf16[256,1024]{1,0:T(8,128)(2,1)S(1)} collective-permute-done((bf16[256,1024]{1,0:T(8,128)(2,1)S(1)}, bf16[256,1024]{1,0:T(8,128)(2,1)S(1)}, u32[]{:S(2)}, u32[]{:S(2)}) %collective-permute-start.12) | collective-permute-done | bytes 524320 | tf_op jit(solution)/shard_map/ppermute | solution.py:36
  151.4 10.6 %project.4 = bf16[512,1024]{1,0:T(8,128)(2,1)} custom-call(s32[8]{0:T(128)} %fusion.21.places_ref.place_ref, bf16[512,4096]{1,0:T(8,128)(2,1)} %bitcast.65, bf16[512,4096]{1,0:T(8,128)(2,1)} %bitcast.66, bf16[512,4096]{1,0:T(8,128)(2,1)} %bitcast.67, bf16[512,4096]{1,0:T(8,128)(2,1)} %bitcast.68, bf16[512,4096]{1,0:T(8,128)(2,1)} %bitcast.69, ...), custom_call_target="tpu_custom_call" | custom-call | flops 4294967296 | bytes 12582912 | tf_op jit(solution)/shard_map/project/pallas_call | solution.py:163
  162.2 7.4 %collective-permute-done.15.refs_14_ = bf16[512,1024]{1,0:T(8,128)(2,1)S(1)} collective-permute-done((bf16[512,1024]{1,0:T(8,128)(2,1)}, bf16[512,1024]{1,0:T(8,128)(2,1)S(1)}, u32[]{:S(2)}, u32[]{:S(2)}) %collective-permute-start.15) | collective-permute-done | bytes 1048608 | tf_op jit(solution)/shard_map/ppermute | solution.py:36
  175.2 11.4 %collective-permute-start.19 = (bf16[4,64,1024]{2,1,0:T(8,128)(2,1)S(1)}, bf16[4,64,1024]{2,1,0:T(8,128)(2,1)S(1)}, u32[]{:S(2)}, u32[]{:S(2)}) collective-permute-start(bf16[4,64,1024]{2,1,0:T(8,128)(2,1)S(1)} %bitcast.115), channel_id=1, source_target_pairs={{0,8},{8,16},{16,24},{24,28},{28,20},{20,12},{12,4},{4,0},{1,9},{9... | collective-permute-start | bytes 1572872 | tf_op jit(solution)/shard_map/ppermute | solution.py:36
  188.4 8.3 %collective-permute-done.22.refs_16_ = bf16[256,1024]{1,0:T(8,128)(2,1)S(1)} collective-permute-done((bf16[256,1024]{1,0:T(8,128)(2,1)S(1)}, bf16[256,1024]{1,0:T(8,128)(2,1)S(1)}, u32[]{:S(2)}, u32[]{:S(2)}) %collective-permute-start.22) | collective-permute-done | bytes 524320 | tf_op jit(solution)/shard_map/ppermute | solution.py:36
  200.0 10.4 %project.5 = bf16[512,1024]{1,0:T(8,128)(2,1)} custom-call(s32[8]{0:T(128)} %fusion.21.places_ref.place_ref, bf16[512,4096]{1,0:T(8,128)(2,1)} %bitcast.78, bf16[512,4096]{1,0:T(8,128)(2,1)} %bitcast.75, bf16[512,4096]{1,0:T(8,128)(2,1)} %bitcast.76, bf16[512,4096]{1,0:T(8,128)(2,1)} %bitcast.77, bf16[512,4096]{1,0:T(8,128)(2,1)} %bitcast.74, ...), custom_call_target="tpu_custom_call" | custom-call | flops 4294967296 | bytes 12582912 | tf_op jit(solution)/shard_map/project/pallas_call | solution.py:163
  213.1 8.9 %leave_mixer.1 = (bf16[512,1024]{1,0:T(8,128)(2,1)}, f32[512,128]{1,0:T(8,128)}, f32[8,64,1024]{2,1,0:T(8,128)}) custom-call(f32[8,64,1024]{2,1,0:T(8,128)} %pad_maximum_fusion.entry_ref, f32[512,128]{1,0:T(8,128)} %get-tuple-element.125.map_ref, f32[8,64,16]{2,1,0:T(8,128)} %bitcast.108, f32[512,1024]{1,0:T(8,128)} %get-tuple-element.126.read_ref, ...), custom_call_target="tpu_custom_call" | custom-call | flops 67108864 | bytes 12582912 | tf_op jit(solution)/shard_map/leave_mixer/pallas_call | solution.py:356
  231.4 7.8 %collective-permute-start.34 = (bf16[4,64,1024]{2,1,0:T(8,128)(2,1)S(1)}, bf16[4,64,1024]{2,1,0:T(8,128)(2,1)S(1)}, u32[]{:S(2)}, u32[]{:S(2)}) collective-permute-start(bf16[4,64,1024]{2,1,0:T(8,128)(2,1)S(1)} %bitcast.112), channel_id=1, source_target_pairs={{0,8},{8,16},{16,24},{24,28},{28,20},{20,12},{12,4},{4,0},{1,9},{9... | collective-permute-start | bytes 1572872 | tf_op jit(solution)/shard_map/ppermute | solution.py:36
  243.3 8.7 %collective-permute-done.29.refs_6_ = bf16[4,64,1024]{2,1,0:T(8,128)(2,1)S(1)} collective-permute-done((bf16[4,64,1024]{2,1,0:T(8,128)(2,1)S(1)}, bf16[4,64,1024]{2,1,0:T(8,128)(2,1)S(1)}, u32[]{:S(2)}, u32[]{:S(2)}) %collective-permute-start.29) | collective-permute-done | bytes 524320 | tf_op jit(solution)/shard_map/ppermute | solution.py:36
  254.1 9.1 %collective-permute-done.35.refs_2_ = bf16[4,64,1024]{2,1,0:T(8,128)(2,1)S(1)} collective-permute-done((bf16[4,64,1024]{2,1,0:T(8,128)(2,1)S(1)}, bf16[4,64,1024]{2,1,0:T(8,128)(2,1)S(1)}, u32[]{:S(2)}, u32[]{:S(2)}) %collective-permute-start.35) | collective-permute-done | bytes 524320 | tf_op jit(solution)/shard_map/ppermute | solution.py:36
  270.9 6.9 %convolution_multiply_fusion = f32[512,2048]{1,0:T(8,128)} fusion(bf16[512,1024]{1,0:T(8,128)(2,1)} %get-tuple-element.161, bf16[1024,2048]{1,0:T(8,128)(2,1)} %param.35, f32[512]{0:T(512)S(1)} %bitcast.125), kind=kOutput, calls=%fused_computation | convolution fusion | flops 2148532224 | bytes 9439232 | tf_op jit(solution)/shard_map/dot_general | solution.py:759
  283.6 23.2 %collective-permute-done.38.refs_5_ = bf16[4,64,1024]{2,1,0:T(8,128)(2,1)S(1)} collective-permute-done((bf16[4,64,1024]{2,1,0:T(8,128)(2,1)S(1)}, bf16[4,64,1024]{2,1,0:T(8,128)(2,1)S(1)}, u32[]{:S(2)}, u32[]{:S(2)}) %collective-permute-start.38) | collective-permute-done | bytes 524320 | tf_op jit(solution)/shard_map/ppermute | solution.py:36
  314.0 22.0 %cache_part.2 = (bf16[4,512,1024]{2,1,0:T(8,128)(2,1)}, bf16[4,1024,512]{2,1,0:T(8,128)(2,1)}, f32[4,8,512]{2,1,0:T(8,128)}, f32[4,8,512]{2,1,0:T(8,128)}) custom-call(s32[1]{0:T(128)} %bitcast.1.first_ref, s32[8]{0:T(128)} %fusion.21.places_ref.place_ref, s32[4]{0:T(128)} %get-tuple-element.251.live_ref, bf16[4,64,1024]{2,1,0:T(8,128)(2,1)} %bitcast.117, ...), custom_call_target="tpu_custom_call" | custom-call | flops 4294967296 | bytes 20971520 | tf_op jit(solution)/shard_map/cache_part/pallas_call | solution.py:442
  339.1 22.1 %cache_part.3 = (bf16[4,512,1024]{2,1,0:T(8,128)(2,1)}, bf16[4,1024,512]{2,1,0:T(8,128)(2,1)}, f32[4,8,512]{2,1,0:T(8,128)}, f32[4,8,512]{2,1,0:T(8,128)}) custom-call(s32[1]{0:T(128)} %bitcast.1.first_ref, s32[8]{0:T(128)} %fusion.21.places_ref.place_ref, s32[4]{0:T(128)} %get-tuple-element.250.live_ref, bf16[4,64,1024]{2,1,0:T(8,128)(2,1)} %bitcast.114, ...), custom_call_target="tpu_custom_call" | custom-call | flops 4294967296 | bytes 20971520 | tf_op jit(solution)/shard_map/cache_part/pallas_call | solution.py:442
  364.4 22.0 %collective-permute-done.48 = f32[8,8,512]{2,1,0:T(8,128)S(1)} collective-permute-done((f32[8,8,512]{2,1,0:T(8,128)S(1)}, f32[8,8,512]{2,1,0:T(8,128)S(1)}, u32[]{:S(2)}, u32[]{:S(2)}) %collective-permute-start.48) | collective-permute-done | bytes 131104 | tf_op jit(solution)/shard_map/ppermute | solution.py:89
  410.5 12.8 %collective-permute-done.50 = f32[8,8,512]{2,1,0:T(8,128)S(1)} collective-permute-done((f32[8,8,512]{2,1,0:T(8,128)S(1)}, f32[8,8,512]{2,1,0:T(8,128)S(1)}, u32[]{:S(2)}, u32[]{:S(2)}) %collective-permute-start.50) | collective-permute-done | bytes 131104 | tf_op jit(solution)/shard_map/ppermute | solution.py:89
  423.9 9.7 %project.6.refs_6_ = f32[512,1024]{1,0:T(8,128)} custom-call(s32[8]{0:T(128)} %fusion.21.places_ref.place_ref, bf16[512,4096]{1,0:T(8,128)(2,1)} %bitcast.83, bf16[512,4096]{1,0:T(8,128)(2,1)} %bitcast.84, bf16[512,4096]{1,0:T(8,128)(2,1)} %bitcast.85, bf16[512,4096]{1,0:T(8,128)(2,1)} %bitcast.86, bf16[512,4096]{1,0:T(8,128)(2,1)} %bitcast.87, ...), custom_call_target="tpu_custom_call" | custom-call | flops 3758096384 | bytes 12582912 | tf_op jit(solution)/shard_map/project/pallas_call | solution.py:163
  440.7 11.2 %finish_part.2 = (f32[4,8,512]{2,1,0:T(8,128)}, bf16[4,64,1024]{2,1,0:T(8,128)(2,1)}, bf16[4,64,1024]{2,1,0:T(8,128)(2,1)}, bf16[4,64,1024]{2,1,0:T(8,128)(2,1)}...) custom-call(s32[1]{0:T(128)} %bitcast.1.first_ref, ...), custom_call_target="tpu_custom_call" | custom-call | flops 536870912 | bytes 12582912 | tf_op jit(solution)/shard_map/finish_part/pallas_call | solution.py:504
  455.9 11.3 %finish_part.3 = (f32[4,8,512]{2,1,0:T(8,128)}, bf16[4,64,1024]{2,1,0:T(8,128)(2,1)}, bf16[4,64,1024]{2,1,0:T(8,128)(2,1)}, bf16[4,64,1024]{2,1,0:T(8,128)(2,1)}...) custom-call(s32[1]{0:T(128)} %bitcast.1.first_ref, ...), custom_call_target="tpu_custom_call" | custom-call | flops 536870912 | bytes 12582912 | tf_op jit(solution)/shard_map/finish_part/pallas_call | solution.py:504
  478.4 6.4 %collective-permute-done.60 = f32[8,8,512]{2,1,0:T(8,128)S(1)} collective-permute-done((f32[8,8,512]{2,1,0:T(8,128)S(1)}, f32[8,8,512]{2,1,0:T(8,128)S(1)}, u32[]{:S(2)}, u32[]{:S(2)}) %collective-permute-start.60) | collective-permute-done | bytes 131104 | tf_op jit(solution)/shard_map/ppermute | solution.py:89
  489.1 8.1 %collective-permute-done.61 = f32[8,8,512]{2,1,0:T(8,128)S(1)} collective-permute-done((f32[8,8,512]{2,1,0:T(8,128)S(1)}, f32[8,8,512]{2,1,0:T(8,128)S(1)}, u32[]{:S(2)}, u32[]{:S(2)}) %collective-permute-start.61) | collective-permute-done | bytes 131104 | tf_op jit(solution)/shard_map/ppermute | solution.py:89
  502.3 6.6 %collective-permute-done.67 = bf16[4,64,1024]{2,1,0:T(8,128)(2,1)} collective-permute-done((bf16[4,64,1024]{2,1,0:T(8,128)(2,1)}, bf16[4,64,1024]{2,1,0:T(8,128)(2,1)}, u32[]{:S(2)}, u32[]{:S(2)}) %collective-permute-start.67) | collective-permute-done | bytes 524320 | tf_op jit(solution)/shard_map/ppermute | solution.py:36
  513.5 6.5 %collective-permute-done.56 = bf16[4,64,1024]{2,1,0:T(8,128)(2,1)S(1)} collective-permute-done((bf16[4,64,1024]{2,1,0:T(8,128)(2,1)S(1)}, bf16[4,64,1024]{2,1,0:T(8,128)(2,1)S(1)}, u32[]{:S(2)}, u32[]{:S(2)}) %collective-permute-start.56) | collective-permute-done | bytes 524320 | tf_op jit(solution)/shard_map/ppermute | solution.py:36
  522.5 8.7 %collective-permute-done.69 = bf16[4,64,1024]{2,1,0:T(8,128)(2,1)S(1)} collective-permute-done((bf16[4,64,1024]{2,1,0:T(8,128)(2,1)S(1)}, bf16[4,64,1024]{2,1,0:T(8,128)(2,1)S(1)}, u32[]{:S(2)}, u32[]{:S(2)}) %collective-permute-start.69) | collective-permute-done | bytes 524320 | tf_op jit(solution)/shard_map/ppermute | solution.py:36
  (355 shorter events, 215.9 us)
Async XLA Ops:
  0.6 47.1 %collective-permute-start = (bf16[512,1024]{1,0:T(8,128)(2,1)}, bf16[512,1024]{1,0:T(8,128)(2,1)}, u32[]{:S(2)}, u32[]{:S(2)}) collective-permute-start(bf16[512,1024]{1,0:T(8,128)(2,1)} %refs_9_.4), channel_id=1, source_target_pairs={{0,8},{8,16},{16,24},{24,28},{28,20},{20,12},{12,4},{4,0},{1,9},{9... | collective-permute-start | bytes 3145736 | tf_op jit(solution)/shard_map/ppermute | solution.py:36
  3.7 44.1 %collective-permute-start.1 = (bf16[512,1024]{1,0:T(8,128)(2,1)}, bf16[512,1024]{1,0:T(8,128)(2,1)}, u32[]{:S(2)}, u32[]{:S(2)}) collective-permute-start(bf16[512,1024]{1,0:T(8,128)(2,1)} %refs_9_.4), channel_id=1, source_target_pairs={{0,4},{8,0},{16,8},{24,16},{28,24},{20,28},{12,20},{4,12},{1,5},{9... | collective-permute-start | bytes 3145736 | tf_op jit(solution)/shard_map/ppermute | solution.py:36
  29.2 33.8 %collective-permute-start.6 = (bf16[512,1024]{1,0:T(8,128)(2,1)S(1)}, bf16[512,1024]{1,0:T(8,128)(2,1)}, u32[]{:S(2)}, u32[]{:S(2)}) collective-permute-start(bf16[512,1024]{1,0:T(8,128)(2,1)S(1)} %copy-done.20), channel_id=1, source_target_pairs={{0,8},{8,16},{16,24},{24,28},{28,20},{20,12},{12,4},{4,0},{1,9},{9... | collective-permute-start | bytes 3145736 | tf_op jit(solution)/shard_map/ppermute | solution.py:36
  31.2 31.8 %collective-permute-start.7 = (bf16[512,1024]{1,0:T(8,128)(2,1)S(1)}, bf16[512,1024]{1,0:T(8,128)(2,1)}, u32[]{:S(2)}, u32[]{:S(2)}) collective-permute-start(bf16[512,1024]{1,0:T(8,128)(2,1)S(1)} %copy-done.20), channel_id=1, source_target_pairs={{0,4},{8,0},{16,8},{24,16},{28,24},{20,28},{12,20},{4,12},{1,5},{9... | collective-permute-start | bytes 3145736 | tf_op jit(solution)/shard_map/ppermute | solution.py:36
  47.8 32.8 %collective-permute-start.2 = (bf16[512,1024]{1,0:T(8,128)(2,1)}, bf16[512,1024]{1,0:T(8,128)(2,1)}, u32[]{:S(2)}, u32[]{:S(2)}) collective-permute-start(bf16[512,1024]{1,0:T(8,128)(2,1)} %collective-permute-done.refs_10_), channel_id=1, source_target_pairs={{0,8},{8,16},{16,24},{24,28},{28,20},{20,12},{12,4},{4,0},{1,9},{9... | collective-permute-start | bytes 3145736 | tf_op jit(solution)/shard_map/ppermute | solution.py:36
  49.8 30.8 %collective-permute-start.3 = (bf16[512,1024]{1,0:T(8,128)(2,1)}, bf16[512,1024]{1,0:T(8,128)(2,1)}, u32[]{:S(2)}, u32[]{:S(2)}) collective-permute-start(bf16[512,1024]{1,0:T(8,128)(2,1)} %collective-permute-done.1.refs_11_), channel_id=1, source_target_pairs={{0,4},{8,0},{16,8},{24,16},{28,24},{20,28},{12,20},{4,12},{1,5},{9... | collective-permute-start | bytes 3145736 | tf_op jit(solution)/shard_map/ppermute | solution.py:36
  64.7 25.0 %collective-permute-start.11 = (bf16[8,64,512]{2,1,0:T(8,128)(2,1)S(1)}, bf16[8,64,512]{2,1,0:T(8,128)(2,1)S(1)}, u32[]{:S(2)}, u32[]{:S(2)}) collective-permute-start(bf16[8,64,512]{2,1,0:T(8,128)(2,1)S(1)} %select_convert_fusion.1), channel_id=1, source_target_pairs={{0,4},{4,0},{8,12},{12,8},{16,20},{20,16},{24,28},{28,24},{1,5},{5... | collective-permute-start | bytes 1572872 | tf_op jit(solution)/shard_map/ppermute | solution.py:583
  66.8 45.9 %collective-permute-start.8 = (bf16[512,1024]{1,0:T(8,128)(2,1)}, bf16[512,1024]{1,0:T(8,128)(2,1)}, u32[]{:S(2)}, u32[]{:S(2)}) collective-permute-start(bf16[512,1024]{1,0:T(8,128)(2,1)} %collective-permute-done.6.refs_10_), channel_id=1, source_target_pairs={{0,8},{8,16},{16,24},{24,28},{28,20},{20,12},{12,4},{4,0},{1,9},{9... | collective-permute-start | bytes 3145736 | tf_op jit(solution)/shard_map/ppermute | solution.py:36
  78.5 34.2 %collective-permute-start.9 = (bf16[512,1024]{1,0:T(8,128)(2,1)}, bf16[512,1024]{1,0:T(8,128)(2,1)}, u32[]{:S(2)}, u32[]{:S(2)}) collective-permute-start(bf16[512,1024]{1,0:T(8,128)(2,1)} %collective-permute-done.7.refs_11_), channel_id=1, source_target_pairs={{0,4},{8,0},{16,8},{24,16},{28,24},{20,28},{12,20},{4,12},{1,5},{9... | collective-permute-start | bytes 3145736 | tf_op jit(solution)/shard_map/ppermute | solution.py:36
  93.9 39.2 %collective-permute-start.4 = (bf16[512,1024]{1,0:T(8,128)(2,1)}, bf16[512,1024]{1,0:T(8,128)(2,1)S(1)}, u32[]{:S(2)}, u32[]{:S(2)}) collective-permute-start(bf16[512,1024]{1,0:T(8,128)(2,1)} %collective-permute-done.2.refs_12_), channel_id=1, source_target_pairs={{0,8},{8,16},{16,24},{24,28},{28,20},{20,12},{12,4},{4,0},{1,9},{9... | collective-permute-start | bytes 3145736 | tf_op jit(solution)/shard_map/ppermute | solution.py:36
  94.0 39.2 %collective-permute-start.5 = (bf16[512,1024]{1,0:T(8,128)(2,1)}, bf16[512,1024]{1,0:T(8,128)(2,1)}, u32[]{:S(2)}, u32[]{:S(2)}) collective-permute-start(bf16[512,1024]{1,0:T(8,128)(2,1)} %collective-permute-done.3.refs_13_), channel_id=1, source_target_pairs={{0,4},{8,0},{16,8},{24,16},{28,24},{20,28},{12,20},{4,12},{1,5},{9... | collective-permute-start | bytes 3145736 | tf_op jit(solution)/shard_map/ppermute | solution.py:36
  113.7 25.0 %collective-permute-start.17 = (bf16[8,64,512]{2,1,0:T(8,128)(2,1)}, bf16[8,64,512]{2,1,0:T(8,128)(2,1)}, u32[]{:S(2)}, u32[]{:S(2)}) collective-permute-start(bf16[8,64,512]{2,1,0:T(8,128)(2,1)} %add_convert_fusion.9), channel_id=1, source_target_pairs={{8,16},{12,20},{9,17},{13,21},{10,18},{14,22},{11,19},{15,23}} | collective-permute-start | bytes 1572872 | tf_op jit(solution)/shard_map/ppermute | solution.py:598
  136.7 32.9 %collective-permute-start.15 = (bf16[512,1024]{1,0:T(8,128)(2,1)}, bf16[512,1024]{1,0:T(8,128)(2,1)S(1)}, u32[]{:S(2)}, u32[]{:S(2)}) collective-permute-start(bf16[512,1024]{1,0:T(8,128)(2,1)} %collective-permute-done.8.refs_12_), channel_id=1, source_target_pairs={{0,8},{8,16},{16,24},{24,28},{28,20},{20,12},{12,4},{4,0},{1,9},{9... | collective-permute-start | bytes 3145736 | tf_op jit(solution)/shard_map/ppermute | solution.py:36
  137.8 32.4 %collective-permute-start.16 = (bf16[512,1024]{1,0:T(8,128)(2,1)}, bf16[512,1024]{1,0:T(8,128)(2,1)}, u32[]{:S(2)}, u32[]{:S(2)}) collective-permute-start(bf16[512,1024]{1,0:T(8,128)(2,1)} %collective-permute-done.9.refs_13_), channel_id=1, source_target_pairs={{0,4},{8,0},{16,8},{24,16},{28,24},{20,28},{12,20},{4,12},{1,5},{9... | collective-permute-start | bytes 3145736 | tf_op jit(solution)/shard_map/ppermute | solution.py:36
  173.0 23.7 %collective-permute-start.22 = (bf16[256,1024]{1,0:T(8,128)(2,1)S(1)}, bf16[256,1024]{1,0:T(8,128)(2,1)S(1)}, u32[]{:S(2)}, u32[]{:S(2)}) collective-permute-start(bf16[256,1024]{1,0:T(8,128)(2,1)S(1)} %slice.198), channel_id=1, source_target_pairs={{0,8},{8,16},{16,24},{24,28},{28,20},{20,12},{12,4},{4,0},{1,9},{9... | collective-permute-start | bytes 1572872 | tf_op jit(solution)/shard_map/ppermute | solution.py:36
  174.6 24.7 %collective-permute-start.23 = (bf16[256,1024]{1,0:T(8,128)(2,1)S(1)}, bf16[256,1024]{1,0:T(8,128)(2,1)S(1)}, u32[]{:S(2)}, u32[]{:S(2)}) collective-permute-start(bf16[256,1024]{1,0:T(8,128)(2,1)S(1)} %slice.199), channel_id=1, source_target_pairs={{0,4},{8,0},{16,8},{24,16},{28,24},{20,28},{12,20},{4,12},{1,5},{9... | collective-permute-start | bytes 1572872 | tf_op jit(solution)/shard_map/ppermute | solution.py:36
  175.2 35.3 %collective-permute-start.19 = (bf16[4,64,1024]{2,1,0:T(8,128)(2,1)S(1)}, bf16[4,64,1024]{2,1,0:T(8,128)(2,1)S(1)}, u32[]{:S(2)}, u32[]{:S(2)}) collective-permute-start(bf16[4,64,1024]{2,1,0:T(8,128)(2,1)S(1)} %bitcast.115), channel_id=1, source_target_pairs={{0,8},{8,16},{16,24},{24,28},{28,20},{20,12},{12,4},{4,0},{1,9},{9... | collective-permute-start | bytes 1572872 | tf_op jit(solution)/shard_map/ppermute | solution.py:36
  186.5 24.0 %collective-permute-start.20 = (bf16[4,64,1024]{2,1,0:T(8,128)(2,1)S(1)}, bf16[4,64,1024]{2,1,0:T(8,128)(2,1)S(1)}, u32[]{:S(2)}, u32[]{:S(2)}) collective-permute-start(bf16[4,64,1024]{2,1,0:T(8,128)(2,1)S(1)} %bitcast.116), channel_id=1, source_target_pairs={{0,4},{8,0},{16,8},{24,16},{28,24},{20,28},{12,20},{4,12},{1,5},{9... | collective-permute-start | bytes 1572872 | tf_op jit(solution)/shard_map/ppermute | solution.py:36
  231.4 22.7 %collective-permute-start.34 = (bf16[4,64,1024]{2,1,0:T(8,128)(2,1)S(1)}, bf16[4,64,1024]{2,1,0:T(8,128)(2,1)S(1)}, u32[]{:S(2)}, u32[]{:S(2)}) collective-permute-start(bf16[4,64,1024]{2,1,0:T(8,128)(2,1)S(1)} %bitcast.112), channel_id=1, source_target_pairs={{0,8},{8,16},{16,24},{24,28},{28,20},{20,12},{12,4},{4,0},{1,9},{9... | collective-permute-start | bytes 1572872 | tf_op jit(solution)/shard_map/ppermute | solution.py:36
  239.2 24.1 %collective-permute-start.35 = (bf16[4,64,1024]{2,1,0:T(8,128)(2,1)S(1)}, bf16[4,64,1024]{2,1,0:T(8,128)(2,1)S(1)}, u32[]{:S(2)}, u32[]{:S(2)}) collective-permute-start(bf16[4,64,1024]{2,1,0:T(8,128)(2,1)S(1)} %bitcast.113), channel_id=1, source_target_pairs={{0,4},{8,0},{16,8},{24,16},{28,24},{20,28},{12,20},{4,12},{1,5},{9... | collective-permute-start | bytes 1572872 | tf_op jit(solution)/shard_map/ppermute | solution.py:36
  268.8 67.3 %collective-permute-start.32 = (bf16[512,1024]{1,0:T(8,128)(2,1)S(1)}, bf16[512,1024]{1,0:T(8,128)(2,1)S(1)}, u32[]{:S(2)}, u32[]{:S(2)}) collective-permute-start(bf16[512,1024]{1,0:T(8,128)(2,1)S(1)} %copy-done.21), channel_id=1, source_target_pairs={{0,8},{8,16},{16,24},{24,28},{28,20},{20,12},{12,4},{4,0},{1,9},{9... | collective-permute-start | bytes 3145736 | tf_op jit(solution)/shard_map/ppermute | solution.py:36
  270.9 65.3 %collective-permute-start.33 = (bf16[512,1024]{1,0:T(8,128)(2,1)S(1)}, bf16[512,1024]{1,0:T(8,128)(2,1)S(1)}, u32[]{:S(2)}, u32[]{:S(2)}) collective-permute-start(bf16[512,1024]{1,0:T(8,128)(2,1)S(1)} %copy-done.21), channel_id=1, source_target_pairs={{0,4},{8,0},{16,8},{24,16},{28,24},{20,28},{12,20},{4,12},{1,5},{9... | collective-permute-start | bytes 3145736 | tf_op jit(solution)/shard_map/ppermute | solution.py:36
  280.1 26.8 %collective-permute-start.38 = (bf16[4,64,1024]{2,1,0:T(8,128)(2,1)S(1)}, bf16[4,64,1024]{2,1,0:T(8,128)(2,1)S(1)}, u32[]{:S(2)}, u32[]{:S(2)}) collective-permute-start(bf16[4,64,1024]{2,1,0:T(8,128)(2,1)S(1)} %collective-permute-done.36.refs_3_), channel_id=1, source_target_pairs={{0,8},{8,16},{16,24},{24,28},{28,20},{20,12},{12,4},{4,0},{1,9},{9... | collective-permute-start | bytes 1572872 | tf_op jit(solution)/shard_map/ppermute | solution.py:36
  282.1 29.7 %collective-permute-start.39 = (bf16[4,64,1024]{2,1,0:T(8,128)(2,1)S(1)}, bf16[4,64,1024]{2,1,0:T(8,128)(2,1)S(1)}, u32[]{:S(2)}, u32[]{:S(2)}) collective-permute-start(bf16[4,64,1024]{2,1,0:T(8,128)(2,1)S(1)} %collective-permute-done.37.refs_4_), channel_id=1, source_target_pairs={{0,4},{8,0},{16,8},{24,16},{28,24},{20,28},{12,20},{4,12},{1,5},{9... | collective-permute-start | bytes 1572872 | tf_op jit(solution)/shard_map/ppermute | solution.py:36
  311.8 24.3 %collective-permute-start.40 = (bf16[2,64,1024]{2,1,0:T(8,128)(2,1)S(1)}, bf16[2,64,1024]{2,1,0:T(8,128)(2,1)S(1)}, u32[]{:S(2)}, u32[]{:S(2)}) collective-permute-start(bf16[2,64,1024]{2,1,0:T(8,128)(2,1)S(1)} %slice.203), channel_id=1, source_target_pairs={{0,8},{8,16},{16,24},{24,28},{28,20},{20,12},{12,4},{4,0},{1,9},{9... | collective-permute-start | bytes 786440 | tf_op jit(solution)/shard_map/ppermute | solution.py:36
  336.2 25.1 %collective-permute-start.42 = (bf16[512,1024]{1,0:T(8,128)(2,1)S(1)}, bf16[512,1024]{1,0:T(8,128)(2,1)S(1)}, u32[]{:S(2)}, u32[]{:S(2)}) collective-permute-start(bf16[512,1024]{1,0:T(8,128)(2,1)S(1)} %collective-permute-done.32.refs_8_), channel_id=1, source_target_pairs={{0,8},{8,16},{16,24},{24,28},{28,20},{20,12},{12,4},{4,0},{1,9},{9... | collective-permute-start | bytes 3145736 | tf_op jit(solution)/shard_map/ppermute | solution.py:36
  338.2 23.0 %collective-permute-start.43 = (bf16[512,1024]{1,0:T(8,128)(2,1)S(1)}, bf16[512,1024]{1,0:T(8,128)(2,1)}, u32[]{:S(2)}, u32[]{:S(2)}) collective-permute-start(bf16[512,1024]{1,0:T(8,128)(2,1)S(1)} %collective-permute-done.33.refs_9_), channel_id=1, source_target_pairs={{0,4},{8,0},{16,8},{24,16},{28,24},{20,28},{12,20},{4,12},{1,5},{9... | collective-permute-start | bytes 3145736 | tf_op jit(solution)/shard_map/ppermute | solution.py:36
  361.3 40.1 %collective-permute-start.44 = (bf16[512,1024]{1,0:T(8,128)(2,1)S(1)}, bf16[512,1024]{1,0:T(8,128)(2,1)S(1)}, u32[]{:S(2)}, u32[]{:S(2)}) collective-permute-start(bf16[512,1024]{1,0:T(8,128)(2,1)S(1)} %collective-permute-done.42.refs_10_), channel_id=1, source_target_pairs={{0,8},{8,16},{16,24},{24,28},{28,20},{20,12},{12,4},{4,0},{1,9},{9... | collective-permute-start | bytes 3145736 | tf_op jit(solution)/shard_map/ppermute | solution.py:36
  363.3 39.0 %collective-permute-start.45 = (bf16[512,1024]{1,0:T(8,128)(2,1)}, bf16[512,1024]{1,0:T(8,128)(2,1)S(1)}, u32[]{:S(2)}, u32[]{:S(2)}) collective-permute-start(bf16[512,1024]{1,0:T(8,128)(2,1)} %collective-permute-done.43.refs_11_), channel_id=1, source_target_pairs={{0,4},{8,0},{16,8},{24,16},{28,24},{20,28},{12,20},{4,12},{1,5},{9... | collective-permute-start | bytes 3145736 | tf_op jit(solution)/shard_map/ppermute | solution.py:36
  364.2 22.2 %collective-permute-start.48 = (f32[8,8,512]{2,1,0:T(8,128)S(1)}, f32[8,8,512]{2,1,0:T(8,128)S(1)}, u32[]{:S(2)}, u32[]{:S(2)}) collective-permute-start(f32[8,8,512]{2,1,0:T(8,128)S(1)} %constant_dynamic-update-slice_fusion), channel_id=1, source_target_pairs={{0,4},{4,0},{8,12},{12,8},{16,20},{20,16},{24,28},{28,24},{1,5},{5... | collective-permute-start | bytes 393224 | tf_op jit(solution)/shard_map/ppermute | solution.py:89
  403.2 30.4 %collective-permute-start.46 = (bf16[256,1024]{1,0:T(8,128)(2,1)}, bf16[256,1024]{1,0:T(8,128)(2,1)S(1)}, u32[]{:S(2)}, u32[]{:S(2)}) collective-permute-start(bf16[256,1024]{1,0:T(8,128)(2,1)} %slice.205), channel_id=1, source_target_pairs={{0,8},{8,16},{16,24},{24,28},{28,20},{20,12},{12,4},{4,0},{1,9},{9... | collective-permute-start | bytes 1572872 | tf_op jit(solution)/shard_map/ppermute | solution.py:36
  405.4 28.2 %collective-permute-start.47 = (bf16[256,1024]{1,0:T(8,128)(2,1)}, bf16[256,1024]{1,0:T(8,128)(2,1)S(1)}, u32[]{:S(2)}, u32[]{:S(2)}) collective-permute-start(bf16[256,1024]{1,0:T(8,128)(2,1)} %slice.206), channel_id=1, source_target_pairs={{0,4},{8,0},{16,8},{24,16},{28,24},{20,28},{12,20},{4,12},{1,5},{9... | collective-permute-start | bytes 1572872 | tf_op jit(solution)/shard_map/ppermute | solution.py:36
  (101 other events, 1909.9 us)

commit v7 on v6

--- a/solution.py
+++ b/solution.py
@@ -63,37 +63,43 @@
 
 
 class Clock:
-    def __init__(self):
-        self.fence = ()
+    def __init__(self, mark):
+        self.mark = mark
         self.late = ()
 
     def hold(self, *values):
-        held = lax.optimization_barrier(tuple(values) + self.fence)[: len(values)]
+        held = lax.optimization_barrier(tuple(values) + (self.mark,))[: len(values)]
         return held[0] if len(values) == 1 else held
 
     def turn(self, ring=None, work=None):
         moved = tuple(ring.step(self)) if ring is not None else ()
         done, deferred = work() if work is not None else ((), ())
-        self.fence = self.late + tuple(done)
+        self.mark = lax.optimization_barrier((self.mark,) + self.late + tuple(done))[0]
         self.late = moved + tuple(deferred)
 
 
 class Exchange:
     def __init__(self, value, axis, count, combine):
         self.value, self.axis, self.count, self.combine = value, axis, count, combine
+        self.got = None
         self.bit = 1
 
-    def step(self):
+    def join(self, clock):
+        if self.got is not None:
+            self.value = self.combine(*clock.hold(self.value, self.got))
+            self.got = None
+
+    def step(self, clock):
+        self.join(clock)
         if self.bit < self.count:
             route = [(i, i ^ self.bit) for i in range(self.count)]
-            got = lax.ppermute(self.value, self.axis, route)
-            self.value = self.combine(self.value, got)
+            self.got = lax.ppermute(self.value, self.axis, route)
             self.bit *= 2
-        return (self.value,)
-
-    def result(self):
+
+    def result(self, clock):
         while self.bit < self.count:
-            self.step()
+            self.step(clock)
+        self.join(clock)
         return self.value
 
 
@@ -667,7 +673,7 @@
     cosine = jnp.concatenate([cosine, cosine], axis=1)
     sine = jnp.concatenate([-sine, sine], axis=1)
 
-    clock = Clock()
+    clock = Clock(jnp.zeros((1,), jnp.int32) + lengths[:1])
     group = requests // GROUPS
     local_inner = w_in.shape[2]
     local_mheads = local_inner // MHEAD_DIM
@@ -751,14 +757,20 @@
         made["gated"] = gated
         made["squares"] = Exchange(
             squares[:, :1].reshape(1, tokens), "head", head_count, jnp.add
-        ).result()
+        )
+        made["squares"].step(clock)
         made["chain"] = chain
-        return (gated,), (made["squares"],)
+        return (gated,), ()
+
+    def join_squares():
+        made["squares"].step(clock)
+        return (), ()
 
     def leave_terms():
+        squares = made["squares"].result(clock).reshape(tokens, 1)
         made["terms"] = jnp.dot(
             clock.hold(made["gated"]), w_out, preferred_element_type=jnp.float32
-        ) * lax.rsqrt(made["squares"].reshape(tokens, 1) / D_INNER + 1e-05)
+        ) * lax.rsqrt(squares / D_INNER + 1e-05)
         return (made["terms"],), ()
 
     def leave_chain():
@@ -811,11 +823,11 @@
     def join_peaks():
         peaks = jnp.concatenate([clock.hold(part[2]) for part in cached], axis=0)
         made["best"] = Exchange(peaks, "seq", seq_count, jnp.maximum)
-        made["best"].step()
+        made["best"].step(clock)
         return leave_chain()
 
     def make_values():
-        made["best"].step()
+        made["best"].step(clock)
         made["values"] = product(
             [(0, 0, clock.hold(value_ring.block))] + value_ring.pieces[1:-2],
             False,
@@ -834,11 +846,19 @@
             )
 
     both = steps([query_ring, key_ring], 0, half - 2) + [query_ring] * 2 + [key_ring] * 2
-    works = [prepare, enter, inside, start_relay, hop, hop, hop]
-    run(both, works + [None] * (len(both) - 1 - len(works)) + [make_queries])
+    def make_queries_hop():
+        done, _ = make_queries()
+        return done, hop()[1]
+
+    def make_keys_hop():
+        deferred = hop()[1]
+        return make_keys()[0], deferred
+
+    works = [prepare, enter, inside, start_relay, None, hop]
+    run(both, works + [None] * (len(both) - 1 - len(works)) + [make_queries_hop])
     run(
         steps(slot_rings, 0, half),
-        [end_relay, make_keys, leave, None, leave_terms],
+        [None, make_keys_hop, None, end_relay, None, leave, join_squares, leave_terms],
     )
     run(
         steps([value_ring], 0, half),
@@ -846,7 +866,7 @@
     )
 
     new_keys = made["keys"]
-    best = made["best"].result()
+    best = made["best"].result(clock)
     new_values = by_request(product(value_ring.pieces[-2:], False, base=(made["values"],)))
 
     own = lambda stat: lax.dynamic_slice_in_dim(stat, seq_index * tok_block, tok_block, 2)
@@ -882,13 +902,13 @@
     def add_sums():
         if "sums" not in made:
             made["sums"] = Exchange(jnp.concatenate(sums, axis=0), "seq", seq_count, jnp.add)
-        made["sums"].step()
+        made["sums"].step(clock)
         return (), ()
 
     run([], [finish(0)])
     run([ring_sums[0]], [finish(1)])
     run(steps(ring_sums[::-1], 0, half)[:-1], [add_sums, None, add_sums, None, add_sums])
-    denominators = jnp.transpose(own(made["sums"].result()), (0, 2, 1))
+    denominators = jnp.transpose(own(made["sums"].result(clock)), (0, 2, 1))
     for index in range(GROUPS):
         begin = index * group
         denominator = denominators[begin : begin + group]

time: 584 us -> 526 us (0.901)
  waiting for transfers between devices: 225 us -> 171 us
    ppermute x8, waiting for transfers between devices: 53.6 us -> 19.2 us  [step(): self.got = lax.ppermute(self.value, self.axis, route)]
    ppermute x56, waiting for transfers between devices: 131 us -> 97.5 us  [ring_step(): return lax.ppermute(block, 'seq', route)]
    ppermute x2, waiting for transfers between devices: 9.11 us -> 36 us  [exchange(): lax.ppermute(value.astype(jnp.bfloat16), 'seq', self.swap)]
    ppermute x3, waiting for transfers between devices: 15 us -> 0.01 us  [advance(): self.entry = entry + lax.ppermute(leaving, 'seq', route).astype(jnp.float32)]
    unnamed x124 -> x98, local copies, waits for them, and re-layouts: 18.6 us -> 16.2 us
  transfers between devices with their start and end apart: 74 -> 74, of which waited for: 36 -> 34; matrix products, arithmetic and copies ran while one was open for 18% -> 20% of each run, Pallas kernels for 20% -> 20%
where the time goes in v7:
time: 526 us; the launch traced here: 516 us
  waiting for transfers between devices  171 us (33%)
  Pallas kernels  133 us (25%)
  starting transfers between devices  97 us (18%)
  local copies, waits for them, and re-layouts  63.8 us (12%)
  other arithmetic  38 us (7%)
  matrix products  11.2 us (2%)
    ppermute x56, waiting for transfers between devices, ring_step(): return lax.ppermute(block, 'seq', route)  97.5 us
    ppermute x56, starting transfers between devices, ring_step(): return lax.ppermute(block, 'seq', route)  75.6 us
    pallas_call x2, Pallas kernels, cache_part(): pl.pallas_call(functools.partial(cache_kernel, slots), grid_spec=pltpu.Pr...  44.1 us
    pallas_call x4, Pallas kernels, project(): pl.pallas_call(functools.partial(project_kernel, len(pieces), turned), gr...  36 us
    ppermute x2, waiting for transfers between devices, exchange(): lax.ppermute(value.astype(jnp.bfloat16), 'seq', self.swap)  36 us
    pallas_call x2, Pallas kernels, finish_part(): pl.pallas_call(functools.partial(finish_kernel, slots), grid_spec=pltpu.P...  22.7 us
    ppermute x8, waiting for transfers between devices, step(): self.got = lax.ppermute(self.value, self.axis, route)  19.2 us
    unnamed x98, local copies, waits for them, and re-layouts  16.2 us
  transfers between devices with their start and end apart: 74, of which 34 were waited for; matrix products, arithmetic and copies ran while one was open for 20% of the time, Pallas kernels for 20%

profile of v7, /device:TPU:0, one launch (start us, length us, event | category | flops | bytes accessed | tf_op | source)
XLA Modules:
  0.0 515.7 jit_solution(2022295930362512669)
XLA Ops:
  8.3 5.6 %copy.40 = f32[8,16,64,64]{2,1,3,0:T(8,128)} copy(f32[8,16,64,64]{3,2,1,0:T(8,128)} %reshape.124) | data formatting | bytes 4194304 | tf_op jit(solution)/shard_map/reshape | solution.py:696
  17.4 10.3 %copy.52 = bf16[256,8,2,1024]{3,1,2,0:T(8,128)(2,1)} copy(bf16[256,8,2,1024]{3,2,1,0:T(2,128)(2,1)} %bitcast.103) | data formatting | bytes 16777216
  30.8 11.6 %enter_mixer.1 = (f32[512,2048]{1,0:T(8,128)}, f32[512,128]{1,0:T(8,128)}, f32[512,16]{1,0:T(8,128)}) custom-call(bf16[512,4096]{1,0:T(8,128)(2,1)} %bitcast.64, f32[1,2048]{1,0:T(1,128)} %bitcast.126, bf16[2048,128]{1,0:T(8,128)(2,1)} %bc_ref.1, bf16[2048,16]{1,0:T(8,128)(2,1)} %copy.41.dt_ref, f32[1,16]{1,0:T(1,128)} %bitcast.127, bf16[2048,2048]{1,0:T(8,128)(2,1)} %bitcast.104), custom_call_target="tpu_custom_call" | custom-call | flops 4294967296 | bytes 14680064 | tf_op jit(solution)/shard_map/enter_mixer/pallas_call | solution.py:231
  50.2 9.6 %inside_block.1 = (f32[512,1024]{1,0:T(8,128)}, f32[8,64,1024]{2,1,0:T(8,128)}, f32[8,1,1024]{2,1,0:T(1,128)}) custom-call(f32[512,2048]{1,0:T(8,128)} %get-tuple-element.166.inner_ref.gate_ref, f32[512,128]{1,0:T(8,128)} %get-tuple-element.167.map_ref, f32[8,64,16]{2,1,0:T(8,128)} %bitcast.107, f32[8,64,16]{2,1,0:T(8,128)} %bitcast.111, ...), custom_call_target="tpu_custom_call" | custom-call | flops 402653184 | bytes 8388608 | tf_op jit(solution)/shard_map/inside_block/pallas_call | solution.py:309
  65.4 11.8 %collective-permute-done.10 = f32[8,1,1024]{2,1,0:T(1,128)S(1)} collective-permute-done((f32[8,1,1024]{2,1,0:T(1,128)}, f32[8,1,1024]{2,1,0:T(1,128)S(1)}, u32[]{:S(2)}, u32[]{:S(2)}) %collective-permute-start.10) | collective-permute-done | bytes 32800 | tf_op jit(solution)/shard_map/ppermute | solution.py:578
  82.7 28.2 %collective-permute-done.11 = bf16[8,64,512]{2,1,0:T(8,128)(2,1)S(1)} collective-permute-done((bf16[8,64,512]{2,1,0:T(8,128)(2,1)S(1)}, bf16[8,64,512]{2,1,0:T(8,128)(2,1)S(1)}, u32[]{:S(2)}, u32[]{:S(2)}) %collective-permute-start.11) | collective-permute-done | bytes 524320 | tf_op jit(solution)/shard_map/ppermute | solution.py:589
  118.0 14.1 %collective-permute-done.6.refs_14_ = bf16[512,1024]{1,0:T(8,128)(2,1)} collective-permute-done((bf16[512,1024]{1,0:T(8,128)(2,1)}, bf16[512,1024]{1,0:T(8,128)(2,1)}, u32[]{:S(2)}, u32[]{:S(2)}) %collective-permute-start.6) | collective-permute-done | bytes 1048608 | tf_op jit(solution)/shard_map/ppermute | solution.py:36
  141.8 7.3 %collective-permute-done.12.refs_16_ = bf16[256,1024]{1,0:T(8,128)(2,1)S(1)} collective-permute-done((bf16[256,1024]{1,0:T(8,128)(2,1)S(1)}, bf16[256,1024]{1,0:T(8,128)(2,1)S(1)}, u32[]{:S(2)}, u32[]{:S(2)}) %collective-permute-start.12) | collective-permute-done | bytes 524320 | tf_op jit(solution)/shard_map/ppermute | solution.py:36
  150.9 10.4 %project.4 = bf16[512,1024]{1,0:T(8,128)(2,1)} custom-call(s32[8]{0:T(128)} %fusion.21.places_ref.place_ref, bf16[512,4096]{1,0:T(8,128)(2,1)} %bitcast.65, bf16[512,4096]{1,0:T(8,128)(2,1)} %bitcast.66, bf16[512,4096]{1,0:T(8,128)(2,1)} %bitcast.67, bf16[512,4096]{1,0:T(8,128)(2,1)} %bitcast.68, bf16[512,4096]{1,0:T(8,128)(2,1)} %bitcast.69, ...), custom_call_target="tpu_custom_call" | custom-call | flops 4294967296 | bytes 12582912 | tf_op jit(solution)/shard_map/project/pallas_call | solution.py:169
  161.4 7.8 %collective-permute-done.15.refs_14_ = bf16[512,1024]{1,0:T(8,128)(2,1)S(1)} collective-permute-done((bf16[512,1024]{1,0:T(8,128)(2,1)}, bf16[512,1024]{1,0:T(8,128)(2,1)S(1)}, u32[]{:S(2)}, u32[]{:S(2)}) %collective-permute-start.15) | collective-permute-done | bytes 1048608 | tf_op jit(solution)/shard_map/ppermute | solution.py:36
  176.7 7.5 %collective-permute-done.17.refs_16_ = bf16[256,1024]{1,0:T(8,128)(2,1)S(1)} collective-permute-done((bf16[256,1024]{1,0:T(8,128)(2,1)S(1)}, bf16[256,1024]{1,0:T(8,128)(2,1)S(1)}, u32[]{:S(2)}, u32[]{:S(2)}) %collective-permute-start.17) | collective-permute-done | bytes 524320 | tf_op jit(solution)/shard_map/ppermute | solution.py:36
  189.8 10.4 %project.5 = bf16[512,1024]{1,0:T(8,128)(2,1)} custom-call(s32[8]{0:T(128)} %fusion.21.places_ref.place_ref, bf16[512,4096]{1,0:T(8,128)(2,1)} %bitcast.78, bf16[512,4096]{1,0:T(8,128)(2,1)} %bitcast.75, bf16[512,4096]{1,0:T(8,128)(2,1)} %bitcast.76, bf16[512,4096]{1,0:T(8,128)(2,1)} %bitcast.77, bf16[512,4096]{1,0:T(8,128)(2,1)} %bitcast.74, ...), custom_call_target="tpu_custom_call" | custom-call | flops 4294967296 | bytes 12582912 | tf_op jit(solution)/shard_map/project/pallas_call | solution.py:169
  209.8 7.3 %collective-permute-start.27 = (bf16[4,64,1024]{2,1,0:T(8,128)(2,1)}, bf16[4,64,1024]{2,1,0:T(8,128)(2,1)S(1)}, u32[]{:S(2)}, u32[]{:S(2)}) collective-permute-start(bf16[4,64,1024]{2,1,0:T(8,128)(2,1)} %collective-permute-done.22.refs_1_), channel_id=1, source_target_pairs={{0,8},{8,16},{16,24},{24,28},{28,20},{20,12},{12,4},{4,0},{1,9},{9... | collective-permute-start | bytes 1572872 | tf_op jit(solution)/shard_map/ppermute | solution.py:36
  222.5 7.8 %collective-permute-done.29 = bf16[8,64,512]{2,1,0:T(8,128)(2,1)S(1)} collective-permute-done((bf16[8,64,512]{2,1,0:T(8,128)(2,1)S(1)}, bf16[8,64,512]{2,1,0:T(8,128)(2,1)S(1)}, u32[]{:S(2)}, u32[]{:S(2)}) %collective-permute-start.29) | collective-permute-done | bytes 524320 | tf_op jit(solution)/shard_map/ppermute | solution.py:589
  232.2 9.3 %collective-permute-done.27.refs_3_ = bf16[4,64,1024]{2,1,0:T(8,128)(2,1)S(1)} collective-permute-done((bf16[4,64,1024]{2,1,0:T(8,128)(2,1)}, bf16[4,64,1024]{2,1,0:T(8,128)(2,1)S(1)}, u32[]{:S(2)}, u32[]{:S(2)}) %collective-permute-start.27) | collective-permute-done | bytes 524320 | tf_op jit(solution)/shard_map/ppermute | solution.py:36
  243.6 8.9 %leave_mixer.1 = (bf16[512,1024]{1,0:T(8,128)(2,1)}, f32[512,128]{1,0:T(8,128)}, f32[8,64,1024]{2,1,0:T(8,128)}) custom-call(f32[8,64,1024]{2,1,0:T(8,128)} %pad_maximum_fusion.entry_ref, f32[512,128]{1,0:T(8,128)} %get-tuple-element.167.map_ref, f32[8,64,16]{2,1,0:T(8,128)} %bitcast.108, f32[512,1024]{1,0:T(8,128)} %get-tuple-element.168.read_ref, ...), custom_call_target="tpu_custom_call" | custom-call | flops 67108864 | bytes 12582912 | tf_op jit(solution)/shard_map/leave_mixer/pallas_call | solution.py:362
  259.8 7.3 %convolution_multiply_fusion = f32[512,2048]{1,0:T(8,128)} fusion(bf16[512,1024]{1,0:T(8,128)(2,1)} %get-tuple-element.215, bf16[1024,2048]{1,0:T(8,128)(2,1)} %param.35, f32[512]{0:T(512)S(1)} %bitcast.125), kind=kOutput, calls=%fused_computation | convolution fusion | flops 2148532224 | bytes 9439232 | tf_op jit(solution)/shard_map/dot_general | solution.py:771
  274.9 22.0 %cache_part.2 = (bf16[4,512,1024]{2,1,0:T(8,128)(2,1)}, bf16[4,1024,512]{2,1,0:T(8,128)(2,1)}, f32[4,8,512]{2,1,0:T(8,128)}, f32[4,8,512]{2,1,0:T(8,128)}) custom-call(s32[1]{0:T(128)} %bitcast.1.first_ref, s32[8]{0:T(128)} %fusion.21.places_ref.place_ref, s32[4]{0:T(128)} %get-tuple-element.330.live_ref, bf16[4,64,1024]{2,1,0:T(8,128)(2,1)} %bitcast.117, ...), custom_call_target="tpu_custom_call" | custom-call | flops 4294967296 | bytes 20971520 | tf_op jit(solution)/shard_map/cache_part/pallas_call | solution.py:448
  303.7 22.1 %cache_part.3 = (bf16[4,512,1024]{2,1,0:T(8,128)(2,1)}, bf16[4,1024,512]{2,1,0:T(8,128)(2,1)}, f32[4,8,512]{2,1,0:T(8,128)}, f32[4,8,512]{2,1,0:T(8,128)}) custom-call(s32[1]{0:T(128)} %bitcast.1.first_ref, s32[8]{0:T(128)} %fusion.21.places_ref.place_ref, s32[4]{0:T(128)} %get-tuple-element.329.live_ref, bf16[4,64,1024]{2,1,0:T(8,128)(2,1)} %bitcast.114, ...), custom_call_target="tpu_custom_call" | custom-call | flops 4294967296 | bytes 20971520 | tf_op jit(solution)/shard_map/cache_part/pallas_call | solution.py:448
  333.4 5.5 %copy.45 = f32[8,16,64,64]{3,2,1,0:T(8,128)} copy(f32[8,16,64,64]{2,1,3,0:T(8,128)} %bitcast.99) | data formatting | bytes 4194304 | tf_op jit(solution)/shard_map/transpose | solution.py:778
  339.0 4.8 reshape.135
  343.7 6.5 %collective-permute-done.44.refs_12_ = bf16[512,1024]{1,0:T(8,128)(2,1)S(1)} collective-permute-done((bf16[512,1024]{1,0:T(8,128)(2,1)S(1)}, bf16[512,1024]{1,0:T(8,128)(2,1)S(1)}, u32[]{:S(2)}, u32[]{:S(2)}) %collective-permute-start.44) | collective-permute-done | bytes 1048608 | tf_op jit(solution)/shard_map/ppermute | solution.py:36
  354.4 9.7 %project.6.refs_6_ = f32[512,1024]{1,0:T(8,128)} custom-call(s32[8]{0:T(128)} %fusion.21.places_ref.place_ref, bf16[512,4096]{1,0:T(8,128)(2,1)} %bitcast.83, bf16[512,4096]{1,0:T(8,128)(2,1)} %bitcast.84, bf16[512,4096]{1,0:T(8,128)(2,1)} %bitcast.85, bf16[512,4096]{1,0:T(8,128)(2,1)} %bitcast.86, bf16[512,4096]{1,0:T(8,128)(2,1)} %bitcast.87, ...), custom_call_target="tpu_custom_call" | custom-call | flops 3758096384 | bytes 12582912 | tf_op jit(solution)/shard_map/project/pallas_call | solution.py:169
  374.7 5.4 %project.7 = bf16[512,1024]{1,0:T(8,128)(2,1)} custom-call(s32[8]{0:T(128)} %fusion.21.places_ref.place_ref, bf16[512,4096]{1,0:T(8,128)(2,1)} %bitcast.90, bf16[512,4096]{1,0:T(8,128)(2,1)} %bitcast.91, bf16[256,1024]{1,0:T(8,128)(2,1)} %copy-done.35, bf16[256,1024]{1,0:T(8,128)(2,1)} %copy-done.36, ...), custom_call_target="tpu_custom_call" | custom-call | flops 536870912 | bytes 12582912 | tf_op jit(solution)/shard_map/project/pallas_call | solution.py:169
  380.1 11.2 %finish_part.2 = (f32[4,8,512]{2,1,0:T(8,128)}, bf16[4,64,1024]{2,1,0:T(8,128)(2,1)}, bf16[4,64,1024]{2,1,0:T(8,128)(2,1)}, bf16[4,64,1024]{2,1,0:T(8,128)(2,1)}...) custom-call(s32[1]{0:T(128)} %bitcast.1.first_ref, ...), custom_call_target="tpu_custom_call" | custom-call | flops 536870912 | bytes 12582912 | tf_op jit(solution)/shard_map/finish_part/pallas_call | solution.py:510
  393.2 11.4 %finish_part.3 = (f32[4,8,512]{2,1,0:T(8,128)}, bf16[4,64,1024]{2,1,0:T(8,128)(2,1)}, bf16[4,64,1024]{2,1,0:T(8,128)(2,1)}, bf16[4,64,1024]{2,1,0:T(8,128)(2,1)}...) custom-call(s32[1]{0:T(128)} %bitcast.1.first_ref, ...), custom_call_target="tpu_custom_call" | custom-call | flops 536870912 | bytes 12582912 | tf_op jit(solution)/shard_map/finish_part/pallas_call | solution.py:510
  413.9 5.6 %collective-permute-done.56 = bf16[2,64,1024]{2,1,0:T(8,128)(2,1)S(1)} collective-permute-done((bf16[2,64,1024]{2,1,0:T(8,128)(2,1)}, bf16[2,64,1024]{2,1,0:T(8,128)(2,1)S(1)}, u32[]{:S(2)}, u32[]{:S(2)}) %collective-permute-start.56) | collective-permute-done | bytes 262176 | tf_op jit(solution)/shard_map/ppermute | solution.py:36
  428.4 5.9 %collective-permute-done.64 = bf16[4,64,1024]{2,1,0:T(8,128)(2,1)S(1)} collective-permute-done((bf16[4,64,1024]{2,1,0:T(8,128)(2,1)S(1)}, bf16[4,64,1024]{2,1,0:T(8,128)(2,1)S(1)}, u32[]{:S(2)}, u32[]{:S(2)}) %collective-permute-start.64) | collective-permute-done | bytes 524320 | tf_op jit(solution)/shard_map/ppermute | solution.py:36
  435.5 6.9 %collective-permute-done.53 = bf16[4,64,1024]{2,1,0:T(8,128)(2,1)S(1)} collective-permute-done((bf16[4,64,1024]{2,1,0:T(8,128)(2,1)S(1)}, bf16[4,64,1024]{2,1,0:T(8,128)(2,1)S(1)}, u32[]{:S(2)}, u32[]{:S(2)}) %collective-permute-start.53) | collective-permute-done | bytes 524320 | tf_op jit(solution)/shard_map/ppermute | solution.py:36
  456.1 11.0 %collective-permute-done.65 = f32[8,8,512]{2,1,0:T(8,128)S(1)} collective-permute-done((f32[8,8,512]{2,1,0:T(8,128)S(1)}, f32[8,8,512]{2,1,0:T(8,128)S(1)}, u32[]{:S(2)}, u32[]{:S(2)}) %collective-permute-start.65) | collective-permute-done | bytes 131104 | tf_op jit(solution)/shard_map/ppermute | solution.py:96
  477.0 4.9 collective-permute-start.59
  507.1 5.5 %collective-permute-done.67 = bf16[256,512]{1,0:T(8,128)(2,1)} collective-permute-done((bf16[256,512]{1,0:T(8,128)(2,1)}, bf16[256,512]{1,0:T(8,128)(2,1)}, u32[]{:S(2)}, u32[]{:S(2)}) %collective-permute-start.67) | collective-permute-done | bytes 262176 | tf_op jit(solution)/shard_map/ppermute | solution.py:557
  (330 shorter events, 199.6 us)
Async XLA Ops:
  0.6 45.6 %collective-permute-start = (bf16[512,1024]{1,0:T(8,128)(2,1)}, bf16[512,1024]{1,0:T(8,128)(2,1)}, u32[]{:S(2)}, u32[]{:S(2)}) collective-permute-start(bf16[512,1024]{1,0:T(8,128)(2,1)} %refs_9_.4), channel_id=1, source_target_pairs={{0,8},{8,16},{16,24},{24,28},{28,20},{20,12},{12,4},{4,0},{1,9},{9... | collective-permute-start | bytes 3145736 | tf_op jit(solution)/shard_map/ppermute | solution.py:36
  3.7 42.6 %collective-permute-start.1 = (bf16[512,1024]{1,0:T(8,128)(2,1)}, bf16[512,1024]{1,0:T(8,128)(2,1)}, u32[]{:S(2)}, u32[]{:S(2)}) collective-permute-start(bf16[512,1024]{1,0:T(8,128)(2,1)} %refs_9_.4), channel_id=1, source_target_pairs={{0,4},{8,0},{16,8},{24,16},{28,24},{20,28},{12,20},{4,12},{1,5},{9... | collective-permute-start | bytes 3145736 | tf_op jit(solution)/shard_map/ppermute | solution.py:36
  27.7 34.0 %collective-permute-start.4 = (bf16[512,1024]{1,0:T(8,128)(2,1)}, bf16[512,1024]{1,0:T(8,128)(2,1)}, u32[]{:S(2)}, u32[]{:S(2)}) collective-permute-start(bf16[512,1024]{1,0:T(8,128)(2,1)} %refs_9_.5), channel_id=1, source_target_pairs={{0,8},{8,16},{16,24},{24,28},{28,20},{20,12},{12,4},{4,0},{1,9},{9... | collective-permute-start | bytes 3145736 | tf_op jit(solution)/shard_map/ppermute | solution.py:36
  29.8 32.0 %collective-permute-start.5 = (bf16[512,1024]{1,0:T(8,128)(2,1)}, bf16[512,1024]{1,0:T(8,128)(2,1)}, u32[]{:S(2)}, u32[]{:S(2)}) collective-permute-start(bf16[512,1024]{1,0:T(8,128)(2,1)} %refs_9_.5), channel_id=1, source_target_pairs={{0,4},{8,0},{16,8},{24,16},{28,24},{20,28},{12,20},{4,12},{1,5},{9... | collective-permute-start | bytes 3145736 | tf_op jit(solution)/shard_map/ppermute | solution.py:36
  46.3 33.9 %collective-permute-start.2 = (bf16[512,1024]{1,0:T(8,128)(2,1)}, bf16[512,1024]{1,0:T(8,128)(2,1)}, u32[]{:S(2)}, u32[]{:S(2)}) collective-permute-start(bf16[512,1024]{1,0:T(8,128)(2,1)} %collective-permute-done.refs_10_), channel_id=1, source_target_pairs={{0,8},{8,16},{16,24},{24,28},{28,20},{20,12},{12,4},{4,0},{1,9},{9... | collective-permute-start | bytes 3145736 | tf_op jit(solution)/shard_map/ppermute | solution.py:36
  48.3 31.9 %collective-permute-start.3 = (bf16[512,1024]{1,0:T(8,128)(2,1)}, bf16[512,1024]{1,0:T(8,128)(2,1)}, u32[]{:S(2)}, u32[]{:S(2)}) collective-permute-start(bf16[512,1024]{1,0:T(8,128)(2,1)} %collective-permute-done.1.refs_11_), channel_id=1, source_target_pairs={{0,4},{8,0},{16,8},{24,16},{28,24},{20,28},{12,20},{4,12},{1,5},{9... | collective-permute-start | bytes 3145736 | tf_op jit(solution)/shard_map/ppermute | solution.py:36
  61.7 52.0 %collective-permute-start.8 = (bf16[512,1024]{1,0:T(8,128)(2,1)}, bf16[512,1024]{1,0:T(8,128)(2,1)}, u32[]{:S(2)}, u32[]{:S(2)}) collective-permute-start(bf16[512,1024]{1,0:T(8,128)(2,1)} %collective-permute-done.4.refs_10_), channel_id=1, source_target_pairs={{0,8},{8,16},{16,24},{24,28},{28,20},{20,12},{12,4},{4,0},{1,9},{9... | collective-permute-start | bytes 3145736 | tf_op jit(solution)/shard_map/ppermute | solution.py:36
  63.3 50.4 %collective-permute-start.9 = (bf16[512,1024]{1,0:T(8,128)(2,1)}, bf16[512,1024]{1,0:T(8,128)(2,1)}, u32[]{:S(2)}, u32[]{:S(2)}) collective-permute-start(bf16[512,1024]{1,0:T(8,128)(2,1)} %collective-permute-done.5.refs_11_), channel_id=1, source_target_pairs={{0,4},{8,0},{16,8},{24,16},{28,24},{20,28},{12,20},{4,12},{1,5},{9... | collective-permute-start | bytes 3145736 | tf_op jit(solution)/shard_map/ppermute | solution.py:36
  77.2 33.7 %collective-permute-start.11 = (bf16[8,64,512]{2,1,0:T(8,128)(2,1)S(1)}, bf16[8,64,512]{2,1,0:T(8,128)(2,1)S(1)}, u32[]{:S(2)}, u32[]{:S(2)}) collective-permute-start(bf16[8,64,512]{2,1,0:T(8,128)(2,1)S(1)} %select_convert_fusion.1), channel_id=1, source_target_pairs={{0,4},{4,0},{8,12},{12,8},{16,20},{20,16},{24,28},{28,24},{1,5},{5... | collective-permute-start | bytes 1572872 | tf_op jit(solution)/shard_map/ppermute | solution.py:589
  80.2 51.9 %collective-permute-start.6 = (bf16[512,1024]{1,0:T(8,128)(2,1)}, bf16[512,1024]{1,0:T(8,128)(2,1)}, u32[]{:S(2)}, u32[]{:S(2)}) collective-permute-start(bf16[512,1024]{1,0:T(8,128)(2,1)} %collective-permute-done.2.refs_12_), channel_id=1, source_target_pairs={{0,8},{8,16},{16,24},{24,28},{28,20},{20,12},{12,4},{4,0},{1,9},{9... | collective-permute-start | bytes 3145736 | tf_op jit(solution)/shard_map/ppermute | solution.py:36
  80.2 52.9 %collective-permute-start.7 = (bf16[512,1024]{1,0:T(8,128)(2,1)}, bf16[512,1024]{1,0:T(8,128)(2,1)}, u32[]{:S(2)}, u32[]{:S(2)}) collective-permute-start(bf16[512,1024]{1,0:T(8,128)(2,1)} %collective-permute-done.3.refs_13_), channel_id=1, source_target_pairs={{0,4},{8,0},{16,8},{24,16},{28,24},{20,28},{12,20},{4,12},{1,5},{9... | collective-permute-start | bytes 3145736 | tf_op jit(solution)/shard_map/ppermute | solution.py:36
  114.8 25.8 %collective-permute-start.14 = (bf16[8,64,512]{2,1,0:T(8,128)(2,1)}, bf16[8,64,512]{2,1,0:T(8,128)(2,1)}, u32[]{:S(2)}, u32[]{:S(2)}) collective-permute-start(bf16[8,64,512]{2,1,0:T(8,128)(2,1)} %add_convert_fusion.10), channel_id=1, source_target_pairs={{0,8},{4,12},{1,9},{5,13},{2,10},{6,14},{3,11},{7,15}} | collective-permute-start | bytes 1572872 | tf_op jit(solution)/shard_map/ppermute | solution.py:604
  137.3 31.9 %collective-permute-start.15 = (bf16[512,1024]{1,0:T(8,128)(2,1)}, bf16[512,1024]{1,0:T(8,128)(2,1)S(1)}, u32[]{:S(2)}, u32[]{:S(2)}) collective-permute-start(bf16[512,1024]{1,0:T(8,128)(2,1)} %collective-permute-done.8.refs_12_), channel_id=1, source_target_pairs={{0,8},{8,16},{16,24},{24,28},{28,20},{20,12},{12,4},{4,0},{1,9},{9... | collective-permute-start | bytes 3145736 | tf_op jit(solution)/shard_map/ppermute | solution.py:36
  137.4 31.9 %collective-permute-start.16 = (bf16[512,1024]{1,0:T(8,128)(2,1)}, bf16[512,1024]{1,0:T(8,128)(2,1)S(1)}, u32[]{:S(2)}, u32[]{:S(2)}) collective-permute-start(bf16[512,1024]{1,0:T(8,128)(2,1)} %collective-permute-done.9.refs_13_), channel_id=1, source_target_pairs={{0,4},{8,0},{16,8},{24,16},{28,24},{20,28},{12,20},{4,12},{1,5},{9... | collective-permute-start | bytes 3145736 | tf_op jit(solution)/shard_map/ppermute | solution.py:36
  149.5 23.6 %collective-permute-start.19 = (bf16[8,64,512]{2,1,0:T(8,128)(2,1)S(1)}, bf16[8,64,512]{2,1,0:T(8,128)(2,1)}, u32[]{:S(2)}, u32[]{:S(2)}) collective-permute-start(bf16[8,64,512]{2,1,0:T(8,128)(2,1)S(1)} %add_convert_fusion.9), channel_id=1, source_target_pairs={{8,16},{12,20},{9,17},{13,21},{10,18},{14,22},{11,19},{15,23}} | collective-permute-start | bytes 1572872 | tf_op jit(solution)/shard_map/ppermute | solution.py:604
  174.6 25.6 %collective-permute-start.20 = (bf16[4,64,1024]{2,1,0:T(8,128)(2,1)S(1)}, bf16[4,64,1024]{2,1,0:T(8,128)(2,1)}, u32[]{:S(2)}, u32[]{:S(2)}) collective-permute-start(bf16[4,64,1024]{2,1,0:T(8,128)(2,1)S(1)} %bitcast.115), channel_id=1, source_target_pairs={{0,8},{8,16},{16,24},{24,28},{28,20},{20,12},{12,4},{4,0},{1,9},{9... | collective-permute-start | bytes 1572872 | tf_op jit(solution)/shard_map/ppermute | solution.py:36
  176.7 23.6 %collective-permute-start.21 = (bf16[4,64,1024]{2,1,0:T(8,128)(2,1)S(1)}, bf16[4,64,1024]{2,1,0:T(8,128)(2,1)}, u32[]{:S(2)}, u32[]{:S(2)}) collective-permute-start(bf16[4,64,1024]{2,1,0:T(8,128)(2,1)S(1)} %bitcast.116), channel_id=1, source_target_pairs={{0,4},{8,0},{16,8},{24,16},{28,24},{20,28},{12,20},{4,12},{1,5},{9... | collective-permute-start | bytes 1572872 | tf_op jit(solution)/shard_map/ppermute | solution.py:36
  209.8 31.6 %collective-permute-start.27 = (bf16[4,64,1024]{2,1,0:T(8,128)(2,1)}, bf16[4,64,1024]{2,1,0:T(8,128)(2,1)S(1)}, u32[]{:S(2)}, u32[]{:S(2)}) collective-permute-start(bf16[4,64,1024]{2,1,0:T(8,128)(2,1)} %collective-permute-done.22.refs_1_), channel_id=1, source_target_pairs={{0,8},{8,16},{16,24},{24,28},{28,20},{20,12},{12,4},{4,0},{1,9},{9... | collective-permute-start | bytes 1572872 | tf_op jit(solution)/shard_map/ppermute | solution.py:36
  217.1 24.4 %collective-permute-start.28 = (bf16[4,64,1024]{2,1,0:T(8,128)(2,1)}, bf16[4,64,1024]{2,1,0:T(8,128)(2,1)S(1)}, u32[]{:S(2)}, u32[]{:S(2)}) collective-permute-start(bf16[4,64,1024]{2,1,0:T(8,128)(2,1)} %collective-permute-done.23.refs_2_), channel_id=1, source_target_pairs={{0,4},{8,0},{16,8},{24,16},{28,24},{20,28},{12,20},{4,12},{1,5},{9... | collective-permute-start | bytes 1572872 | tf_op jit(solution)/shard_map/ppermute | solution.py:36
  219.1 34.5 %collective-permute-start.30 = (bf16[4,64,1024]{2,1,0:T(8,128)(2,1)}, bf16[4,64,1024]{2,1,0:T(8,128)(2,1)S(1)}, u32[]{:S(2)}, u32[]{:S(2)}) collective-permute-start(bf16[4,64,1024]{2,1,0:T(8,128)(2,1)} %collective-permute-done.25.refs_3_), channel_id=1, source_target_pairs={{0,8},{8,16},{16,24},{24,28},{28,20},{20,12},{12,4},{4,0},{1,9},{9... | collective-permute-start | bytes 1572872 | tf_op jit(solution)/shard_map/ppermute | solution.py:36
  222.5 31.2 %collective-permute-start.31 = (bf16[4,64,1024]{2,1,0:T(8,128)(2,1)}, bf16[4,64,1024]{2,1,0:T(8,128)(2,1)S(1)}, u32[]{:S(2)}, u32[]{:S(2)}) collective-permute-start(bf16[4,64,1024]{2,1,0:T(8,128)(2,1)} %collective-permute-done.26.refs_4_), channel_id=1, source_target_pairs={{0,4},{8,0},{16,8},{24,16},{28,24},{20,28},{12,20},{4,12},{1,5},{9... | collective-permute-start | bytes 1572872 | tf_op jit(solution)/shard_map/ppermute | solution.py:36
  269.2 31.6 %collective-permute-start.40 = (bf16[512,1024]{1,0:T(8,128)(2,1)S(1)}, bf16[512,1024]{1,0:T(8,128)(2,1)S(1)}, u32[]{:S(2)}, u32[]{:S(2)}) collective-permute-start(bf16[512,1024]{1,0:T(8,128)(2,1)S(1)} %copy-done.16), channel_id=1, source_target_pairs={{0,8},{8,16},{16,24},{24,28},{28,20},{20,12},{12,4},{4,0},{1,9},{9... | collective-permute-start | bytes 3145736 | tf_op jit(solution)/shard_map/ppermute | solution.py:36
  271.2 29.6 %collective-permute-start.41 = (bf16[512,1024]{1,0:T(8,128)(2,1)S(1)}, bf16[512,1024]{1,0:T(8,128)(2,1)S(1)}, u32[]{:S(2)}, u32[]{:S(2)}) collective-permute-start(bf16[512,1024]{1,0:T(8,128)(2,1)S(1)} %copy-done.16), channel_id=1, source_target_pairs={{0,4},{8,0},{16,8},{24,16},{28,24},{20,28},{12,20},{4,12},{1,5},{9... | collective-permute-start | bytes 3145736 | tf_op jit(solution)/shard_map/ppermute | solution.py:36
  272.7 26.2 %collective-permute-start.38 = (bf16[2,64,1024]{2,1,0:T(8,128)(2,1)S(1)}, bf16[2,64,1024]{2,1,0:T(8,128)(2,1)S(1)}, u32[]{:S(2)}, u32[]{:S(2)}) collective-permute-start(bf16[2,64,1024]{2,1,0:T(8,128)(2,1)S(1)} %slice.207), channel_id=1, source_target_pairs={{0,8},{8,16},{16,24},{24,28},{28,20},{20,12},{12,4},{4,0},{1,9},{9... | collective-permute-start | bytes 786440 | tf_op jit(solution)/shard_map/ppermute | solution.py:36
  274.8 26.0 %collective-permute-start.39 = (bf16[2,64,1024]{2,1,0:T(8,128)(2,1)S(1)}, bf16[2,64,1024]{2,1,0:T(8,128)(2,1)S(1)}, u32[]{:S(2)}, u32[]{:S(2)}) collective-permute-start(bf16[2,64,1024]{2,1,0:T(8,128)(2,1)S(1)} %slice.208), channel_id=1, source_target_pairs={{0,4},{8,0},{16,8},{24,16},{28,24},{20,28},{12,20},{4,12},{1,5},{9... | collective-permute-start | bytes 786440 | tf_op jit(solution)/shard_map/ppermute | solution.py:36
  300.8 25.1 %collective-permute-start.42 = (bf16[512,1024]{1,0:T(8,128)(2,1)S(1)}, bf16[512,1024]{1,0:T(8,128)(2,1)S(1)}, u32[]{:S(2)}, u32[]{:S(2)}) collective-permute-start(bf16[512,1024]{1,0:T(8,128)(2,1)S(1)} %collective-permute-done.40.refs_8_), channel_id=1, source_target_pairs={{0,8},{8,16},{16,24},{24,28},{28,20},{20,12},{12,4},{4,0},{1,9},{9... | collective-permute-start | bytes 3145736 | tf_op jit(solution)/shard_map/ppermute | solution.py:36
  302.6 23.3 %collective-permute-start.43 = (bf16[512,1024]{1,0:T(8,128)(2,1)S(1)}, bf16[512,1024]{1,0:T(8,128)(2,1)}, u32[]{:S(2)}, u32[]{:S(2)}) collective-permute-start(bf16[512,1024]{1,0:T(8,128)(2,1)S(1)} %collective-permute-done.41.refs_9_), channel_id=1, source_target_pairs={{0,4},{8,0},{16,8},{24,16},{28,24},{20,28},{12,20},{4,12},{1,5},{9... | collective-permute-start | bytes 3145736 | tf_op jit(solution)/shard_map/ppermute | solution.py:36
  325.9 24.4 %collective-permute-start.44 = (bf16[512,1024]{1,0:T(8,128)(2,1)S(1)}, bf16[512,1024]{1,0:T(8,128)(2,1)S(1)}, u32[]{:S(2)}, u32[]{:S(2)}) collective-permute-start(bf16[512,1024]{1,0:T(8,128)(2,1)S(1)} %collective-permute-done.42.refs_10_), channel_id=1, source_target_pairs={{0,8},{8,16},{16,24},{24,28},{28,20},{20,12},{12,4},{4,0},{1,9},{9... | collective-permute-start | bytes 3145736 | tf_op jit(solution)/shard_map/ppermute | solution.py:36
  328.8 24.3 %collective-permute-start.48 = (f32[8,8,512]{2,1,0:T(8,128)S(1)}, f32[8,8,512]{2,1,0:T(8,128)S(1)}, u32[]{:S(2)}, u32[]{:S(2)}) collective-permute-start(f32[8,8,512]{2,1,0:T(8,128)S(1)} %constant_dynamic-update-slice_fusion), channel_id=1, source_target_pairs={{0,4},{4,0},{8,12},{12,8},{16,20},{20,16},{24,28},{28,24},{1,5},{5... | collective-permute-start | bytes 393224 | tf_op jit(solution)/shard_map/ppermute | solution.py:96
  350.4 22.7 %collective-permute-start.46 = (bf16[256,1024]{1,0:T(8,128)(2,1)S(1)}, bf16[256,1024]{1,0:T(8,128)(2,1)S(1)}, u32[]{:S(2)}, u32[]{:S(2)}) collective-permute-start(bf16[256,1024]{1,0:T(8,128)(2,1)S(1)} %slice.209), channel_id=1, source_target_pairs={{0,8},{8,16},{16,24},{24,28},{28,20},{20,12},{12,4},{4,0},{1,9},{9... | collective-permute-start | bytes 1572872 | tf_op jit(solution)/shard_map/ppermute | solution.py:36
  426.4 22.9 %collective-permute-start.62 = (f32[8,8,512]{2,1,0:T(8,128)S(1)}, f32[8,8,512]{2,1,0:T(8,128)S(1)}, u32[]{:S(2)}, u32[]{:S(2)}) collective-permute-start(f32[8,8,512]{2,1,0:T(8,128)S(1)} %add.234), channel_id=1, source_target_pairs={{0,8},{4,12},{8,0},{12,4},{16,24},{20,28},{24,16},{28,20},{1,9},{5... | collective-permute-start | bytes 393224 | tf_op jit(solution)/shard_map/ppermute | solution.py:96
  446.0 22.7 %collective-permute-start.68 = (bf16[4,64,1024]{2,1,0:T(8,128)(2,1)}, bf16[4,64,1024]{2,1,0:T(8,128)(2,1)}, u32[]{:S(2)}, u32[]{:S(2)}) collective-permute-start(bf16[4,64,1024]{2,1,0:T(8,128)(2,1)} %add_convert_fusion.3), channel_id=1, source_target_pairs={{0,8},{8,16},{16,24},{24,28},{28,20},{20,12},{12,4},{4,0},{1,9},{9... | collective-permute-start | bytes 1572872 | tf_op jit(solution)/shard_map/ppermute | solution.py:36
  (88 other events, 1332.5 us)

commit v8 on v7

--- a/solution.py
+++ b/solution.py
@@ -18,6 +18,7 @@
 DEAD = -1e30
 GROUPS = 2
 VMEM_BYTES = 56 * 1024 * 1024
+LIGHT = pl.CostEstimate(flops=0, bytes_accessed=0, transcendentals=0)
 
 
 def ring_order(count):
@@ -179,11 +180,7 @@
         ),
         out_shape=jax.ShapeDtypeStruct((tokens, width), kind),
         compiler_params=pltpu.CompilerParams(vmem_limit_bytes=VMEM_BYTES),
-        cost_estimate=pl.CostEstimate(
-            flops=2 * tokens * sum(piece.shape[0] for _, _, piece in pieces) * width,
-            bytes_accessed=2 * (tokens + width) * value.shape[1],
-            transcendentals=0,
-        ),
+        cost_estimate=LIGHT,
         name="project",
     )(places, *[value] * len(pieces), *[piece for _, _, piece in pieces], cosine, sine, *base)
 
@@ -251,11 +248,7 @@
         ],
         scratch_shapes=[pltpu.VMEM((tokens, D), jnp.bfloat16)],
         compiler_params=pltpu.CompilerParams(vmem_limit_bytes=VMEM_BYTES),
-        cost_estimate=pl.CostEstimate(
-            flops=2 * tokens * D * width,
-            bytes_accessed=2 * D * (width + tokens) + 4 * tokens * width,
-            transcendentals=tokens * width,
-        ),
+        cost_estimate=LIGHT,
         name="enter_mixer",
     )(flat_input, norm_gain.reshape(1, D), w_bc, w_dt, dt_bias.reshape(1, heads), weight)
 
@@ -329,11 +322,7 @@
             jax.ShapeDtypeStruct((requests, 1, inner), jnp.float32),
         ],
         compiler_params=pltpu.CompilerParams(vmem_limit_bytes=VMEM_BYTES),
-        cost_estimate=pl.CostEstimate(
-            flops=12 * requests * tokens * tokens * inner,
-            bytes_accessed=16 * requests * tokens * inner,
-            transcendentals=requests * tokens * tokens * heads,
-        ),
+        cost_estimate=LIGHT,
         name="inside_block",
     )(act, maps, decay, size, decay_row, size_row, skip)
 
@@ -379,11 +368,7 @@
             jax.ShapeDtypeStruct((requests, STATE, inner), jnp.float32),
         ],
         compiler_params=pltpu.CompilerParams(vmem_limit_bytes=VMEM_BYTES),
-        cost_estimate=pl.CostEstimate(
-            flops=2 * requests * tokens * STATE * inner,
-            bytes_accessed=24 * requests * tokens * inner,
-            transcendentals=requests * tokens * heads,
-        ),
+        cost_estimate=LIGHT,
         name="leave_mixer",
     )(entry, maps, decay, read, act, gain, local, through)
 
@@ -467,11 +452,7 @@
             jax.ShapeDtypeStruct((requests, heads, tokens), jnp.float32),
         ],
         compiler_params=pltpu.CompilerParams(vmem_limit_bytes=VMEM_BYTES),
-        cost_estimate=pl.CostEstimate(
-            flops=4 * requests * tokens * cache_block * width,
-            bytes_accessed=2 * requests * width * (3 * tokens + 2 * cache_block),
-            transcendentals=requests * tokens * cache_block * heads,
-        ),
+        cost_estimate=LIGHT,
         name="cache_part",
     )(first, places, live, *query_slots, keys, values, new_keys)
 
@@ -527,11 +508,7 @@
         out_shape=[jax.ShapeDtypeStruct((requests, heads, tokens), jnp.float32)]
         + [jax.ShapeDtypeStruct((requests, tok_block, width), jnp.bfloat16)] * slots,
         compiler_params=pltpu.CompilerParams(vmem_limit_bytes=VMEM_BYTES),
-        cost_estimate=pl.CostEstimate(
-            flops=4 * requests * tokens * tok_block * width,
-            bytes_accessed=6 * requests * width * tokens,
-            transcendentals=requests * tokens * tok_block * heads,
-        ),
+        cost_estimate=LIGHT,
         name="finish_part",
     )(first, places, queries, new_keys, new_values, cached, peaks, totals, best)
 
@@ -773,9 +750,18 @@
         ) * lax.rsqrt(squares / D_INNER + 1e-05)
         return (made["terms"],), ()
 
-    def leave_chain():
-        chain = clock.hold(made["chain"]).reshape(requests, STATE, local_mheads, MHEAD_DIM)
-        made["chain"] = jnp.transpose(chain, (0, 2, 3, 1)).reshape(
+    def chain_split():
+        made["chain"] = clock.hold(made["chain"]).reshape(
+            requests, STATE, local_mheads, MHEAD_DIM
+        )
+        return (made["chain"],), ()
+
+    def chain_turn():
+        made["chain"] = jnp.transpose(clock.hold(made["chain"]), (0, 2, 3, 1))
+        return (made["chain"],), ()
+
+    def chain_join():
+        made["chain"] = clock.hold(made["chain"]).reshape(
             requests, 1, local_mheads, MHEAD_DIM * STATE
         )
         return (made["chain"],), ()
@@ -824,16 +810,16 @@
         peaks = jnp.concatenate([clock.hold(part[2]) for part in cached], axis=0)
         made["best"] = Exchange(peaks, "seq", seq_count, jnp.maximum)
         made["best"].step(clock)
-        return leave_chain()
-
-    def make_values():
+        pieces = value_ring.pieces[1:-2]
+        made["used"] = 1 + len(pieces)
+        made["values"] = product(
+            [(0, 0, clock.hold(value_ring.block))] + pieces, False, kind=jnp.float32
+        )
+        return (made["values"],), ()
+
+    def join_more():
         made["best"].step(clock)
-        made["values"] = product(
-            [(0, 0, clock.hold(value_ring.block))] + value_ring.pieces[1:-2],
-            False,
-            kind=jnp.float32,
-        )
-        return (made["values"],), ()
+        return leave_terms()
 
     def steps(rings, begin, end):
         return [ring for _ in range(begin, end) for ring in rings]
@@ -858,16 +844,18 @@
     run(both, works + [None] * (len(both) - 1 - len(works)) + [make_queries_hop])
     run(
         steps(slot_rings, 0, half),
-        [None, make_keys_hop, None, end_relay, None, leave, join_squares, leave_terms],
+        [None, make_keys_hop, None, end_relay, None, leave, join_squares],
     )
     run(
         steps([value_ring], 0, half),
-        [meet_cache(0), meet_cache(1)] + [None] * (half - 4) + [join_peaks, make_values],
+        [meet_cache(0), meet_cache(1)] + [None] * (half - 4) + [join_peaks, join_more],
     )
 
     new_keys = made["keys"]
     best = made["best"].result(clock)
-    new_values = by_request(product(value_ring.pieces[-2:], False, base=(made["values"],)))
+    new_values = by_request(
+        product(value_ring.pieces[made["used"] :], False, base=(made["values"],))
+    )
 
     own = lambda stat: lax.dynamic_slice_in_dim(stat, seq_index * tok_block, tok_block, 2)
     greatest_logit = jnp.transpose(own(best), (0, 2, 1)) * SCALE
@@ -907,7 +895,10 @@
 
     run([], [finish(0)])
     run([ring_sums[0]], [finish(1)])
-    run(steps(ring_sums[::-1], 0, half)[:-1], [add_sums, None, add_sums, None, add_sums])
+    run(
+        steps(ring_sums[::-1], 0, half)[:-1],
+        [add_sums, chain_split, add_sums, chain_turn, add_sums, chain_join],
+    )
     denominators = jnp.transpose(own(made["sums"].result(clock)), (0, 2, 1))
     for index in range(GROUPS):
         begin = index * group

time: 526 us -> 524 us (level)
  other arithmetic: 38 us -> 50.7 us
  waiting for transfers between devices: 171 us -> 164 us
  starting transfers between devices: 97 us -> 90.2 us
    ppermute x1, waiting for transfers between devices: 11.8 us -> 32.7 us  [__init__(): other_factor = side(lax.ppermute(through, 'seq', self.swap))]
    ppermute x2, waiting for transfers between devices: 36 us -> 15.4 us  [exchange(): lax.ppermute(value.astype(jnp.bfloat16), 'seq', self.swap)]
    ppermute x56, waiting for transfers between devices: 97.5 us -> 87.4 us  [ring_step(): return lax.ppermute(block, 'seq', route)]
    ppermute x8, waiting for transfers between devices: 19.2 us -> 28.4 us  [step(): self.got = lax.ppermute(self.value, self.axis, route)]
    ppermute x56, starting transfers between devices: 75.6 us -> 67.7 us  [ring_step(): return lax.ppermute(block, 'seq', route)]
    ppermute x2, waiting for transfers between devices: 6.04 us -> 0.01 us  [head_sum(): lax.ppermute(give.astype(jnp.bfloat16), 'head', [(h, h ^ 2) for h in rang...]
    optimization_barrier x0 -> x1, local copies, waits for them, and re-layouts: none -> 5.56 us  [hold(): held = lax.optimization_barrier(tuple(values) + (self.mark,))[:len(values)]]
    transpose x1 -> x0, local copies, waits for them, and re-layouts: 5.54 us -> none  [leave_chain(): jnp.transpose(chain, (0, 2, 3, 1))]
  transfers between devices with their start and end apart: 74 -> 74, of which waited for: 34 -> 27; matrix products, arithmetic and copies ran while one was open for 20% -> 22% of each run, Pallas kernels for 20% -> 22%
where the time goes in v8:
time: 524 us; the launch traced here: 514 us
  waiting for transfers between devices  164 us (31%)
  Pallas kernels  133 us (25%)
  starting transfers between devices  90.2 us (17%)
  local copies, waits for them, and re-layouts  63.8 us (12%)
  other arithmetic  50.7 us (10%)
  matrix products  10.5 us (2%)
    ppermute x56, waiting for transfers between devices, ring_step(): return lax.ppermute(block, 'seq', route)  87.4 us
    ppermute x56, starting transfers between devices, ring_step(): return lax.ppermute(block, 'seq', route)  67.7 us
    pallas_call x2, Pallas kernels, cache_part(): pl.pallas_call(functools.partial(cache_kernel, slots), grid_spec=pltpu.Pr...  44.1 us
    pallas_call x4, Pallas kernels, project(): pl.pallas_call(functools.partial(project_kernel, len(pieces), turned), gr...  36 us
    ppermute x1, waiting for transfers between devices, __init__(): other_factor = side(lax.ppermute(through, 'seq', self.swap))  32.7 us
    ppermute x8, waiting for transfers between devices, step(): self.got = lax.ppermute(self.value, self.axis, route)  28.4 us
    pallas_call x2, Pallas kernels, finish_part(): pl.pallas_call(functools.partial(finish_kernel, slots), grid_spec=pltpu.P...  22.7 us
    unnamed x126, local copies, waits for them, and re-layouts  18.4 us
  transfers between devices with their start and end apart: 74, of which 27 were waited for; matrix products, arithmetic and copies ran while one was open for 22% of the time, Pallas kernels for 22%

profile of v8, /device:TPU:0, one launch (start us, length us, event | category | flops | bytes accessed | tf_op | source)
XLA Modules:
  0.0 514.3 jit_solution(926325060638939290)
XLA Ops:
  3.7 10.5 %copy.52 = bf16[256,8,2,1024]{3,1,2,0:T(8,128)(2,1)} copy(bf16[256,8,2,1024]{3,2,1,0:T(2,128)(2,1)} %bitcast.104) | data formatting | bytes 16777216
  17.2 5.6 %copy.40 = f32[8,16,64,64]{2,1,3,0:T(8,128)} copy(f32[8,16,64,64]{3,2,1,0:T(8,128)} %reshape.124) | data formatting | bytes 4194304 | tf_op jit(solution)/shard_map/reshape | solution.py:673
  22.8 4.9 reshape.125
  30.8 11.7 %enter_mixer.1 = (f32[512,2048]{1,0:T(8,128)}, f32[512,128]{1,0:T(8,128)}, f32[512,16]{1,0:T(8,128)}) custom-call(bf16[512,4096]{1,0:T(8,128)(2,1)} %bitcast.64, f32[1,2048]{1,0:T(1,128)} %bitcast.122, bf16[2048,128]{1,0:T(8,128)(2,1)} %bc_ref.1, bf16[2048,16]{1,0:T(8,128)(2,1)} %copy.41.dt_ref, f32[1,16]{1,0:T(1,128)} %bitcast.127, bf16[2048,2048]{1,0:T(8,128)(2,1)} %bitcast.93), custom_call_target="tpu_custom_call" | custom-call | tf_op jit(solution)/shard_map/enter_mixer/pallas_call | solution.py:228
  49.9 9.6 %inside_block.1 = (f32[512,1024]{1,0:T(8,128)}, f32[8,64,1024]{2,1,0:T(8,128)}, f32[8,1,1024]{2,1,0:T(1,128)}) custom-call(f32[512,2048]{1,0:T(8,128)} %get-tuple-element.169.inner_ref.gate_ref, f32[512,128]{1,0:T(8,128)} %get-tuple-element.170.map_ref, f32[8,64,16]{2,1,0:T(8,128)} %bitcast.107, f32[8,64,16]{2,1,0:T(8,128)} %bitcast.111, ...), custom_call_target="tpu_custom_call" | custom-call | tf_op jit(solution)/shard_map/inside_block/pallas_call | solution.py:302
  65.3 32.7 %collective-permute-done.10 = f32[8,1,1024]{2,1,0:T(1,128)S(1)} collective-permute-done((f32[8,1,1024]{2,1,0:T(1,128)}, f32[8,1,1024]{2,1,0:T(1,128)S(1)}, u32[]{:S(2)}, u32[]{:S(2)}) %collective-permute-start.10) | collective-permute-done | bytes 32800 | tf_op jit(solution)/shard_map/ppermute | solution.py:555
  105.1 7.8 %collective-permute-done.11 = bf16[8,64,512]{2,1,0:T(8,128)(2,1)S(1)} collective-permute-done((bf16[8,64,512]{2,1,0:T(8,128)(2,1)S(1)}, bf16[8,64,512]{2,1,0:T(8,128)(2,1)S(1)}, u32[]{:S(2)}, u32[]{:S(2)}) %collective-permute-start.11) | collective-permute-done | bytes 524320 | tf_op jit(solution)/shard_map/ppermute | solution.py:566
  118.6 14.4 %collective-permute-done.6.refs_14_ = bf16[512,1024]{1,0:T(8,128)(2,1)S(1)} collective-permute-done((bf16[512,1024]{1,0:T(8,128)(2,1)}, bf16[512,1024]{1,0:T(8,128)(2,1)S(1)}, u32[]{:S(2)}, u32[]{:S(2)}) %collective-permute-start.6) | collective-permute-done | bytes 1048608 | tf_op jit(solution)/shard_map/ppermute | solution.py:37
  142.1 9.7 %collective-permute-done.12.refs_16_ = bf16[256,1024]{1,0:T(8,128)(2,1)} collective-permute-done((bf16[256,1024]{1,0:T(8,128)(2,1)}, bf16[256,1024]{1,0:T(8,128)(2,1)}, u32[]{:S(2)}, u32[]{:S(2)}) %collective-permute-start.12) | collective-permute-done | bytes 524320 | tf_op jit(solution)/shard_map/ppermute | solution.py:37
  157.6 10.4 %project.4 = bf16[512,1024]{1,0:T(8,128)(2,1)} custom-call(s32[8]{0:T(128)} %fusion.21.places_ref.place_ref, bf16[512,4096]{1,0:T(8,128)(2,1)} %bitcast.65, bf16[512,4096]{1,0:T(8,128)(2,1)} %bitcast.66, bf16[512,4096]{1,0:T(8,128)(2,1)} %bitcast.67, bf16[512,4096]{1,0:T(8,128)(2,1)} %bitcast.68, bf16[512,4096]{1,0:T(8,128)(2,1)} %bitcast.69, ...), custom_call_target="tpu_custom_call" | custom-call | tf_op jit(solution)/shard_map/project/pallas_call | solution.py:170
  180.6 7.5 %collective-permute-done.17.refs_16_ = bf16[256,1024]{1,0:T(8,128)(2,1)S(1)} collective-permute-done((bf16[256,1024]{1,0:T(8,128)(2,1)S(1)}, bf16[256,1024]{1,0:T(8,128)(2,1)S(1)}, u32[]{:S(2)}, u32[]{:S(2)}) %collective-permute-start.17) | collective-permute-done | bytes 524320 | tf_op jit(solution)/shard_map/ppermute | solution.py:37
  194.3 10.6 %project.5 = bf16[512,1024]{1,0:T(8,128)(2,1)} custom-call(s32[8]{0:T(128)} %fusion.21.places_ref.place_ref, bf16[512,4096]{1,0:T(8,128)(2,1)} %bitcast.78, bf16[512,4096]{1,0:T(8,128)(2,1)} %bitcast.75, bf16[512,4096]{1,0:T(8,128)(2,1)} %bitcast.76, bf16[512,4096]{1,0:T(8,128)(2,1)} %bitcast.77, bf16[512,4096]{1,0:T(8,128)(2,1)} %bitcast.74, ...), custom_call_target="tpu_custom_call" | custom-call | tf_op jit(solution)/shard_map/project/pallas_call | solution.py:170
  212.3 6.4 %collective-permute-start.27 = (bf16[4,64,1024]{2,1,0:T(8,128)(2,1)S(1)}, bf16[4,64,1024]{2,1,0:T(8,128)(2,1)S(1)}, u32[]{:S(2)}, u32[]{:S(2)}) collective-permute-start(bf16[4,64,1024]{2,1,0:T(8,128)(2,1)S(1)} %collective-permute-done.22.refs_1_), channel_id=1, source_target_pairs={{0,8},{8,16},{16,24},{24,28},{28,20},{20,12},{12,4},{4,0},{1,9},{9... | collective-permute-start | bytes 1572872 | tf_op jit(solution)/shard_map/ppermute | solution.py:37
  225.1 7.6 %collective-permute-done.29 = bf16[8,64,512]{2,1,0:T(8,128)(2,1)S(1)} collective-permute-done((bf16[8,64,512]{2,1,0:T(8,128)(2,1)S(1)}, bf16[8,64,512]{2,1,0:T(8,128)(2,1)S(1)}, u32[]{:S(2)}, u32[]{:S(2)}) %collective-permute-start.29) | collective-permute-done | bytes 524320 | tf_op jit(solution)/shard_map/ppermute | solution.py:566
  234.6 9.4 %collective-permute-done.27.refs_3_ = bf16[4,64,1024]{2,1,0:T(8,128)(2,1)S(1)} collective-permute-done((bf16[4,64,1024]{2,1,0:T(8,128)(2,1)S(1)}, bf16[4,64,1024]{2,1,0:T(8,128)(2,1)S(1)}, u32[]{:S(2)}, u32[]{:S(2)}) %collective-permute-start.27) | collective-permute-done | bytes 524320 | tf_op jit(solution)/shard_map/ppermute | solution.py:37
  246.0 8.9 %leave_mixer.1 = (bf16[512,1024]{1,0:T(8,128)(2,1)}, f32[512,128]{1,0:T(8,128)}, f32[8,64,1024]{2,1,0:T(8,128)}) custom-call(f32[8,64,1024]{2,1,0:T(8,128)} %pad_maximum_fusion.entry_ref, f32[512,128]{1,0:T(8,128)} %get-tuple-element.170.map_ref, f32[8,64,16]{2,1,0:T(8,128)} %bitcast.108, f32[512,1024]{1,0:T(8,128)} %get-tuple-element.171.read_ref, ...), custom_call_target="tpu_custom_call" | custom-call | tf_op jit(solution)/shard_map/leave_mixer/pallas_call | solution.py:351
  257.3 8.2 %collective-permute-done.32.refs_5_ = bf16[4,64,1024]{2,1,0:T(8,128)(2,1)S(1)} collective-permute-done((bf16[4,64,1024]{2,1,0:T(8,128)(2,1)S(1)}, bf16[4,64,1024]{2,1,0:T(8,128)(2,1)S(1)}, u32[]{:S(2)}, u32[]{:S(2)}) %collective-permute-start.32) | collective-permute-done | bytes 524320 | tf_op jit(solution)/shard_map/ppermute | solution.py:37
  275.0 22.0 %cache_part.2 = (bf16[4,512,1024]{2,1,0:T(8,128)(2,1)}, bf16[4,1024,512]{2,1,0:T(8,128)(2,1)}, f32[4,8,512]{2,1,0:T(8,128)}, f32[4,8,512]{2,1,0:T(8,128)}) custom-call(s32[1]{0:T(128)} %bitcast.1.first_ref, s32[8]{0:T(128)} %fusion.21.places_ref.place_ref, s32[4]{0:T(128)} %get-tuple-element.336.live_ref, bf16[4,64,1024]{2,1,0:T(8,128)(2,1)} %bitcast.117, ...), custom_call_target="tpu_custom_call" | custom-call | tf_op jit(solution)/shard_map/cache_part/pallas_call | solution.py:433
  301.1 22.1 %cache_part.3 = (bf16[4,512,1024]{2,1,0:T(8,128)(2,1)}, bf16[4,1024,512]{2,1,0:T(8,128)(2,1)}, f32[4,8,512]{2,1,0:T(8,128)}, f32[4,8,512]{2,1,0:T(8,128)}) custom-call(s32[1]{0:T(128)} %bitcast.1.first_ref, s32[8]{0:T(128)} %fusion.21.places_ref.place_ref, s32[4]{0:T(128)} %get-tuple-element.335.live_ref, bf16[4,64,1024]{2,1,0:T(8,128)(2,1)} %bitcast.114, ...), custom_call_target="tpu_custom_call" | custom-call | tf_op jit(solution)/shard_map/cache_part/pallas_call | solution.py:433
  330.5 8.1 %project.6.refs_10_ = f32[512,1024]{1,0:T(8,128)} custom-call(s32[8]{0:T(128)} %fusion.21.places_ref.place_ref, bf16[512,4096]{1,0:T(8,128)(2,1)} %bitcast.83, bf16[512,4096]{1,0:T(8,128)(2,1)} %bitcast.84, bf16[512,4096]{1,0:T(8,128)(2,1)} %bitcast.85, bf16[512,4096]{1,0:T(8,128)(2,1)} %bitcast.86, bf16[512,4096]{1,0:T(8,128)(2,1)} %bitcast.87, ...), custom_call_target="tpu_custom_call" | custom-call | tf_op jit(solution)/shard_map/project/pallas_call | solution.py:170
  338.6 8.2 %collective-permute-done.48 = f32[8,8,512]{2,1,0:T(8,128)S(1)} collective-permute-done((f32[8,8,512]{2,1,0:T(8,128)S(1)}, f32[8,8,512]{2,1,0:T(8,128)S(1)}, u32[]{:S(2)}, u32[]{:S(2)}) %collective-permute-start.48) | collective-permute-done | bytes 131104 | tf_op jit(solution)/shard_map/ppermute | solution.py:97
  349.4 6.6 %convolution_multiply_fusion = f32[512,2048]{1,0:T(8,128)} fusion(bf16[512,1024]{1,0:T(8,128)(2,1)S(1)} %copy-done.58, bf16[1024,2048]{1,0:T(8,128)(2,1)} %param.35, f32[512]{0:T(512)S(1)} %bitcast.126), kind=kOutput, calls=%fused_computation | convolution fusion | flops 2148532224 | bytes 9439232 | tf_op jit(solution)/shard_map/dot_general | solution.py:748
  356.0 5.4 %collective-permute-start.50 = (f32[8,8,512]{2,1,0:T(8,128)S(1)}, f32[8,8,512]{2,1,0:T(8,128)S(1)}, u32[]{:S(2)}, u32[]{:S(2)}) collective-permute-start(f32[8,8,512]{2,1,0:T(8,128)S(1)} %max.17), channel_id=1, source_target_pairs={{0,16},{4,20},{8,24},{12,28},{16,0},{20,4},{24,8},{28,12},{1,17},{... | collective-permute-start | bytes 393224 | tf_op jit(solution)/shard_map/ppermute | solution.py:97
  368.1 6.8 %project.7 = bf16[512,1024]{1,0:T(8,128)(2,1)} custom-call(s32[8]{0:T(128)} %fusion.21.places_ref.place_ref, bf16[512,4096]{1,0:T(8,128)(2,1)} %bitcast.88, bf16[512,4096]{1,0:T(8,128)(2,1)} %bitcast.89, bf16[512,4096]{1,0:T(8,128)(2,1)} %bitcast.90, bf16[512,4096]{1,0:T(8,128)(2,1)} %bitcast.91, bf16[512,1024]{1,0:T(8,128)(2,1)} %copy-done.12, ...), custom_call_target="tpu_custom_call" | custom-call | tf_op jit(solution)/shard_map/project/pallas_call | solution.py:170
  374.9 11.2 %finish_part.2 = (f32[4,8,512]{2,1,0:T(8,128)}, bf16[4,64,1024]{2,1,0:T(8,128)(2,1)}, bf16[4,64,1024]{2,1,0:T(8,128)(2,1)}, bf16[4,64,1024]{2,1,0:T(8,128)(2,1)}...) custom-call(s32[1]{0:T(128)} %bitcast.1.first_ref, ...), custom_call_target="tpu_custom_call" | custom-call | tf_op jit(solution)/shard_map/finish_part/pallas_call | solution.py:491
  387.5 11.4 %finish_part.3 = (f32[4,8,512]{2,1,0:T(8,128)}, bf16[4,64,1024]{2,1,0:T(8,128)(2,1)}, bf16[4,64,1024]{2,1,0:T(8,128)(2,1)}, bf16[4,64,1024]{2,1,0:T(8,128)(2,1)}...) custom-call(s32[1]{0:T(128)} %bitcast.1.first_ref, ...), custom_call_target="tpu_custom_call" | custom-call | tf_op jit(solution)/shard_map/finish_part/pallas_call | solution.py:491
  422.8 9.8 %collective-permute-done.63 = f32[8,8,512]{2,1,0:T(8,128)S(1)} collective-permute-done((f32[8,8,512]{2,1,0:T(8,128)S(1)}, f32[8,8,512]{2,1,0:T(8,128)S(1)}, u32[]{:S(2)}, u32[]{:S(2)}) %collective-permute-start.63) | collective-permute-done | bytes 131104 | tf_op jit(solution)/shard_map/ppermute | solution.py:97
  432.8 4.9 collective-permute-done.64
  451.8 6.1 %collective-permute-done.57 = bf16[4,64,1024]{2,1,0:T(8,128)(2,1)} collective-permute-done((bf16[4,64,1024]{2,1,0:T(8,128)(2,1)}, bf16[4,64,1024]{2,1,0:T(8,128)(2,1)}, u32[]{:S(2)}, u32[]{:S(2)}) %collective-permute-start.57) | collective-permute-done | bytes 524320 | tf_op jit(solution)/shard_map/ppermute | solution.py:37
  473.9 5.0 collective-permute-done.62
  500.7 5.6 %copy.47 = f32[8,16,64,64]{3,2,1,0:T(8,128)} copy(f32[8,16,64,64]{2,1,3,0:T(8,128)} %bitcast.99) | data formatting | bytes 4194304 | tf_op jit(solution)/shard_map/optimization_barrier | solution.py:72
  506.3 4.8 reshape.140
  (358 shorter events, 198.2 us)
Async XLA Ops:
  0.6 45.7 %collective-permute-start = (bf16[512,1024]{1,0:T(8,128)(2,1)}, bf16[512,1024]{1,0:T(8,128)(2,1)}, u32[]{:S(2)}, u32[]{:S(2)}) collective-permute-start(bf16[512,1024]{1,0:T(8,128)(2,1)} %refs_9_.4), channel_id=1, source_target_pairs={{0,8},{8,16},{16,24},{24,28},{28,20},{20,12},{12,4},{4,0},{1,9},{9... | collective-permute-start | bytes 3145736 | tf_op jit(solution)/shard_map/ppermute | solution.py:37
  3.7 42.6 %collective-permute-start.1 = (bf16[512,1024]{1,0:T(8,128)(2,1)}, bf16[512,1024]{1,0:T(8,128)(2,1)}, u32[]{:S(2)}, u32[]{:S(2)}) collective-permute-start(bf16[512,1024]{1,0:T(8,128)(2,1)} %refs_9_.4), channel_id=1, source_target_pairs={{0,4},{8,0},{16,8},{24,16},{28,24},{20,28},{12,20},{4,12},{1,5},{9... | collective-permute-start | bytes 3145736 | tf_op jit(solution)/shard_map/ppermute | solution.py:37
  27.7 31.8 %collective-permute-start.4 = (bf16[512,1024]{1,0:T(8,128)(2,1)S(1)}, bf16[512,1024]{1,0:T(8,128)(2,1)}, u32[]{:S(2)}, u32[]{:S(2)}) collective-permute-start(bf16[512,1024]{1,0:T(8,128)(2,1)S(1)} %copy-done.22), channel_id=1, source_target_pairs={{0,8},{8,16},{16,24},{24,28},{28,20},{20,12},{12,4},{4,0},{1,9},{9... | collective-permute-start | bytes 3145736 | tf_op jit(solution)/shard_map/ppermute | solution.py:37
  29.7 29.8 %collective-permute-start.5 = (bf16[512,1024]{1,0:T(8,128)(2,1)S(1)}, bf16[512,1024]{1,0:T(8,128)(2,1)}, u32[]{:S(2)}, u32[]{:S(2)}) collective-permute-start(bf16[512,1024]{1,0:T(8,128)(2,1)S(1)} %copy-done.22), channel_id=1, source_target_pairs={{0,4},{8,0},{16,8},{24,16},{28,24},{20,28},{12,20},{4,12},{1,5},{9... | collective-permute-start | bytes 3145736 | tf_op jit(solution)/shard_map/ppermute | solution.py:37
  46.3 56.2 %collective-permute-start.2 = (bf16[512,1024]{1,0:T(8,128)(2,1)}, bf16[512,1024]{1,0:T(8,128)(2,1)}, u32[]{:S(2)}, u32[]{:S(2)}) collective-permute-start(bf16[512,1024]{1,0:T(8,128)(2,1)} %collective-permute-done.refs_10_), channel_id=1, source_target_pairs={{0,8},{8,16},{16,24},{24,28},{28,20},{20,12},{12,4},{4,0},{1,9},{9... | collective-permute-start | bytes 3145736 | tf_op jit(solution)/shard_map/ppermute | solution.py:37
  48.3 54.2 %collective-permute-start.3 = (bf16[512,1024]{1,0:T(8,128)(2,1)}, bf16[512,1024]{1,0:T(8,128)(2,1)}, u32[]{:S(2)}, u32[]{:S(2)}) collective-permute-start(bf16[512,1024]{1,0:T(8,128)(2,1)} %collective-permute-done.1.refs_11_), channel_id=1, source_target_pairs={{0,4},{8,0},{16,8},{24,16},{28,24},{20,28},{12,20},{4,12},{1,5},{9... | collective-permute-start | bytes 3145736 | tf_op jit(solution)/shard_map/ppermute | solution.py:37
  59.6 56.5 %collective-permute-start.8 = (bf16[512,1024]{1,0:T(8,128)(2,1)}, bf16[512,1024]{1,0:T(8,128)(2,1)}, u32[]{:S(2)}, u32[]{:S(2)}) collective-permute-start(bf16[512,1024]{1,0:T(8,128)(2,1)} %collective-permute-done.4.refs_10_), channel_id=1, source_target_pairs={{0,8},{8,16},{16,24},{24,28},{28,20},{20,12},{12,4},{4,0},{1,9},{9... | collective-permute-start | bytes 3145736 | tf_op jit(solution)/shard_map/ppermute | solution.py:37
  61.6 54.4 %collective-permute-start.9 = (bf16[512,1024]{1,0:T(8,128)(2,1)}, bf16[512,1024]{1,0:T(8,128)(2,1)}, u32[]{:S(2)}, u32[]{:S(2)}) collective-permute-start(bf16[512,1024]{1,0:T(8,128)(2,1)} %collective-permute-done.5.refs_11_), channel_id=1, source_target_pairs={{0,4},{8,0},{16,8},{24,16},{28,24},{20,28},{12,20},{4,12},{1,5},{9... | collective-permute-start | bytes 3145736 | tf_op jit(solution)/shard_map/ppermute | solution.py:37
  61.7 36.3 %collective-permute-start.10 = (f32[8,1,1024]{2,1,0:T(1,128)}, f32[8,1,1024]{2,1,0:T(1,128)S(1)}, u32[]{:S(2)}, u32[]{:S(2)}) collective-permute-start(f32[8,1,1024]{2,1,0:T(1,128)} %get-tuple-element.179.through_ref), channel_id=1, source_target_pairs={{0,4},{4,0},{8,12},{12,8},{16,20},{20,16},{24,28},{28,24},{1,5},{5... | collective-permute-start | bytes 98312 | tf_op jit(solution)/shard_map/ppermute | solution.py:555
  102.6 30.5 %collective-permute-start.6 = (bf16[512,1024]{1,0:T(8,128)(2,1)}, bf16[512,1024]{1,0:T(8,128)(2,1)S(1)}, u32[]{:S(2)}, u32[]{:S(2)}) collective-permute-start(bf16[512,1024]{1,0:T(8,128)(2,1)} %collective-permute-done.2.refs_12_), channel_id=1, source_target_pairs={{0,8},{8,16},{16,24},{24,28},{28,20},{20,12},{12,4},{4,0},{1,9},{9... | collective-permute-start | bytes 3145736 | tf_op jit(solution)/shard_map/ppermute | solution.py:37
  102.6 32.2 %collective-permute-start.7 = (bf16[512,1024]{1,0:T(8,128)(2,1)}, bf16[512,1024]{1,0:T(8,128)(2,1)S(1)}, u32[]{:S(2)}, u32[]{:S(2)}) collective-permute-start(bf16[512,1024]{1,0:T(8,128)(2,1)} %collective-permute-done.3.refs_13_), channel_id=1, source_target_pairs={{0,4},{8,0},{16,8},{24,16},{28,24},{20,28},{12,20},{4,12},{1,5},{9... | collective-permute-start | bytes 3145736 | tf_op jit(solution)/shard_map/ppermute | solution.py:37
  116.3 24.5 %collective-permute-start.14 = (bf16[8,64,512]{2,1,0:T(8,128)(2,1)S(1)}, bf16[8,64,512]{2,1,0:T(8,128)(2,1)}, u32[]{:S(2)}, u32[]{:S(2)}) collective-permute-start(bf16[8,64,512]{2,1,0:T(8,128)(2,1)S(1)} %add_convert_fusion.10), channel_id=1, source_target_pairs={{0,8},{4,12},{1,9},{5,13},{2,10},{6,14},{3,11},{7,15}} | collective-permute-start | bytes 1572872 | tf_op jit(solution)/shard_map/ppermute | solution.py:581
  138.8 32.3 %collective-permute-start.15 = (bf16[512,1024]{1,0:T(8,128)(2,1)}, bf16[512,1024]{1,0:T(8,128)(2,1)}, u32[]{:S(2)}, u32[]{:S(2)}) collective-permute-start(bf16[512,1024]{1,0:T(8,128)(2,1)} %collective-permute-done.8.refs_12_), channel_id=1, source_target_pairs={{0,8},{8,16},{16,24},{24,28},{28,20},{20,12},{12,4},{4,0},{1,9},{9... | collective-permute-start | bytes 3145736 | tf_op jit(solution)/shard_map/ppermute | solution.py:37
  138.9 33.3 %collective-permute-start.16 = (bf16[512,1024]{1,0:T(8,128)(2,1)}, bf16[512,1024]{1,0:T(8,128)(2,1)}, u32[]{:S(2)}, u32[]{:S(2)}) collective-permute-start(bf16[512,1024]{1,0:T(8,128)(2,1)} %collective-permute-done.9.refs_13_), channel_id=1, source_target_pairs={{0,4},{8,0},{16,8},{24,16},{28,24},{20,28},{12,20},{4,12},{1,5},{9... | collective-permute-start | bytes 3145736 | tf_op jit(solution)/shard_map/ppermute | solution.py:37
  152.9 24.1 %collective-permute-start.19 = (bf16[8,64,512]{2,1,0:T(8,128)(2,1)}, bf16[8,64,512]{2,1,0:T(8,128)(2,1)}, u32[]{:S(2)}, u32[]{:S(2)}) collective-permute-start(bf16[8,64,512]{2,1,0:T(8,128)(2,1)} %add_convert_fusion.9), channel_id=1, source_target_pairs={{8,16},{12,20},{9,17},{13,21},{10,18},{14,22},{11,19},{15,23}} | collective-permute-start | bytes 1572872 | tf_op jit(solution)/shard_map/ppermute | solution.py:581
  178.6 26.3 %collective-permute-start.20 = (bf16[4,64,1024]{2,1,0:T(8,128)(2,1)S(1)}, bf16[4,64,1024]{2,1,0:T(8,128)(2,1)S(1)}, u32[]{:S(2)}, u32[]{:S(2)}) collective-permute-start(bf16[4,64,1024]{2,1,0:T(8,128)(2,1)S(1)} %bitcast.115), channel_id=1, source_target_pairs={{0,8},{8,16},{16,24},{24,28},{28,20},{20,12},{12,4},{4,0},{1,9},{9... | collective-permute-start | bytes 1572872 | tf_op jit(solution)/shard_map/ppermute | solution.py:37
  180.6 24.3 %collective-permute-start.21 = (bf16[4,64,1024]{2,1,0:T(8,128)(2,1)S(1)}, bf16[4,64,1024]{2,1,0:T(8,128)(2,1)S(1)}, u32[]{:S(2)}, u32[]{:S(2)}) collective-permute-start(bf16[4,64,1024]{2,1,0:T(8,128)(2,1)S(1)} %bitcast.116), channel_id=1, source_target_pairs={{0,4},{8,0},{16,8},{24,16},{28,24},{20,28},{12,20},{4,12},{1,5},{9... | collective-permute-start | bytes 1572872 | tf_op jit(solution)/shard_map/ppermute | solution.py:37
  212.3 31.6 %collective-permute-start.27 = (bf16[4,64,1024]{2,1,0:T(8,128)(2,1)S(1)}, bf16[4,64,1024]{2,1,0:T(8,128)(2,1)S(1)}, u32[]{:S(2)}, u32[]{:S(2)}) collective-permute-start(bf16[4,64,1024]{2,1,0:T(8,128)(2,1)S(1)} %collective-permute-done.22.refs_1_), channel_id=1, source_target_pairs={{0,8},{8,16},{16,24},{24,28},{28,20},{20,12},{12,4},{4,0},{1,9},{9... | collective-permute-start | bytes 1572872 | tf_op jit(solution)/shard_map/ppermute | solution.py:37
  218.7 25.2 %collective-permute-start.28 = (bf16[4,64,1024]{2,1,0:T(8,128)(2,1)S(1)}, bf16[4,64,1024]{2,1,0:T(8,128)(2,1)S(1)}, u32[]{:S(2)}, u32[]{:S(2)}) collective-permute-start(bf16[4,64,1024]{2,1,0:T(8,128)(2,1)S(1)} %collective-permute-done.23.refs_2_), channel_id=1, source_target_pairs={{0,4},{8,0},{16,8},{24,16},{28,24},{20,28},{12,20},{4,12},{1,5},{9... | collective-permute-start | bytes 1572872 | tf_op jit(solution)/shard_map/ppermute | solution.py:37
  221.6 33.6 %collective-permute-start.30 = (bf16[4,64,1024]{2,1,0:T(8,128)(2,1)}, bf16[4,64,1024]{2,1,0:T(8,128)(2,1)S(1)}, u32[]{:S(2)}, u32[]{:S(2)}) collective-permute-start(bf16[4,64,1024]{2,1,0:T(8,128)(2,1)} %collective-permute-done.25.refs_3_), channel_id=1, source_target_pairs={{0,8},{8,16},{16,24},{24,28},{28,20},{20,12},{12,4},{4,0},{1,9},{9... | collective-permute-start | bytes 1572872 | tf_op jit(solution)/shard_map/ppermute | solution.py:37
  225.1 30.1 %collective-permute-start.31 = (bf16[4,64,1024]{2,1,0:T(8,128)(2,1)}, bf16[4,64,1024]{2,1,0:T(8,128)(2,1)S(1)}, u32[]{:S(2)}, u32[]{:S(2)}) collective-permute-start(bf16[4,64,1024]{2,1,0:T(8,128)(2,1)} %collective-permute-done.26.refs_4_), channel_id=1, source_target_pairs={{0,4},{8,0},{16,8},{24,16},{28,24},{20,28},{12,20},{4,12},{1,5},{9... | collective-permute-start | bytes 1572872 | tf_op jit(solution)/shard_map/ppermute | solution.py:37
  243.9 21.6 %collective-permute-start.32 = (bf16[4,64,1024]{2,1,0:T(8,128)(2,1)S(1)}, bf16[4,64,1024]{2,1,0:T(8,128)(2,1)S(1)}, u32[]{:S(2)}, u32[]{:S(2)}) collective-permute-start(bf16[4,64,1024]{2,1,0:T(8,128)(2,1)S(1)} %collective-permute-done.27.refs_3_), channel_id=1, source_target_pairs={{0,8},{8,16},{16,24},{24,28},{28,20},{20,12},{12,4},{4,0},{1,9},{9... | collective-permute-start | bytes 1572872 | tf_op jit(solution)/shard_map/ppermute | solution.py:37
  244.0 21.5 %collective-permute-start.33 = (bf16[4,64,1024]{2,1,0:T(8,128)(2,1)S(1)}, bf16[4,64,1024]{2,1,0:T(8,128)(2,1)S(1)}, u32[]{:S(2)}, u32[]{:S(2)}) collective-permute-start(bf16[4,64,1024]{2,1,0:T(8,128)(2,1)S(1)} %collective-permute-done.28.refs_4_), channel_id=1, source_target_pairs={{0,4},{8,0},{16,8},{24,16},{28,24},{20,28},{12,20},{4,12},{1,5},{9... | collective-permute-start | bytes 1572872 | tf_op jit(solution)/shard_map/ppermute | solution.py:37
  269.2 28.9 %collective-permute-start.38 = (bf16[512,1024]{1,0:T(8,128)(2,1)S(1)}, bf16[512,1024]{1,0:T(8,128)(2,1)S(1)}, u32[]{:S(2)}, u32[]{:S(2)}) collective-permute-start(bf16[512,1024]{1,0:T(8,128)(2,1)S(1)} %copy-done.23), channel_id=1, source_target_pairs={{0,8},{8,16},{16,24},{24,28},{28,20},{20,12},{12,4},{4,0},{1,9},{9... | collective-permute-start | bytes 3145736 | tf_op jit(solution)/shard_map/ppermute | solution.py:37
  269.3 28.9 %collective-permute-start.39 = (bf16[512,1024]{1,0:T(8,128)(2,1)S(1)}, bf16[512,1024]{1,0:T(8,128)(2,1)S(1)}, u32[]{:S(2)}, u32[]{:S(2)}) collective-permute-start(bf16[512,1024]{1,0:T(8,128)(2,1)S(1)} %copy-done.23), channel_id=1, source_target_pairs={{0,4},{8,0},{16,8},{24,16},{28,24},{20,28},{12,20},{4,12},{1,5},{9... | collective-permute-start | bytes 3145736 | tf_op jit(solution)/shard_map/ppermute | solution.py:37
  271.3 26.8 %collective-permute-start.36 = (bf16[2,64,1024]{2,1,0:T(8,128)(2,1)S(1)}, bf16[2,64,1024]{2,1,0:T(8,128)(2,1)S(1)}, u32[]{:S(2)}, u32[]{:S(2)}) collective-permute-start(bf16[2,64,1024]{2,1,0:T(8,128)(2,1)S(1)} %slice.207), channel_id=1, source_target_pairs={{0,8},{8,16},{16,24},{24,28},{28,20},{20,12},{12,4},{4,0},{1,9},{9... | collective-permute-start | bytes 786440 | tf_op jit(solution)/shard_map/ppermute | solution.py:37
  271.7 26.4 %collective-permute-start.37 = (bf16[2,64,1024]{2,1,0:T(8,128)(2,1)S(1)}, bf16[2,64,1024]{2,1,0:T(8,128)(2,1)S(1)}, u32[]{:S(2)}, u32[]{:S(2)}) collective-permute-start(bf16[2,64,1024]{2,1,0:T(8,128)(2,1)S(1)} %slice.208), channel_id=1, source_target_pairs={{0,4},{8,0},{16,8},{24,16},{28,24},{20,28},{12,20},{4,12},{1,5},{9... | collective-permute-start | bytes 786440 | tf_op jit(solution)/shard_map/ppermute | solution.py:37
  298.1 25.1 %collective-permute-start.40 = (bf16[512,1024]{1,0:T(8,128)(2,1)S(1)}, bf16[512,1024]{1,0:T(8,128)(2,1)S(1)}, u32[]{:S(2)}, u32[]{:S(2)}) collective-permute-start(bf16[512,1024]{1,0:T(8,128)(2,1)S(1)} %collective-permute-done.38.refs_6_), channel_id=1, source_target_pairs={{0,8},{8,16},{16,24},{24,28},{28,20},{20,12},{12,4},{4,0},{1,9},{9... | collective-permute-start | bytes 3145736 | tf_op jit(solution)/shard_map/ppermute | solution.py:37
  298.2 25.0 %collective-permute-start.41 = (bf16[512,1024]{1,0:T(8,128)(2,1)S(1)}, bf16[512,1024]{1,0:T(8,128)(2,1)S(1)}, u32[]{:S(2)}, u32[]{:S(2)}) collective-permute-start(bf16[512,1024]{1,0:T(8,128)(2,1)S(1)} %collective-permute-done.39.refs_7_), channel_id=1, source_target_pairs={{0,4},{8,0},{16,8},{24,16},{28,24},{20,28},{12,20},{4,12},{1,5},{9... | collective-permute-start | bytes 3145736 | tf_op jit(solution)/shard_map/ppermute | solution.py:37
  323.3 23.7 %collective-permute-start.42 = (bf16[512,1024]{1,0:T(8,128)(2,1)S(1)}, bf16[512,1024]{1,0:T(8,128)(2,1)S(1)}, u32[]{:S(2)}, u32[]{:S(2)}) collective-permute-start(bf16[512,1024]{1,0:T(8,128)(2,1)S(1)} %collective-permute-done.40.refs_8_), channel_id=1, source_target_pairs={{0,8},{8,16},{16,24},{24,28},{28,20},{20,12},{12,4},{4,0},{1,9},{9... | collective-permute-start | bytes 3145736 | tf_op jit(solution)/shard_map/ppermute | solution.py:37
  323.4 23.7 %collective-permute-start.43 = (bf16[512,1024]{1,0:T(8,128)(2,1)S(1)}, bf16[512,1024]{1,0:T(8,128)(2,1)S(1)}, u32[]{:S(2)}, u32[]{:S(2)}) collective-permute-start(bf16[512,1024]{1,0:T(8,128)(2,1)S(1)} %collective-permute-done.41.refs_9_), channel_id=1, source_target_pairs={{0,4},{8,0},{16,8},{24,16},{28,24},{20,28},{12,20},{4,12},{1,5},{9... | collective-permute-start | bytes 3145736 | tf_op jit(solution)/shard_map/ppermute | solution.py:37
  326.2 20.7 %collective-permute-start.48 = (f32[8,8,512]{2,1,0:T(8,128)S(1)}, f32[8,8,512]{2,1,0:T(8,128)S(1)}, u32[]{:S(2)}, u32[]{:S(2)}) collective-permute-start(f32[8,8,512]{2,1,0:T(8,128)S(1)} %constant_dynamic-update-slice_fusion), channel_id=1, source_target_pairs={{0,4},{4,0},{8,12},{12,8},{16,20},{20,16},{24,28},{28,24},{1,5},{5... | collective-permute-start | bytes 393224 | tf_op jit(solution)/shard_map/ppermute | solution.py:97
  (102 other events, 1643.8 us)

commit v9 on v8

--- a/solution.py
+++ b/solution.py
@@ -129,9 +129,6 @@
         self.back = ring_step(back, self.order, -1)
         self.left -= 1
         return [self.ahead, self.back]
-
-    def total(self):
-        return sum(value.astype(jnp.float32) for value in (self.ahead, self.back, self.parts[0]))
 
 
 def project_kernel(count, turned, places_ref, *refs):
@@ -457,9 +454,9 @@
     )(first, places, live, *query_slots, keys, values, new_keys)
 
 
-def finish_kernel(slots, first_ref, place_ref, *refs):
+def finish_kernel(slots, filled, first_ref, place_ref, *refs):
     query_ref, key_ref, value_ref, cache_ref, peak_ref, total_ref, best_ref = refs[:7]
-    sum_ref, *part_refs = refs[7:-1]
+    sum_ref, *part_refs = refs[7 + filled : -1]
     joined_ref = refs[-1]
     tok_block = key_ref.shape[1]
     for head in range(query_ref.shape[2] // HEAD_DIM):
@@ -481,59 +478,110 @@
         part_refs[slot][0] = joined_ref[pl.ds(start, tok_block), :]
 
 
-def finish_part(begin, first, places, queries, new_keys, new_values, cached, peaks, totals, best):
+def finish_part(begin, at, count, first, places, queries, new_keys, new_values, cached, peaks, totals, best, filled=()):
     requests, tokens, width = queries.shape
     tok_block = new_keys.shape[1]
     slots = tokens // tok_block
     heads = width // HEAD_DIM
     one = lambda rows, start: pl.BlockSpec((1, rows, width), lambda r, *_: (r + start, 0, 0))
     stat = lambda start: pl.BlockSpec((1, heads, tokens), lambda r, *_: (r + start, 0, 0))
+    inputs = (queries, new_keys, new_values, cached, peaks, totals, best)
     return pl.pallas_call(
-        functools.partial(finish_kernel, slots),
+        functools.partial(finish_kernel, slots, len(filled)),
         grid_spec=pltpu.PrefetchScalarGridSpec(
             num_scalar_prefetch=2,
-            grid=(requests,),
+            grid=(count,),
             in_specs=[
-                one(tokens, 0),
-                one(tok_block, begin),
-                one(tok_block, begin),
-                pl.BlockSpec((1, width, tokens), lambda r, *_: (r, 0, 0)),
-                stat(0),
-                stat(0),
-                stat(begin),
-            ],
-            out_specs=[stat(0)] + [one(tok_block, 0)] * slots,
+                one(tokens, at),
+                one(tok_block, begin + at),
+                one(tok_block, begin + at),
+                pl.BlockSpec((1, width, tokens), lambda r, *_: (r + at, 0, 0)),
+                stat(at),
+                stat(at),
+                stat(begin + at),
+            ]
+            + [pl.BlockSpec(memory_space=pl.ANY)] * len(filled),
+            out_specs=[stat(at)] + [one(tok_block, at)] * slots,
             scratch_shapes=[pltpu.VMEM((tokens, width), jnp.bfloat16)],
         ),
         out_shape=[jax.ShapeDtypeStruct((requests, heads, tokens), jnp.float32)]
         + [jax.ShapeDtypeStruct((requests, tok_block, width), jnp.bfloat16)] * slots,
+        input_output_aliases={2 + len(inputs) + i: i for i in range(len(filled))},
+        compiler_params=pltpu.CompilerParams(vmem_limit_bytes=VMEM_BYTES),
+        cost_estimate=pl.CostEstimate(
+            flops=4 * count * tokens * tok_block * width,
+            bytes_accessed=6 * count * width * tokens,
+            transcendentals=count * tokens * tok_block * heads,
+        ),
+        name="finish_part",
+    )(first, places, *inputs, *filled)
+
+
+def leave_attention_kernel(order_ref, *refs):
+    ahead_ref, back_ref, own_ref, sums_ref, weight_ref, terms_ref, give_ref, keep_ref, attended_ref = refs
+    step = pl.program_id(0)
+
+    @pl.when(step == 0)
+    def _():
+        for head in range(attended_ref.shape[1] // HEAD_DIM):
+            at = slice(head * HEAD_DIM, (head + 1) * HEAD_DIM)
+            total = ahead_ref[:, at].astype(jnp.float32) + back_ref[:, at].astype(jnp.float32)
+            total = total + own_ref[:, at].astype(jnp.float32)
+            attended_ref[:, at] = (total / sums_ref[:, head : head + 1]).astype(jnp.bfloat16)
+
+    terms = terms_ref[...] + jnp.dot(
+        attended_ref[...], weight_ref[...], preferred_element_type=jnp.float32
+    )
+
+    @pl.when(step < 2)
+    def _():
+        give_ref[...] = terms.astype(jnp.bfloat16)
+
+    @pl.when(step >= 2)
+    def _():
+        keep_ref[...] = terms
+
+
+def leave_attention(order, index, ahead, back, own, sums, weight, terms):
+    rows, width = ahead.shape
+    heads = sums.shape[1]
+    block = weight.shape[1] // 4
+    whole = lambda *shape: pl.BlockSpec(shape, lambda j, *_: (0, 0))
+    return pl.pallas_call(
+        leave_attention_kernel,
+        grid_spec=pltpu.PrefetchScalarGridSpec(
+            num_scalar_prefetch=1,
+            grid=(4,),
+            in_specs=[
+                whole(rows, width),
+                whole(rows, width),
+                whole(rows, width),
+                whole(rows, heads),
+                pl.BlockSpec((width, block), lambda j, order_ref: (0, order_ref[j])),
+                pl.BlockSpec((rows, block), lambda j, order_ref: (index, order_ref[j])),
+            ],
+            out_specs=[
+                pl.BlockSpec((rows, block), lambda j, *_: (0, jnp.minimum(j, 1))),
+                pl.BlockSpec((rows, block), lambda j, *_: (0, jnp.maximum(j - 2, 0))),
+            ],
+            scratch_shapes=[pltpu.VMEM((rows, width), jnp.bfloat16)],
+        ),
+        out_shape=[
+            jax.ShapeDtypeStruct((rows, 2 * block), jnp.bfloat16),
+            jax.ShapeDtypeStruct((rows, 2 * block), jnp.float32),
+        ],
         compiler_params=pltpu.CompilerParams(vmem_limit_bytes=VMEM_BYTES),
         cost_estimate=LIGHT,
-        name="finish_part",
-    )(first, places, queries, new_keys, new_values, cached, peaks, totals, best)
-
-
-def head_sum(terms, head_count, head_index):
-    if head_count != 4:
-        return lax.psum_scatter(
-            terms.astype(jnp.bfloat16), "head", scatter_dimension=1, tiled=True
-        ).astype(jnp.float32)
-    width = terms.shape[1] // 4
-    chunk = lambda index: lax.dynamic_slice_in_dim(terms, index * width, width, 1)
-    core, column = head_index % 2, head_index // 2
-    near, far = 2 * column, 2 * (1 - column)
-    got = lax.ppermute(
-        jnp.concatenate([chunk(near + 1 - core), chunk(far + 1 - core)], axis=1).astype(
-            jnp.bfloat16
-        ),
-        "head",
-        [(h, h ^ 1) for h in range(4)],
-    ).astype(jnp.float32)
-    keep = chunk(near + core) + got[:, :width]
-    give = chunk(far + core) + got[:, width:]
-    return keep + lax.ppermute(
-        give.astype(jnp.bfloat16), "head", [(h, h ^ 2) for h in range(4)]
-    ).astype(jnp.float32)
+        name="leave_attention",
+    )(order, ahead, back, own, sums, weight, terms)
+
+
+def head_sum(give, keep):
+    width = keep.shape[1] // 2
+    got = lax.ppermute(give, "head", [(h, h ^ 1) for h in range(4)]).astype(jnp.float32)
+    leaving = (keep[:, width:] + got[:, width:]).astype(jnp.bfloat16)
+    last = lax.ppermute(leaving, "head", [(h, h ^ 2) for h in range(4)]).astype(jnp.float32)
+    return keep[:, :width] + got[:, :width] + last
 
 
 class Relay:
@@ -815,11 +863,11 @@
         made["values"] = product(
             [(0, 0, clock.hold(value_ring.block))] + pieces, False, kind=jnp.float32
         )
-        return (made["values"],), ()
+        return (made["values"],) + leave_terms()[0], ()
 
     def join_more():
         made["best"].step(clock)
-        return leave_terms()
+        return (), ()
 
     def steps(rings, begin, end):
         return [ring for _ in range(begin, end) for ring in rings]
@@ -862,13 +910,17 @@
     residual = lax.dynamic_slice_in_dim(
         flat_input, head_index * local_width, local_width, 1
     ).astype(jnp.float32)
-    sums, ring_sums, mixed = [], [], []
-
-    def finish(index):
+    mixed = []
+
+    filled = {}
+
+    def finish(index, at, count):
         def work():
             joined, out, peaks, totals = cached[index]
-            some_sums, *parts = finish_part(
+            filled[index] = finish_part(
                 index * group,
+                at,
+                count,
                 first,
                 places,
                 clock.hold(joined),
@@ -878,40 +930,80 @@
                 peaks,
                 totals,
                 best,
+                filled.get(index, ()),
             )
-            sums.append(some_sums)
-            terms = {-offset: part for offset, part in zip(offsets, parts)}
-            terms[half] = terms[-half]
-            ring_sums.append(RingSum(terms, order))
-            return (some_sums, *parts), ()
+            return tuple(filled[index]), ()
 
         return work
+
+    def ring_sum(index):
+        terms = {-offset: part for offset, part in zip(offsets, filled[index][1:])}
+        terms[half] = terms[-half]
+        return RingSum(terms, order)
 
     def add_sums():
         if "sums" not in made:
-            made["sums"] = Exchange(jnp.concatenate(sums, axis=0), "seq", seq_count, jnp.add)
+            sums = jnp.concatenate([filled[index][0] for index in range(GROUPS)], axis=0)
+            made["sums"] = Exchange(sums, "seq", seq_count, jnp.add)
         made["sums"].step(clock)
         return (), ()
 
-    run([], [finish(0)])
-    run([ring_sums[0]], [finish(1)])
+    def together(*works):
+        def work():
+            done = [work() for work in works]
+            return sum((d for d, _ in done), ()), sum((d for _, d in done), ())
+
+        return work
+
+    run([], [finish(0, 0, group)])
+    sum_rings = [ring_sum(0)]
+    run(sum_rings, [finish(1, 0, group // 2)])
+    clock.mark = clock.hold(clock.mark, sum_rings[0].ahead)[0]
+    run([], [finish(1, group // 2, group - group // 2)])
+    sum_rings.append(ring_sum(1))
     run(
-        steps(ring_sums[::-1], 0, half)[:-1],
-        [add_sums, chain_split, add_sums, chain_turn, add_sums, chain_join],
-    )
-    denominators = jnp.transpose(own(made["sums"].result(clock)), (0, 2, 1))
+        steps(sum_rings[::-1], 0, half)[:-1],
+        [
+            together(add_sums, chain_split),
+            chain_turn,
+            together(add_sums, chain_join),
+            None,
+            add_sums,
+        ],
+    )
+    denominators = jnp.transpose(own(made["sums"].result(clock)), (0, 2, 1)).reshape(
+        tokens, local_heads
+    )
+    if head_count == 4:
+        core, column = head_index % 2, head_index // 2
+        near, far = 2 * column, 2 * (1 - column)
+        blocks = jnp.stack([near + 1 - core, far + 1 - core, near + core, far + core])
+    else:
+        blocks = jnp.arange(4)
+    group_rows = group * tok_block
     for index in range(GROUPS):
-        begin = index * group
-        denominator = denominators[begin : begin + group]
-        numerator = ring_sums[index].total().reshape(group, tok_block, local_heads, HEAD_DIM)
-        attended = (
-            (numerator / denominator[..., None])
-            .astype(jnp.bfloat16)
-            .reshape(group * tok_block, local_att)
-        )
-        at = slice(begin * tok_block, (begin + group) * tok_block)
-        attn_terms = jnp.dot(attended, w_attn_out, preferred_element_type=jnp.float32)
-        summed = head_sum(attn_terms + made["terms"][at], head_count, head_index)
+        at = slice(index * group_rows, (index + 1) * group_rows)
+        ring = sum_rings[index]
+        give, keep = leave_attention(
+            blocks.astype(jnp.int32),
+            index,
+            *(
+                value.reshape(group_rows, local_att)
+                for value in (ring.ahead, ring.back, ring.parts[0])
+            ),
+            denominators[at],
+            w_attn_out,
+            made["terms"],
+        )
+        if head_count == 4:
+            summed = head_sum(give, keep)
+        else:
+            summed = lax.psum_scatter(
+                jnp.concatenate([give, keep.astype(jnp.bfloat16)], axis=1),
+                "head",
+                scatter_dimension=1,
+                tiled=True,
+            ).astype(jnp.float32)
         mixed.append(
             (residual[at] + summed)
             .astype(jnp.bfloat16)

time: 524 us -> 542 us (1.034)
  Pallas kernels: 133 us -> 151 us
  waiting for transfers between devices: 164 us -> 182 us
  other arithmetic: 50.7 us -> 34.7 us
    pallas_call x2 -> x5, Pallas kernels: 22.7 us -> 40.2 us  [the longest x3 25.9 us: finish_part(): pl.pallas_call(functools.partial(finish_kernel, slots, len(filled)), grid...]
    ppermute x8, waiting for transfers between devices: 28.4 us -> 37 us  [step(): self.got = lax.ppermute(self.value, self.axis, route)]
    ppermute x4, waiting for transfers between devices: 0.01 us -> 8.45 us  [the longest x2 8.45 us: head_sum(): lax.ppermute(leaving, 'head', [(h, h ^ 2) for h in range(4)])]
    convert_element_type x12, other arithmetic: 13.8 us -> 5.61 us  [add(): return (a.astype(jnp.float32) + b.astype(jnp.float32)).astype(jnp.bfloat16)]
    unnamed x126 -> x130, local copies, waits for them, and re-layouts: 18.4 us -> 17 us
  transfers between devices with their start and end apart: 74 -> 74, of which waited for: 27 -> 30; matrix products, arithmetic and copies ran while one was open for 22% -> 18% of each run, Pallas kernels for 22% -> 25%
where the time goes in v9:
time: 542 us; the launch traced here: 532 us
  waiting for transfers between devices  182 us (34%)
  Pallas kernels  151 us (28%)
  starting transfers between devices  89.9 us (17%)
  local copies, waits for them, and re-layouts  64.7 us (12%)
  other arithmetic  34.7 us (6%)
  matrix products  7.87 us (1%)
    ppermute x56, waiting for transfers between devices, ring_step(): return lax.ppermute(block, 'seq', route)  88.3 us
    ppermute x56, starting transfers between devices, ring_step(): return lax.ppermute(block, 'seq', route)  70.2 us
    pallas_call x2, Pallas kernels, cache_part(): pl.pallas_call(functools.partial(cache_kernel, slots), grid_spec=pltpu.Pr...  44.1 us
    ppermute x8, waiting for transfers between devices, step(): self.got = lax.ppermute(self.value, self.axis, route)  37 us
    pallas_call x4, Pallas kernels, project(): pl.pallas_call(functools.partial(project_kernel, len(pieces), turned), gr...  36.1 us
    ppermute x1, waiting for transfers between devices, __init__(): other_factor = side(lax.ppermute(through, 'seq', self.swap))  32.8 us
    pallas_call x3, Pallas kernels, finish_part(): pl.pallas_call(functools.partial(finish_kernel, slots, len(filled)), grid...  25.9 us
    unnamed x130, local copies, waits for them, and re-layouts  17 us
  transfers between devices with their start and end apart: 74, of which 30 were waited for; matrix products, arithmetic and copies ran while one was open for 18% of the time, Pallas kernels for 25%

profile of v9, /device:TPU:0, one launch (start us, length us, event | category | flops | bytes accessed | tf_op | source)
XLA Modules:
  0.0 531.8 jit_solution(14128827374740891823)
XLA Ops:
  3.7 10.4 %copy.61 = bf16[256,8,2,1024]{3,1,2,0:T(8,128)(2,1)} copy(bf16[256,8,2,1024]{3,2,1,0:T(2,128)(2,1)} %bitcast.98) | data formatting | bytes 16777216
  17.2 5.6 %copy.49 = f32[8,16,64,64]{2,1,3,0:T(8,128)} copy(f32[8,16,64,64]{3,2,1,0:T(8,128)} %reshape.131) | data formatting | bytes 4194304 | tf_op jit(solution)/shard_map/reshape | solution.py:721
  22.8 4.9 reshape.132
  30.7 11.7 %enter_mixer.1 = (f32[512,2048]{1,0:T(8,128)}, f32[512,128]{1,0:T(8,128)}, f32[512,16]{1,0:T(8,128)}) custom-call(bf16[512,4096]{1,0:T(8,128)(2,1)} %bitcast.56, f32[1,2048]{1,0:T(1,128)} %bitcast.121, bf16[2048,128]{1,0:T(8,128)(2,1)} %bc_ref.1, bf16[2048,16]{1,0:T(8,128)(2,1)} %copy.50.dt_ref, f32[1,16]{1,0:T(1,128)} %bitcast.126, bf16[2048,2048]{1,0:T(8,128)(2,1)} %bitcast.91), custom_call_target="tpu_custom_call" | custom-call | tf_op jit(solution)/shard_map/enter_mixer/pallas_call | solution.py:225
  49.8 9.6 %inside_block.1 = (f32[512,1024]{1,0:T(8,128)}, f32[8,64,1024]{2,1,0:T(8,128)}, f32[8,1,1024]{2,1,0:T(1,128)}) custom-call(f32[512,2048]{1,0:T(8,128)} %get-tuple-element.184.inner_ref.gate_ref, f32[512,128]{1,0:T(8,128)} %get-tuple-element.185.map_ref, f32[8,64,16]{2,1,0:T(8,128)} %bitcast.99, f32[8,64,16]{2,1,0:T(8,128)} %bitcast.103, ...), custom_call_target="tpu_custom_call" | custom-call | tf_op jit(solution)/shard_map/inside_block/pallas_call | solution.py:299
  65.2 32.8 %collective-permute-done.10 = f32[8,1,1024]{2,1,0:T(1,128)S(1)} collective-permute-done((f32[8,1,1024]{2,1,0:T(1,128)}, f32[8,1,1024]{2,1,0:T(1,128)S(1)}, u32[]{:S(2)}, u32[]{:S(2)}) %collective-permute-start.10) | collective-permute-done | bytes 32800 | tf_op jit(solution)/shard_map/ppermute | solution.py:603
  104.8 8.0 %collective-permute-done.11 = bf16[8,64,512]{2,1,0:T(8,128)(2,1)S(1)} collective-permute-done((bf16[8,64,512]{2,1,0:T(8,128)(2,1)S(1)}, bf16[8,64,512]{2,1,0:T(8,128)(2,1)S(1)}, u32[]{:S(2)}, u32[]{:S(2)}) %collective-permute-start.11) | collective-permute-done | bytes 524320 | tf_op jit(solution)/shard_map/ppermute | solution.py:614
  118.6 14.4 %collective-permute-done.6.refs_14_ = bf16[512,1024]{1,0:T(8,128)(2,1)S(1)} collective-permute-done((bf16[512,1024]{1,0:T(8,128)(2,1)}, bf16[512,1024]{1,0:T(8,128)(2,1)S(1)}, u32[]{:S(2)}, u32[]{:S(2)}) %collective-permute-start.6) | collective-permute-done | bytes 1048608 | tf_op jit(solution)/shard_map/ppermute | solution.py:37
  142.1 9.7 %collective-permute-done.12.refs_16_ = bf16[256,1024]{1,0:T(8,128)(2,1)} collective-permute-done((bf16[256,1024]{1,0:T(8,128)(2,1)}, bf16[256,1024]{1,0:T(8,128)(2,1)}, u32[]{:S(2)}, u32[]{:S(2)}) %collective-permute-start.12) | collective-permute-done | bytes 524320 | tf_op jit(solution)/shard_map/ppermute | solution.py:37
  157.5 10.4 %project.4 = bf16[512,1024]{1,0:T(8,128)(2,1)} custom-call(s32[8]{0:T(128)} %fusion.19.places_ref.place_ref, bf16[512,4096]{1,0:T(8,128)(2,1)} %bitcast.57, bf16[512,4096]{1,0:T(8,128)(2,1)} %bitcast.58, bf16[512,4096]{1,0:T(8,128)(2,1)} %bitcast.59, bf16[512,4096]{1,0:T(8,128)(2,1)} %bitcast.60, bf16[512,4096]{1,0:T(8,128)(2,1)} %bitcast.61, ...), custom_call_target="tpu_custom_call" | custom-call | tf_op jit(solution)/shard_map/project/pallas_call | solution.py:167
  180.5 7.6 %collective-permute-done.17.refs_16_ = bf16[256,1024]{1,0:T(8,128)(2,1)S(1)} collective-permute-done((bf16[256,1024]{1,0:T(8,128)(2,1)S(1)}, bf16[256,1024]{1,0:T(8,128)(2,1)S(1)}, u32[]{:S(2)}, u32[]{:S(2)}) %collective-permute-start.17) | collective-permute-done | bytes 524320 | tf_op jit(solution)/shard_map/ppermute | solution.py:37
  194.3 10.6 %project.5 = bf16[512,1024]{1,0:T(8,128)(2,1)} custom-call(s32[8]{0:T(128)} %fusion.19.places_ref.place_ref, bf16[512,4096]{1,0:T(8,128)(2,1)} %bitcast.70, bf16[512,4096]{1,0:T(8,128)(2,1)} %bitcast.67, bf16[512,4096]{1,0:T(8,128)(2,1)} %bitcast.68, bf16[512,4096]{1,0:T(8,128)(2,1)} %bitcast.69, bf16[512,4096]{1,0:T(8,128)(2,1)} %bitcast.66, ...), custom_call_target="tpu_custom_call" | custom-call | tf_op jit(solution)/shard_map/project/pallas_call | solution.py:167
  212.8 5.9 %collective-permute-start.27 = (bf16[4,64,1024]{2,1,0:T(8,128)(2,1)S(1)}, bf16[4,64,1024]{2,1,0:T(8,128)(2,1)S(1)}, u32[]{:S(2)}, u32[]{:S(2)}) collective-permute-start(bf16[4,64,1024]{2,1,0:T(8,128)(2,1)S(1)} %collective-permute-done.22.refs_1_), channel_id=1, source_target_pairs={{0,8},{8,16},{16,24},{24,28},{28,20},{20,12},{12,4},{4,0},{1,9},{9... | collective-permute-start | bytes 1572872 | tf_op jit(solution)/shard_map/ppermute | solution.py:37
  225.0 7.6 %collective-permute-done.29 = bf16[8,64,512]{2,1,0:T(8,128)(2,1)S(1)} collective-permute-done((bf16[8,64,512]{2,1,0:T(8,128)(2,1)S(1)}, bf16[8,64,512]{2,1,0:T(8,128)(2,1)S(1)}, u32[]{:S(2)}, u32[]{:S(2)}) %collective-permute-start.29) | collective-permute-done | bytes 524320 | tf_op jit(solution)/shard_map/ppermute | solution.py:614
  234.5 9.4 %collective-permute-done.27.refs_3_ = bf16[4,64,1024]{2,1,0:T(8,128)(2,1)S(1)} collective-permute-done((bf16[4,64,1024]{2,1,0:T(8,128)(2,1)S(1)}, bf16[4,64,1024]{2,1,0:T(8,128)(2,1)S(1)}, u32[]{:S(2)}, u32[]{:S(2)}) %collective-permute-start.27) | collective-permute-done | bytes 524320 | tf_op jit(solution)/shard_map/ppermute | solution.py:37
  246.0 8.9 %leave_mixer.1 = (bf16[512,1024]{1,0:T(8,128)(2,1)}, f32[512,128]{1,0:T(8,128)}, f32[8,64,1024]{2,1,0:T(8,128)}) custom-call(f32[8,64,1024]{2,1,0:T(8,128)} %pad_maximum_fusion.entry_ref, f32[512,128]{1,0:T(8,128)} %get-tuple-element.185.map_ref, f32[8,64,16]{2,1,0:T(8,128)} %bitcast.100, f32[512,1024]{1,0:T(8,128)} %get-tuple-element.186.read_ref, ...), custom_call_target="tpu_custom_call" | custom-call | tf_op jit(solution)/shard_map/leave_mixer/pallas_call | solution.py:348
  257.2 8.2 %collective-permute-done.32.refs_5_ = bf16[4,64,1024]{2,1,0:T(8,128)(2,1)S(1)} collective-permute-done((bf16[4,64,1024]{2,1,0:T(8,128)(2,1)S(1)}, bf16[4,64,1024]{2,1,0:T(8,128)(2,1)S(1)}, u32[]{:S(2)}, u32[]{:S(2)}) %collective-permute-start.32) | collective-permute-done | bytes 524320 | tf_op jit(solution)/shard_map/ppermute | solution.py:37
  275.2 22.0 %cache_part.2 = (bf16[4,512,1024]{2,1,0:T(8,128)(2,1)}, bf16[4,1024,512]{2,1,0:T(8,128)(2,1)}, f32[4,8,512]{2,1,0:T(8,128)}, f32[4,8,512]{2,1,0:T(8,128)}) custom-call(s32[1]{0:T(128)} %bitcast.5.first_ref, s32[8]{0:T(128)} %fusion.19.places_ref.place_ref, s32[4]{0:T(128)} %get-tuple-element.361.live_ref, bf16[4,64,1024]{2,1,0:T(8,128)(2,1)} %bitcast.109, ...), custom_call_target="tpu_custom_call" | custom-call | tf_op jit(solution)/shard_map/cache_part/pallas_call | solution.py:430
  301.0 22.1 %cache_part.3 = (bf16[4,512,1024]{2,1,0:T(8,128)(2,1)}, bf16[4,1024,512]{2,1,0:T(8,128)(2,1)}, f32[4,8,512]{2,1,0:T(8,128)}, f32[4,8,512]{2,1,0:T(8,128)}) custom-call(s32[1]{0:T(128)} %bitcast.5.first_ref, s32[8]{0:T(128)} %fusion.19.places_ref.place_ref, s32[4]{0:T(128)} %get-tuple-element.362.live_ref, bf16[4,64,1024]{2,1,0:T(8,128)(2,1)} %bitcast.106, ...), custom_call_target="tpu_custom_call" | custom-call | tf_op jit(solution)/shard_map/cache_part/pallas_call | solution.py:430
  330.4 6.5 %convolution_multiply_fusion.refs_5_ = f32[512,2048]{1,0:T(8,128)} fusion(bf16[512,1024]{1,0:T(8,128)(2,1)S(1)} %copy-done.60, bf16[1024,2048]{1,0:T(8,128)(2,1)} %param.35, f32[512]{0:T(512)S(1)} %bitcast.125), kind=kOutput, calls=%fused_computation | convolution fusion | flops 2148532224 | bytes 9439232 | tf_op jit(solution)/shard_map/dot_general | solution.py:796
  336.9 8.3 %project.6.refs_10_ = f32[512,1024]{1,0:T(8,128)} custom-call(s32[8]{0:T(128)} %fusion.19.places_ref.place_ref, bf16[512,4096]{1,0:T(8,128)(2,1)} %bitcast.75, bf16[512,4096]{1,0:T(8,128)(2,1)} %bitcast.76, bf16[512,4096]{1,0:T(8,128)(2,1)} %bitcast.77, bf16[512,4096]{1,0:T(8,128)(2,1)} %bitcast.78, bf16[512,4096]{1,0:T(8,128)(2,1)} %bitcast.79, ...), custom_call_target="tpu_custom_call" | custom-call | tf_op jit(solution)/shard_map/project/pallas_call | solution.py:167
  349.3 12.1 %collective-permute-done.48 = f32[8,8,512]{2,1,0:T(8,128)S(1)} collective-permute-done((f32[8,8,512]{2,1,0:T(8,128)S(1)}, f32[8,8,512]{2,1,0:T(8,128)S(1)}, u32[]{:S(2)}, u32[]{:S(2)}) %collective-permute-start.48) | collective-permute-done | bytes 131104 | tf_op jit(solution)/shard_map/ppermute | solution.py:97
  361.5 5.0 collective-permute-done.49
  374.8 6.8 %project.7 = bf16[512,1024]{1,0:T(8,128)(2,1)} custom-call(s32[8]{0:T(128)} %fusion.19.places_ref.place_ref, bf16[512,4096]{1,0:T(8,128)(2,1)} %bitcast.80, bf16[512,4096]{1,0:T(8,128)(2,1)} %bitcast.81, bf16[512,4096]{1,0:T(8,128)(2,1)} %bitcast.82, bf16[512,4096]{1,0:T(8,128)(2,1)} %bitcast.83, bf16[512,1024]{1,0:T(8,128)(2,1)} %copy-done.8, ...), custom_call_target="tpu_custom_call" | custom-call | tf_op jit(solution)/shard_map/project/pallas_call | solution.py:167
  381.6 11.2 %finish_part.3 = (f32[4,8,512]{2,1,0:T(8,128)}, bf16[4,64,1024]{2,1,0:T(8,128)(2,1)}, bf16[4,64,1024]{2,1,0:T(8,128)(2,1)}, bf16[4,64,1024]{2,1,0:T(8,128)(2,1)}...) custom-call(s32[1]{0:T(128)} %bitcast.5.first_ref, ...), custom_call_target="tpu_custom_call" | custom-call | flops 536870912 | bytes 12582912 | tf_op jit(solution)/shard_map/finish_part/pallas_call | solution.py:489
  400.3 7.2 %finish_part.4 = (f32[4,8,512]{2,1,0:T(8,128)}, bf16[4,64,1024]{2,1,0:T(8,128)(2,1)}, bf16[4,64,1024]{2,1,0:T(8,128)(2,1)}, bf16[4,64,1024]{2,1,0:T(8,128)(2,1)}...) custom-call(s32[1]{0:T(128)} %bitcast.5.first_ref, ...), custom_call_target="tpu_custom_call" | custom-call | flops 268435456 | bytes 6291456 | tf_op jit(solution)/shard_map/finish_part/pallas_call | solution.py:489
  407.6 7.4 %finish_part.5 = (f32[4,8,512]{2,1,0:T(8,128)}, bf16[4,64,1024]{2,1,0:T(8,128)(2,1)}, bf16[4,64,1024]{2,1,0:T(8,128)(2,1)}, bf16[4,64,1024]{2,1,0:T(8,128)(2,1)}...) custom-call(s32[1]{0:T(128)} %bitcast.5.first_ref, ...), custom_call_target="tpu_custom_call", output_to_operand_aliasing={{0}: (9, {}), {1}: (10, {}), {2}: (11, {}), {3}: (12, {}), ... | custom-call | flops 268435456 | bytes 6291456 | tf_op jit(solution)/shard_map/finish_part/pallas_call | solution.py:489
  430.1 5.5 %copy.54 = f32[8,16,64,64]{3,2,1,0:T(8,128)} copy(f32[8,16,64,64]{2,1,3,0:T(8,128)} %bitcast.92) | data formatting | bytes 4194304 | tf_op jit(solution)/shard_map/optimization_barrier | solution.py:72
  449.8 9.1 %collective-permute-done.63 = bf16[4,64,1024]{2,1,0:T(8,128)(2,1)S(1)} collective-permute-done((bf16[4,64,1024]{2,1,0:T(8,128)(2,1)S(1)}, bf16[4,64,1024]{2,1,0:T(8,128)(2,1)S(1)}, u32[]{:S(2)}, u32[]{:S(2)}) %collective-permute-start.63) | collective-permute-done | bytes 524320 | tf_op jit(solution)/shard_map/ppermute | solution.py:37
  465.3 13.5 %collective-permute-done.65 = f32[8,8,512]{2,1,0:T(8,128)S(1)} collective-permute-done((f32[8,8,512]{2,1,0:T(8,128)S(1)}, f32[8,8,512]{2,1,0:T(8,128)S(1)}, u32[]{:S(2)}, u32[]{:S(2)}) %collective-permute-start.65) | collective-permute-done | bytes 131104 | tf_op jit(solution)/shard_map/ppermute | solution.py:97
  497.6 7.0 %leave_attention.2 = (bf16[256,1024]{1,0:T(8,128)(2,1)}, f32[256,1024]{1,0:T(8,128)}) custom-call(s32[4]{0:T(128)} %pad_add_fusion.order_ref, bf16[256,1024]{1,0:T(8,128)(2,1)} %bitcast.117, bf16[256,1024]{1,0:T(8,128)(2,1)} %bitcast.22.refs_1_, bf16[256,1024]{1,0:T(8,128)(2,1)} %bitcast.115, f32[256,8]{1,0:T(8,128)} %bitcast.114, ...), custom_call_target="tpu_custom_call" | custom-call | tf_op jit(solution)/shard_map/leave_attention/pallas_call | solution.py:550
  506.3 7.3 %leave_attention.3 = (bf16[256,1024]{1,0:T(8,128)(2,1)}, f32[256,1024]{1,0:T(8,128)}) custom-call(s32[4]{0:T(128)} %pad_add_fusion.order_ref, bf16[256,1024]{1,0:T(8,128)(2,1)} %bitcast.116, bf16[256,1024]{1,0:T(8,128)(2,1)} %bitcast.118, bf16[256,1024]{1,0:T(8,128)(2,1)} %bitcast.110, f32[256,8]{1,0:T(8,128)} %bitcast.113, bf16[1024,2048]{1,0:T(8,128)(2,1)} %refs_4_.3, ...), custom_call_target="tpu_custom_call" | custom-call | tf_op jit(solution)/shard_map/leave_attention/pallas_call | solution.py:550
  (354 shorter events, 203.0 us)
Async XLA Ops:
  0.6 45.6 %collective-permute-start = (bf16[512,1024]{1,0:T(8,128)(2,1)}, bf16[512,1024]{1,0:T(8,128)(2,1)}, u32[]{:S(2)}, u32[]{:S(2)}) collective-permute-start(bf16[512,1024]{1,0:T(8,128)(2,1)} %refs_9_.4), channel_id=1, source_target_pairs={{0,8},{8,16},{16,24},{24,28},{28,20},{20,12},{12,4},{4,0},{1,9},{9... | collective-permute-start | bytes 3145736 | tf_op jit(solution)/shard_map/ppermute | solution.py:37
  3.7 42.5 %collective-permute-start.1 = (bf16[512,1024]{1,0:T(8,128)(2,1)}, bf16[512,1024]{1,0:T(8,128)(2,1)}, u32[]{:S(2)}, u32[]{:S(2)}) collective-permute-start(bf16[512,1024]{1,0:T(8,128)(2,1)} %refs_9_.4), channel_id=1, source_target_pairs={{0,4},{8,0},{16,8},{24,16},{28,24},{20,28},{12,20},{4,12},{1,5},{9... | collective-permute-start | bytes 3145736 | tf_op jit(solution)/shard_map/ppermute | solution.py:37
  27.7 31.8 %collective-permute-start.4 = (bf16[512,1024]{1,0:T(8,128)(2,1)S(1)}, bf16[512,1024]{1,0:T(8,128)(2,1)}, u32[]{:S(2)}, u32[]{:S(2)}) collective-permute-start(bf16[512,1024]{1,0:T(8,128)(2,1)S(1)} %copy-done.24), channel_id=1, source_target_pairs={{0,8},{8,16},{16,24},{24,28},{28,20},{20,12},{12,4},{4,0},{1,9},{9... | collective-permute-start | bytes 3145736 | tf_op jit(solution)/shard_map/ppermute | solution.py:37
  29.7 29.8 %collective-permute-start.5 = (bf16[512,1024]{1,0:T(8,128)(2,1)S(1)}, bf16[512,1024]{1,0:T(8,128)(2,1)}, u32[]{:S(2)}, u32[]{:S(2)}) collective-permute-start(bf16[512,1024]{1,0:T(8,128)(2,1)S(1)} %copy-done.24), channel_id=1, source_target_pairs={{0,4},{8,0},{16,8},{24,16},{28,24},{20,28},{12,20},{4,12},{1,5},{9... | collective-permute-start | bytes 3145736 | tf_op jit(solution)/shard_map/ppermute | solution.py:37
  46.2 56.3 %collective-permute-start.2 = (bf16[512,1024]{1,0:T(8,128)(2,1)}, bf16[512,1024]{1,0:T(8,128)(2,1)}, u32[]{:S(2)}, u32[]{:S(2)}) collective-permute-start(bf16[512,1024]{1,0:T(8,128)(2,1)} %collective-permute-done.refs_10_), channel_id=1, source_target_pairs={{0,8},{8,16},{16,24},{24,28},{28,20},{20,12},{12,4},{4,0},{1,9},{9... | collective-permute-start | bytes 3145736 | tf_op jit(solution)/shard_map/ppermute | solution.py:37
  48.2 54.3 %collective-permute-start.3 = (bf16[512,1024]{1,0:T(8,128)(2,1)}, bf16[512,1024]{1,0:T(8,128)(2,1)}, u32[]{:S(2)}, u32[]{:S(2)}) collective-permute-start(bf16[512,1024]{1,0:T(8,128)(2,1)} %collective-permute-done.1.refs_11_), channel_id=1, source_target_pairs={{0,4},{8,0},{16,8},{24,16},{28,24},{20,28},{12,20},{4,12},{1,5},{9... | collective-permute-start | bytes 3145736 | tf_op jit(solution)/shard_map/ppermute | solution.py:37
  59.5 56.5 %collective-permute-start.8 = (bf16[512,1024]{1,0:T(8,128)(2,1)}, bf16[512,1024]{1,0:T(8,128)(2,1)}, u32[]{:S(2)}, u32[]{:S(2)}) collective-permute-start(bf16[512,1024]{1,0:T(8,128)(2,1)} %collective-permute-done.4.refs_10_), channel_id=1, source_target_pairs={{0,8},{8,16},{16,24},{24,28},{28,20},{20,12},{12,4},{4,0},{1,9},{9... | collective-permute-start | bytes 3145736 | tf_op jit(solution)/shard_map/ppermute | solution.py:37
  61.6 54.5 %collective-permute-start.9 = (bf16[512,1024]{1,0:T(8,128)(2,1)}, bf16[512,1024]{1,0:T(8,128)(2,1)}, u32[]{:S(2)}, u32[]{:S(2)}) collective-permute-start(bf16[512,1024]{1,0:T(8,128)(2,1)} %collective-permute-done.5.refs_11_), channel_id=1, source_target_pairs={{0,4},{8,0},{16,8},{24,16},{28,24},{20,28},{12,20},{4,12},{1,5},{9... | collective-permute-start | bytes 3145736 | tf_op jit(solution)/shard_map/ppermute | solution.py:37
  61.6 36.4 %collective-permute-start.10 = (f32[8,1,1024]{2,1,0:T(1,128)}, f32[8,1,1024]{2,1,0:T(1,128)S(1)}, u32[]{:S(2)}, u32[]{:S(2)}) collective-permute-start(f32[8,1,1024]{2,1,0:T(1,128)} %get-tuple-element.194.through_ref), channel_id=1, source_target_pairs={{0,4},{4,0},{8,12},{12,8},{16,20},{20,16},{24,28},{28,24},{1,5},{5... | collective-permute-start | bytes 98312 | tf_op jit(solution)/shard_map/ppermute | solution.py:603
  102.5 30.5 %collective-permute-start.6 = (bf16[512,1024]{1,0:T(8,128)(2,1)}, bf16[512,1024]{1,0:T(8,128)(2,1)S(1)}, u32[]{:S(2)}, u32[]{:S(2)}) collective-permute-start(bf16[512,1024]{1,0:T(8,128)(2,1)} %collective-permute-done.2.refs_12_), channel_id=1, source_target_pairs={{0,8},{8,16},{16,24},{24,28},{28,20},{20,12},{12,4},{4,0},{1,9},{9... | collective-permute-start | bytes 3145736 | tf_op jit(solution)/shard_map/ppermute | solution.py:37
  102.6 32.2 %collective-permute-start.7 = (bf16[512,1024]{1,0:T(8,128)(2,1)}, bf16[512,1024]{1,0:T(8,128)(2,1)S(1)}, u32[]{:S(2)}, u32[]{:S(2)}) collective-permute-start(bf16[512,1024]{1,0:T(8,128)(2,1)} %collective-permute-done.3.refs_13_), channel_id=1, source_target_pairs={{0,4},{8,0},{16,8},{24,16},{28,24},{20,28},{12,20},{4,12},{1,5},{9... | collective-permute-start | bytes 3145736 | tf_op jit(solution)/shard_map/ppermute | solution.py:37
  116.3 24.5 %collective-permute-start.14 = (bf16[8,64,512]{2,1,0:T(8,128)(2,1)S(1)}, bf16[8,64,512]{2,1,0:T(8,128)(2,1)}, u32[]{:S(2)}, u32[]{:S(2)}) collective-permute-start(bf16[8,64,512]{2,1,0:T(8,128)(2,1)S(1)} %add_convert_fusion.10), channel_id=1, source_target_pairs={{0,8},{4,12},{1,9},{5,13},{2,10},{6,14},{3,11},{7,15}} | collective-permute-start | bytes 1572872 | tf_op jit(solution)/shard_map/ppermute | solution.py:629
  138.8 32.3 %collective-permute-start.15 = (bf16[512,1024]{1,0:T(8,128)(2,1)}, bf16[512,1024]{1,0:T(8,128)(2,1)}, u32[]{:S(2)}, u32[]{:S(2)}) collective-permute-start(bf16[512,1024]{1,0:T(8,128)(2,1)} %collective-permute-done.8.refs_12_), channel_id=1, source_target_pairs={{0,8},{8,16},{16,24},{24,28},{28,20},{20,12},{12,4},{4,0},{1,9},{9... | collective-permute-start | bytes 3145736 | tf_op jit(solution)/shard_map/ppermute | solution.py:37
  138.8 33.3 %collective-permute-start.16 = (bf16[512,1024]{1,0:T(8,128)(2,1)}, bf16[512,1024]{1,0:T(8,128)(2,1)}, u32[]{:S(2)}, u32[]{:S(2)}) collective-permute-start(bf16[512,1024]{1,0:T(8,128)(2,1)} %collective-permute-done.9.refs_13_), channel_id=1, source_target_pairs={{0,4},{8,0},{16,8},{24,16},{28,24},{20,28},{12,20},{4,12},{1,5},{9... | collective-permute-start | bytes 3145736 | tf_op jit(solution)/shard_map/ppermute | solution.py:37
  152.9 24.0 %collective-permute-start.19 = (bf16[8,64,512]{2,1,0:T(8,128)(2,1)}, bf16[8,64,512]{2,1,0:T(8,128)(2,1)}, u32[]{:S(2)}, u32[]{:S(2)}) collective-permute-start(bf16[8,64,512]{2,1,0:T(8,128)(2,1)} %add_convert_fusion.9), channel_id=1, source_target_pairs={{8,16},{12,20},{9,17},{13,21},{10,18},{14,22},{11,19},{15,23}} | collective-permute-start | bytes 1572872 | tf_op jit(solution)/shard_map/ppermute | solution.py:629
  178.5 26.5 %collective-permute-start.20 = (bf16[4,64,1024]{2,1,0:T(8,128)(2,1)S(1)}, bf16[4,64,1024]{2,1,0:T(8,128)(2,1)S(1)}, u32[]{:S(2)}, u32[]{:S(2)}) collective-permute-start(bf16[4,64,1024]{2,1,0:T(8,128)(2,1)S(1)} %bitcast.107), channel_id=1, source_target_pairs={{0,8},{8,16},{16,24},{24,28},{28,20},{20,12},{12,4},{4,0},{1,9},{9... | collective-permute-start | bytes 1572872 | tf_op jit(solution)/shard_map/ppermute | solution.py:37
  180.5 24.4 %collective-permute-start.21 = (bf16[4,64,1024]{2,1,0:T(8,128)(2,1)S(1)}, bf16[4,64,1024]{2,1,0:T(8,128)(2,1)S(1)}, u32[]{:S(2)}, u32[]{:S(2)}) collective-permute-start(bf16[4,64,1024]{2,1,0:T(8,128)(2,1)S(1)} %bitcast.108), channel_id=1, source_target_pairs={{0,4},{8,0},{16,8},{24,16},{28,24},{20,28},{12,20},{4,12},{1,5},{9... | collective-permute-start | bytes 1572872 | tf_op jit(solution)/shard_map/ppermute | solution.py:37
  212.8 31.1 %collective-permute-start.27 = (bf16[4,64,1024]{2,1,0:T(8,128)(2,1)S(1)}, bf16[4,64,1024]{2,1,0:T(8,128)(2,1)S(1)}, u32[]{:S(2)}, u32[]{:S(2)}) collective-permute-start(bf16[4,64,1024]{2,1,0:T(8,128)(2,1)S(1)} %collective-permute-done.22.refs_1_), channel_id=1, source_target_pairs={{0,8},{8,16},{16,24},{24,28},{28,20},{20,12},{12,4},{4,0},{1,9},{9... | collective-permute-start | bytes 1572872 | tf_op jit(solution)/shard_map/ppermute | solution.py:37
  218.7 25.2 %collective-permute-start.28 = (bf16[4,64,1024]{2,1,0:T(8,128)(2,1)S(1)}, bf16[4,64,1024]{2,1,0:T(8,128)(2,1)S(1)}, u32[]{:S(2)}, u32[]{:S(2)}) collective-permute-start(bf16[4,64,1024]{2,1,0:T(8,128)(2,1)S(1)} %collective-permute-done.23.refs_2_), channel_id=1, source_target_pairs={{0,4},{8,0},{16,8},{24,16},{28,24},{20,28},{12,20},{4,12},{1,5},{9... | collective-permute-start | bytes 1572872 | tf_op jit(solution)/shard_map/ppermute | solution.py:37
  221.5 33.6 %collective-permute-start.30 = (bf16[4,64,1024]{2,1,0:T(8,128)(2,1)}, bf16[4,64,1024]{2,1,0:T(8,128)(2,1)S(1)}, u32[]{:S(2)}, u32[]{:S(2)}) collective-permute-start(bf16[4,64,1024]{2,1,0:T(8,128)(2,1)} %collective-permute-done.25.refs_3_), channel_id=1, source_target_pairs={{0,8},{8,16},{16,24},{24,28},{28,20},{20,12},{12,4},{4,0},{1,9},{9... | collective-permute-start | bytes 1572872 | tf_op jit(solution)/shard_map/ppermute | solution.py:37
  225.0 30.1 %collective-permute-start.31 = (bf16[4,64,1024]{2,1,0:T(8,128)(2,1)}, bf16[4,64,1024]{2,1,0:T(8,128)(2,1)S(1)}, u32[]{:S(2)}, u32[]{:S(2)}) collective-permute-start(bf16[4,64,1024]{2,1,0:T(8,128)(2,1)} %collective-permute-done.26.refs_4_), channel_id=1, source_target_pairs={{0,4},{8,0},{16,8},{24,16},{28,24},{20,28},{12,20},{4,12},{1,5},{9... | collective-permute-start | bytes 1572872 | tf_op jit(solution)/shard_map/ppermute | solution.py:37
  269.2 28.9 %collective-permute-start.38 = (bf16[512,1024]{1,0:T(8,128)(2,1)S(1)}, bf16[512,1024]{1,0:T(8,128)(2,1)S(1)}, u32[]{:S(2)}, u32[]{:S(2)}) collective-permute-start(bf16[512,1024]{1,0:T(8,128)(2,1)S(1)} %copy-done.28), channel_id=1, source_target_pairs={{0,8},{8,16},{16,24},{24,28},{28,20},{20,12},{12,4},{4,0},{1,9},{9... | collective-permute-start | bytes 3145736 | tf_op jit(solution)/shard_map/ppermute | solution.py:37
  269.2 28.9 %collective-permute-start.39 = (bf16[512,1024]{1,0:T(8,128)(2,1)S(1)}, bf16[512,1024]{1,0:T(8,128)(2,1)S(1)}, u32[]{:S(2)}, u32[]{:S(2)}) collective-permute-start(bf16[512,1024]{1,0:T(8,128)(2,1)S(1)} %copy-done.28), channel_id=1, source_target_pairs={{0,4},{8,0},{16,8},{24,16},{28,24},{20,28},{12,20},{4,12},{1,5},{9... | collective-permute-start | bytes 3145736 | tf_op jit(solution)/shard_map/ppermute | solution.py:37
  271.3 26.8 %collective-permute-start.36 = (bf16[2,64,1024]{2,1,0:T(8,128)(2,1)S(1)}, bf16[2,64,1024]{2,1,0:T(8,128)(2,1)S(1)}, u32[]{:S(2)}, u32[]{:S(2)}) collective-permute-start(bf16[2,64,1024]{2,1,0:T(8,128)(2,1)S(1)} %slice.223), channel_id=1, source_target_pairs={{0,8},{8,16},{16,24},{24,28},{28,20},{20,12},{12,4},{4,0},{1,9},{9... | collective-permute-start | bytes 786440 | tf_op jit(solution)/shard_map/ppermute | solution.py:37
  271.7 26.4 %collective-permute-start.37 = (bf16[2,64,1024]{2,1,0:T(8,128)(2,1)S(1)}, bf16[2,64,1024]{2,1,0:T(8,128)(2,1)S(1)}, u32[]{:S(2)}, u32[]{:S(2)}) collective-permute-start(bf16[2,64,1024]{2,1,0:T(8,128)(2,1)S(1)} %slice.224), channel_id=1, source_target_pairs={{0,4},{8,0},{16,8},{24,16},{28,24},{20,28},{12,20},{4,12},{1,5},{9... | collective-permute-start | bytes 786440 | tf_op jit(solution)/shard_map/ppermute | solution.py:37
  298.1 25.1 %collective-permute-start.40 = (bf16[512,1024]{1,0:T(8,128)(2,1)S(1)}, bf16[512,1024]{1,0:T(8,128)(2,1)S(1)}, u32[]{:S(2)}, u32[]{:S(2)}) collective-permute-start(bf16[512,1024]{1,0:T(8,128)(2,1)S(1)} %collective-permute-done.38.refs_6_), channel_id=1, source_target_pairs={{0,8},{8,16},{16,24},{24,28},{28,20},{20,12},{12,4},{4,0},{1,9},{9... | collective-permute-start | bytes 3145736 | tf_op jit(solution)/shard_map/ppermute | solution.py:37
  298.2 25.0 %collective-permute-start.41 = (bf16[512,1024]{1,0:T(8,128)(2,1)S(1)}, bf16[512,1024]{1,0:T(8,128)(2,1)S(1)}, u32[]{:S(2)}, u32[]{:S(2)}) collective-permute-start(bf16[512,1024]{1,0:T(8,128)(2,1)S(1)} %collective-permute-done.39.refs_7_), channel_id=1, source_target_pairs={{0,4},{8,0},{16,8},{24,16},{28,24},{20,28},{12,20},{4,12},{1,5},{9... | collective-permute-start | bytes 3145736 | tf_op jit(solution)/shard_map/ppermute | solution.py:37
  323.2 22.0 %collective-permute-start.44 = (bf16[512,1024]{1,0:T(8,128)(2,1)S(1)}, bf16[512,1024]{1,0:T(8,128)(2,1)S(1)}, u32[]{:S(2)}, u32[]{:S(2)}) collective-permute-start(bf16[512,1024]{1,0:T(8,128)(2,1)S(1)} %collective-permute-done.40.refs_8_), channel_id=1, source_target_pairs={{0,8},{8,16},{16,24},{24,28},{28,20},{20,12},{12,4},{4,0},{1,9},{9... | collective-permute-start | bytes 3145736 | tf_op jit(solution)/shard_map/ppermute | solution.py:37
  345.3 27.9 %collective-permute-start.46 = (bf16[256,1024]{1,0:T(8,128)(2,1)S(1)}, bf16[256,1024]{1,0:T(8,128)(2,1)S(1)}, u32[]{:S(2)}, u32[]{:S(2)}) collective-permute-start(bf16[256,1024]{1,0:T(8,128)(2,1)S(1)} %slice.225), channel_id=1, source_target_pairs={{0,8},{8,16},{16,24},{24,28},{28,20},{20,12},{12,4},{4,0},{1,9},{9... | collective-permute-start | bytes 1572872 | tf_op jit(solution)/shard_map/ppermute | solution.py:37
  346.3 26.9 %collective-permute-start.47 = (bf16[256,1024]{1,0:T(8,128)(2,1)S(1)}, bf16[256,1024]{1,0:T(8,128)(2,1)S(1)}, u32[]{:S(2)}, u32[]{:S(2)}) collective-permute-start(bf16[256,1024]{1,0:T(8,128)(2,1)S(1)} %slice.226), channel_id=1, source_target_pairs={{0,4},{8,0},{16,8},{24,16},{28,24},{20,28},{12,20},{4,12},{1,5},{9... | collective-permute-start | bytes 1572872 | tf_op jit(solution)/shard_map/ppermute | solution.py:37
  447.7 31.2 %collective-permute-start.57 = (bf16[4,64,1024]{2,1,0:T(8,128)(2,1)S(1)}, bf16[4,64,1024]{2,1,0:T(8,128)(2,1)S(1)}, u32[]{:S(2)}, u32[]{:S(2)}) collective-permute-start(bf16[4,64,1024]{2,1,0:T(8,128)(2,1)S(1)} %add_convert_fusion.7), channel_id=1, source_target_pairs={{0,8},{8,16},{16,24},{24,28},{28,20},{20,12},{12,4},{4,0},{1,9},{9... | collective-permute-start | bytes 1572872 | tf_op jit(solution)/shard_map/ppermute | solution.py:37
  449.7 29.4 %collective-permute-start.58 = (bf16[4,64,1024]{2,1,0:T(8,128)(2,1)S(1)}, bf16[4,64,1024]{2,1,0:T(8,128)(2,1)S(1)}, u32[]{:S(2)}, u32[]{:S(2)}) collective-permute-start(bf16[4,64,1024]{2,1,0:T(8,128)(2,1)S(1)} %add_convert_fusion.6), channel_id=1, source_target_pairs={{0,4},{8,0},{16,8},{24,16},{28,24},{20,28},{12,20},{4,12},{1,5},{9... | collective-permute-start | bytes 1572872 | tf_op jit(solution)/shard_map/ppermute | solution.py:37
  (104 other events, 1687.0 us)

commit v10 on v8

--- a/solution.py
+++ b/solution.py
@@ -457,9 +457,9 @@
     )(first, places, live, *query_slots, keys, values, new_keys)
 
 
-def finish_kernel(slots, first_ref, place_ref, *refs):
+def finish_kernel(slots, filled, first_ref, place_ref, *refs):
     query_ref, key_ref, value_ref, cache_ref, peak_ref, total_ref, best_ref = refs[:7]
-    sum_ref, *part_refs = refs[7:-1]
+    sum_ref, *part_refs = refs[7 + filled : -1]
     joined_ref = refs[-1]
     tok_block = key_ref.shape[1]
     for head in range(query_ref.shape[2] // HEAD_DIM):
@@ -481,36 +481,43 @@
         part_refs[slot][0] = joined_ref[pl.ds(start, tok_block), :]
 
 
-def finish_part(begin, first, places, queries, new_keys, new_values, cached, peaks, totals, best):
+def finish_part(begin, at, count, first, places, queries, new_keys, new_values, cached, peaks, totals, best, filled=()):
     requests, tokens, width = queries.shape
     tok_block = new_keys.shape[1]
     slots = tokens // tok_block
     heads = width // HEAD_DIM
     one = lambda rows, start: pl.BlockSpec((1, rows, width), lambda r, *_: (r + start, 0, 0))
     stat = lambda start: pl.BlockSpec((1, heads, tokens), lambda r, *_: (r + start, 0, 0))
+    inputs = (queries, new_keys, new_values, cached, peaks, totals, best)
     return pl.pallas_call(
-        functools.partial(finish_kernel, slots),
+        functools.partial(finish_kernel, slots, len(filled)),
         grid_spec=pltpu.PrefetchScalarGridSpec(
             num_scalar_prefetch=2,
-            grid=(requests,),
+            grid=(count,),
             in_specs=[
-                one(tokens, 0),
-                one(tok_block, begin),
-                one(tok_block, begin),
-                pl.BlockSpec((1, width, tokens), lambda r, *_: (r, 0, 0)),
-                stat(0),
-                stat(0),
-                stat(begin),
-            ],
-            out_specs=[stat(0)] + [one(tok_block, 0)] * slots,
+                one(tokens, at),
+                one(tok_block, begin + at),
+                one(tok_block, begin + at),
+                pl.BlockSpec((1, width, tokens), lambda r, *_: (r + at, 0, 0)),
+                stat(at),
+                stat(at),
+                stat(begin + at),
+            ]
+            + [pl.BlockSpec(memory_space=pl.ANY)] * len(filled),
+            out_specs=[stat(at)] + [one(tok_block, at)] * slots,
             scratch_shapes=[pltpu.VMEM((tokens, width), jnp.bfloat16)],
         ),
         out_shape=[jax.ShapeDtypeStruct((requests, heads, tokens), jnp.float32)]
         + [jax.ShapeDtypeStruct((requests, tok_block, width), jnp.bfloat16)] * slots,
+        input_output_aliases={2 + len(inputs) + i: i for i in range(len(filled))},
         compiler_params=pltpu.CompilerParams(vmem_limit_bytes=VMEM_BYTES),
-        cost_estimate=LIGHT,
+        cost_estimate=pl.CostEstimate(
+            flops=4 * count * tokens * tok_block * width,
+            bytes_accessed=6 * count * width * tokens,
+            transcendentals=count * tokens * tok_block * heads,
+        ),
         name="finish_part",
-    )(first, places, queries, new_keys, new_values, cached, peaks, totals, best)
+    )(first, places, *inputs, *filled)
 
 
 def head_sum(terms, head_count, head_index):
@@ -815,11 +822,13 @@
         made["values"] = product(
             [(0, 0, clock.hold(value_ring.block))] + pieces, False, kind=jnp.float32
         )
-        return (made["values"],), ()
+        return (made["values"],) + leave_terms()[0], ()
 
     def join_more():
         made["best"].step(clock)
-        return leave_terms()
+        chain_split()
+        chain_turn()
+        return chain_join()
 
     def steps(rings, begin, end):
         return [ring for _ in range(begin, end) for ring in rings]
@@ -862,13 +871,17 @@
     residual = lax.dynamic_slice_in_dim(
         flat_input, head_index * local_width, local_width, 1
     ).astype(jnp.float32)
-    sums, ring_sums, mixed = [], [], []
-
-    def finish(index):
+    mixed = []
+
+    filled = {}
+
+    def finish(index, at, count):
         def work():
             joined, out, peaks, totals = cached[index]
-            some_sums, *parts = finish_part(
+            filled[index] = finish_part(
                 index * group,
+                at,
+                count,
                 first,
                 places,
                 clock.hold(joined),
@@ -878,32 +891,41 @@
                 peaks,
                 totals,
                 best,
+                filled.get(index, ()),
             )
-            sums.append(some_sums)
-            terms = {-offset: part for offset, part in zip(offsets, parts)}
-            terms[half] = terms[-half]
-            ring_sums.append(RingSum(terms, order))
-            return (some_sums, *parts), ()
+            return tuple(filled[index]), ()
 
         return work
+
+    def ring_sum(index):
+        terms = {-offset: part for offset, part in zip(offsets, filled[index][1:])}
+        terms[half] = terms[-half]
+        return RingSum(terms, order)
 
     def add_sums():
         if "sums" not in made:
-            made["sums"] = Exchange(jnp.concatenate(sums, axis=0), "seq", seq_count, jnp.add)
+            sums = jnp.concatenate([filled[index][0] for index in range(GROUPS)], axis=0)
+            made["sums"] = Exchange(sums, "seq", seq_count, jnp.add)
         made["sums"].step(clock)
         return (), ()
 
-    run([], [finish(0)])
-    run([ring_sums[0]], [finish(1)])
-    run(
-        steps(ring_sums[::-1], 0, half)[:-1],
-        [add_sums, chain_split, add_sums, chain_turn, add_sums, chain_join],
-    )
+    run([], [finish(0, 0, group)])
+    sum_rings = [ring_sum(0)]
+    run(sum_rings, [finish(1, 0, group // 2)])
+    clock.mark = clock.hold(clock.mark, sum_rings[0].ahead)[0]
+    run(sum_rings, [finish(1, group // 2, group - group // 2)])
+    sum_rings.append(ring_sum(1))
+    turns = steps(sum_rings[::-1], 0, half)
+    run(turns[: 2 * half - 3], [add_sums, None, add_sums, None, add_sums])
     denominators = jnp.transpose(own(made["sums"].result(clock)), (0, 2, 1))
+    last = sum_rings[1]
+    while last.left > 0:
+        run([last], [])
+
     for index in range(GROUPS):
         begin = index * group
         denominator = denominators[begin : begin + group]
-        numerator = ring_sums[index].total().reshape(group, tok_block, local_heads, HEAD_DIM)
+        numerator = sum_rings[index].total().reshape(group, tok_block, local_heads, HEAD_DIM)
         attended = (
             (numerator / denominator[..., None])
             .astype(jnp.bfloat16)

time: 524 us -> 548 us (1.046)
  waiting for transfers between devices: 164 us -> 187 us
  other arithmetic: 50.7 us -> 42 us
    ppermute x56, waiting for transfers between devices: 87.4 us -> 107 us  [ring_step(): return lax.ppermute(block, 'seq', route)]
    convert_element_type x12, other arithmetic: 13.8 us -> 7.59 us  [add(): return (a.astype(jnp.float32) + b.astype(jnp.float32)).astype(jnp.bfloat16)]
    ppermute x2, waiting for transfers between devices: 0.01 us -> 6.01 us  [head_sum(): lax.ppermute(give.astype(jnp.bfloat16), 'head', [(h, h ^ 2) for h in rang...]
    pallas_call x2 -> x3, Pallas kernels: 22.7 us -> 26 us  [finish_part(): pl.pallas_call(functools.partial(finish_kernel, slots, len(filled)), grid...]
    unnamed x126 -> x134, local copies, waits for them, and re-layouts: 18.4 us -> 18.4 us
  transfers between devices with their start and end apart: 74 -> 74, of which waited for: 27 -> 33; matrix products, arithmetic and copies ran while one was open for 22% -> 20% of each run, Pallas kernels for 22% -> 22%
where the time goes in v10:
time: 548 us; the launch traced here: 538 us
  waiting for transfers between devices  187 us (34%)
  Pallas kernels  136 us (25%)
  starting transfers between devices  90.9 us (17%)
  local copies, waits for them, and re-layouts  67.7 us (12%)
  other arithmetic  42 us (8%)
  matrix products  12.1 us (2%)
    ppermute x56, waiting for transfers between devices, ring_step(): return lax.ppermute(block, 'seq', route)  107 us
    ppermute x56, starting transfers between devices, ring_step(): return lax.ppermute(block, 'seq', route)  66.1 us
    pallas_call x2, Pallas kernels, cache_part(): pl.pallas_call(functools.partial(cache_kernel, slots), grid_spec=pltpu.Pr...  44.1 us
    pallas_call x4, Pallas kernels, project(): pl.pallas_call(functools.partial(project_kernel, len(pieces), turned), gr...  36.2 us
    ppermute x1, waiting for transfers between devices, __init__(): other_factor = side(lax.ppermute(through, 'seq', self.swap))  32.8 us
    pallas_call x3, Pallas kernels, finish_part(): pl.pallas_call(functools.partial(finish_kernel, slots, len(filled)), grid...  26 us
    ppermute x8, waiting for transfers between devices, step(): self.got = lax.ppermute(self.value, self.axis, route)  25.3 us
    unnamed x134, local copies, waits for them, and re-layouts  18.4 us
  transfers between devices with their start and end apart: 74, of which 33 were waited for; matrix products, arithmetic and copies ran while one was open for 20% of the time, Pallas kernels for 22%

profile of v10, /device:TPU:0, one launch (start us, length us, event | category | flops | bytes accessed | tf_op | source)
XLA Modules:
  0.0 537.9 jit_solution(13769284464463002758)
XLA Ops:
  3.7 10.5 %copy.61 = bf16[256,8,2,1024]{3,1,2,0:T(8,128)(2,1)} copy(bf16[256,8,2,1024]{3,2,1,0:T(2,128)(2,1)} %bitcast.106) | data formatting | bytes 16777216
  17.2 5.6 %copy.49 = f32[8,16,64,64]{2,1,3,0:T(8,128)} copy(f32[8,16,64,64]{3,2,1,0:T(8,128)} %reshape.124) | data formatting | bytes 4194304 | tf_op jit(solution)/shard_map/reshape | solution.py:680
  22.8 4.9 reshape.125
  30.7 11.6 %enter_mixer.1 = (f32[512,2048]{1,0:T(8,128)}, f32[512,128]{1,0:T(8,128)}, f32[512,16]{1,0:T(8,128)}) custom-call(bf16[512,4096]{1,0:T(8,128)(2,1)} %bitcast.64, f32[1,2048]{1,0:T(1,128)} %bitcast.124, bf16[2048,128]{1,0:T(8,128)(2,1)} %bc_ref.1, bf16[2048,16]{1,0:T(8,128)(2,1)} %copy.50.dt_ref, f32[1,16]{1,0:T(1,128)} %bitcast.129, bf16[2048,2048]{1,0:T(8,128)(2,1)} %bitcast.99), custom_call_target="tpu_custom_call" | custom-call | tf_op jit(solution)/shard_map/enter_mixer/pallas_call | solution.py:228
  49.8 9.6 %inside_block.1 = (f32[512,1024]{1,0:T(8,128)}, f32[8,64,1024]{2,1,0:T(8,128)}, f32[8,1,1024]{2,1,0:T(1,128)}) custom-call(f32[512,2048]{1,0:T(8,128)} %get-tuple-element.181.inner_ref.gate_ref, f32[512,128]{1,0:T(8,128)} %get-tuple-element.182.map_ref, f32[8,64,16]{2,1,0:T(8,128)} %bitcast.109, f32[8,64,16]{2,1,0:T(8,128)} %bitcast.113, ...), custom_call_target="tpu_custom_call" | custom-call | tf_op jit(solution)/shard_map/inside_block/pallas_call | solution.py:302
  65.1 32.8 %collective-permute-done.10 = f32[8,1,1024]{2,1,0:T(1,128)S(1)} collective-permute-done((f32[8,1,1024]{2,1,0:T(1,128)}, f32[8,1,1024]{2,1,0:T(1,128)S(1)}, u32[]{:S(2)}, u32[]{:S(2)}) %collective-permute-start.10) | collective-permute-done | bytes 32800 | tf_op jit(solution)/shard_map/ppermute | solution.py:562
  105.1 7.8 %collective-permute-done.11 = bf16[8,64,512]{2,1,0:T(8,128)(2,1)S(1)} collective-permute-done((bf16[8,64,512]{2,1,0:T(8,128)(2,1)S(1)}, bf16[8,64,512]{2,1,0:T(8,128)(2,1)S(1)}, u32[]{:S(2)}, u32[]{:S(2)}) %collective-permute-start.11) | collective-permute-done | bytes 524320 | tf_op jit(solution)/shard_map/ppermute | solution.py:573
  118.6 14.4 %collective-permute-done.6.refs_14_ = bf16[512,1024]{1,0:T(8,128)(2,1)S(1)} collective-permute-done((bf16[512,1024]{1,0:T(8,128)(2,1)}, bf16[512,1024]{1,0:T(8,128)(2,1)S(1)}, u32[]{:S(2)}, u32[]{:S(2)}) %collective-permute-start.6) | collective-permute-done | bytes 1048608 | tf_op jit(solution)/shard_map/ppermute | solution.py:37
  142.1 9.7 %collective-permute-done.12.refs_16_ = bf16[256,1024]{1,0:T(8,128)(2,1)} collective-permute-done((bf16[256,1024]{1,0:T(8,128)(2,1)}, bf16[256,1024]{1,0:T(8,128)(2,1)}, u32[]{:S(2)}, u32[]{:S(2)}) %collective-permute-start.12) | collective-permute-done | bytes 524320 | tf_op jit(solution)/shard_map/ppermute | solution.py:37
  157.5 10.4 %project.4 = bf16[512,1024]{1,0:T(8,128)(2,1)} custom-call(s32[8]{0:T(128)} %fusion.21.places_ref.place_ref, bf16[512,4096]{1,0:T(8,128)(2,1)} %bitcast.65, bf16[512,4096]{1,0:T(8,128)(2,1)} %bitcast.66, bf16[512,4096]{1,0:T(8,128)(2,1)} %bitcast.67, bf16[512,4096]{1,0:T(8,128)(2,1)} %bitcast.68, bf16[512,4096]{1,0:T(8,128)(2,1)} %bitcast.69, ...), custom_call_target="tpu_custom_call" | custom-call | tf_op jit(solution)/shard_map/project/pallas_call | solution.py:170
  180.5 7.6 %collective-permute-done.17.refs_16_ = bf16[256,1024]{1,0:T(8,128)(2,1)S(1)} collective-permute-done((bf16[256,1024]{1,0:T(8,128)(2,1)S(1)}, bf16[256,1024]{1,0:T(8,128)(2,1)S(1)}, u32[]{:S(2)}, u32[]{:S(2)}) %collective-permute-start.17) | collective-permute-done | bytes 524320 | tf_op jit(solution)/shard_map/ppermute | solution.py:37
  194.6 10.6 %project.5 = bf16[512,1024]{1,0:T(8,128)(2,1)} custom-call(s32[8]{0:T(128)} %fusion.21.places_ref.place_ref, bf16[512,4096]{1,0:T(8,128)(2,1)} %bitcast.78, bf16[512,4096]{1,0:T(8,128)(2,1)} %bitcast.75, bf16[512,4096]{1,0:T(8,128)(2,1)} %bitcast.76, bf16[512,4096]{1,0:T(8,128)(2,1)} %bitcast.77, bf16[512,4096]{1,0:T(8,128)(2,1)} %bitcast.74, ...), custom_call_target="tpu_custom_call" | custom-call | tf_op jit(solution)/shard_map/project/pallas_call | solution.py:170
  225.1 8.1 %collective-permute-done.29 = bf16[8,64,512]{2,1,0:T(8,128)(2,1)S(1)} collective-permute-done((bf16[8,64,512]{2,1,0:T(8,128)(2,1)S(1)}, bf16[8,64,512]{2,1,0:T(8,128)(2,1)S(1)}, u32[]{:S(2)}, u32[]{:S(2)}) %collective-permute-start.29) | collective-permute-done | bytes 524320 | tf_op jit(solution)/shard_map/ppermute | solution.py:573
  235.1 9.4 %collective-permute-done.27.refs_3_ = bf16[4,64,1024]{2,1,0:T(8,128)(2,1)S(1)} collective-permute-done((bf16[4,64,1024]{2,1,0:T(8,128)(2,1)S(1)}, bf16[4,64,1024]{2,1,0:T(8,128)(2,1)S(1)}, u32[]{:S(2)}, u32[]{:S(2)}) %collective-permute-start.27) | collective-permute-done | bytes 524320 | tf_op jit(solution)/shard_map/ppermute | solution.py:37
  246.6 8.9 %leave_mixer.1 = (bf16[512,1024]{1,0:T(8,128)(2,1)}, f32[512,128]{1,0:T(8,128)}, f32[8,64,1024]{2,1,0:T(8,128)}) custom-call(f32[8,64,1024]{2,1,0:T(8,128)} %pad_maximum_fusion.entry_ref, f32[512,128]{1,0:T(8,128)} %get-tuple-element.182.map_ref, f32[8,64,16]{2,1,0:T(8,128)} %bitcast.110, f32[512,1024]{1,0:T(8,128)} %get-tuple-element.183.read_ref, ...), custom_call_target="tpu_custom_call" | custom-call | tf_op jit(solution)/shard_map/leave_mixer/pallas_call | solution.py:351
  257.9 7.5 %collective-permute-done.32.refs_5_ = bf16[4,64,1024]{2,1,0:T(8,128)(2,1)S(1)} collective-permute-done((bf16[4,64,1024]{2,1,0:T(8,128)(2,1)S(1)}, bf16[4,64,1024]{2,1,0:T(8,128)(2,1)S(1)}, u32[]{:S(2)}, u32[]{:S(2)}) %collective-permute-start.32) | collective-permute-done | bytes 524320 | tf_op jit(solution)/shard_map/ppermute | solution.py:37
  275.5 22.0 %cache_part.2 = (bf16[4,512,1024]{2,1,0:T(8,128)(2,1)}, bf16[4,1024,512]{2,1,0:T(8,128)(2,1)}, f32[4,8,512]{2,1,0:T(8,128)}, f32[4,8,512]{2,1,0:T(8,128)}) custom-call(s32[1]{0:T(128)} %bitcast.1.first_ref, s32[8]{0:T(128)} %fusion.21.places_ref.place_ref, s32[4]{0:T(128)} %get-tuple-element.360.live_ref, bf16[4,64,1024]{2,1,0:T(8,128)(2,1)} %bitcast.119, ...), custom_call_target="tpu_custom_call" | custom-call | tf_op jit(solution)/shard_map/cache_part/pallas_call | solution.py:433
  301.6 22.1 %cache_part.3 = (bf16[4,512,1024]{2,1,0:T(8,128)(2,1)}, bf16[4,1024,512]{2,1,0:T(8,128)(2,1)}, f32[4,8,512]{2,1,0:T(8,128)}, f32[4,8,512]{2,1,0:T(8,128)}) custom-call(s32[1]{0:T(128)} %bitcast.1.first_ref, s32[8]{0:T(128)} %fusion.21.places_ref.place_ref, s32[4]{0:T(128)} %get-tuple-element.359.live_ref, bf16[4,64,1024]{2,1,0:T(8,128)(2,1)} %bitcast.116, ...), custom_call_target="tpu_custom_call" | custom-call | tf_op jit(solution)/shard_map/cache_part/pallas_call | solution.py:433
  331.0 6.5 %convolution_multiply_fusion = f32[512,2048]{1,0:T(8,128)} fusion(bf16[512,1024]{1,0:T(8,128)(2,1)S(1)} %copy-done.62, bf16[1024,2048]{1,0:T(8,128)(2,1)} %param.35, f32[512]{0:T(512)S(1)} %bitcast.128), kind=kOutput, calls=%fused_computation | convolution fusion | flops 2148532224 | bytes 9439232 | tf_op jit(solution)/shard_map/dot_general | solution.py:755
  337.6 8.3 %project.6.refs_10_ = f32[512,1024]{1,0:T(8,128)} custom-call(s32[8]{0:T(128)} %fusion.21.places_ref.place_ref, bf16[512,4096]{1,0:T(8,128)(2,1)} %bitcast.83, bf16[512,4096]{1,0:T(8,128)(2,1)} %bitcast.84, bf16[512,4096]{1,0:T(8,128)(2,1)} %bitcast.85, bf16[512,4096]{1,0:T(8,128)(2,1)} %bitcast.86, bf16[512,4096]{1,0:T(8,128)(2,1)} %bitcast.87, ...), custom_call_target="tpu_custom_call" | custom-call | tf_op jit(solution)/shard_map/project/pallas_call | solution.py:170
  351.5 12.3 %collective-permute-done.48 = f32[8,8,512]{2,1,0:T(8,128)S(1)} collective-permute-done((f32[8,8,512]{2,1,0:T(8,128)S(1)}, f32[8,8,512]{2,1,0:T(8,128)S(1)}, u32[]{:S(2)}, u32[]{:S(2)}) %collective-permute-start.48) | collective-permute-done | bytes 131104 | tf_op jit(solution)/shard_map/ppermute | solution.py:97
  368.5 5.6 %copy.54 = f32[8,16,64,64]{3,2,1,0:T(8,128)} copy(f32[8,16,64,64]{2,1,3,0:T(8,128)} %bitcast.101) | data formatting | bytes 4194304 | tf_op jit(solution)/shard_map/optimization_barrier | solution.py:72
  390.4 6.8 %project.7 = bf16[512,1024]{1,0:T(8,128)(2,1)} custom-call(s32[8]{0:T(128)} %fusion.21.places_ref.place_ref, bf16[512,4096]{1,0:T(8,128)(2,1)} %bitcast.88, bf16[512,4096]{1,0:T(8,128)(2,1)} %bitcast.89, bf16[512,4096]{1,0:T(8,128)(2,1)} %bitcast.90, bf16[512,4096]{1,0:T(8,128)(2,1)} %bitcast.91, bf16[512,1024]{1,0:T(8,128)(2,1)} %copy-done.13, ...), custom_call_target="tpu_custom_call" | custom-call | tf_op jit(solution)/shard_map/project/pallas_call | solution.py:170
  397.2 11.3 %finish_part.3 = (f32[4,8,512]{2,1,0:T(8,128)}, bf16[4,64,1024]{2,1,0:T(8,128)(2,1)}, bf16[4,64,1024]{2,1,0:T(8,128)(2,1)}, bf16[4,64,1024]{2,1,0:T(8,128)(2,1)}...) custom-call(s32[1]{0:T(128)} %bitcast.1.first_ref, ...), custom_call_target="tpu_custom_call" | custom-call | flops 536870912 | bytes 12582912 | tf_op jit(solution)/shard_map/finish_part/pallas_call | solution.py:492
  411.5 7.4 %finish_part.4 = (f32[4,8,512]{2,1,0:T(8,128)}, bf16[4,64,1024]{2,1,0:T(8,128)(2,1)}, bf16[4,64,1024]{2,1,0:T(8,128)(2,1)}, bf16[4,64,1024]{2,1,0:T(8,128)(2,1)}...) custom-call(s32[1]{0:T(128)} %bitcast.1.first_ref, ...), custom_call_target="tpu_custom_call" | custom-call | flops 268435456 | bytes 6291456 | tf_op jit(solution)/shard_map/finish_part/pallas_call | solution.py:492
  421.1 5.1 collective-permute-done.52
  428.5 7.3 %finish_part.5 = (f32[4,8,512]{2,1,0:T(8,128)}, bf16[4,64,1024]{2,1,0:T(8,128)(2,1)}, bf16[4,64,1024]{2,1,0:T(8,128)(2,1)}, bf16[4,64,1024]{2,1,0:T(8,128)(2,1)}...) custom-call(s32[1]{0:T(128)} %bitcast.1.first_ref, ...), custom_call_target="tpu_custom_call", output_to_operand_aliasing={{0}: (9, {}), {1}: (10, {}), {2}: (11, {}), {3}: (12, {}), ... | custom-call | flops 268435456 | bytes 6291456 | tf_op jit(solution)/shard_map/finish_part/pallas_call | solution.py:492
  455.2 6.9 %collective-permute-done.55 = bf16[4,64,1024]{2,1,0:T(8,128)(2,1)S(1)} collective-permute-done((bf16[4,64,1024]{2,1,0:T(8,128)(2,1)S(1)}, bf16[4,64,1024]{2,1,0:T(8,128)(2,1)S(1)}, u32[]{:S(2)}, u32[]{:S(2)}) %collective-permute-start.55) | collective-permute-done | bytes 524320 | tf_op jit(solution)/shard_map/ppermute | solution.py:37
  467.3 7.5 %collective-permute-done.63 = bf16[4,64,1024]{2,1,0:T(8,128)(2,1)S(1)} collective-permute-done((bf16[4,64,1024]{2,1,0:T(8,128)(2,1)S(1)}, bf16[4,64,1024]{2,1,0:T(8,128)(2,1)S(1)}, u32[]{:S(2)}, u32[]{:S(2)}) %collective-permute-start.63) | collective-permute-done | bytes 524320 | tf_op jit(solution)/shard_map/ppermute | solution.py:37
  486.2 4.9 collective-permute-done.60
  491.1 5.2 collective-permute-done.65
  529.6 5.3 collective-permute-done.73
  (367 shorter events, 221.6 us)
Async XLA Ops:
  0.6 45.6 %collective-permute-start = (bf16[512,1024]{1,0:T(8,128)(2,1)}, bf16[512,1024]{1,0:T(8,128)(2,1)}, u32[]{:S(2)}, u32[]{:S(2)}) collective-permute-start(bf16[512,1024]{1,0:T(8,128)(2,1)} %refs_9_.4), channel_id=1, source_target_pairs={{0,8},{8,16},{16,24},{24,28},{28,20},{20,12},{12,4},{4,0},{1,9},{9... | collective-permute-start | bytes 3145736 | tf_op jit(solution)/shard_map/ppermute | solution.py:37
  3.7 42.5 %collective-permute-start.1 = (bf16[512,1024]{1,0:T(8,128)(2,1)}, bf16[512,1024]{1,0:T(8,128)(2,1)}, u32[]{:S(2)}, u32[]{:S(2)}) collective-permute-start(bf16[512,1024]{1,0:T(8,128)(2,1)} %refs_9_.4), channel_id=1, source_target_pairs={{0,4},{8,0},{16,8},{24,16},{28,24},{20,28},{12,20},{4,12},{1,5},{9... | collective-permute-start | bytes 3145736 | tf_op jit(solution)/shard_map/ppermute | solution.py:37
  27.7 31.7 %collective-permute-start.4 = (bf16[512,1024]{1,0:T(8,128)(2,1)S(1)}, bf16[512,1024]{1,0:T(8,128)(2,1)}, u32[]{:S(2)}, u32[]{:S(2)}) collective-permute-start(bf16[512,1024]{1,0:T(8,128)(2,1)S(1)} %copy-done.29), channel_id=1, source_target_pairs={{0,8},{8,16},{16,24},{24,28},{28,20},{20,12},{12,4},{4,0},{1,9},{9... | collective-permute-start | bytes 3145736 | tf_op jit(solution)/shard_map/ppermute | solution.py:37
  29.7 29.7 %collective-permute-start.5 = (bf16[512,1024]{1,0:T(8,128)(2,1)S(1)}, bf16[512,1024]{1,0:T(8,128)(2,1)}, u32[]{:S(2)}, u32[]{:S(2)}) collective-permute-start(bf16[512,1024]{1,0:T(8,128)(2,1)S(1)} %copy-done.29), channel_id=1, source_target_pairs={{0,4},{8,0},{16,8},{24,16},{28,24},{20,28},{12,20},{4,12},{1,5},{9... | collective-permute-start | bytes 3145736 | tf_op jit(solution)/shard_map/ppermute | solution.py:37
  46.2 56.3 %collective-permute-start.2 = (bf16[512,1024]{1,0:T(8,128)(2,1)}, bf16[512,1024]{1,0:T(8,128)(2,1)}, u32[]{:S(2)}, u32[]{:S(2)}) collective-permute-start(bf16[512,1024]{1,0:T(8,128)(2,1)} %collective-permute-done.refs_10_), channel_id=1, source_target_pairs={{0,8},{8,16},{16,24},{24,28},{28,20},{20,12},{12,4},{4,0},{1,9},{9... | collective-permute-start | bytes 3145736 | tf_op jit(solution)/shard_map/ppermute | solution.py:37
  48.2 54.3 %collective-permute-start.3 = (bf16[512,1024]{1,0:T(8,128)(2,1)}, bf16[512,1024]{1,0:T(8,128)(2,1)}, u32[]{:S(2)}, u32[]{:S(2)}) collective-permute-start(bf16[512,1024]{1,0:T(8,128)(2,1)} %collective-permute-done.1.refs_11_), channel_id=1, source_target_pairs={{0,4},{8,0},{16,8},{24,16},{28,24},{20,28},{12,20},{4,12},{1,5},{9... | collective-permute-start | bytes 3145736 | tf_op jit(solution)/shard_map/ppermute | solution.py:37
  59.5 56.6 %collective-permute-start.8 = (bf16[512,1024]{1,0:T(8,128)(2,1)}, bf16[512,1024]{1,0:T(8,128)(2,1)}, u32[]{:S(2)}, u32[]{:S(2)}) collective-permute-start(bf16[512,1024]{1,0:T(8,128)(2,1)} %collective-permute-done.4.refs_10_), channel_id=1, source_target_pairs={{0,8},{8,16},{16,24},{24,28},{28,20},{20,12},{12,4},{4,0},{1,9},{9... | collective-permute-start | bytes 3145736 | tf_op jit(solution)/shard_map/ppermute | solution.py:37
  61.5 54.5 %collective-permute-start.9 = (bf16[512,1024]{1,0:T(8,128)(2,1)}, bf16[512,1024]{1,0:T(8,128)(2,1)}, u32[]{:S(2)}, u32[]{:S(2)}) collective-permute-start(bf16[512,1024]{1,0:T(8,128)(2,1)} %collective-permute-done.5.refs_11_), channel_id=1, source_target_pairs={{0,4},{8,0},{16,8},{24,16},{28,24},{20,28},{12,20},{4,12},{1,5},{9... | collective-permute-start | bytes 3145736 | tf_op jit(solution)/shard_map/ppermute | solution.py:37
  61.5 36.4 %collective-permute-start.10 = (f32[8,1,1024]{2,1,0:T(1,128)}, f32[8,1,1024]{2,1,0:T(1,128)S(1)}, u32[]{:S(2)}, u32[]{:S(2)}) collective-permute-start(f32[8,1,1024]{2,1,0:T(1,128)} %get-tuple-element.191.through_ref), channel_id=1, source_target_pairs={{0,4},{4,0},{8,12},{12,8},{16,20},{20,16},{24,28},{28,24},{1,5},{5... | collective-permute-start | bytes 98312 | tf_op jit(solution)/shard_map/ppermute | solution.py:562
  102.5 30.5 %collective-permute-start.6 = (bf16[512,1024]{1,0:T(8,128)(2,1)}, bf16[512,1024]{1,0:T(8,128)(2,1)S(1)}, u32[]{:S(2)}, u32[]{:S(2)}) collective-permute-start(bf16[512,1024]{1,0:T(8,128)(2,1)} %collective-permute-done.2.refs_12_), channel_id=1, source_target_pairs={{0,8},{8,16},{16,24},{24,28},{28,20},{20,12},{12,4},{4,0},{1,9},{9... | collective-permute-start | bytes 3145736 | tf_op jit(solution)/shard_map/ppermute | solution.py:37
  102.6 32.2 %collective-permute-start.7 = (bf16[512,1024]{1,0:T(8,128)(2,1)}, bf16[512,1024]{1,0:T(8,128)(2,1)S(1)}, u32[]{:S(2)}, u32[]{:S(2)}) collective-permute-start(bf16[512,1024]{1,0:T(8,128)(2,1)} %collective-permute-done.3.refs_13_), channel_id=1, source_target_pairs={{0,4},{8,0},{16,8},{24,16},{28,24},{20,28},{12,20},{4,12},{1,5},{9... | collective-permute-start | bytes 3145736 | tf_op jit(solution)/shard_map/ppermute | solution.py:37
  116.3 24.5 %collective-permute-start.14 = (bf16[8,64,512]{2,1,0:T(8,128)(2,1)S(1)}, bf16[8,64,512]{2,1,0:T(8,128)(2,1)}, u32[]{:S(2)}, u32[]{:S(2)}) collective-permute-start(bf16[8,64,512]{2,1,0:T(8,128)(2,1)S(1)} %add_convert_fusion.10), channel_id=1, source_target_pairs={{0,8},{4,12},{1,9},{5,13},{2,10},{6,14},{3,11},{7,15}} | collective-permute-start | bytes 1572872 | tf_op jit(solution)/shard_map/ppermute | solution.py:588
  138.8 32.3 %collective-permute-start.15 = (bf16[512,1024]{1,0:T(8,128)(2,1)}, bf16[512,1024]{1,0:T(8,128)(2,1)}, u32[]{:S(2)}, u32[]{:S(2)}) collective-permute-start(bf16[512,1024]{1,0:T(8,128)(2,1)} %collective-permute-done.8.refs_12_), channel_id=1, source_target_pairs={{0,8},{8,16},{16,24},{24,28},{28,20},{20,12},{12,4},{4,0},{1,9},{9... | collective-permute-start | bytes 3145736 | tf_op jit(solution)/shard_map/ppermute | solution.py:37
  138.8 33.3 %collective-permute-start.16 = (bf16[512,1024]{1,0:T(8,128)(2,1)}, bf16[512,1024]{1,0:T(8,128)(2,1)}, u32[]{:S(2)}, u32[]{:S(2)}) collective-permute-start(bf16[512,1024]{1,0:T(8,128)(2,1)} %collective-permute-done.9.refs_13_), channel_id=1, source_target_pairs={{0,4},{8,0},{16,8},{24,16},{28,24},{20,28},{12,20},{4,12},{1,5},{9... | collective-permute-start | bytes 3145736 | tf_op jit(solution)/shard_map/ppermute | solution.py:37
  152.9 24.0 %collective-permute-start.19 = (bf16[8,64,512]{2,1,0:T(8,128)(2,1)}, bf16[8,64,512]{2,1,0:T(8,128)(2,1)}, u32[]{:S(2)}, u32[]{:S(2)}) collective-permute-start(bf16[8,64,512]{2,1,0:T(8,128)(2,1)} %add_convert_fusion.9), channel_id=1, source_target_pairs={{8,16},{12,20},{9,17},{13,21},{10,18},{14,22},{11,19},{15,23}} | collective-permute-start | bytes 1572872 | tf_op jit(solution)/shard_map/ppermute | solution.py:588
  178.4 26.8 %collective-permute-start.20 = (bf16[4,64,1024]{2,1,0:T(8,128)(2,1)S(1)}, bf16[4,64,1024]{2,1,0:T(8,128)(2,1)S(1)}, u32[]{:S(2)}, u32[]{:S(2)}) collective-permute-start(bf16[4,64,1024]{2,1,0:T(8,128)(2,1)S(1)} %bitcast.117), channel_id=1, source_target_pairs={{0,8},{8,16},{16,24},{24,28},{28,20},{20,12},{12,4},{4,0},{1,9},{9... | collective-permute-start | bytes 1572872 | tf_op jit(solution)/shard_map/ppermute | solution.py:37
  180.5 24.8 %collective-permute-start.21 = (bf16[4,64,1024]{2,1,0:T(8,128)(2,1)S(1)}, bf16[4,64,1024]{2,1,0:T(8,128)(2,1)S(1)}, u32[]{:S(2)}, u32[]{:S(2)}) collective-permute-start(bf16[4,64,1024]{2,1,0:T(8,128)(2,1)S(1)} %bitcast.118), channel_id=1, source_target_pairs={{0,4},{8,0},{16,8},{24,16},{28,24},{20,28},{12,20},{4,12},{1,5},{9... | collective-permute-start | bytes 1572872 | tf_op jit(solution)/shard_map/ppermute | solution.py:37
  214.0 30.5 %collective-permute-start.27 = (bf16[4,64,1024]{2,1,0:T(8,128)(2,1)S(1)}, bf16[4,64,1024]{2,1,0:T(8,128)(2,1)S(1)}, u32[]{:S(2)}, u32[]{:S(2)}) collective-permute-start(bf16[4,64,1024]{2,1,0:T(8,128)(2,1)S(1)} %collective-permute-done.22.refs_1_), channel_id=1, source_target_pairs={{0,8},{8,16},{16,24},{24,28},{28,20},{20,12},{12,4},{4,0},{1,9},{9... | collective-permute-start | bytes 1572872 | tf_op jit(solution)/shard_map/ppermute | solution.py:37
  218.7 25.8 %collective-permute-start.28 = (bf16[4,64,1024]{2,1,0:T(8,128)(2,1)S(1)}, bf16[4,64,1024]{2,1,0:T(8,128)(2,1)S(1)}, u32[]{:S(2)}, u32[]{:S(2)}) collective-permute-start(bf16[4,64,1024]{2,1,0:T(8,128)(2,1)S(1)} %collective-permute-done.23.refs_2_), channel_id=1, source_target_pairs={{0,4},{8,0},{16,8},{24,16},{28,24},{20,28},{12,20},{4,12},{1,5},{9... | collective-permute-start | bytes 1572872 | tf_op jit(solution)/shard_map/ppermute | solution.py:37
  222.0 33.7 %collective-permute-start.30 = (bf16[4,64,1024]{2,1,0:T(8,128)(2,1)S(1)}, bf16[4,64,1024]{2,1,0:T(8,128)(2,1)S(1)}, u32[]{:S(2)}, u32[]{:S(2)}) collective-permute-start(bf16[4,64,1024]{2,1,0:T(8,128)(2,1)S(1)} %collective-permute-done.25.refs_3_), channel_id=1, source_target_pairs={{0,8},{8,16},{16,24},{24,28},{28,20},{20,12},{12,4},{4,0},{1,9},{9... | collective-permute-start | bytes 1572872 | tf_op jit(solution)/shard_map/ppermute | solution.py:37
  225.1 30.6 %collective-permute-start.31 = (bf16[4,64,1024]{2,1,0:T(8,128)(2,1)S(1)}, bf16[4,64,1024]{2,1,0:T(8,128)(2,1)S(1)}, u32[]{:S(2)}, u32[]{:S(2)}) collective-permute-start(bf16[4,64,1024]{2,1,0:T(8,128)(2,1)S(1)} %collective-permute-done.26.refs_4_), channel_id=1, source_target_pairs={{0,4},{8,0},{16,8},{24,16},{28,24},{20,28},{12,20},{4,12},{1,5},{9... | collective-permute-start | bytes 1572872 | tf_op jit(solution)/shard_map/ppermute | solution.py:37
  269.8 28.9 %collective-permute-start.38 = (bf16[512,1024]{1,0:T(8,128)(2,1)S(1)}, bf16[512,1024]{1,0:T(8,128)(2,1)S(1)}, u32[]{:S(2)}, u32[]{:S(2)}) collective-permute-start(bf16[512,1024]{1,0:T(8,128)(2,1)S(1)} %copy-done.30), channel_id=1, source_target_pairs={{0,8},{8,16},{16,24},{24,28},{28,20},{20,12},{12,4},{4,0},{1,9},{9... | collective-permute-start | bytes 3145736 | tf_op jit(solution)/shard_map/ppermute | solution.py:37
  269.8 28.9 %collective-permute-start.39 = (bf16[512,1024]{1,0:T(8,128)(2,1)S(1)}, bf16[512,1024]{1,0:T(8,128)(2,1)S(1)}, u32[]{:S(2)}, u32[]{:S(2)}) collective-permute-start(bf16[512,1024]{1,0:T(8,128)(2,1)S(1)} %copy-done.30), channel_id=1, source_target_pairs={{0,4},{8,0},{16,8},{24,16},{28,24},{20,28},{12,20},{4,12},{1,5},{9... | collective-permute-start | bytes 3145736 | tf_op jit(solution)/shard_map/ppermute | solution.py:37
  271.8 26.8 %collective-permute-start.36 = (bf16[2,64,1024]{2,1,0:T(8,128)(2,1)S(1)}, bf16[2,64,1024]{2,1,0:T(8,128)(2,1)S(1)}, u32[]{:S(2)}, u32[]{:S(2)}) collective-permute-start(bf16[2,64,1024]{2,1,0:T(8,128)(2,1)S(1)} %slice.207), channel_id=1, source_target_pairs={{0,8},{8,16},{16,24},{24,28},{28,20},{20,12},{12,4},{4,0},{1,9},{9... | collective-permute-start | bytes 786440 | tf_op jit(solution)/shard_map/ppermute | solution.py:37
  272.0 26.7 %collective-permute-start.37 = (bf16[2,64,1024]{2,1,0:T(8,128)(2,1)S(1)}, bf16[2,64,1024]{2,1,0:T(8,128)(2,1)S(1)}, u32[]{:S(2)}, u32[]{:S(2)}) collective-permute-start(bf16[2,64,1024]{2,1,0:T(8,128)(2,1)S(1)} %slice.208), channel_id=1, source_target_pairs={{0,4},{8,0},{16,8},{24,16},{28,24},{20,28},{12,20},{4,12},{1,5},{9... | collective-permute-start | bytes 786440 | tf_op jit(solution)/shard_map/ppermute | solution.py:37
  298.7 25.1 %collective-permute-start.40 = (bf16[512,1024]{1,0:T(8,128)(2,1)S(1)}, bf16[512,1024]{1,0:T(8,128)(2,1)S(1)}, u32[]{:S(2)}, u32[]{:S(2)}) collective-permute-start(bf16[512,1024]{1,0:T(8,128)(2,1)S(1)} %collective-permute-done.38.refs_6_), channel_id=1, source_target_pairs={{0,8},{8,16},{16,24},{24,28},{28,20},{20,12},{12,4},{4,0},{1,9},{9... | collective-permute-start | bytes 3145736 | tf_op jit(solution)/shard_map/ppermute | solution.py:37
  298.9 24.9 %collective-permute-start.41 = (bf16[512,1024]{1,0:T(8,128)(2,1)S(1)}, bf16[512,1024]{1,0:T(8,128)(2,1)S(1)}, u32[]{:S(2)}, u32[]{:S(2)}) collective-permute-start(bf16[512,1024]{1,0:T(8,128)(2,1)S(1)} %collective-permute-done.39.refs_7_), channel_id=1, source_target_pairs={{0,4},{8,0},{16,8},{24,16},{28,24},{20,28},{12,20},{4,12},{1,5},{9... | collective-permute-start | bytes 3145736 | tf_op jit(solution)/shard_map/ppermute | solution.py:37
  347.7 41.1 %collective-permute-start.46 = (bf16[256,1024]{1,0:T(8,128)(2,1)}, bf16[256,1024]{1,0:T(8,128)(2,1)S(1)}, u32[]{:S(2)}, u32[]{:S(2)}) collective-permute-start(bf16[256,1024]{1,0:T(8,128)(2,1)} %slice.209), channel_id=1, source_target_pairs={{0,8},{8,16},{16,24},{24,28},{28,20},{20,12},{12,4},{4,0},{1,9},{9... | collective-permute-start | bytes 1572872 | tf_op jit(solution)/shard_map/ppermute | solution.py:37
  348.9 39.9 %collective-permute-start.47 = (bf16[256,1024]{1,0:T(8,128)(2,1)}, bf16[256,1024]{1,0:T(8,128)(2,1)S(1)}, u32[]{:S(2)}, u32[]{:S(2)}) collective-permute-start(bf16[256,1024]{1,0:T(8,128)(2,1)} %slice.210), channel_id=1, source_target_pairs={{0,4},{8,0},{16,8},{24,16},{28,24},{20,28},{12,20},{4,12},{1,5},{9... | collective-permute-start | bytes 1572872 | tf_op jit(solution)/shard_map/ppermute | solution.py:37
  452.3 26.3 %collective-permute-start.62 = (f32[8,8,512]{2,1,0:T(8,128)S(1)}, f32[8,8,512]{2,1,0:T(8,128)S(1)}, u32[]{:S(2)}, u32[]{:S(2)}) collective-permute-start(f32[8,8,512]{2,1,0:T(8,128)S(1)} %add.234), channel_id=1, source_target_pairs={{0,8},{4,12},{8,0},{12,4},{16,24},{20,28},{24,16},{28,20},{1,9},{5... | collective-permute-start | bytes 393224 | tf_op jit(solution)/shard_map/ppermute | solution.py:97
  454.4 23.0 %collective-permute-start.64 = (bf16[4,64,1024]{2,1,0:T(8,128)(2,1)S(1)}, bf16[4,64,1024]{2,1,0:T(8,128)(2,1)S(1)}, u32[]{:S(2)}, u32[]{:S(2)}) collective-permute-start(bf16[4,64,1024]{2,1,0:T(8,128)(2,1)S(1)} %pad_maximum_fusion.6), channel_id=1, source_target_pairs={{0,4},{8,0},{16,8},{24,16},{28,24},{20,28},{12,20},{4,12},{1,5},{9... | collective-permute-start | bytes 1572872 | tf_op jit(solution)/shard_map/ppermute | solution.py:37
  466.2 24.9 %collective-permute-start.60 = (bf16[4,64,1024]{2,1,0:T(8,128)(2,1)}, bf16[4,64,1024]{2,1,0:T(8,128)(2,1)S(1)}, u32[]{:S(2)}, u32[]{:S(2)}) collective-permute-start(bf16[4,64,1024]{2,1,0:T(8,128)(2,1)} %add_convert_fusion.4), channel_id=1, source_target_pairs={{0,4},{8,0},{16,8},{24,16},{28,24},{20,28},{12,20},{4,12},{1,5},{9... | collective-permute-start | bytes 1572872 | tf_op jit(solution)/shard_map/ppermute | solution.py:37
  (106 other events, 1779.0 us)

commit v11 on v7

--- a/solution.py
+++ b/solution.py
@@ -351,7 +351,7 @@
     squares = jnp.sum(mixed * mixed, axis=1, keepdims=True)
     square_ref[...] = jnp.broadcast_to(squares, square_ref.shape)
     gated_ref[...] = (mixed * gain_ref[...]).astype(jnp.bfloat16)
-    chain_ref[0] = through_ref[0] * entry + local_ref[0]
+    chain_ref[0] = (through_ref[0] * entry + local_ref[0]).T
 
 
 def leave_mixer(entry, maps, decay, read, act, gain, local, through):
@@ -372,11 +372,11 @@
             one(STATE, inner),
             one(1, inner),
         ],
-        out_specs=[flat(inner), flat(128), one(STATE, inner)],
+        out_specs=[flat(inner), flat(128), one(inner, STATE)],
         out_shape=[
             jax.ShapeDtypeStruct((requests * tokens, inner), jnp.bfloat16),
             jax.ShapeDtypeStruct((requests * tokens, 128), jnp.float32),
-            jax.ShapeDtypeStruct((requests, STATE, inner), jnp.float32),
+            jax.ShapeDtypeStruct((requests, inner, STATE), jnp.float32),
         ],
         compiler_params=pltpu.CompilerParams(vmem_limit_bytes=VMEM_BYTES),
         cost_estimate=pl.CostEstimate(
@@ -774,9 +774,10 @@
         return (made["terms"],), ()
 
     def leave_chain():
-        chain = clock.hold(made["chain"]).reshape(requests, STATE, local_mheads, MHEAD_DIM)
-        made["chain"] = jnp.transpose(chain, (0, 2, 3, 1)).reshape(
-            requests, 1, local_mheads, MHEAD_DIM * STATE
+        made["chain"] = (
+            clock.hold(made["chain"])
+            .reshape(requests, local_mheads, MHEAD_DIM, STATE)
+            .reshape(requests, 1, local_mheads, MHEAD_DIM * STATE)
         )
         return (made["chain"],), ()
 
@@ -824,16 +825,16 @@
         peaks = jnp.concatenate([clock.hold(part[2]) for part in cached], axis=0)
         made["best"] = Exchange(peaks, "seq", seq_count, jnp.maximum)
         made["best"].step(clock)
+        pieces = value_ring.pieces[1:-2]
+        made["used"] = 1 + len(pieces)
+        made["values"] = product(
+            [(0, 0, clock.hold(value_ring.block))] + pieces, False, kind=jnp.float32
+        )
+        return (made["values"],) + leave_terms()[0], ()
+
+    def join_more():
+        made["best"].step(clock)
         return leave_chain()
-
-    def make_values():
-        made["best"].step(clock)
-        made["values"] = product(
-            [(0, 0, clock.hold(value_ring.block))] + value_ring.pieces[1:-2],
-            False,
-            kind=jnp.float32,
-        )
-        return (made["values"],), ()
 
     def steps(rings, begin, end):
         return [ring for _ in range(begin, end) for ring in rings]
@@ -858,16 +859,18 @@
     run(both, works + [None] * (len(both) - 1 - len(works)) + [make_queries_hop])
     run(
         steps(slot_rings, 0, half),
-        [None, make_keys_hop, None, end_relay, None, leave, join_squares, leave_terms],
+        [None, make_keys_hop, None, end_relay, None, leave, join_squares],
     )
     run(
         steps([value_ring], 0, half),
-        [meet_cache(0), meet_cache(1)] + [None] * (half - 4) + [join_peaks, make_values],
+        [meet_cache(0), meet_cache(1)] + [None] * (half - 4) + [join_peaks, join_more],
     )
 
     new_keys = made["keys"]
     best = made["best"].result(clock)
-    new_values = by_request(product(value_ring.pieces[-2:], False, base=(made["values"],)))
+    new_values = by_request(
+        product(value_ring.pieces[made["used"] :], False, base=(made["values"],))
+    )
 
     own = lambda stat: lax.dynamic_slice_in_dim(stat, seq_index * tok_block, tok_block, 2)
     greatest_logit = jnp.transpose(own(best), (0, 2, 1)) * SCALE

time: 526 us -> 540 us (1.027)
  waiting for transfers between devices: 171 us -> 199 us
  local copies, waits for them, and re-layouts: 63.8 us -> 50 us
  starting transfers between devices: 97 us -> 91.6 us
    ppermute x8, waiting for transfers between devices: 19.2 us -> 41.8 us  [step(): self.got = lax.ppermute(self.value, self.axis, route)]
    ppermute x1, waiting for transfers between devices: 11.8 us -> 32.8 us  [__init__(): other_factor = side(lax.ppermute(through, 'seq', self.swap))]
    ppermute x2, waiting for transfers between devices: 36 us -> 17.7 us  [exchange(): lax.ppermute(value.astype(jnp.bfloat16), 'seq', self.swap)]
    reshape x2 -> x0, local copies, waits for them, and re-layouts: 9.24 us -> none  [the longest x1 4.76 us: leave_chain(): jnp.transpose(chain, (0, 2, 3, 1))]
    transpose x1 -> x0, local copies, waits for them, and re-layouts: 5.54 us -> none  [leave_chain(): jnp.transpose(chain, (0, 2, 3, 1))]
    unnamed x98 -> x112, local copies, waits for them, and re-layouts: 16.2 us -> 16.4 us
  transfers between devices with their start and end apart: 74 -> 74, of which waited for: 34 -> 34; matrix products, arithmetic and copies ran while one was open for 20% -> 17% of each run, Pallas kernels for 20% -> 20%
where the time goes in v11:
time: 540 us; the launch traced here: 530 us
  waiting for transfers between devices  199 us (37%)
  Pallas kernels  134 us (25%)
  starting transfers between devices  91.6 us (17%)
  local copies, waits for them, and re-layouts  50 us (9%)
  other arithmetic  43.4 us (8%)
  matrix products  10.5 us (2%)
    ppermute x56, waiting for transfers between devices, ring_step(): return lax.ppermute(block, 'seq', route)  100 us
    ppermute x56, starting transfers between devices, ring_step(): return lax.ppermute(block, 'seq', route)  71.6 us
    pallas_call x2, Pallas kernels, cache_part(): pl.pallas_call(functools.partial(cache_kernel, slots), grid_spec=pltpu.Pr...  44.3 us
    ppermute x8, waiting for transfers between devices, step(): self.got = lax.ppermute(self.value, self.axis, route)  41.8 us
    pallas_call x4, Pallas kernels, project(): pl.pallas_call(functools.partial(project_kernel, len(pieces), turned), gr...  36 us
    ppermute x1, waiting for transfers between devices, __init__(): other_factor = side(lax.ppermute(through, 'seq', self.swap))  32.8 us
    pallas_call x2, Pallas kernels, finish_part(): pl.pallas_call(functools.partial(finish_kernel, slots), grid_spec=pltpu.P...  22.7 us
    ppermute x2, waiting for transfers between devices, exchange(): lax.ppermute(value.astype(jnp.bfloat16), 'seq', self.swap)  17.7 us
  transfers between devices with their start and end apart: 74, of which 34 were waited for; matrix products, arithmetic and copies ran while one was open for 17% of the time, Pallas kernels for 20%

profile of v11, /device:TPU:0, one launch (start us, length us, event | category | flops | bytes accessed | tf_op | source)
XLA Modules:
  0.0 529.7 jit_solution(1381030530274235692)
XLA Ops:
  3.7 10.4 %copy.52 = bf16[256,8,2,1024]{3,1,2,0:T(8,128)(2,1)} copy(bf16[256,8,2,1024]{3,2,1,0:T(2,128)(2,1)} %bitcast.100) | data formatting | bytes 16777216
  17.2 5.6 %copy.40 = f32[8,16,64,64]{2,1,3,0:T(8,128)} copy(f32[8,16,64,64]{3,2,1,0:T(8,128)} %reshape.118) | data formatting | bytes 4194304 | tf_op jit(solution)/shard_map/reshape | solution.py:696
  29.4 11.6 %enter_mixer.1 = (f32[512,2048]{1,0:T(8,128)}, f32[512,128]{1,0:T(8,128)}, f32[512,16]{1,0:T(8,128)}) custom-call(bf16[512,4096]{1,0:T(8,128)(2,1)} %bitcast.62, f32[1,2048]{1,0:T(1,128)} %bitcast.124, bf16[2048,128]{1,0:T(8,128)(2,1)} %bc_ref.1, bf16[2048,16]{1,0:T(8,128)(2,1)} %copy.41.dt_ref, f32[1,16]{1,0:T(1,128)} %bitcast.125, bf16[2048,2048]{1,0:T(8,128)(2,1)} %bitcast.101), custom_call_target="tpu_custom_call" | custom-call | flops 4294967296 | bytes 14680064 | tf_op jit(solution)/shard_map/enter_mixer/pallas_call | solution.py:231
  48.8 9.6 %inside_block.1 = (f32[512,1024]{1,0:T(8,128)}, f32[8,64,1024]{2,1,0:T(8,128)}, f32[8,1,1024]{2,1,0:T(1,128)}) custom-call(f32[512,2048]{1,0:T(8,128)} %get-tuple-element.166.inner_ref.gate_ref, f32[512,128]{1,0:T(8,128)} %get-tuple-element.167.map_ref, f32[8,64,16]{2,1,0:T(8,128)} %bitcast.104, f32[8,64,16]{2,1,0:T(8,128)} %bitcast.108, ...), custom_call_target="tpu_custom_call" | custom-call | flops 402653184 | bytes 8388608 | tf_op jit(solution)/shard_map/inside_block/pallas_call | solution.py:309
  64.1 32.8 %collective-permute-done.10 = f32[8,1,1024]{2,1,0:T(1,128)S(1)} collective-permute-done((f32[8,1,1024]{2,1,0:T(1,128)}, f32[8,1,1024]{2,1,0:T(1,128)S(1)}, u32[]{:S(2)}, u32[]{:S(2)}) %collective-permute-start.10) | collective-permute-done | bytes 32800 | tf_op jit(solution)/shard_map/ppermute | solution.py:578
  101.8 9.9 %collective-permute-done.11 = bf16[8,64,512]{2,1,0:T(8,128)(2,1)S(1)} collective-permute-done((bf16[8,64,512]{2,1,0:T(8,128)(2,1)S(1)}, bf16[8,64,512]{2,1,0:T(8,128)(2,1)S(1)}, u32[]{:S(2)}, u32[]{:S(2)}) %collective-permute-start.11) | collective-permute-done | bytes 524320 | tf_op jit(solution)/shard_map/ppermute | solution.py:589
  118.8 13.2 %collective-permute-done.6.refs_14_ = bf16[512,1024]{1,0:T(8,128)(2,1)} collective-permute-done((bf16[512,1024]{1,0:T(8,128)(2,1)}, bf16[512,1024]{1,0:T(8,128)(2,1)}, u32[]{:S(2)}, u32[]{:S(2)}) %collective-permute-start.6) | collective-permute-done | bytes 1048608 | tf_op jit(solution)/shard_map/ppermute | solution.py:36
  141.8 7.4 %collective-permute-done.12.refs_16_ = bf16[256,1024]{1,0:T(8,128)(2,1)S(1)} collective-permute-done((bf16[256,1024]{1,0:T(8,128)(2,1)S(1)}, bf16[256,1024]{1,0:T(8,128)(2,1)S(1)}, u32[]{:S(2)}, u32[]{:S(2)}) %collective-permute-start.12) | collective-permute-done | bytes 524320 | tf_op jit(solution)/shard_map/ppermute | solution.py:36
  150.9 10.5 %project.4 = bf16[512,1024]{1,0:T(8,128)(2,1)} custom-call(s32[8]{0:T(128)} %fusion.21.places_ref.place_ref, bf16[512,4096]{1,0:T(8,128)(2,1)} %bitcast.63, bf16[512,4096]{1,0:T(8,128)(2,1)} %bitcast.64, bf16[512,4096]{1,0:T(8,128)(2,1)} %bitcast.65, bf16[512,4096]{1,0:T(8,128)(2,1)} %bitcast.66, bf16[512,4096]{1,0:T(8,128)(2,1)} %bitcast.67, ...), custom_call_target="tpu_custom_call" | custom-call | flops 4294967296 | bytes 12582912 | tf_op jit(solution)/shard_map/project/pallas_call | solution.py:169
  161.4 7.3 %collective-permute-done.15.refs_14_ = bf16[512,1024]{1,0:T(8,128)(2,1)S(1)} collective-permute-done((bf16[512,1024]{1,0:T(8,128)(2,1)}, bf16[512,1024]{1,0:T(8,128)(2,1)S(1)}, u32[]{:S(2)}, u32[]{:S(2)}) %collective-permute-start.15) | collective-permute-done | bytes 1048608 | tf_op jit(solution)/shard_map/ppermute | solution.py:36
  175.8 7.9 %collective-permute-done.17.refs_16_ = bf16[256,1024]{1,0:T(8,128)(2,1)S(1)} collective-permute-done((bf16[256,1024]{1,0:T(8,128)(2,1)S(1)}, bf16[256,1024]{1,0:T(8,128)(2,1)S(1)}, u32[]{:S(2)}, u32[]{:S(2)}) %collective-permute-start.17) | collective-permute-done | bytes 524320 | tf_op jit(solution)/shard_map/ppermute | solution.py:36
  188.6 10.5 %project.5 = bf16[512,1024]{1,0:T(8,128)(2,1)} custom-call(s32[8]{0:T(128)} %fusion.21.places_ref.place_ref, bf16[512,4096]{1,0:T(8,128)(2,1)} %bitcast.76, bf16[512,4096]{1,0:T(8,128)(2,1)} %bitcast.73, bf16[512,4096]{1,0:T(8,128)(2,1)} %bitcast.74, bf16[512,4096]{1,0:T(8,128)(2,1)} %bitcast.75, bf16[512,4096]{1,0:T(8,128)(2,1)} %bitcast.72, ...), custom_call_target="tpu_custom_call" | custom-call | flops 4294967296 | bytes 12582912 | tf_op jit(solution)/shard_map/project/pallas_call | solution.py:169
  209.6 7.3 %collective-permute-start.27 = (bf16[4,64,1024]{2,1,0:T(8,128)(2,1)}, bf16[4,64,1024]{2,1,0:T(8,128)(2,1)S(1)}, u32[]{:S(2)}, u32[]{:S(2)}) collective-permute-start(bf16[4,64,1024]{2,1,0:T(8,128)(2,1)} %collective-permute-done.22.refs_1_), channel_id=1, source_target_pairs={{0,8},{8,16},{16,24},{24,28},{28,20},{20,12},{12,4},{4,0},{1,9},{9... | collective-permute-start | bytes 1572872 | tf_op jit(solution)/shard_map/ppermute | solution.py:36
  222.2 7.8 %collective-permute-done.29 = bf16[8,64,512]{2,1,0:T(8,128)(2,1)S(1)} collective-permute-done((bf16[8,64,512]{2,1,0:T(8,128)(2,1)S(1)}, bf16[8,64,512]{2,1,0:T(8,128)(2,1)S(1)}, u32[]{:S(2)}, u32[]{:S(2)}) %collective-permute-start.29) | collective-permute-done | bytes 524320 | tf_op jit(solution)/shard_map/ppermute | solution.py:589
  231.9 9.3 %collective-permute-done.27.refs_3_ = bf16[4,64,1024]{2,1,0:T(8,128)(2,1)S(1)} collective-permute-done((bf16[4,64,1024]{2,1,0:T(8,128)(2,1)}, bf16[4,64,1024]{2,1,0:T(8,128)(2,1)S(1)}, u32[]{:S(2)}, u32[]{:S(2)}) %collective-permute-start.27) | collective-permute-done | bytes 524320 | tf_op jit(solution)/shard_map/ppermute | solution.py:36
  243.3 9.5 %leave_mixer.1 = (bf16[512,1024]{1,0:T(8,128)(2,1)}, f32[512,128]{1,0:T(8,128)}, f32[8,1024,64]{2,1,0:T(8,128)}) custom-call(f32[8,64,1024]{2,1,0:T(8,128)} %pad_maximum_fusion.entry_ref, f32[512,128]{1,0:T(8,128)} %get-tuple-element.167.map_ref, f32[8,64,16]{2,1,0:T(8,128)} %bitcast.105, f32[512,1024]{1,0:T(8,128)} %get-tuple-element.168.read_ref, ...), custom_call_target="tpu_custom_call" | custom-call | flops 67108864 | bytes 12582912 | tf_op jit(solution)/shard_map/leave_mixer/pallas_call | solution.py:362
  255.1 6.0 %collective-permute-done.32.refs_5_ = bf16[4,64,1024]{2,1,0:T(8,128)(2,1)S(1)} collective-permute-done((bf16[4,64,1024]{2,1,0:T(8,128)(2,1)S(1)}, bf16[4,64,1024]{2,1,0:T(8,128)(2,1)S(1)}, u32[]{:S(2)}, u32[]{:S(2)}) %collective-permute-start.32) | collective-permute-done | bytes 524320 | tf_op jit(solution)/shard_map/ppermute | solution.py:36
  261.1 5.4 %collective-permute-done.34 = bf16[2,64,1024]{2,1,0:T(8,128)(2,1)S(1)} collective-permute-done((bf16[2,64,1024]{2,1,0:T(8,128)(2,1)S(1)}, bf16[2,64,1024]{2,1,0:T(8,128)(2,1)S(1)}, u32[]{:S(2)}, u32[]{:S(2)}) %collective-permute-start.34) | collective-permute-done | bytes 262176 | tf_op jit(solution)/shard_map/ppermute | solution.py:36
  272.5 22.2 %cache_part.2 = (bf16[4,512,1024]{2,1,0:T(8,128)(2,1)}, bf16[4,1024,512]{2,1,0:T(8,128)(2,1)}, f32[4,8,512]{2,1,0:T(8,128)}, f32[4,8,512]{2,1,0:T(8,128)}) custom-call(s32[1]{0:T(128)} %bitcast.1.first_ref, s32[8]{0:T(128)} %fusion.21.places_ref.place_ref, s32[4]{0:T(128)} %get-tuple-element.345.live_ref, bf16[4,64,1024]{2,1,0:T(8,128)(2,1)} %bitcast.115, ...), custom_call_target="tpu_custom_call" | custom-call | flops 4294967296 | bytes 20971520 | tf_op jit(solution)/shard_map/cache_part/pallas_call | solution.py:448
  300.4 22.1 %cache_part.3 = (bf16[4,512,1024]{2,1,0:T(8,128)(2,1)}, bf16[4,1024,512]{2,1,0:T(8,128)(2,1)}, f32[4,8,512]{2,1,0:T(8,128)}, f32[4,8,512]{2,1,0:T(8,128)}) custom-call(s32[1]{0:T(128)} %bitcast.1.first_ref, s32[8]{0:T(128)} %fusion.21.places_ref.place_ref, s32[4]{0:T(128)} %get-tuple-element.344.live_ref, bf16[4,64,1024]{2,1,0:T(8,128)(2,1)} %bitcast.112, ...), custom_call_target="tpu_custom_call" | custom-call | flops 4294967296 | bytes 20971520 | tf_op jit(solution)/shard_map/cache_part/pallas_call | solution.py:448
  324.9 6.6 %convolution_multiply_fusion = f32[512,2048]{1,0:T(8,128)} fusion(bf16[512,1024]{1,0:T(8,128)(2,1)S(1)} %copy-done.51, bf16[1024,2048]{1,0:T(8,128)(2,1)} %param.35, f32[512]{0:T(512)S(1)} %bitcast.123), kind=kOutput, calls=%fused_computation | convolution fusion | flops 2148532224 | bytes 9439232 | tf_op jit(solution)/shard_map/dot_general | solution.py:771
  331.4 8.3 %project.6.refs_10_ = f32[512,1024]{1,0:T(8,128)} custom-call(s32[8]{0:T(128)} %fusion.21.places_ref.place_ref, bf16[512,4096]{1,0:T(8,128)(2,1)} %bitcast.81, bf16[512,4096]{1,0:T(8,128)(2,1)} %bitcast.82, bf16[512,4096]{1,0:T(8,128)(2,1)} %bitcast.83, bf16[512,4096]{1,0:T(8,128)(2,1)} %bitcast.84, bf16[512,4096]{1,0:T(8,128)(2,1)} %bitcast.85, ...), custom_call_target="tpu_custom_call" | custom-call | flops 2684354560 | bytes 12582912 | tf_op jit(solution)/shard_map/project/pallas_call | solution.py:169
  339.7 7.9 %collective-permute-done.44.refs_4_ = bf16[512,1024]{1,0:T(8,128)(2,1)S(1)} collective-permute-done((bf16[512,1024]{1,0:T(8,128)(2,1)S(1)}, bf16[512,1024]{1,0:T(8,128)(2,1)S(1)}, u32[]{:S(2)}, u32[]{:S(2)}) %collective-permute-start.44) | collective-permute-done | bytes 1048608 | tf_op jit(solution)/shard_map/ppermute | solution.py:36
  353.3 13.7 %collective-permute-done.48 = f32[8,8,512]{2,1,0:T(8,128)S(1)} collective-permute-done((f32[8,8,512]{2,1,0:T(8,128)S(1)}, f32[8,8,512]{2,1,0:T(8,128)S(1)}, u32[]{:S(2)}, u32[]{:S(2)}) %collective-permute-start.48) | collective-permute-done | bytes 131104 | tf_op jit(solution)/shard_map/ppermute | solution.py:96
  383.0 6.8 %project.7 = bf16[512,1024]{1,0:T(8,128)(2,1)} custom-call(s32[8]{0:T(128)} %fusion.21.places_ref.place_ref, bf16[512,4096]{1,0:T(8,128)(2,1)} %bitcast.86, bf16[512,4096]{1,0:T(8,128)(2,1)} %bitcast.87, bf16[512,4096]{1,0:T(8,128)(2,1)} %bitcast.88, bf16[512,4096]{1,0:T(8,128)(2,1)} %bitcast.89, bf16[512,1024]{1,0:T(8,128)(2,1)} %copy-done.8, ...), custom_call_target="tpu_custom_call" | custom-call | flops 1610612736 | bytes 12582912 | tf_op jit(solution)/shard_map/project/pallas_call | solution.py:169
  389.8 11.2 %finish_part.2 = (f32[4,8,512]{2,1,0:T(8,128)}, bf16[4,64,1024]{2,1,0:T(8,128)(2,1)}, bf16[4,64,1024]{2,1,0:T(8,128)(2,1)}, bf16[4,64,1024]{2,1,0:T(8,128)(2,1)}...) custom-call(s32[1]{0:T(128)} %bitcast.1.first_ref, ...), custom_call_target="tpu_custom_call" | custom-call | flops 536870912 | bytes 12582912 | tf_op jit(solution)/shard_map/finish_part/pallas_call | solution.py:510
  402.1 11.5 %finish_part.3 = (f32[4,8,512]{2,1,0:T(8,128)}, bf16[4,64,1024]{2,1,0:T(8,128)(2,1)}, bf16[4,64,1024]{2,1,0:T(8,128)(2,1)}, bf16[4,64,1024]{2,1,0:T(8,128)(2,1)}...) custom-call(s32[1]{0:T(128)} %bitcast.1.first_ref, ...), custom_call_target="tpu_custom_call" | custom-call | flops 536870912 | bytes 12582912 | tf_op jit(solution)/shard_map/finish_part/pallas_call | solution.py:510
  435.0 16.2 %collective-permute-done.61 = f32[8,8,512]{2,1,0:T(8,128)S(1)} collective-permute-done((f32[8,8,512]{2,1,0:T(8,128)S(1)}, f32[8,8,512]{2,1,0:T(8,128)S(1)}, u32[]{:S(2)}, u32[]{:S(2)}) %collective-permute-start.61) | collective-permute-done | bytes 131104 | tf_op jit(solution)/shard_map/ppermute | solution.py:96
  451.4 6.3 %collective-permute-done.62 = f32[8,8,512]{2,1,0:T(8,128)S(1)} collective-permute-done((f32[8,8,512]{2,1,0:T(8,128)S(1)}, f32[8,8,512]{2,1,0:T(8,128)S(1)}, u32[]{:S(2)}, u32[]{:S(2)}) %collective-permute-start.62) | collective-permute-done | bytes 131104 | tf_op jit(solution)/shard_map/ppermute | solution.py:96
  470.8 6.0 %collective-permute-done.57 = bf16[4,64,1024]{2,1,0:T(8,128)(2,1)} collective-permute-done((bf16[4,64,1024]{2,1,0:T(8,128)(2,1)}, bf16[4,64,1024]{2,1,0:T(8,128)(2,1)}, u32[]{:S(2)}, u32[]{:S(2)}) %collective-permute-start.57) | collective-permute-done | bytes 524320 | tf_op jit(solution)/shard_map/ppermute | solution.py:36
  482.7 5.4 %collective-permute-done.68 = bf16[4,64,1024]{2,1,0:T(8,128)(2,1)} collective-permute-done((bf16[4,64,1024]{2,1,0:T(8,128)(2,1)}, bf16[4,64,1024]{2,1,0:T(8,128)(2,1)}, u32[]{:S(2)}, u32[]{:S(2)}) %collective-permute-start.68) | collective-permute-done | bytes 524320 | tf_op jit(solution)/shard_map/ppermute | solution.py:36
  493.0 7.2 %collective-permute-done.60 = bf16[4,64,1024]{2,1,0:T(8,128)(2,1)S(1)} collective-permute-done((bf16[4,64,1024]{2,1,0:T(8,128)(2,1)S(1)}, bf16[4,64,1024]{2,1,0:T(8,128)(2,1)S(1)}, u32[]{:S(2)}, u32[]{:S(2)}) %collective-permute-start.60) | collective-permute-done | bytes 524320 | tf_op jit(solution)/shard_map/ppermute | solution.py:36
  (342 shorter events, 194.5 us)
Async XLA Ops:
  0.6 44.3 %collective-permute-start = (bf16[512,1024]{1,0:T(8,128)(2,1)}, bf16[512,1024]{1,0:T(8,128)(2,1)}, u32[]{:S(2)}, u32[]{:S(2)}) collective-permute-start(bf16[512,1024]{1,0:T(8,128)(2,1)} %refs_9_.4), channel_id=1, source_target_pairs={{0,8},{8,16},{16,24},{24,28},{28,20},{20,12},{12,4},{4,0},{1,9},{9... | collective-permute-start | bytes 3145736 | tf_op jit(solution)/shard_map/ppermute | solution.py:36
  3.7 41.2 %collective-permute-start.1 = (bf16[512,1024]{1,0:T(8,128)(2,1)}, bf16[512,1024]{1,0:T(8,128)(2,1)}, u32[]{:S(2)}, u32[]{:S(2)}) collective-permute-start(bf16[512,1024]{1,0:T(8,128)(2,1)} %refs_9_.4), channel_id=1, source_target_pairs={{0,4},{8,0},{16,8},{24,16},{28,24},{20,28},{12,20},{4,12},{1,5},{9... | collective-permute-start | bytes 3145736 | tf_op jit(solution)/shard_map/ppermute | solution.py:36
  26.4 32.0 %collective-permute-start.4 = (bf16[512,1024]{1,0:T(8,128)(2,1)}, bf16[512,1024]{1,0:T(8,128)(2,1)}, u32[]{:S(2)}, u32[]{:S(2)}) collective-permute-start(bf16[512,1024]{1,0:T(8,128)(2,1)} %refs_9_.5), channel_id=1, source_target_pairs={{0,8},{8,16},{16,24},{24,28},{28,20},{20,12},{12,4},{4,0},{1,9},{9... | collective-permute-start | bytes 3145736 | tf_op jit(solution)/shard_map/ppermute | solution.py:36
  28.4 30.0 %collective-permute-start.5 = (bf16[512,1024]{1,0:T(8,128)(2,1)}, bf16[512,1024]{1,0:T(8,128)(2,1)}, u32[]{:S(2)}, u32[]{:S(2)}) collective-permute-start(bf16[512,1024]{1,0:T(8,128)(2,1)} %refs_9_.5), channel_id=1, source_target_pairs={{0,4},{8,0},{16,8},{24,16},{28,24},{20,28},{12,20},{4,12},{1,5},{9... | collective-permute-start | bytes 3145736 | tf_op jit(solution)/shard_map/ppermute | solution.py:36
  44.9 54.6 %collective-permute-start.2 = (bf16[512,1024]{1,0:T(8,128)(2,1)}, bf16[512,1024]{1,0:T(8,128)(2,1)}, u32[]{:S(2)}, u32[]{:S(2)}) collective-permute-start(bf16[512,1024]{1,0:T(8,128)(2,1)} %collective-permute-done.refs_10_), channel_id=1, source_target_pairs={{0,8},{8,16},{16,24},{24,28},{28,20},{20,12},{12,4},{4,0},{1,9},{9... | collective-permute-start | bytes 3145736 | tf_op jit(solution)/shard_map/ppermute | solution.py:36
  46.9 52.6 %collective-permute-start.3 = (bf16[512,1024]{1,0:T(8,128)(2,1)}, bf16[512,1024]{1,0:T(8,128)(2,1)}, u32[]{:S(2)}, u32[]{:S(2)}) collective-permute-start(bf16[512,1024]{1,0:T(8,128)(2,1)} %collective-permute-done.1.refs_11_), channel_id=1, source_target_pairs={{0,4},{8,0},{16,8},{24,16},{28,24},{20,28},{12,20},{4,12},{1,5},{9... | collective-permute-start | bytes 3145736 | tf_op jit(solution)/shard_map/ppermute | solution.py:36
  58.4 56.2 %collective-permute-start.8 = (bf16[512,1024]{1,0:T(8,128)(2,1)}, bf16[512,1024]{1,0:T(8,128)(2,1)}, u32[]{:S(2)}, u32[]{:S(2)}) collective-permute-start(bf16[512,1024]{1,0:T(8,128)(2,1)} %collective-permute-done.4.refs_10_), channel_id=1, source_target_pairs={{0,8},{8,16},{16,24},{24,28},{28,20},{20,12},{12,4},{4,0},{1,9},{9... | collective-permute-start | bytes 3145736 | tf_op jit(solution)/shard_map/ppermute | solution.py:36
  60.5 54.1 %collective-permute-start.9 = (bf16[512,1024]{1,0:T(8,128)(2,1)}, bf16[512,1024]{1,0:T(8,128)(2,1)}, u32[]{:S(2)}, u32[]{:S(2)}) collective-permute-start(bf16[512,1024]{1,0:T(8,128)(2,1)} %collective-permute-done.5.refs_11_), channel_id=1, source_target_pairs={{0,4},{8,0},{16,8},{24,16},{28,24},{20,28},{12,20},{4,12},{1,5},{9... | collective-permute-start | bytes 3145736 | tf_op jit(solution)/shard_map/ppermute | solution.py:36
  60.5 36.4 %collective-permute-start.10 = (f32[8,1,1024]{2,1,0:T(1,128)}, f32[8,1,1024]{2,1,0:T(1,128)S(1)}, u32[]{:S(2)}, u32[]{:S(2)}) collective-permute-start(f32[8,1,1024]{2,1,0:T(1,128)} %get-tuple-element.176.through_ref), channel_id=1, source_target_pairs={{0,4},{4,0},{8,12},{12,8},{16,20},{20,16},{24,28},{28,24},{1,5},{5... | collective-permute-start | bytes 98312 | tf_op jit(solution)/shard_map/ppermute | solution.py:578
  99.5 32.5 %collective-permute-start.6 = (bf16[512,1024]{1,0:T(8,128)(2,1)}, bf16[512,1024]{1,0:T(8,128)(2,1)}, u32[]{:S(2)}, u32[]{:S(2)}) collective-permute-start(bf16[512,1024]{1,0:T(8,128)(2,1)} %collective-permute-done.2.refs_12_), channel_id=1, source_target_pairs={{0,8},{8,16},{16,24},{24,28},{28,20},{20,12},{12,4},{4,0},{1,9},{9... | collective-permute-start | bytes 3145736 | tf_op jit(solution)/shard_map/ppermute | solution.py:36
  99.6 33.5 %collective-permute-start.7 = (bf16[512,1024]{1,0:T(8,128)(2,1)}, bf16[512,1024]{1,0:T(8,128)(2,1)}, u32[]{:S(2)}, u32[]{:S(2)}) collective-permute-start(bf16[512,1024]{1,0:T(8,128)(2,1)} %collective-permute-done.3.refs_13_), channel_id=1, source_target_pairs={{0,4},{8,0},{16,8},{24,16},{28,24},{20,28},{12,20},{4,12},{1,5},{9... | collective-permute-start | bytes 3145736 | tf_op jit(solution)/shard_map/ppermute | solution.py:36
  115.7 24.9 %collective-permute-start.14 = (bf16[8,64,512]{2,1,0:T(8,128)(2,1)}, bf16[8,64,512]{2,1,0:T(8,128)(2,1)}, u32[]{:S(2)}, u32[]{:S(2)}) collective-permute-start(bf16[8,64,512]{2,1,0:T(8,128)(2,1)} %add_convert_fusion.10), channel_id=1, source_target_pairs={{0,8},{4,12},{1,9},{5,13},{2,10},{6,14},{3,11},{7,15}} | collective-permute-start | bytes 1572872 | tf_op jit(solution)/shard_map/ppermute | solution.py:604
  137.3 31.4 %collective-permute-start.15 = (bf16[512,1024]{1,0:T(8,128)(2,1)}, bf16[512,1024]{1,0:T(8,128)(2,1)S(1)}, u32[]{:S(2)}, u32[]{:S(2)}) collective-permute-start(bf16[512,1024]{1,0:T(8,128)(2,1)} %collective-permute-done.8.refs_12_), channel_id=1, source_target_pairs={{0,8},{8,16},{16,24},{24,28},{28,20},{20,12},{12,4},{4,0},{1,9},{9... | collective-permute-start | bytes 3145736 | tf_op jit(solution)/shard_map/ppermute | solution.py:36
  137.4 31.3 %collective-permute-start.16 = (bf16[512,1024]{1,0:T(8,128)(2,1)}, bf16[512,1024]{1,0:T(8,128)(2,1)S(1)}, u32[]{:S(2)}, u32[]{:S(2)}) collective-permute-start(bf16[512,1024]{1,0:T(8,128)(2,1)} %collective-permute-done.9.refs_13_), channel_id=1, source_target_pairs={{0,4},{8,0},{16,8},{24,16},{28,24},{20,28},{12,20},{4,12},{1,5},{9... | collective-permute-start | bytes 3145736 | tf_op jit(solution)/shard_map/ppermute | solution.py:36
  173.7 25.3 %collective-permute-start.20 = (bf16[4,64,1024]{2,1,0:T(8,128)(2,1)S(1)}, bf16[4,64,1024]{2,1,0:T(8,128)(2,1)}, u32[]{:S(2)}, u32[]{:S(2)}) collective-permute-start(bf16[4,64,1024]{2,1,0:T(8,128)(2,1)S(1)} %bitcast.113), channel_id=1, source_target_pairs={{0,8},{8,16},{16,24},{24,28},{28,20},{20,12},{12,4},{4,0},{1,9},{9... | collective-permute-start | bytes 1572872 | tf_op jit(solution)/shard_map/ppermute | solution.py:36
  175.3 23.8 %collective-permute-start.21 = (bf16[4,64,1024]{2,1,0:T(8,128)(2,1)S(1)}, bf16[4,64,1024]{2,1,0:T(8,128)(2,1)}, u32[]{:S(2)}, u32[]{:S(2)}) collective-permute-start(bf16[4,64,1024]{2,1,0:T(8,128)(2,1)S(1)} %bitcast.114), channel_id=1, source_target_pairs={{0,4},{8,0},{16,8},{24,16},{28,24},{20,28},{12,20},{4,12},{1,5},{9... | collective-permute-start | bytes 1572872 | tf_op jit(solution)/shard_map/ppermute | solution.py:36
  209.6 31.6 %collective-permute-start.27 = (bf16[4,64,1024]{2,1,0:T(8,128)(2,1)}, bf16[4,64,1024]{2,1,0:T(8,128)(2,1)S(1)}, u32[]{:S(2)}, u32[]{:S(2)}) collective-permute-start(bf16[4,64,1024]{2,1,0:T(8,128)(2,1)} %collective-permute-done.22.refs_1_), channel_id=1, source_target_pairs={{0,8},{8,16},{16,24},{24,28},{28,20},{20,12},{12,4},{4,0},{1,9},{9... | collective-permute-start | bytes 1572872 | tf_op jit(solution)/shard_map/ppermute | solution.py:36
  216.8 24.4 %collective-permute-start.28 = (bf16[4,64,1024]{2,1,0:T(8,128)(2,1)}, bf16[4,64,1024]{2,1,0:T(8,128)(2,1)S(1)}, u32[]{:S(2)}, u32[]{:S(2)}) collective-permute-start(bf16[4,64,1024]{2,1,0:T(8,128)(2,1)} %collective-permute-done.23.refs_2_), channel_id=1, source_target_pairs={{0,4},{8,0},{16,8},{24,16},{28,24},{20,28},{12,20},{4,12},{1,5},{9... | collective-permute-start | bytes 1572872 | tf_op jit(solution)/shard_map/ppermute | solution.py:36
  218.8 33.9 %collective-permute-start.30 = (bf16[4,64,1024]{2,1,0:T(8,128)(2,1)}, bf16[4,64,1024]{2,1,0:T(8,128)(2,1)S(1)}, u32[]{:S(2)}, u32[]{:S(2)}) collective-permute-start(bf16[4,64,1024]{2,1,0:T(8,128)(2,1)} %collective-permute-done.25.refs_3_), channel_id=1, source_target_pairs={{0,8},{8,16},{16,24},{24,28},{28,20},{20,12},{12,4},{4,0},{1,9},{9... | collective-permute-start | bytes 1572872 | tf_op jit(solution)/shard_map/ppermute | solution.py:36
  222.2 30.6 %collective-permute-start.31 = (bf16[4,64,1024]{2,1,0:T(8,128)(2,1)}, bf16[4,64,1024]{2,1,0:T(8,128)(2,1)S(1)}, u32[]{:S(2)}, u32[]{:S(2)}) collective-permute-start(bf16[4,64,1024]{2,1,0:T(8,128)(2,1)} %collective-permute-done.26.refs_4_), channel_id=1, source_target_pairs={{0,4},{8,0},{16,8},{24,16},{28,24},{20,28},{12,20},{4,12},{1,5},{9... | collective-permute-start | bytes 1572872 | tf_op jit(solution)/shard_map/ppermute | solution.py:36
  266.5 28.2 %collective-permute-start.38 = (bf16[512,1024]{1,0:T(8,128)(2,1)S(1)}, bf16[512,1024]{1,0:T(8,128)(2,1)S(1)}, u32[]{:S(2)}, u32[]{:S(2)}) collective-permute-start(bf16[512,1024]{1,0:T(8,128)(2,1)S(1)} %copy-done.17), channel_id=1, source_target_pairs={{0,8},{8,16},{16,24},{24,28},{28,20},{20,12},{12,4},{4,0},{1,9},{9... | collective-permute-start | bytes 3145736 | tf_op jit(solution)/shard_map/ppermute | solution.py:36
  267.1 27.7 %collective-permute-start.39 = (bf16[512,1024]{1,0:T(8,128)(2,1)S(1)}, bf16[512,1024]{1,0:T(8,128)(2,1)S(1)}, u32[]{:S(2)}, u32[]{:S(2)}) collective-permute-start(bf16[512,1024]{1,0:T(8,128)(2,1)S(1)} %copy-done.17), channel_id=1, source_target_pairs={{0,4},{8,0},{16,8},{24,16},{28,24},{20,28},{12,20},{4,12},{1,5},{9... | collective-permute-start | bytes 3145736 | tf_op jit(solution)/shard_map/ppermute | solution.py:36
  270.1 24.7 %collective-permute-start.36 = (bf16[2,64,1024]{2,1,0:T(8,128)(2,1)S(1)}, bf16[2,64,1024]{2,1,0:T(8,128)(2,1)S(1)}, u32[]{:S(2)}, u32[]{:S(2)}) collective-permute-start(bf16[2,64,1024]{2,1,0:T(8,128)(2,1)S(1)} %slice.207), channel_id=1, source_target_pairs={{0,8},{8,16},{16,24},{24,28},{28,20},{20,12},{12,4},{4,0},{1,9},{9... | collective-permute-start | bytes 786440 | tf_op jit(solution)/shard_map/ppermute | solution.py:36
  270.7 24.1 %collective-permute-start.37 = (bf16[2,64,1024]{2,1,0:T(8,128)(2,1)S(1)}, bf16[2,64,1024]{2,1,0:T(8,128)(2,1)S(1)}, u32[]{:S(2)}, u32[]{:S(2)}) collective-permute-start(bf16[2,64,1024]{2,1,0:T(8,128)(2,1)S(1)} %slice.208), channel_id=1, source_target_pairs={{0,4},{8,0},{16,8},{24,16},{28,24},{20,28},{12,20},{4,12},{1,5},{9... | collective-permute-start | bytes 786440 | tf_op jit(solution)/shard_map/ppermute | solution.py:36
  294.8 27.8 %collective-permute-start.40 = (bf16[512,1024]{1,0:T(8,128)(2,1)S(1)}, bf16[512,1024]{1,0:T(8,128)(2,1)S(1)}, u32[]{:S(2)}, u32[]{:S(2)}) collective-permute-start(bf16[512,1024]{1,0:T(8,128)(2,1)S(1)} %collective-permute-done.38.refs_6_), channel_id=1, source_target_pairs={{0,8},{8,16},{16,24},{24,28},{28,20},{20,12},{12,4},{4,0},{1,9},{9... | collective-permute-start | bytes 3145736 | tf_op jit(solution)/shard_map/ppermute | solution.py:36
  296.5 26.1 %collective-permute-start.41 = (bf16[512,1024]{1,0:T(8,128)(2,1)S(1)}, bf16[512,1024]{1,0:T(8,128)(2,1)S(1)}, u32[]{:S(2)}, u32[]{:S(2)}) collective-permute-start(bf16[512,1024]{1,0:T(8,128)(2,1)S(1)} %collective-permute-done.39.refs_7_), channel_id=1, source_target_pairs={{0,4},{8,0},{16,8},{24,16},{28,24},{20,28},{12,20},{4,12},{1,5},{9... | collective-permute-start | bytes 3145736 | tf_op jit(solution)/shard_map/ppermute | solution.py:36
  298.2 24.3 %collective-permute-start.43 = (f32[1,512]{1,0:T(1,128)S(1)}, f32[1,512]{1,0:T(1,128)S(1)}, u32[]{:S(2)}, u32[]{:S(2)}) collective-permute-start(f32[1,512]{1,0:T(1,128)S(1)} %add.222), channel_id=1, source_target_pairs={{0,2},{1,3},{2,0},{3,1},{4,6},{5,7},{6,4},{7,5},{8,10},{9,11},{10,... | collective-permute-start | bytes 6152 | tf_op jit(solution)/shard_map/ppermute | solution.py:96
  322.6 25.0 %collective-permute-start.44 = (bf16[512,1024]{1,0:T(8,128)(2,1)S(1)}, bf16[512,1024]{1,0:T(8,128)(2,1)S(1)}, u32[]{:S(2)}, u32[]{:S(2)}) collective-permute-start(bf16[512,1024]{1,0:T(8,128)(2,1)S(1)} %collective-permute-done.40.refs_8_), channel_id=1, source_target_pairs={{0,8},{8,16},{16,24},{24,28},{28,20},{20,12},{12,4},{4,0},{1,9},{9... | collective-permute-start | bytes 3145736 | tf_op jit(solution)/shard_map/ppermute | solution.py:36
  324.6 25.6 %collective-permute-start.45 = (bf16[512,1024]{1,0:T(8,128)(2,1)S(1)}, bf16[512,1024]{1,0:T(8,128)(2,1)S(1)}, u32[]{:S(2)}, u32[]{:S(2)}) collective-permute-start(bf16[512,1024]{1,0:T(8,128)(2,1)S(1)} %collective-permute-done.41.refs_9_), channel_id=1, source_target_pairs={{0,4},{8,0},{16,8},{24,16},{28,24},{20,28},{12,20},{4,12},{1,5},{9... | collective-permute-start | bytes 3145736 | tf_op jit(solution)/shard_map/ppermute | solution.py:36
  351.1 30.2 %collective-permute-start.46 = (bf16[256,1024]{1,0:T(8,128)(2,1)}, bf16[256,1024]{1,0:T(8,128)(2,1)S(1)}, u32[]{:S(2)}, u32[]{:S(2)}) collective-permute-start(bf16[256,1024]{1,0:T(8,128)(2,1)} %slice.209), channel_id=1, source_target_pairs={{0,8},{8,16},{16,24},{24,28},{28,20},{20,12},{12,4},{4,0},{1,9},{9... | collective-permute-start | bytes 1572872 | tf_op jit(solution)/shard_map/ppermute | solution.py:36
  353.2 28.2 %collective-permute-start.47 = (bf16[256,1024]{1,0:T(8,128)(2,1)}, bf16[256,1024]{1,0:T(8,128)(2,1)S(1)}, u32[]{:S(2)}, u32[]{:S(2)}) collective-permute-start(bf16[256,1024]{1,0:T(8,128)(2,1)} %slice.210), channel_id=1, source_target_pairs={{0,4},{8,0},{16,8},{24,16},{28,24},{20,28},{12,20},{4,12},{1,5},{9... | collective-permute-start | bytes 1572872 | tf_op jit(solution)/shard_map/ppermute | solution.py:36
  427.4 23.9 %collective-permute-start.53 = (bf16[4,64,1024]{2,1,0:T(8,128)(2,1)}, bf16[4,64,1024]{2,1,0:T(8,128)(2,1)S(1)}, u32[]{:S(2)}, u32[]{:S(2)}) collective-permute-start(bf16[4,64,1024]{2,1,0:T(8,128)(2,1)} %pad_maximum_fusion.3), channel_id=1, source_target_pairs={{0,8},{8,16},{16,24},{24,28},{28,20},{20,12},{12,4},{4,0},{1,9},{9... | collective-permute-start | bytes 1572872 | tf_op jit(solution)/shard_map/ppermute | solution.py:36
  (95 other events, 1555.0 us)

commit v12 on v7

--- a/solution.py
+++ b/solution.py
@@ -691,13 +691,9 @@
 
     by_request = lambda value: value.reshape(requests, tok_block, local_att)
 
-    def prepare():
+    def order_weight():
         made["w_in"] = w_in.reshape(D, 2 * local_inner)
-        first_state = ssm_init.reshape(requests, local_mheads, MHEAD_DIM, STATE)
-        made["initial"] = jnp.transpose(first_state, (0, 3, 1, 2)).reshape(
-            requests, STATE, local_inner
-        )
-        return (made["w_in"], made["initial"]), ()
+        return (made["w_in"],), ()
 
     def enter():
         made["act"], made["maps"], size = enter_mixer(
@@ -730,10 +726,12 @@
         return (made["read"], made["local"]), ()
 
     def start_relay():
+        first_state = clock.hold(ssm_init).reshape(requests, local_mheads, MHEAD_DIM, STATE)
+        initial = jnp.transpose(first_state, (0, 3, 1, 2)).reshape(requests, STATE, local_inner)
         made["relay"] = relay = Relay(
-            made["through"], clock.hold(made["local"]), made["initial"], seq_index, seq_count
-        )
-        return (), ((relay.pair_state,) if relay.paired else ())
+            made["through"], clock.hold(made["local"]), initial, seq_index, seq_count
+        )
+        return (initial,), ((relay.pair_state,) if relay.paired else ())
 
     def hop():
         made["relay"].advance(clock)
@@ -846,19 +844,11 @@
             )
 
     both = steps([query_ring, key_ring], 0, half - 2) + [query_ring] * 2 + [key_ring] * 2
-    def make_queries_hop():
-        done, _ = make_queries()
-        return done, hop()[1]
-
-    def make_keys_hop():
-        deferred = hop()[1]
-        return make_keys()[0], deferred
-
-    works = [prepare, enter, inside, start_relay, None, hop]
-    run(both, works + [None] * (len(both) - 1 - len(works)) + [make_queries_hop])
+    works = [order_weight, enter, inside, start_relay, hop, None, hop]
+    run(both, works + [None] * (len(both) - 1 - len(works)) + [make_queries])
     run(
         steps(slot_rings, 0, half),
-        [None, make_keys_hop, None, end_relay, None, leave, join_squares, leave_terms],
+        [hop, make_keys, end_relay, None, leave, join_squares, leave_terms],
     )
     run(
         steps([value_ring], 0, half),

time: 526 us -> 560 us (1.065)
  starting transfers between devices: 97 us -> 112 us
  waiting for transfers between devices: 171 us -> 183 us
    ppermute x2, waiting for transfers between devices: 36 us -> 6.89 us  [exchange(): lax.ppermute(value.astype(jnp.bfloat16), 'seq', self.swap)]
    ppermute x56, waiting for transfers between devices: 97.5 us -> 124 us  [ring_step(): return lax.ppermute(block, 'seq', route)]
    ppermute x56, starting transfers between devices: 75.6 us -> 95.7 us  [ring_step(): return lax.ppermute(block, 'seq', route)]
    ppermute x3, waiting for transfers between devices: 0.01 us -> 16.4 us  [advance(): self.entry = entry + lax.ppermute(leaving, 'seq', route).astype(jnp.float32)]
    ppermute x8, starting transfers between devices: 10.3 us -> 3.49 us  [step(): self.got = lax.ppermute(self.value, self.axis, route)]
    unnamed x98 -> x116, local copies, waits for them, and re-layouts: 16.2 us -> 17.2 us
  transfers between devices with their start and end apart: 74 -> 74, of which waited for: 34 -> 39; matrix products, arithmetic and copies ran while one was open for 20% -> 19% of each run, Pallas kernels for 20% -> 19%
where the time goes in v12:
time: 560 us; the launch traced here: 549 us
  waiting for transfers between devices  183 us (33%)
  Pallas kernels  133 us (24%)
  starting transfers between devices  112 us (20%)
  local copies, waits for them, and re-layouts  68.6 us (12%)
  other arithmetic  39 us (7%)
  matrix products  11 us (2%)
    ppermute x56, waiting for transfers between devices, ring_step(): return lax.ppermute(block, 'seq', route)  124 us
    ppermute x56, starting transfers between devices, ring_step(): return lax.ppermute(block, 'seq', route)  95.7 us
    pallas_call x2, Pallas kernels, cache_part(): pl.pallas_call(functools.partial(cache_kernel, slots), grid_spec=pltpu.Pr...  44.2 us
    pallas_call x4, Pallas kernels, project(): pl.pallas_call(functools.partial(project_kernel, len(pieces), turned), gr...  36.1 us
    pallas_call x2, Pallas kernels, finish_part(): pl.pallas_call(functools.partial(finish_kernel, slots), grid_spec=pltpu.P...  22.7 us
    ppermute x8, waiting for transfers between devices, step(): self.got = lax.ppermute(self.value, self.axis, route)  19 us
    unnamed x116, local copies, waits for them, and re-layouts  17.2 us
    ppermute x3, waiting for transfers between devices, advance(): self.entry = entry + lax.ppermute(leaving, 'seq', route).astype(jnp.float32)  16.4 us
  transfers between devices with their start and end apart: 74, of which 39 were waited for; matrix products, arithmetic and copies ran while one was open for 19% of the time, Pallas kernels for 19%

profile of v12, /device:TPU:0, one launch (start us, length us, event | category | flops | bytes accessed | tf_op | source)
XLA Modules:
  0.0 549.3 jit_solution(2157950853464565613)
XLA Ops:
  3.7 10.4 %copy.52 = bf16[256,8,2,1024]{3,1,2,0:T(8,128)(2,1)} copy(bf16[256,8,2,1024]{3,2,1,0:T(2,128)(2,1)} %bitcast.103) | data formatting | bytes 16777216
  17.1 11.7 %enter_mixer.1 = (f32[512,2048]{1,0:T(8,128)}, f32[512,128]{1,0:T(8,128)}, f32[512,16]{1,0:T(8,128)}) custom-call(bf16[512,4096]{1,0:T(8,128)(2,1)} %bitcast.64, f32[1,2048]{1,0:T(1,128)} %bitcast.126, bf16[2048,128]{1,0:T(8,128)(2,1)} %bc_ref.1, bf16[2048,16]{1,0:T(8,128)(2,1)} %copy.40.dt_ref, f32[1,16]{1,0:T(1,128)} %bitcast.127, bf16[2048,2048]{1,0:T(8,128)(2,1)} %bitcast.104), custom_call_target="tpu_custom_call" | custom-call | flops 4294967296 | bytes 14680064 | tf_op jit(solution)/shard_map/enter_mixer/pallas_call | solution.py:231
  36.4 9.6 %inside_block.1 = (f32[512,1024]{1,0:T(8,128)}, f32[8,64,1024]{2,1,0:T(8,128)}, f32[8,1,1024]{2,1,0:T(1,128)}) custom-call(f32[512,2048]{1,0:T(8,128)} %get-tuple-element.167.inner_ref.gate_ref, f32[512,128]{1,0:T(8,128)} %get-tuple-element.168.map_ref, f32[8,64,16]{2,1,0:T(8,128)} %bitcast.107, f32[8,64,16]{2,1,0:T(8,128)} %bitcast.111, ...), custom_call_target="tpu_custom_call" | custom-call | flops 402653184 | bytes 8388608 | tf_op jit(solution)/shard_map/inside_block/pallas_call | solution.py:309
  59.3 5.6 %copy.44 = f32[8,16,64,64]{2,1,3,0:T(8,128)} copy(f32[8,16,64,64]{3,2,1,0:T(8,128)} %reshape.129) | data formatting | bytes 4194304 | tf_op jit(solution)/shard_map/reshape | solution.py:729
  73.4 11.4 %collective-permute-done.10 = f32[8,1,1024]{2,1,0:T(1,128)S(1)} collective-permute-done((f32[8,1,1024]{2,1,0:T(1,128)}, f32[8,1,1024]{2,1,0:T(1,128)S(1)}, u32[]{:S(2)}, u32[]{:S(2)}) %collective-permute-start.10) | collective-permute-done | bytes 32800 | tf_op jit(solution)/shard_map/ppermute | solution.py:578
  94.9 12.4 %collective-permute-done.8.refs_12_ = bf16[512,1024]{1,0:T(8,128)(2,1)} collective-permute-done((bf16[512,1024]{1,0:T(8,128)(2,1)}, bf16[512,1024]{1,0:T(8,128)(2,1)}, u32[]{:S(2)}, u32[]{:S(2)}) %collective-permute-start.8) | collective-permute-done | bytes 1048608 | tf_op jit(solution)/shard_map/ppermute | solution.py:36
  111.1 16.4 %collective-permute-done.14 = bf16[8,64,512]{2,1,0:T(8,128)(2,1)S(1)} collective-permute-done((bf16[8,64,512]{2,1,0:T(8,128)(2,1)}, bf16[8,64,512]{2,1,0:T(8,128)(2,1)S(1)}, u32[]{:S(2)}, u32[]{:S(2)}) %collective-permute-start.14) | collective-permute-done | bytes 524320 | tf_op jit(solution)/shard_map/ppermute | solution.py:604
  131.4 11.8 %collective-permute-start.16 = (bf16[512,1024]{1,0:T(8,128)(2,1)}, bf16[512,1024]{1,0:T(8,128)(2,1)}, u32[]{:S(2)}, u32[]{:S(2)}) collective-permute-start(bf16[512,1024]{1,0:T(8,128)(2,1)} %collective-permute-done.9.refs_13_), channel_id=1, source_target_pairs={{0,4},{8,0},{16,8},{24,16},{28,24},{20,28},{12,20},{4,12},{1,5},{9... | collective-permute-start | bytes 3145736 | tf_op jit(solution)/shard_map/ppermute | solution.py:36
  155.3 21.2 %collective-permute-done.12.refs_16_ = bf16[256,1024]{1,0:T(8,128)(2,1)} collective-permute-done((bf16[256,1024]{1,0:T(8,128)(2,1)}, bf16[256,1024]{1,0:T(8,128)(2,1)}, u32[]{:S(2)}, u32[]{:S(2)}) %collective-permute-start.12) | collective-permute-done | bytes 524320 | tf_op jit(solution)/shard_map/ppermute | solution.py:36
  178.7 10.5 %project.4 = bf16[512,1024]{1,0:T(8,128)(2,1)} custom-call(s32[8]{0:T(128)} %fusion.21.places_ref.place_ref, bf16[512,4096]{1,0:T(8,128)(2,1)} %bitcast.65, bf16[512,4096]{1,0:T(8,128)(2,1)} %bitcast.66, bf16[512,4096]{1,0:T(8,128)(2,1)} %bitcast.67, bf16[512,4096]{1,0:T(8,128)(2,1)} %bitcast.68, bf16[512,4096]{1,0:T(8,128)(2,1)} %bitcast.69, ...), custom_call_target="tpu_custom_call" | custom-call | flops 4294967296 | bytes 12582912 | tf_op jit(solution)/shard_map/project/pallas_call | solution.py:169
  197.8 9.7 %collective-permute-start.21 = (bf16[4,64,1024]{2,1,0:T(8,128)(2,1)S(1)}, bf16[4,64,1024]{2,1,0:T(8,128)(2,1)S(1)}, u32[]{:S(2)}, u32[]{:S(2)}) collective-permute-start(bf16[4,64,1024]{2,1,0:T(8,128)(2,1)S(1)} %bitcast.116), channel_id=1, source_target_pairs={{0,4},{8,0},{16,8},{24,16},{28,24},{20,28},{12,20},{4,12},{1,5},{9... | collective-permute-start | bytes 1572872 | tf_op jit(solution)/shard_map/ppermute | solution.py:36
  210.1 10.4 %project.5 = bf16[512,1024]{1,0:T(8,128)(2,1)} custom-call(s32[8]{0:T(128)} %fusion.21.places_ref.place_ref, bf16[512,4096]{1,0:T(8,128)(2,1)} %bitcast.78, bf16[512,4096]{1,0:T(8,128)(2,1)} %bitcast.75, bf16[512,4096]{1,0:T(8,128)(2,1)} %bitcast.76, bf16[512,4096]{1,0:T(8,128)(2,1)} %bitcast.77, bf16[512,4096]{1,0:T(8,128)(2,1)} %bitcast.74, ...), custom_call_target="tpu_custom_call" | custom-call | flops 4294967296 | bytes 12582912 | tf_op jit(solution)/shard_map/project/pallas_call | solution.py:169
  222.7 8.4 %collective-permute-start.24 = (bf16[4,64,1024]{2,1,0:T(8,128)(2,1)S(1)}, bf16[4,64,1024]{2,1,0:T(8,128)(2,1)S(1)}, u32[]{:S(2)}, u32[]{:S(2)}) collective-permute-start(bf16[4,64,1024]{2,1,0:T(8,128)(2,1)S(1)} %bitcast.113), channel_id=1, source_target_pairs={{0,4},{8,0},{16,8},{24,16},{28,24},{20,28},{12,20},{4,12},{1,5},{9... | collective-permute-start | bytes 1572872 | tf_op jit(solution)/shard_map/ppermute | solution.py:36
  236.6 7.2 %collective-permute-done.23.refs_1_ = bf16[4,64,1024]{2,1,0:T(8,128)(2,1)S(1)} collective-permute-done((bf16[4,64,1024]{2,1,0:T(8,128)(2,1)S(1)}, bf16[4,64,1024]{2,1,0:T(8,128)(2,1)S(1)}, u32[]{:S(2)}, u32[]{:S(2)}) %collective-permute-start.23) | collective-permute-done | bytes 524320 | tf_op jit(solution)/shard_map/ppermute | solution.py:36
  248.2 6.9 %collective-permute-done.27 = bf16[8,64,512]{2,1,0:T(8,128)(2,1)S(1)} collective-permute-done((bf16[8,64,512]{2,1,0:T(8,128)(2,1)S(1)}, bf16[8,64,512]{2,1,0:T(8,128)(2,1)S(1)}, u32[]{:S(2)}, u32[]{:S(2)}) %collective-permute-start.27) | collective-permute-done | bytes 524320 | tf_op jit(solution)/shard_map/ppermute | solution.py:589
  256.9 9.4 %collective-permute-done.25.refs_3_ = bf16[4,64,1024]{2,1,0:T(8,128)(2,1)S(1)} collective-permute-done((bf16[4,64,1024]{2,1,0:T(8,128)(2,1)S(1)}, bf16[4,64,1024]{2,1,0:T(8,128)(2,1)S(1)}, u32[]{:S(2)}, u32[]{:S(2)}) %collective-permute-start.25) | collective-permute-done | bytes 524320 | tf_op jit(solution)/shard_map/ppermute | solution.py:36
  268.4 8.8 %leave_mixer.1 = (bf16[512,1024]{1,0:T(8,128)(2,1)}, f32[512,128]{1,0:T(8,128)}, f32[8,64,1024]{2,1,0:T(8,128)}) custom-call(f32[8,64,1024]{2,1,0:T(8,128)} %pad_maximum_fusion.entry_ref, f32[512,128]{1,0:T(8,128)} %get-tuple-element.168.map_ref, f32[8,64,16]{2,1,0:T(8,128)} %bitcast.108, f32[512,1024]{1,0:T(8,128)} %get-tuple-element.169.read_ref, ...), custom_call_target="tpu_custom_call" | custom-call | flops 67108864 | bytes 12582912 | tf_op jit(solution)/shard_map/leave_mixer/pallas_call | solution.py:362
  287.1 7.0 %convolution_multiply_fusion = f32[512,2048]{1,0:T(8,128)} fusion(bf16[512,1024]{1,0:T(8,128)(2,1)} %get-tuple-element.214, bf16[1024,2048]{1,0:T(8,128)(2,1)} %param.35, f32[512]{0:T(512)S(1)} %bitcast.125), kind=kOutput, calls=%fused_computation | convolution fusion | flops 2148532224 | bytes 9439232 | tf_op jit(solution)/shard_map/dot_general | solution.py:769
  310.0 22.0 %cache_part.2 = (bf16[4,512,1024]{2,1,0:T(8,128)(2,1)}, bf16[4,1024,512]{2,1,0:T(8,128)(2,1)}, f32[4,8,512]{2,1,0:T(8,128)}, f32[4,8,512]{2,1,0:T(8,128)}) custom-call(s32[1]{0:T(128)} %bitcast.1.first_ref, s32[8]{0:T(128)} %fusion.21.places_ref.place_ref, s32[4]{0:T(128)} %get-tuple-element.333.live_ref, bf16[4,64,1024]{2,1,0:T(8,128)(2,1)} %bitcast.117, ...), custom_call_target="tpu_custom_call" | custom-call | flops 4294967296 | bytes 20971520 | tf_op jit(solution)/shard_map/cache_part/pallas_call | solution.py:448
  338.6 22.1 %cache_part.3 = (bf16[4,512,1024]{2,1,0:T(8,128)(2,1)}, bf16[4,1024,512]{2,1,0:T(8,128)(2,1)}, f32[4,8,512]{2,1,0:T(8,128)}, f32[4,8,512]{2,1,0:T(8,128)}) custom-call(s32[1]{0:T(128)} %bitcast.1.first_ref, s32[8]{0:T(128)} %fusion.21.places_ref.place_ref, s32[4]{0:T(128)} %get-tuple-element.332.live_ref, bf16[4,64,1024]{2,1,0:T(8,128)(2,1)} %bitcast.114, ...), custom_call_target="tpu_custom_call" | custom-call | flops 4294967296 | bytes 20971520 | tf_op jit(solution)/shard_map/cache_part/pallas_call | solution.py:448
  368.6 5.6 %copy.45 = f32[8,16,64,64]{3,2,1,0:T(8,128)} copy(f32[8,16,64,64]{2,1,3,0:T(8,128)} %bitcast.99) | data formatting | bytes 4194304 | tf_op jit(solution)/shard_map/transpose | solution.py:776
  378.9 7.6 %collective-permute-done.44.refs_12_ = bf16[512,1024]{1,0:T(8,128)(2,1)S(1)} collective-permute-done((bf16[512,1024]{1,0:T(8,128)(2,1)S(1)}, bf16[512,1024]{1,0:T(8,128)(2,1)S(1)}, u32[]{:S(2)}, u32[]{:S(2)}) %collective-permute-start.44) | collective-permute-done | bytes 1048608 | tf_op jit(solution)/shard_map/ppermute | solution.py:36
  389.4 9.7 %project.6.refs_6_ = f32[512,1024]{1,0:T(8,128)} custom-call(s32[8]{0:T(128)} %fusion.21.places_ref.place_ref, bf16[512,4096]{1,0:T(8,128)(2,1)} %bitcast.83, bf16[512,4096]{1,0:T(8,128)(2,1)} %bitcast.84, bf16[512,4096]{1,0:T(8,128)(2,1)} %bitcast.85, bf16[512,4096]{1,0:T(8,128)(2,1)} %bitcast.86, bf16[512,4096]{1,0:T(8,128)(2,1)} %bitcast.87, ...), custom_call_target="tpu_custom_call" | custom-call | flops 3758096384 | bytes 12582912 | tf_op jit(solution)/shard_map/project/pallas_call | solution.py:169
  401.6 5.5 collective-permute-done.50
  409.4 5.4 project.7
  414.8 11.2 %finish_part.2 = (f32[4,8,512]{2,1,0:T(8,128)}, bf16[4,64,1024]{2,1,0:T(8,128)(2,1)}, bf16[4,64,1024]{2,1,0:T(8,128)(2,1)}, bf16[4,64,1024]{2,1,0:T(8,128)(2,1)}...) custom-call(s32[1]{0:T(128)} %bitcast.1.first_ref, ...), custom_call_target="tpu_custom_call" | custom-call | flops 536870912 | bytes 12582912 | tf_op jit(solution)/shard_map/finish_part/pallas_call | solution.py:510
  427.8 11.5 %finish_part.3 = (f32[4,8,512]{2,1,0:T(8,128)}, bf16[4,64,1024]{2,1,0:T(8,128)(2,1)}, bf16[4,64,1024]{2,1,0:T(8,128)(2,1)}, bf16[4,64,1024]{2,1,0:T(8,128)(2,1)}...) custom-call(s32[1]{0:T(128)} %bitcast.1.first_ref, ...), custom_call_target="tpu_custom_call" | custom-call | flops 536870912 | bytes 12582912 | tf_op jit(solution)/shard_map/finish_part/pallas_call | solution.py:510
  450.0 5.7 %collective-permute-done.56 = bf16[2,64,1024]{2,1,0:T(8,128)(2,1)S(1)} collective-permute-done((bf16[2,64,1024]{2,1,0:T(8,128)(2,1)}, bf16[2,64,1024]{2,1,0:T(8,128)(2,1)S(1)}, u32[]{:S(2)}, u32[]{:S(2)}) %collective-permute-start.56) | collective-permute-done | bytes 262176 | tf_op jit(solution)/shard_map/ppermute | solution.py:36
  461.9 8.8 %collective-permute-done.64 = bf16[4,64,1024]{2,1,0:T(8,128)(2,1)S(1)} collective-permute-done((bf16[4,64,1024]{2,1,0:T(8,128)(2,1)S(1)}, bf16[4,64,1024]{2,1,0:T(8,128)(2,1)S(1)}, u32[]{:S(2)}, u32[]{:S(2)}) %collective-permute-start.64) | collective-permute-done | bytes 524320 | tf_op jit(solution)/shard_map/ppermute | solution.py:36
  471.9 7.7 %collective-permute-done.53 = bf16[4,64,1024]{2,1,0:T(8,128)(2,1)S(1)} collective-permute-done((bf16[4,64,1024]{2,1,0:T(8,128)(2,1)S(1)}, bf16[4,64,1024]{2,1,0:T(8,128)(2,1)S(1)}, u32[]{:S(2)}, u32[]{:S(2)}) %collective-permute-start.53) | collective-permute-done | bytes 524320 | tf_op jit(solution)/shard_map/ppermute | solution.py:36
  490.3 10.7 %collective-permute-done.65 = f32[8,8,512]{2,1,0:T(8,128)S(1)} collective-permute-done((f32[8,8,512]{2,1,0:T(8,128)S(1)}, f32[8,8,512]{2,1,0:T(8,128)S(1)}, u32[]{:S(2)}, u32[]{:S(2)}) %collective-permute-start.65) | collective-permute-done | bytes 131104 | tf_op jit(solution)/shard_map/ppermute | solution.py:96
  540.9 5.3 collective-permute-done.67
  (347 shorter events, 219.3 us)
Async XLA Ops:
  0.6 32.2 %collective-permute-start = (bf16[512,1024]{1,0:T(8,128)(2,1)}, bf16[512,1024]{1,0:T(8,128)(2,1)}, u32[]{:S(2)}, u32[]{:S(2)}) collective-permute-start(bf16[512,1024]{1,0:T(8,128)(2,1)} %refs_9_.4), channel_id=1, source_target_pairs={{0,8},{8,16},{16,24},{24,28},{28,20},{20,12},{12,4},{4,0},{1,9},{9... | collective-permute-start | bytes 3145736 | tf_op jit(solution)/shard_map/ppermute | solution.py:36
  3.7 29.1 %collective-permute-start.1 = (bf16[512,1024]{1,0:T(8,128)(2,1)}, bf16[512,1024]{1,0:T(8,128)(2,1)}, u32[]{:S(2)}, u32[]{:S(2)}) collective-permute-start(bf16[512,1024]{1,0:T(8,128)(2,1)} %refs_9_.4), channel_id=1, source_target_pairs={{0,4},{8,0},{16,8},{24,16},{28,24},{20,28},{12,20},{4,12},{1,5},{9... | collective-permute-start | bytes 3145736 | tf_op jit(solution)/shard_map/ppermute | solution.py:36
  14.1 36.3 %collective-permute-start.4 = (bf16[512,1024]{1,0:T(8,128)(2,1)S(1)}, bf16[512,1024]{1,0:T(8,128)(2,1)}, u32[]{:S(2)}, u32[]{:S(2)}) collective-permute-start(bf16[512,1024]{1,0:T(8,128)(2,1)S(1)} %copy-done.18), channel_id=1, source_target_pairs={{0,8},{8,16},{16,24},{24,28},{28,20},{20,12},{12,4},{4,0},{1,9},{9... | collective-permute-start | bytes 3145736 | tf_op jit(solution)/shard_map/ppermute | solution.py:36
  16.1 36.5 %collective-permute-start.5 = (bf16[512,1024]{1,0:T(8,128)(2,1)S(1)}, bf16[512,1024]{1,0:T(8,128)(2,1)}, u32[]{:S(2)}, u32[]{:S(2)}) collective-permute-start(bf16[512,1024]{1,0:T(8,128)(2,1)S(1)} %copy-done.18), channel_id=1, source_target_pairs={{0,4},{8,0},{16,8},{24,16},{28,24},{20,28},{12,20},{4,12},{1,5},{9... | collective-permute-start | bytes 3145736 | tf_op jit(solution)/shard_map/ppermute | solution.py:36
  32.8 53.0 %collective-permute-start.2 = (bf16[512,1024]{1,0:T(8,128)(2,1)}, bf16[512,1024]{1,0:T(8,128)(2,1)}, u32[]{:S(2)}, u32[]{:S(2)}) collective-permute-start(bf16[512,1024]{1,0:T(8,128)(2,1)} %collective-permute-done.refs_10_), channel_id=1, source_target_pairs={{0,8},{8,16},{16,24},{24,28},{28,20},{20,12},{12,4},{4,0},{1,9},{9... | collective-permute-start | bytes 3145736 | tf_op jit(solution)/shard_map/ppermute | solution.py:36
  34.8 51.0 %collective-permute-start.3 = (bf16[512,1024]{1,0:T(8,128)(2,1)}, bf16[512,1024]{1,0:T(8,128)(2,1)}, u32[]{:S(2)}, u32[]{:S(2)}) collective-permute-start(bf16[512,1024]{1,0:T(8,128)(2,1)} %collective-permute-done.1.refs_11_), channel_id=1, source_target_pairs={{0,4},{8,0},{16,8},{24,16},{28,24},{20,28},{12,20},{4,12},{1,5},{9... | collective-permute-start | bytes 3145736 | tf_op jit(solution)/shard_map/ppermute | solution.py:36
  54.2 33.7 %collective-permute-start.11 = (bf16[8,64,512]{2,1,0:T(8,128)(2,1)S(1)}, bf16[8,64,512]{2,1,0:T(8,128)(2,1)S(1)}, u32[]{:S(2)}, u32[]{:S(2)}) collective-permute-start(bf16[8,64,512]{2,1,0:T(8,128)(2,1)S(1)} %select_convert_fusion.1), channel_id=1, source_target_pairs={{0,4},{4,0},{8,12},{12,8},{16,20},{20,16},{24,28},{28,24},{1,5},{5... | collective-permute-start | bytes 1572872 | tf_op jit(solution)/shard_map/ppermute | solution.py:589
  54.3 30.4 %collective-permute-start.10 = (f32[8,1,1024]{2,1,0:T(1,128)}, f32[8,1,1024]{2,1,0:T(1,128)S(1)}, u32[]{:S(2)}, u32[]{:S(2)}) collective-permute-start(f32[8,1,1024]{2,1,0:T(1,128)} %get-tuple-element.178.through_ref), channel_id=1, source_target_pairs={{0,4},{4,0},{8,12},{12,8},{16,20},{20,16},{24,28},{28,24},{1,5},{5... | collective-permute-start | bytes 98312 | tf_op jit(solution)/shard_map/ppermute | solution.py:578
  70.0 37.3 %collective-permute-start.8 = (bf16[512,1024]{1,0:T(8,128)(2,1)}, bf16[512,1024]{1,0:T(8,128)(2,1)}, u32[]{:S(2)}, u32[]{:S(2)}) collective-permute-start(bf16[512,1024]{1,0:T(8,128)(2,1)} %collective-permute-done.4.refs_10_), channel_id=1, source_target_pairs={{0,8},{8,16},{16,24},{24,28},{28,20},{20,12},{12,4},{4,0},{1,9},{9... | collective-permute-start | bytes 3145736 | tf_op jit(solution)/shard_map/ppermute | solution.py:36
  84.7 26.4 %collective-permute-start.9 = (bf16[512,1024]{1,0:T(8,128)(2,1)}, bf16[512,1024]{1,0:T(8,128)(2,1)}, u32[]{:S(2)}, u32[]{:S(2)}) collective-permute-start(bf16[512,1024]{1,0:T(8,128)(2,1)} %collective-permute-done.5.refs_11_), channel_id=1, source_target_pairs={{0,4},{8,0},{16,8},{24,16},{28,24},{20,28},{12,20},{4,12},{1,5},{9... | collective-permute-start | bytes 3145736 | tf_op jit(solution)/shard_map/ppermute | solution.py:36
  85.8 43.2 %collective-permute-start.6 = (bf16[512,1024]{1,0:T(8,128)(2,1)}, bf16[512,1024]{1,0:T(8,128)(2,1)}, u32[]{:S(2)}, u32[]{:S(2)}) collective-permute-start(bf16[512,1024]{1,0:T(8,128)(2,1)} %collective-permute-done.2.refs_12_), channel_id=1, source_target_pairs={{0,8},{8,16},{16,24},{24,28},{28,20},{20,12},{12,4},{4,0},{1,9},{9... | collective-permute-start | bytes 3145736 | tf_op jit(solution)/shard_map/ppermute | solution.py:36
  86.9 44.1 %collective-permute-start.7 = (bf16[512,1024]{1,0:T(8,128)(2,1)}, bf16[512,1024]{1,0:T(8,128)(2,1)}, u32[]{:S(2)}, u32[]{:S(2)}) collective-permute-start(bf16[512,1024]{1,0:T(8,128)(2,1)} %collective-permute-done.3.refs_13_), channel_id=1, source_target_pairs={{0,4},{8,0},{16,8},{24,16},{28,24},{20,28},{12,20},{4,12},{1,5},{9... | collective-permute-start | bytes 3145736 | tf_op jit(solution)/shard_map/ppermute | solution.py:36
  91.4 36.1 %collective-permute-start.14 = (bf16[8,64,512]{2,1,0:T(8,128)(2,1)}, bf16[8,64,512]{2,1,0:T(8,128)(2,1)S(1)}, u32[]{:S(2)}, u32[]{:S(2)}) collective-permute-start(bf16[8,64,512]{2,1,0:T(8,128)(2,1)} %get-tuple-element.307), channel_id=1, source_target_pairs={{0,8},{4,12},{1,9},{5,13},{2,10},{6,14},{3,11},{7,15}} | collective-permute-start | bytes 1572872 | tf_op jit(solution)/shard_map/ppermute | solution.py:604
  131.0 46.7 %collective-permute-start.15 = (bf16[512,1024]{1,0:T(8,128)(2,1)}, bf16[512,1024]{1,0:T(8,128)(2,1)}, u32[]{:S(2)}, u32[]{:S(2)}) collective-permute-start(bf16[512,1024]{1,0:T(8,128)(2,1)} %collective-permute-done.8.refs_12_), channel_id=1, source_target_pairs={{0,8},{8,16},{16,24},{24,28},{28,20},{20,12},{12,4},{4,0},{1,9},{9... | collective-permute-start | bytes 3145736 | tf_op jit(solution)/shard_map/ppermute | solution.py:36
  131.4 46.3 %collective-permute-start.16 = (bf16[512,1024]{1,0:T(8,128)(2,1)}, bf16[512,1024]{1,0:T(8,128)(2,1)}, u32[]{:S(2)}, u32[]{:S(2)}) collective-permute-start(bf16[512,1024]{1,0:T(8,128)(2,1)} %collective-permute-done.9.refs_13_), channel_id=1, source_target_pairs={{0,4},{8,0},{16,8},{24,16},{28,24},{20,28},{12,20},{4,12},{1,5},{9... | collective-permute-start | bytes 3145736 | tf_op jit(solution)/shard_map/ppermute | solution.py:36
  147.0 29.5 %collective-permute-start.12 = (bf16[256,1024]{1,0:T(8,128)(2,1)}, bf16[256,1024]{1,0:T(8,128)(2,1)}, u32[]{:S(2)}, u32[]{:S(2)}) collective-permute-start(bf16[256,1024]{1,0:T(8,128)(2,1)} %slice.195), channel_id=1, source_target_pairs={{0,8},{8,16},{16,24},{24,28},{28,20},{20,12},{12,4},{4,0},{1,9},{9... | collective-permute-start | bytes 1572872 | tf_op jit(solution)/shard_map/ppermute | solution.py:36
  147.0 29.5 %collective-permute-start.13 = (bf16[256,1024]{1,0:T(8,128)(2,1)}, bf16[256,1024]{1,0:T(8,128)(2,1)}, u32[]{:S(2)}, u32[]{:S(2)}) collective-permute-start(bf16[256,1024]{1,0:T(8,128)(2,1)} %slice.196), channel_id=1, source_target_pairs={{0,4},{8,0},{16,8},{24,16},{28,24},{20,28},{12,20},{4,12},{1,5},{9... | collective-permute-start | bytes 1572872 | tf_op jit(solution)/shard_map/ppermute | solution.py:36
  150.4 26.1 %collective-permute-start.17 = (bf16[8,64,512]{2,1,0:T(8,128)(2,1)}, bf16[8,64,512]{2,1,0:T(8,128)(2,1)}, u32[]{:S(2)}, u32[]{:S(2)}) collective-permute-start(bf16[8,64,512]{2,1,0:T(8,128)(2,1)} %add_convert_fusion.9), channel_id=1, source_target_pairs={{8,16},{12,20},{9,17},{13,21},{10,18},{14,22},{11,19},{15,23}} | collective-permute-start | bytes 1572872 | tf_op jit(solution)/shard_map/ppermute | solution.py:604
  178.0 29.5 %collective-permute-start.22 = (bf16[8,64,512]{2,1,0:T(8,128)(2,1)S(1)}, bf16[8,64,512]{2,1,0:T(8,128)(2,1)S(1)}, u32[]{:S(2)}, u32[]{:S(2)}) collective-permute-start(bf16[8,64,512]{2,1,0:T(8,128)(2,1)S(1)} %add_convert_fusion.8), channel_id=1, source_target_pairs={{16,24},{20,28},{17,25},{21,29},{18,26},{22,30},{19,27},{23,31}} | collective-permute-start | bytes 1572872 | tf_op jit(solution)/shard_map/ppermute | solution.py:604
  195.1 25.4 %collective-permute-start.20 = (bf16[4,64,1024]{2,1,0:T(8,128)(2,1)S(1)}, bf16[4,64,1024]{2,1,0:T(8,128)(2,1)S(1)}, u32[]{:S(2)}, u32[]{:S(2)}) collective-permute-start(bf16[4,64,1024]{2,1,0:T(8,128)(2,1)S(1)} %bitcast.115), channel_id=1, source_target_pairs={{0,8},{8,16},{16,24},{24,28},{28,20},{20,12},{12,4},{4,0},{1,9},{9... | collective-permute-start | bytes 1572872 | tf_op jit(solution)/shard_map/ppermute | solution.py:36
  234.6 31.7 %collective-permute-start.25 = (bf16[4,64,1024]{2,1,0:T(8,128)(2,1)S(1)}, bf16[4,64,1024]{2,1,0:T(8,128)(2,1)S(1)}, u32[]{:S(2)}, u32[]{:S(2)}) collective-permute-start(bf16[4,64,1024]{2,1,0:T(8,128)(2,1)S(1)} %collective-permute-done.20.refs_1_), channel_id=1, source_target_pairs={{0,8},{8,16},{16,24},{24,28},{28,20},{20,12},{12,4},{4,0},{1,9},{9... | collective-permute-start | bytes 1572872 | tf_op jit(solution)/shard_map/ppermute | solution.py:36
  236.6 29.7 %collective-permute-start.26 = (bf16[4,64,1024]{2,1,0:T(8,128)(2,1)S(1)}, bf16[4,64,1024]{2,1,0:T(8,128)(2,1)S(1)}, u32[]{:S(2)}, u32[]{:S(2)}) collective-permute-start(bf16[4,64,1024]{2,1,0:T(8,128)(2,1)S(1)} %collective-permute-done.21.refs_2_), channel_id=1, source_target_pairs={{0,4},{8,0},{16,8},{24,16},{28,24},{20,28},{12,20},{4,12},{1,5},{9... | collective-permute-start | bytes 1572872 | tf_op jit(solution)/shard_map/ppermute | solution.py:36
  243.8 34.6 %collective-permute-start.28 = (bf16[4,64,1024]{2,1,0:T(8,128)(2,1)S(1)}, bf16[4,64,1024]{2,1,0:T(8,128)(2,1)S(1)}, u32[]{:S(2)}, u32[]{:S(2)}) collective-permute-start(bf16[4,64,1024]{2,1,0:T(8,128)(2,1)S(1)} %collective-permute-done.23.refs_1_), channel_id=1, source_target_pairs={{0,8},{8,16},{16,24},{24,28},{28,20},{20,12},{12,4},{4,0},{1,9},{9... | collective-permute-start | bytes 1572872 | tf_op jit(solution)/shard_map/ppermute | solution.py:36
  248.2 30.3 %collective-permute-start.29 = (bf16[4,64,1024]{2,1,0:T(8,128)(2,1)S(1)}, bf16[4,64,1024]{2,1,0:T(8,128)(2,1)S(1)}, u32[]{:S(2)}, u32[]{:S(2)}) collective-permute-start(bf16[4,64,1024]{2,1,0:T(8,128)(2,1)S(1)} %collective-permute-done.24.refs_2_), channel_id=1, source_target_pairs={{0,4},{8,0},{16,8},{24,16},{28,24},{20,28},{12,20},{4,12},{1,5},{9... | collective-permute-start | bytes 1572872 | tf_op jit(solution)/shard_map/ppermute | solution.py:36
  304.3 31.4 %collective-permute-start.40 = (bf16[512,1024]{1,0:T(8,128)(2,1)S(1)}, bf16[512,1024]{1,0:T(8,128)(2,1)S(1)}, u32[]{:S(2)}, u32[]{:S(2)}) collective-permute-start(bf16[512,1024]{1,0:T(8,128)(2,1)S(1)} %copy-done.19), channel_id=1, source_target_pairs={{0,8},{8,16},{16,24},{24,28},{28,20},{20,12},{12,4},{4,0},{1,9},{9... | collective-permute-start | bytes 3145736 | tf_op jit(solution)/shard_map/ppermute | solution.py:36
  306.3 29.4 %collective-permute-start.41 = (bf16[512,1024]{1,0:T(8,128)(2,1)S(1)}, bf16[512,1024]{1,0:T(8,128)(2,1)S(1)}, u32[]{:S(2)}, u32[]{:S(2)}) collective-permute-start(bf16[512,1024]{1,0:T(8,128)(2,1)S(1)} %copy-done.19), channel_id=1, source_target_pairs={{0,4},{8,0},{16,8},{24,16},{28,24},{20,28},{12,20},{4,12},{1,5},{9... | collective-permute-start | bytes 3145736 | tf_op jit(solution)/shard_map/ppermute | solution.py:36
  307.8 26.2 %collective-permute-start.38 = (bf16[2,64,1024]{2,1,0:T(8,128)(2,1)S(1)}, bf16[2,64,1024]{2,1,0:T(8,128)(2,1)S(1)}, u32[]{:S(2)}, u32[]{:S(2)}) collective-permute-start(bf16[2,64,1024]{2,1,0:T(8,128)(2,1)S(1)} %slice.207), channel_id=1, source_target_pairs={{0,8},{8,16},{16,24},{24,28},{28,20},{20,12},{12,4},{4,0},{1,9},{9... | collective-permute-start | bytes 786440 | tf_op jit(solution)/shard_map/ppermute | solution.py:36
  309.8 25.9 %collective-permute-start.39 = (bf16[2,64,1024]{2,1,0:T(8,128)(2,1)S(1)}, bf16[2,64,1024]{2,1,0:T(8,128)(2,1)S(1)}, u32[]{:S(2)}, u32[]{:S(2)}) collective-permute-start(bf16[2,64,1024]{2,1,0:T(8,128)(2,1)S(1)} %slice.208), channel_id=1, source_target_pairs={{0,4},{8,0},{16,8},{24,16},{28,24},{20,28},{12,20},{4,12},{1,5},{9... | collective-permute-start | bytes 786440 | tf_op jit(solution)/shard_map/ppermute | solution.py:36
  335.7 25.1 %collective-permute-start.42 = (bf16[512,1024]{1,0:T(8,128)(2,1)S(1)}, bf16[512,1024]{1,0:T(8,128)(2,1)S(1)}, u32[]{:S(2)}, u32[]{:S(2)}) collective-permute-start(bf16[512,1024]{1,0:T(8,128)(2,1)S(1)} %collective-permute-done.40.refs_8_), channel_id=1, source_target_pairs={{0,8},{8,16},{16,24},{24,28},{28,20},{20,12},{12,4},{4,0},{1,9},{9... | collective-permute-start | bytes 3145736 | tf_op jit(solution)/shard_map/ppermute | solution.py:36
  360.8 25.6 %collective-permute-start.44 = (bf16[512,1024]{1,0:T(8,128)(2,1)S(1)}, bf16[512,1024]{1,0:T(8,128)(2,1)S(1)}, u32[]{:S(2)}, u32[]{:S(2)}) collective-permute-start(bf16[512,1024]{1,0:T(8,128)(2,1)S(1)} %collective-permute-done.42.refs_10_), channel_id=1, source_target_pairs={{0,8},{8,16},{16,24},{24,28},{28,20},{20,12},{12,4},{4,0},{1,9},{9... | collective-permute-start | bytes 3145736 | tf_op jit(solution)/shard_map/ppermute | solution.py:36
  363.8 25.5 %collective-permute-start.48 = (f32[8,8,512]{2,1,0:T(8,128)S(1)}, f32[8,8,512]{2,1,0:T(8,128)S(1)}, u32[]{:S(2)}, u32[]{:S(2)}) collective-permute-start(f32[8,8,512]{2,1,0:T(8,128)S(1)} %constant_dynamic-update-slice_fusion), channel_id=1, source_target_pairs={{0,4},{4,0},{8,12},{12,8},{16,20},{20,16},{24,28},{28,24},{1,5},{5... | collective-permute-start | bytes 393224 | tf_op jit(solution)/shard_map/ppermute | solution.py:96
  461.8 24.3 %collective-permute-start.62 = (f32[8,8,512]{2,1,0:T(8,128)S(1)}, f32[8,8,512]{2,1,0:T(8,128)S(1)}, u32[]{:S(2)}, u32[]{:S(2)}) collective-permute-start(f32[8,8,512]{2,1,0:T(8,128)S(1)} %add.234), channel_id=1, source_target_pairs={{0,8},{4,12},{8,0},{12,4},{16,24},{20,28},{24,16},{28,20},{1,9},{5... | collective-permute-start | bytes 393224 | tf_op jit(solution)/shard_map/ppermute | solution.py:96
  (97 other events, 1635.5 us)

commit v13 on v8

--- a/solution.py
+++ b/solution.py
@@ -340,7 +340,7 @@
     squares = jnp.sum(mixed * mixed, axis=1, keepdims=True)
     square_ref[...] = jnp.broadcast_to(squares, square_ref.shape)
     gated_ref[...] = (mixed * gain_ref[...]).astype(jnp.bfloat16)
-    chain_ref[0] = through_ref[0] * entry + local_ref[0]
+    chain_ref[0] = (through_ref[0] * entry + local_ref[0]).T
 
 
 def leave_mixer(entry, maps, decay, read, act, gain, local, through):
@@ -361,11 +361,11 @@
             one(STATE, inner),
             one(1, inner),
         ],
-        out_specs=[flat(inner), flat(128), one(STATE, inner)],
+        out_specs=[flat(inner), flat(128), one(inner, STATE)],
         out_shape=[
             jax.ShapeDtypeStruct((requests * tokens, inner), jnp.bfloat16),
             jax.ShapeDtypeStruct((requests * tokens, 128), jnp.float32),
-            jax.ShapeDtypeStruct((requests, STATE, inner), jnp.float32),
+            jax.ShapeDtypeStruct((requests, inner, STATE), jnp.float32),
         ],
         compiler_params=pltpu.CompilerParams(vmem_limit_bytes=VMEM_BYTES),
         cost_estimate=LIGHT,
@@ -750,22 +750,6 @@
         ) * lax.rsqrt(squares / D_INNER + 1e-05)
         return (made["terms"],), ()
 
-    def chain_split():
-        made["chain"] = clock.hold(made["chain"]).reshape(
-            requests, STATE, local_mheads, MHEAD_DIM
-        )
-        return (made["chain"],), ()
-
-    def chain_turn():
-        made["chain"] = jnp.transpose(clock.hold(made["chain"]), (0, 2, 3, 1))
-        return (made["chain"],), ()
-
-    def chain_join():
-        made["chain"] = clock.hold(made["chain"]).reshape(
-            requests, 1, local_mheads, MHEAD_DIM * STATE
-        )
-        return (made["chain"],), ()
-
     query_ring, key_ring, value_ring = (Ring(w, order) for w in (w_query, w_key, w_value))
     slot_rings = []
     live = jnp.clip(lengths - seq_index * cache_block, 0, cache_block).astype(jnp.int32)
@@ -897,7 +881,7 @@
     run([ring_sums[0]], [finish(1)])
     run(
         steps(ring_sums[::-1], 0, half)[:-1],
-        [add_sums, chain_split, add_sums, chain_turn, add_sums, chain_join],
+        [add_sums, None, add_sums, None, add_sums],
     )
     denominators = jnp.transpose(own(made["sums"].result(clock)), (0, 2, 1))
     for index in range(GROUPS):
@@ -921,7 +905,7 @@
         jnp.concatenate(mixed, axis=0),
         new_keys,
         new_values,
-        made["chain"],
+        made["chain"].reshape(requests, 1, local_mheads, MHEAD_DIM * STATE),
         greatest_logit,
     )
 

time: 524 us -> 532 us (1.015)
  waiting for transfers between devices: 164 us -> 186 us
  other arithmetic: 50.7 us -> 40.6 us
  local copies, waits for them, and re-layouts: 63.8 us -> 57.6 us
    ppermute x56, waiting for transfers between devices: 87.4 us -> 125 us  [ring_step(): return lax.ppermute(block, 'seq', route)]
    ppermute x1, waiting for transfers between devices: 32.7 us -> 11.8 us  [__init__(): other_factor = side(lax.ppermute(through, 'seq', self.swap))]
    ppermute x2, waiting for transfers between devices: 15.4 us -> 33.4 us  [exchange(): lax.ppermute(value.astype(jnp.bfloat16), 'seq', self.swap)]
    ppermute x8, waiting for transfers between devices: 28.4 us -> 16 us  [step(): self.got = lax.ppermute(self.value, self.axis, route)]
    optimization_barrier x1 -> x0, local copies, waits for them, and re-layouts: 5.56 us -> none  [hold(): held = lax.optimization_barrier(tuple(values) + (self.mark,))[:len(values)]]
    unnamed x126 -> x120, local copies, waits for them, and re-layouts: 18.4 us -> 18 us
  transfers between devices with their start and end apart: 74 -> 74, of which waited for: 27 -> 32; matrix products, arithmetic and copies ran while one was open for 22% -> 18% of each run, Pallas kernels for 22% -> 20%
where the time goes in v13:
time: 532 us; the launch traced here: 522 us
  waiting for transfers between devices  186 us (35%)
  Pallas kernels  133 us (25%)
  starting transfers between devices  91.5 us (17%)
  local copies, waits for them, and re-layouts  57.6 us (11%)
  other arithmetic  40.6 us (8%)
  matrix products  10.5 us (2%)
    ppermute x56, waiting for transfers between devices, ring_step(): return lax.ppermute(block, 'seq', route)  125 us
    ppermute x56, starting transfers between devices, ring_step(): return lax.ppermute(block, 'seq', route)  68 us
    pallas_call x2, Pallas kernels, cache_part(): pl.pallas_call(functools.partial(cache_kernel, slots), grid_spec=pltpu.Pr...  44.1 us
    pallas_call x4, Pallas kernels, project(): pl.pallas_call(functools.partial(project_kernel, len(pieces), turned), gr...  36 us
    ppermute x2, waiting for transfers between devices, exchange(): lax.ppermute(value.astype(jnp.bfloat16), 'seq', self.swap)  33.4 us
    pallas_call x2, Pallas kernels, finish_part(): pl.pallas_call(functools.partial(finish_kernel, slots), grid_spec=pltpu.P...  22.7 us
    unnamed x120, local copies, waits for them, and re-layouts  18 us
    ppermute x8, waiting for transfers between devices, step(): self.got = lax.ppermute(self.value, self.axis, route)  16 us
  transfers between devices with their start and end apart: 74, of which 32 were waited for; matrix products, arithmetic and copies ran while one was open for 18% of the time, Pallas kernels for 20%

profile of v13, /device:TPU:0, one launch (start us, length us, event | category | flops | bytes accessed | tf_op | source)
XLA Modules:
  0.0 521.5 jit_solution(4846323481679992664)
XLA Ops:
  8.3 5.6 %copy.40 = f32[8,16,64,64]{2,1,3,0:T(8,128)} copy(f32[8,16,64,64]{3,2,1,0:T(8,128)} %reshape.121) | data formatting | bytes 4194304 | tf_op jit(solution)/shard_map/reshape | solution.py:673
  14.0 4.8 reshape.122
  18.8 10.4 %copy.52 = bf16[256,8,2,1024]{3,1,2,0:T(8,128)(2,1)} copy(bf16[256,8,2,1024]{3,2,1,0:T(2,128)(2,1)} %bitcast.101) | data formatting | bytes 16777216
  32.2 11.6 %enter_mixer.1 = (f32[512,2048]{1,0:T(8,128)}, f32[512,128]{1,0:T(8,128)}, f32[512,16]{1,0:T(8,128)}) custom-call(bf16[512,4096]{1,0:T(8,128)(2,1)} %bitcast.62, f32[1,2048]{1,0:T(1,128)} %bitcast.120, bf16[2048,128]{1,0:T(8,128)(2,1)} %bc_ref.1, bf16[2048,16]{1,0:T(8,128)(2,1)} %copy.41.dt_ref, f32[1,16]{1,0:T(1,128)} %bitcast.125, bf16[2048,2048]{1,0:T(8,128)(2,1)} %bitcast.91), custom_call_target="tpu_custom_call" | custom-call | tf_op jit(solution)/shard_map/enter_mixer/pallas_call | solution.py:228
  51.3 9.6 %inside_block.1 = (f32[512,1024]{1,0:T(8,128)}, f32[8,64,1024]{2,1,0:T(8,128)}, f32[8,1,1024]{2,1,0:T(1,128)}) custom-call(f32[512,2048]{1,0:T(8,128)} %get-tuple-element.165.inner_ref.gate_ref, f32[512,128]{1,0:T(8,128)} %get-tuple-element.166.map_ref, f32[8,64,16]{2,1,0:T(8,128)} %bitcast.104, f32[8,64,16]{2,1,0:T(8,128)} %bitcast.108, ...), custom_call_target="tpu_custom_call" | custom-call | tf_op jit(solution)/shard_map/inside_block/pallas_call | solution.py:302
  66.6 11.8 %collective-permute-done.10 = f32[8,1,1024]{2,1,0:T(1,128)S(1)} collective-permute-done((f32[8,1,1024]{2,1,0:T(1,128)}, f32[8,1,1024]{2,1,0:T(1,128)S(1)}, u32[]{:S(2)}, u32[]{:S(2)}) %collective-permute-start.10) | collective-permute-done | bytes 32800 | tf_op jit(solution)/shard_map/ppermute | solution.py:555
  85.6 26.6 %collective-permute-done.11 = bf16[8,64,512]{2,1,0:T(8,128)(2,1)S(1)} collective-permute-done((bf16[8,64,512]{2,1,0:T(8,128)(2,1)S(1)}, bf16[8,64,512]{2,1,0:T(8,128)(2,1)S(1)}, u32[]{:S(2)}, u32[]{:S(2)}) %collective-permute-start.11) | collective-permute-done | bytes 524320 | tf_op jit(solution)/shard_map/ppermute | solution.py:566
  117.9 15.3 %collective-permute-done.6.refs_14_ = bf16[512,1024]{1,0:T(8,128)(2,1)S(1)} collective-permute-done((bf16[512,1024]{1,0:T(8,128)(2,1)}, bf16[512,1024]{1,0:T(8,128)(2,1)S(1)}, u32[]{:S(2)}, u32[]{:S(2)}) %collective-permute-start.6) | collective-permute-done | bytes 1048608 | tf_op jit(solution)/shard_map/ppermute | solution.py:37
  142.2 9.7 %collective-permute-done.12.refs_16_ = bf16[256,1024]{1,0:T(8,128)(2,1)} collective-permute-done((bf16[256,1024]{1,0:T(8,128)(2,1)}, bf16[256,1024]{1,0:T(8,128)(2,1)}, u32[]{:S(2)}, u32[]{:S(2)}) %collective-permute-start.12) | collective-permute-done | bytes 524320 | tf_op jit(solution)/shard_map/ppermute | solution.py:37
  156.9 10.4 %project.4 = bf16[512,1024]{1,0:T(8,128)(2,1)} custom-call(s32[8]{0:T(128)} %fusion.21.places_ref.place_ref, bf16[512,4096]{1,0:T(8,128)(2,1)} %bitcast.63, bf16[512,4096]{1,0:T(8,128)(2,1)} %bitcast.64, bf16[512,4096]{1,0:T(8,128)(2,1)} %bitcast.65, bf16[512,4096]{1,0:T(8,128)(2,1)} %bitcast.66, bf16[512,4096]{1,0:T(8,128)(2,1)} %bitcast.67, ...), custom_call_target="tpu_custom_call" | custom-call | tf_op jit(solution)/shard_map/project/pallas_call | solution.py:170
  179.8 9.3 %collective-permute-done.17.refs_16_ = bf16[256,1024]{1,0:T(8,128)(2,1)S(1)} collective-permute-done((bf16[256,1024]{1,0:T(8,128)(2,1)S(1)}, bf16[256,1024]{1,0:T(8,128)(2,1)S(1)}, u32[]{:S(2)}, u32[]{:S(2)}) %collective-permute-start.17) | collective-permute-done | bytes 524320 | tf_op jit(solution)/shard_map/ppermute | solution.py:37
  193.9 10.6 %project.5 = bf16[512,1024]{1,0:T(8,128)(2,1)} custom-call(s32[8]{0:T(128)} %fusion.21.places_ref.place_ref, bf16[512,4096]{1,0:T(8,128)(2,1)} %bitcast.76, bf16[512,4096]{1,0:T(8,128)(2,1)} %bitcast.73, bf16[512,4096]{1,0:T(8,128)(2,1)} %bitcast.74, bf16[512,4096]{1,0:T(8,128)(2,1)} %bitcast.75, bf16[512,4096]{1,0:T(8,128)(2,1)} %bitcast.72, ...), custom_call_target="tpu_custom_call" | custom-call | tf_op jit(solution)/shard_map/project/pallas_call | solution.py:170
  214.0 5.2 collective-permute-start.27
  227.2 6.9 %collective-permute-done.29 = bf16[8,64,512]{2,1,0:T(8,128)(2,1)S(1)} collective-permute-done((bf16[8,64,512]{2,1,0:T(8,128)(2,1)S(1)}, bf16[8,64,512]{2,1,0:T(8,128)(2,1)S(1)}, u32[]{:S(2)}, u32[]{:S(2)}) %collective-permute-start.29) | collective-permute-done | bytes 524320 | tf_op jit(solution)/shard_map/ppermute | solution.py:566
  235.9 9.4 %collective-permute-done.27.refs_3_ = bf16[4,64,1024]{2,1,0:T(8,128)(2,1)S(1)} collective-permute-done((bf16[4,64,1024]{2,1,0:T(8,128)(2,1)S(1)}, bf16[4,64,1024]{2,1,0:T(8,128)(2,1)S(1)}, u32[]{:S(2)}, u32[]{:S(2)}) %collective-permute-start.27) | collective-permute-done | bytes 524320 | tf_op jit(solution)/shard_map/ppermute | solution.py:37
  247.4 9.4 %leave_mixer.1 = (bf16[512,1024]{1,0:T(8,128)(2,1)}, f32[512,128]{1,0:T(8,128)}, f32[8,1024,64]{2,1,0:T(8,128)}) custom-call(f32[8,64,1024]{2,1,0:T(8,128)} %pad_maximum_fusion.entry_ref, f32[512,128]{1,0:T(8,128)} %get-tuple-element.166.map_ref, f32[8,64,16]{2,1,0:T(8,128)} %bitcast.105, f32[512,1024]{1,0:T(8,128)} %get-tuple-element.167.read_ref, ...), custom_call_target="tpu_custom_call" | custom-call | tf_op jit(solution)/shard_map/leave_mixer/pallas_call | solution.py:351
  259.0 8.2 %collective-permute-done.32.refs_5_ = bf16[4,64,1024]{2,1,0:T(8,128)(2,1)S(1)} collective-permute-done((bf16[4,64,1024]{2,1,0:T(8,128)(2,1)S(1)}, bf16[4,64,1024]{2,1,0:T(8,128)(2,1)S(1)}, u32[]{:S(2)}, u32[]{:S(2)}) %collective-permute-start.32) | collective-permute-done | bytes 524320 | tf_op jit(solution)/shard_map/ppermute | solution.py:37
  276.6 22.0 %cache_part.2 = (bf16[4,512,1024]{2,1,0:T(8,128)(2,1)}, bf16[4,1024,512]{2,1,0:T(8,128)(2,1)}, f32[4,8,512]{2,1,0:T(8,128)}, f32[4,8,512]{2,1,0:T(8,128)}) custom-call(s32[1]{0:T(128)} %bitcast.1.first_ref, s32[8]{0:T(128)} %fusion.21.places_ref.place_ref, s32[4]{0:T(128)} %get-tuple-element.343.live_ref, bf16[4,64,1024]{2,1,0:T(8,128)(2,1)} %bitcast.115, ...), custom_call_target="tpu_custom_call" | custom-call | tf_op jit(solution)/shard_map/cache_part/pallas_call | solution.py:433
  302.4 22.1 %cache_part.3 = (bf16[4,512,1024]{2,1,0:T(8,128)(2,1)}, bf16[4,1024,512]{2,1,0:T(8,128)(2,1)}, f32[4,8,512]{2,1,0:T(8,128)}, f32[4,8,512]{2,1,0:T(8,128)}) custom-call(s32[1]{0:T(128)} %bitcast.1.first_ref, s32[8]{0:T(128)} %fusion.21.places_ref.place_ref, s32[4]{0:T(128)} %get-tuple-element.342.live_ref, bf16[4,64,1024]{2,1,0:T(8,128)(2,1)} %bitcast.112, ...), custom_call_target="tpu_custom_call" | custom-call | tf_op jit(solution)/shard_map/cache_part/pallas_call | solution.py:433
  332.0 8.1 %project.6.refs_10_ = f32[512,1024]{1,0:T(8,128)} custom-call(s32[8]{0:T(128)} %fusion.21.places_ref.place_ref, bf16[512,4096]{1,0:T(8,128)(2,1)} %bitcast.81, bf16[512,4096]{1,0:T(8,128)(2,1)} %bitcast.82, bf16[512,4096]{1,0:T(8,128)(2,1)} %bitcast.83, bf16[512,4096]{1,0:T(8,128)(2,1)} %bitcast.84, bf16[512,4096]{1,0:T(8,128)(2,1)} %bitcast.85, ...), custom_call_target="tpu_custom_call" | custom-call | tf_op jit(solution)/shard_map/project/pallas_call | solution.py:170
  340.1 9.6 %collective-permute-done.48 = f32[8,8,512]{2,1,0:T(8,128)S(1)} collective-permute-done((f32[8,8,512]{2,1,0:T(8,128)S(1)}, f32[8,8,512]{2,1,0:T(8,128)S(1)}, u32[]{:S(2)}, u32[]{:S(2)}) %collective-permute-start.48) | collective-permute-done | bytes 131104 | tf_op jit(solution)/shard_map/ppermute | solution.py:97
  352.2 6.6 %convolution_multiply_fusion = f32[512,2048]{1,0:T(8,128)} fusion(bf16[512,1024]{1,0:T(8,128)(2,1)S(1)} %copy-done.55, bf16[1024,2048]{1,0:T(8,128)(2,1)} %param.35, f32[512]{0:T(512)S(1)} %bitcast.124), kind=kOutput, calls=%fused_computation | convolution fusion | flops 2148532224 | bytes 9439232 | tf_op jit(solution)/shard_map/dot_general | solution.py:748
  358.8 5.2 collective-permute-start.50
  370.6 6.8 %project.7 = bf16[512,1024]{1,0:T(8,128)(2,1)} custom-call(s32[8]{0:T(128)} %fusion.21.places_ref.place_ref, bf16[512,4096]{1,0:T(8,128)(2,1)} %bitcast.86, bf16[512,4096]{1,0:T(8,128)(2,1)} %bitcast.87, bf16[512,4096]{1,0:T(8,128)(2,1)} %bitcast.88, bf16[512,4096]{1,0:T(8,128)(2,1)} %bitcast.89, bf16[512,1024]{1,0:T(8,128)(2,1)} %copy-done.12, ...), custom_call_target="tpu_custom_call" | custom-call | tf_op jit(solution)/shard_map/project/pallas_call | solution.py:170
  377.4 11.2 %finish_part.2 = (f32[4,8,512]{2,1,0:T(8,128)}, bf16[4,64,1024]{2,1,0:T(8,128)(2,1)}, bf16[4,64,1024]{2,1,0:T(8,128)(2,1)}, bf16[4,64,1024]{2,1,0:T(8,128)(2,1)}...) custom-call(s32[1]{0:T(128)} %bitcast.1.first_ref, ...), custom_call_target="tpu_custom_call" | custom-call | tf_op jit(solution)/shard_map/finish_part/pallas_call | solution.py:491
  390.4 11.5 %finish_part.3 = (f32[4,8,512]{2,1,0:T(8,128)}, bf16[4,64,1024]{2,1,0:T(8,128)(2,1)}, bf16[4,64,1024]{2,1,0:T(8,128)(2,1)}, bf16[4,64,1024]{2,1,0:T(8,128)(2,1)}...) custom-call(s32[1]{0:T(128)} %bitcast.1.first_ref, ...), custom_call_target="tpu_custom_call" | custom-call | tf_op jit(solution)/shard_map/finish_part/pallas_call | solution.py:491
  413.3 5.6 %collective-permute-done.55 = bf16[2,64,1024]{2,1,0:T(8,128)(2,1)S(1)} collective-permute-done((bf16[2,64,1024]{2,1,0:T(8,128)(2,1)}, bf16[2,64,1024]{2,1,0:T(8,128)(2,1)S(1)}, u32[]{:S(2)}, u32[]{:S(2)}) %collective-permute-start.55) | collective-permute-done | bytes 262176 | tf_op jit(solution)/shard_map/ppermute | solution.py:37
  426.5 5.8 %collective-permute-done.63 = bf16[4,64,1024]{2,1,0:T(8,128)(2,1)S(1)} collective-permute-done((bf16[4,64,1024]{2,1,0:T(8,128)(2,1)S(1)}, bf16[4,64,1024]{2,1,0:T(8,128)(2,1)S(1)}, u32[]{:S(2)}, u32[]{:S(2)}) %collective-permute-start.63) | collective-permute-done | bytes 524320 | tf_op jit(solution)/shard_map/ppermute | solution.py:37
  434.6 11.7 %collective-permute-done.53 = bf16[4,64,1024]{2,1,0:T(8,128)(2,1)S(1)} collective-permute-done((bf16[4,64,1024]{2,1,0:T(8,128)(2,1)S(1)}, bf16[4,64,1024]{2,1,0:T(8,128)(2,1)S(1)}, u32[]{:S(2)}, u32[]{:S(2)}) %collective-permute-start.53) | collective-permute-done | bytes 524320 | tf_op jit(solution)/shard_map/ppermute | solution.py:37
  455.9 5.1 collective-permute-done.68
  462.3 15.5 %collective-permute-done.69 = bf16[4,64,1024]{2,1,0:T(8,128)(2,1)} collective-permute-done((bf16[4,64,1024]{2,1,0:T(8,128)(2,1)}, bf16[4,64,1024]{2,1,0:T(8,128)(2,1)}, u32[]{:S(2)}, u32[]{:S(2)}) %collective-permute-start.69) | collective-permute-done | bytes 524320 | tf_op jit(solution)/shard_map/ppermute | solution.py:37
  512.0 4.8 reshape.136
  (350 shorter events, 193.2 us)
Async XLA Ops:
  0.6 47.0 %collective-permute-start = (bf16[512,1024]{1,0:T(8,128)(2,1)}, bf16[512,1024]{1,0:T(8,128)(2,1)}, u32[]{:S(2)}, u32[]{:S(2)}) collective-permute-start(bf16[512,1024]{1,0:T(8,128)(2,1)} %refs_9_.4), channel_id=1, source_target_pairs={{0,8},{8,16},{16,24},{24,28},{28,20},{20,12},{12,4},{4,0},{1,9},{9... | collective-permute-start | bytes 3145736 | tf_op jit(solution)/shard_map/ppermute | solution.py:37
  3.7 44.0 %collective-permute-start.1 = (bf16[512,1024]{1,0:T(8,128)(2,1)}, bf16[512,1024]{1,0:T(8,128)(2,1)}, u32[]{:S(2)}, u32[]{:S(2)}) collective-permute-start(bf16[512,1024]{1,0:T(8,128)(2,1)} %refs_9_.4), channel_id=1, source_target_pairs={{0,4},{8,0},{16,8},{24,16},{28,24},{20,28},{12,20},{4,12},{1,5},{9... | collective-permute-start | bytes 3145736 | tf_op jit(solution)/shard_map/ppermute | solution.py:37
  29.2 31.7 %collective-permute-start.4 = (bf16[512,1024]{1,0:T(8,128)(2,1)S(1)}, bf16[512,1024]{1,0:T(8,128)(2,1)}, u32[]{:S(2)}, u32[]{:S(2)}) collective-permute-start(bf16[512,1024]{1,0:T(8,128)(2,1)S(1)} %copy-done.20), channel_id=1, source_target_pairs={{0,8},{8,16},{16,24},{24,28},{28,20},{20,12},{12,4},{4,0},{1,9},{9... | collective-permute-start | bytes 3145736 | tf_op jit(solution)/shard_map/ppermute | solution.py:37
  31.2 29.7 %collective-permute-start.5 = (bf16[512,1024]{1,0:T(8,128)(2,1)S(1)}, bf16[512,1024]{1,0:T(8,128)(2,1)}, u32[]{:S(2)}, u32[]{:S(2)}) collective-permute-start(bf16[512,1024]{1,0:T(8,128)(2,1)S(1)} %copy-done.20), channel_id=1, source_target_pairs={{0,4},{8,0},{16,8},{24,16},{28,24},{20,28},{12,20},{4,12},{1,5},{9... | collective-permute-start | bytes 3145736 | tf_op jit(solution)/shard_map/ppermute | solution.py:37
  47.7 35.7 %collective-permute-start.2 = (bf16[512,1024]{1,0:T(8,128)(2,1)}, bf16[512,1024]{1,0:T(8,128)(2,1)}, u32[]{:S(2)}, u32[]{:S(2)}) collective-permute-start(bf16[512,1024]{1,0:T(8,128)(2,1)} %collective-permute-done.refs_10_), channel_id=1, source_target_pairs={{0,8},{8,16},{16,24},{24,28},{28,20},{20,12},{12,4},{4,0},{1,9},{9... | collective-permute-start | bytes 3145736 | tf_op jit(solution)/shard_map/ppermute | solution.py:37
  49.7 33.6 %collective-permute-start.3 = (bf16[512,1024]{1,0:T(8,128)(2,1)}, bf16[512,1024]{1,0:T(8,128)(2,1)}, u32[]{:S(2)}, u32[]{:S(2)}) collective-permute-start(bf16[512,1024]{1,0:T(8,128)(2,1)} %collective-permute-done.1.refs_11_), channel_id=1, source_target_pairs={{0,4},{8,0},{16,8},{24,16},{28,24},{20,28},{12,20},{4,12},{1,5},{9... | collective-permute-start | bytes 3145736 | tf_op jit(solution)/shard_map/ppermute | solution.py:37
  63.0 52.4 %collective-permute-start.8 = (bf16[512,1024]{1,0:T(8,128)(2,1)}, bf16[512,1024]{1,0:T(8,128)(2,1)}, u32[]{:S(2)}, u32[]{:S(2)}) collective-permute-start(bf16[512,1024]{1,0:T(8,128)(2,1)} %collective-permute-done.4.refs_10_), channel_id=1, source_target_pairs={{0,8},{8,16},{16,24},{24,28},{28,20},{20,12},{12,4},{4,0},{1,9},{9... | collective-permute-start | bytes 3145736 | tf_op jit(solution)/shard_map/ppermute | solution.py:37
  64.5 50.8 %collective-permute-start.9 = (bf16[512,1024]{1,0:T(8,128)(2,1)}, bf16[512,1024]{1,0:T(8,128)(2,1)}, u32[]{:S(2)}, u32[]{:S(2)}) collective-permute-start(bf16[512,1024]{1,0:T(8,128)(2,1)} %collective-permute-done.5.refs_11_), channel_id=1, source_target_pairs={{0,4},{8,0},{16,8},{24,16},{28,24},{20,28},{12,20},{4,12},{1,5},{9... | collective-permute-start | bytes 3145736 | tf_op jit(solution)/shard_map/ppermute | solution.py:37
  78.5 33.7 %collective-permute-start.11 = (bf16[8,64,512]{2,1,0:T(8,128)(2,1)S(1)}, bf16[8,64,512]{2,1,0:T(8,128)(2,1)S(1)}, u32[]{:S(2)}, u32[]{:S(2)}) collective-permute-start(bf16[8,64,512]{2,1,0:T(8,128)(2,1)S(1)} %select_convert_fusion.1), channel_id=1, source_target_pairs={{0,4},{4,0},{8,12},{12,8},{16,20},{20,16},{24,28},{28,24},{1,5},{5... | collective-permute-start | bytes 1572872 | tf_op jit(solution)/shard_map/ppermute | solution.py:566
  83.3 49.8 %collective-permute-start.6 = (bf16[512,1024]{1,0:T(8,128)(2,1)}, bf16[512,1024]{1,0:T(8,128)(2,1)S(1)}, u32[]{:S(2)}, u32[]{:S(2)}) collective-permute-start(bf16[512,1024]{1,0:T(8,128)(2,1)} %collective-permute-done.2.refs_12_), channel_id=1, source_target_pairs={{0,8},{8,16},{16,24},{24,28},{28,20},{20,12},{12,4},{4,0},{1,9},{9... | collective-permute-start | bytes 3145736 | tf_op jit(solution)/shard_map/ppermute | solution.py:37
  83.4 51.6 %collective-permute-start.7 = (bf16[512,1024]{1,0:T(8,128)(2,1)}, bf16[512,1024]{1,0:T(8,128)(2,1)S(1)}, u32[]{:S(2)}, u32[]{:S(2)}) collective-permute-start(bf16[512,1024]{1,0:T(8,128)(2,1)} %collective-permute-done.3.refs_13_), channel_id=1, source_target_pairs={{0,4},{8,0},{16,8},{24,16},{28,24},{20,28},{12,20},{4,12},{1,5},{9... | collective-permute-start | bytes 3145736 | tf_op jit(solution)/shard_map/ppermute | solution.py:37
  115.6 25.4 %collective-permute-start.14 = (bf16[8,64,512]{2,1,0:T(8,128)(2,1)S(1)}, bf16[8,64,512]{2,1,0:T(8,128)(2,1)}, u32[]{:S(2)}, u32[]{:S(2)}) collective-permute-start(bf16[8,64,512]{2,1,0:T(8,128)(2,1)S(1)} %add_convert_fusion.10), channel_id=1, source_target_pairs={{0,8},{4,12},{1,9},{5,13},{2,10},{6,14},{3,11},{7,15}} | collective-permute-start | bytes 1572872 | tf_op jit(solution)/shard_map/ppermute | solution.py:581
  139.0 33.1 %collective-permute-start.15 = (bf16[512,1024]{1,0:T(8,128)(2,1)}, bf16[512,1024]{1,0:T(8,128)(2,1)}, u32[]{:S(2)}, u32[]{:S(2)}) collective-permute-start(bf16[512,1024]{1,0:T(8,128)(2,1)} %collective-permute-done.8.refs_12_), channel_id=1, source_target_pairs={{0,8},{8,16},{16,24},{24,28},{28,20},{20,12},{12,4},{4,0},{1,9},{9... | collective-permute-start | bytes 3145736 | tf_op jit(solution)/shard_map/ppermute | solution.py:37
  139.0 34.1 %collective-permute-start.16 = (bf16[512,1024]{1,0:T(8,128)(2,1)}, bf16[512,1024]{1,0:T(8,128)(2,1)}, u32[]{:S(2)}, u32[]{:S(2)}) collective-permute-start(bf16[512,1024]{1,0:T(8,128)(2,1)} %collective-permute-done.9.refs_13_), channel_id=1, source_target_pairs={{0,4},{8,0},{16,8},{24,16},{28,24},{20,28},{12,20},{4,12},{1,5},{9... | collective-permute-start | bytes 3145736 | tf_op jit(solution)/shard_map/ppermute | solution.py:37
  153.0 24.6 %collective-permute-start.19 = (bf16[8,64,512]{2,1,0:T(8,128)(2,1)}, bf16[8,64,512]{2,1,0:T(8,128)(2,1)S(1)}, u32[]{:S(2)}, u32[]{:S(2)}) collective-permute-start(bf16[8,64,512]{2,1,0:T(8,128)(2,1)} %add_convert_fusion.9), channel_id=1, source_target_pairs={{8,16},{12,20},{9,17},{13,21},{10,18},{14,22},{11,19},{15,23}} | collective-permute-start | bytes 1572872 | tf_op jit(solution)/shard_map/ppermute | solution.py:581
  177.8 26.8 %collective-permute-start.20 = (bf16[4,64,1024]{2,1,0:T(8,128)(2,1)S(1)}, bf16[4,64,1024]{2,1,0:T(8,128)(2,1)S(1)}, u32[]{:S(2)}, u32[]{:S(2)}) collective-permute-start(bf16[4,64,1024]{2,1,0:T(8,128)(2,1)S(1)} %bitcast.113), channel_id=1, source_target_pairs={{0,8},{8,16},{16,24},{24,28},{28,20},{20,12},{12,4},{4,0},{1,9},{9... | collective-permute-start | bytes 1572872 | tf_op jit(solution)/shard_map/ppermute | solution.py:37
  178.8 25.8 %collective-permute-start.21 = (bf16[4,64,1024]{2,1,0:T(8,128)(2,1)S(1)}, bf16[4,64,1024]{2,1,0:T(8,128)(2,1)}, u32[]{:S(2)}, u32[]{:S(2)}) collective-permute-start(bf16[4,64,1024]{2,1,0:T(8,128)(2,1)S(1)} %bitcast.114), channel_id=1, source_target_pairs={{0,4},{8,0},{16,8},{24,16},{28,24},{20,28},{12,20},{4,12},{1,5},{9... | collective-permute-start | bytes 1572872 | tf_op jit(solution)/shard_map/ppermute | solution.py:37
  214.0 31.3 %collective-permute-start.27 = (bf16[4,64,1024]{2,1,0:T(8,128)(2,1)S(1)}, bf16[4,64,1024]{2,1,0:T(8,128)(2,1)S(1)}, u32[]{:S(2)}, u32[]{:S(2)}) collective-permute-start(bf16[4,64,1024]{2,1,0:T(8,128)(2,1)S(1)} %collective-permute-done.22.refs_1_), channel_id=1, source_target_pairs={{0,8},{8,16},{16,24},{24,28},{28,20},{20,12},{12,4},{4,0},{1,9},{9... | collective-permute-start | bytes 1572872 | tf_op jit(solution)/shard_map/ppermute | solution.py:37
  219.2 26.1 %collective-permute-start.28 = (bf16[4,64,1024]{2,1,0:T(8,128)(2,1)S(1)}, bf16[4,64,1024]{2,1,0:T(8,128)(2,1)S(1)}, u32[]{:S(2)}, u32[]{:S(2)}) collective-permute-start(bf16[4,64,1024]{2,1,0:T(8,128)(2,1)S(1)} %collective-permute-done.23.refs_2_), channel_id=1, source_target_pairs={{0,4},{8,0},{16,8},{24,16},{28,24},{20,28},{12,20},{4,12},{1,5},{9... | collective-permute-start | bytes 1572872 | tf_op jit(solution)/shard_map/ppermute | solution.py:37
  222.9 33.9 %collective-permute-start.30 = (bf16[4,64,1024]{2,1,0:T(8,128)(2,1)}, bf16[4,64,1024]{2,1,0:T(8,128)(2,1)S(1)}, u32[]{:S(2)}, u32[]{:S(2)}) collective-permute-start(bf16[4,64,1024]{2,1,0:T(8,128)(2,1)} %collective-permute-done.25.refs_3_), channel_id=1, source_target_pairs={{0,8},{8,16},{16,24},{24,28},{28,20},{20,12},{12,4},{4,0},{1,9},{9... | collective-permute-start | bytes 1572872 | tf_op jit(solution)/shard_map/ppermute | solution.py:37
  227.2 29.7 %collective-permute-start.31 = (bf16[4,64,1024]{2,1,0:T(8,128)(2,1)}, bf16[4,64,1024]{2,1,0:T(8,128)(2,1)S(1)}, u32[]{:S(2)}, u32[]{:S(2)}) collective-permute-start(bf16[4,64,1024]{2,1,0:T(8,128)(2,1)} %collective-permute-done.26.refs_4_), channel_id=1, source_target_pairs={{0,4},{8,0},{16,8},{24,16},{28,24},{20,28},{12,20},{4,12},{1,5},{9... | collective-permute-start | bytes 1572872 | tf_op jit(solution)/shard_map/ppermute | solution.py:37
  270.6 28.9 %collective-permute-start.38 = (bf16[512,1024]{1,0:T(8,128)(2,1)S(1)}, bf16[512,1024]{1,0:T(8,128)(2,1)S(1)}, u32[]{:S(2)}, u32[]{:S(2)}) collective-permute-start(bf16[512,1024]{1,0:T(8,128)(2,1)S(1)} %copy-done.21), channel_id=1, source_target_pairs={{0,8},{8,16},{16,24},{24,28},{28,20},{20,12},{12,4},{4,0},{1,9},{9... | collective-permute-start | bytes 3145736 | tf_op jit(solution)/shard_map/ppermute | solution.py:37
  270.6 28.9 %collective-permute-start.39 = (bf16[512,1024]{1,0:T(8,128)(2,1)S(1)}, bf16[512,1024]{1,0:T(8,128)(2,1)S(1)}, u32[]{:S(2)}, u32[]{:S(2)}) collective-permute-start(bf16[512,1024]{1,0:T(8,128)(2,1)S(1)} %copy-done.21), channel_id=1, source_target_pairs={{0,4},{8,0},{16,8},{24,16},{28,24},{20,28},{12,20},{4,12},{1,5},{9... | collective-permute-start | bytes 3145736 | tf_op jit(solution)/shard_map/ppermute | solution.py:37
  272.7 26.8 %collective-permute-start.36 = (bf16[2,64,1024]{2,1,0:T(8,128)(2,1)S(1)}, bf16[2,64,1024]{2,1,0:T(8,128)(2,1)S(1)}, u32[]{:S(2)}, u32[]{:S(2)}) collective-permute-start(bf16[2,64,1024]{2,1,0:T(8,128)(2,1)S(1)} %slice.207), channel_id=1, source_target_pairs={{0,8},{8,16},{16,24},{24,28},{28,20},{20,12},{12,4},{4,0},{1,9},{9... | collective-permute-start | bytes 786440 | tf_op jit(solution)/shard_map/ppermute | solution.py:37
  273.0 26.5 %collective-permute-start.37 = (bf16[2,64,1024]{2,1,0:T(8,128)(2,1)S(1)}, bf16[2,64,1024]{2,1,0:T(8,128)(2,1)S(1)}, u32[]{:S(2)}, u32[]{:S(2)}) collective-permute-start(bf16[2,64,1024]{2,1,0:T(8,128)(2,1)S(1)} %slice.208), channel_id=1, source_target_pairs={{0,4},{8,0},{16,8},{24,16},{28,24},{20,28},{12,20},{4,12},{1,5},{9... | collective-permute-start | bytes 786440 | tf_op jit(solution)/shard_map/ppermute | solution.py:37
  299.5 25.0 %collective-permute-start.40 = (bf16[512,1024]{1,0:T(8,128)(2,1)S(1)}, bf16[512,1024]{1,0:T(8,128)(2,1)S(1)}, u32[]{:S(2)}, u32[]{:S(2)}) collective-permute-start(bf16[512,1024]{1,0:T(8,128)(2,1)S(1)} %collective-permute-done.38.refs_6_), channel_id=1, source_target_pairs={{0,8},{8,16},{16,24},{24,28},{28,20},{20,12},{12,4},{4,0},{1,9},{9... | collective-permute-start | bytes 3145736 | tf_op jit(solution)/shard_map/ppermute | solution.py:37
  324.6 25.2 %collective-permute-start.42 = (bf16[512,1024]{1,0:T(8,128)(2,1)S(1)}, bf16[512,1024]{1,0:T(8,128)(2,1)S(1)}, u32[]{:S(2)}, u32[]{:S(2)}) collective-permute-start(bf16[512,1024]{1,0:T(8,128)(2,1)S(1)} %collective-permute-done.40.refs_8_), channel_id=1, source_target_pairs={{0,8},{8,16},{16,24},{24,28},{28,20},{20,12},{12,4},{4,0},{1,9},{9... | collective-permute-start | bytes 3145736 | tf_op jit(solution)/shard_map/ppermute | solution.py:37
  325.3 24.6 %collective-permute-start.43 = (bf16[512,1024]{1,0:T(8,128)(2,1)S(1)}, bf16[512,1024]{1,0:T(8,128)(2,1)S(1)}, u32[]{:S(2)}, u32[]{:S(2)}) collective-permute-start(bf16[512,1024]{1,0:T(8,128)(2,1)S(1)} %collective-permute-done.41.refs_9_), channel_id=1, source_target_pairs={{0,4},{8,0},{16,8},{24,16},{28,24},{20,28},{12,20},{4,12},{1,5},{9... | collective-permute-start | bytes 3145736 | tf_op jit(solution)/shard_map/ppermute | solution.py:37
  422.5 25.2 %collective-permute-start.62 = (f32[8,8,512]{2,1,0:T(8,128)S(1)}, f32[8,8,512]{2,1,0:T(8,128)S(1)}, u32[]{:S(2)}, u32[]{:S(2)}) collective-permute-start(f32[8,8,512]{2,1,0:T(8,128)S(1)} %add.234), channel_id=1, source_target_pairs={{0,8},{4,12},{8,0},{12,4},{16,24},{20,28},{24,16},{28,20},{1,9},{5... | collective-permute-start | bytes 393224 | tf_op jit(solution)/shard_map/ppermute | solution.py:97
  451.0 30.1 %collective-permute-start.57 = (bf16[4,64,1024]{2,1,0:T(8,128)(2,1)}, bf16[4,64,1024]{2,1,0:T(8,128)(2,1)}, u32[]{:S(2)}, u32[]{:S(2)}) collective-permute-start(bf16[4,64,1024]{2,1,0:T(8,128)(2,1)} %add_convert_fusion.7), channel_id=1, source_target_pairs={{0,8},{8,16},{16,24},{24,28},{28,20},{20,12},{12,4},{4,0},{1,9},{9... | collective-permute-start | bytes 1572872 | tf_op jit(solution)/shard_map/ppermute | solution.py:37
  453.3 29.1 %collective-permute-start.58 = (bf16[4,64,1024]{2,1,0:T(8,128)(2,1)}, bf16[4,64,1024]{2,1,0:T(8,128)(2,1)}, u32[]{:S(2)}, u32[]{:S(2)}) collective-permute-start(bf16[4,64,1024]{2,1,0:T(8,128)(2,1)} %add_convert_fusion.6), channel_id=1, source_target_pairs={{0,4},{8,0},{16,8},{24,16},{28,24},{20,28},{12,20},{4,12},{1,5},{9... | collective-permute-start | bytes 1572872 | tf_op jit(solution)/shard_map/ppermute | solution.py:37
  453.3 24.5 %collective-permute-start.69 = (bf16[4,64,1024]{2,1,0:T(8,128)(2,1)}, bf16[4,64,1024]{2,1,0:T(8,128)(2,1)}, u32[]{:S(2)}, u32[]{:S(2)}) collective-permute-start(bf16[4,64,1024]{2,1,0:T(8,128)(2,1)} %add_convert_fusion.2), channel_id=1, source_target_pairs={{0,4},{8,0},{16,8},{24,16},{28,24},{20,28},{12,20},{4,12},{1,5},{9... | collective-permute-start | bytes 1572872 | tf_op jit(solution)/shard_map/ppermute | solution.py:37
  (99 other events, 1701.7 us)

commit v14 on v11

--- a/solution.py
+++ b/solution.py
@@ -351,7 +351,7 @@
     squares = jnp.sum(mixed * mixed, axis=1, keepdims=True)
     square_ref[...] = jnp.broadcast_to(squares, square_ref.shape)
     gated_ref[...] = (mixed * gain_ref[...]).astype(jnp.bfloat16)
-    chain_ref[0] = (through_ref[0] * entry + local_ref[0]).T
+    chain_ref[0] = through_ref[0] * entry + local_ref[0]
 
 
 def leave_mixer(entry, maps, decay, read, act, gain, local, through):
@@ -372,11 +372,11 @@
             one(STATE, inner),
             one(1, inner),
         ],
-        out_specs=[flat(inner), flat(128), one(inner, STATE)],
+        out_specs=[flat(inner), flat(128), one(STATE, inner)],
         out_shape=[
             jax.ShapeDtypeStruct((requests * tokens, inner), jnp.bfloat16),
             jax.ShapeDtypeStruct((requests * tokens, 128), jnp.float32),
-            jax.ShapeDtypeStruct((requests, inner, STATE), jnp.float32),
+            jax.ShapeDtypeStruct((requests, STATE, inner), jnp.float32),
         ],
         compiler_params=pltpu.CompilerParams(vmem_limit_bytes=VMEM_BYTES),
         cost_estimate=pl.CostEstimate(
@@ -774,10 +774,9 @@
         return (made["terms"],), ()
 
     def leave_chain():
-        made["chain"] = (
-            clock.hold(made["chain"])
-            .reshape(requests, local_mheads, MHEAD_DIM, STATE)
-            .reshape(requests, 1, local_mheads, MHEAD_DIM * STATE)
+        chain = clock.hold(made["chain"]).reshape(requests, STATE, local_mheads, MHEAD_DIM)
+        made["chain"] = jnp.transpose(chain, (0, 2, 3, 1)).reshape(
+            requests, 1, local_mheads, MHEAD_DIM * STATE
         )
         return (made["chain"],), ()
 
@@ -830,11 +829,11 @@
         made["values"] = product(
             [(0, 0, clock.hold(value_ring.block))] + pieces, False, kind=jnp.float32
         )
-        return (made["values"],) + leave_terms()[0], ()
+        return (made["values"],) + leave_chain()[0], ()
 
     def join_more():
         made["best"].step(clock)
-        return leave_chain()
+        return leave_terms()
 
     def steps(rings, begin, end):
         return [ring for _ in range(begin, end) for ring in rings]

time: 540 us -> 530 us (0.981)
  waiting for transfers between devices: 199 us -> 182 us
  local copies, waits for them, and re-layouts: 50 us -> 62.8 us
    ppermute x1, waiting for transfers between devices: 32.8 us -> 11.8 us  [__init__(): other_factor = side(lax.ppermute(through, 'seq', self.swap))]
    ppermute x2, waiting for transfers between devices: 17.7 us -> 36 us  [exchange(): lax.ppermute(value.astype(jnp.bfloat16), 'seq', self.swap)]
    ppermute x8, waiting for transfers between devices: 41.8 us -> 25.5 us  [step(): self.got = lax.ppermute(self.value, self.axis, route)]
    reshape x0 -> x2, local copies, waits for them, and re-layouts: none -> 9.29 us  [the longest x1 4.76 us: leave_chain(): jnp.transpose(chain, (0, 2, 3, 1))]
    transpose x0 -> x1, local copies, waits for them, and re-layouts: none -> 5.52 us  [leave_chain(): jnp.transpose(chain, (0, 2, 3, 1))]
    unnamed x112 -> x98, local copies, waits for them, and re-layouts: 16.4 us -> 16.2 us
  transfers between devices with their start and end apart: 74 -> 74, of which waited for: 34 -> 34; matrix products, arithmetic and copies ran while one was open for 17% -> 19% of each run, Pallas kernels for 20% -> 20%
where the time goes in v14:
time: 530 us; the launch traced here: 520 us
  waiting for transfers between devices  182 us (34%)
  Pallas kernels  133 us (25%)
  starting transfers between devices  91.7 us (17%)
  local copies, waits for them, and re-layouts  62.8 us (12%)
  other arithmetic  38 us (7%)
  matrix products  10.5 us (2%)
    ppermute x56, waiting for transfers between devices, ring_step(): return lax.ppermute(block, 'seq', route)  102 us
    ppermute x56, starting transfers between devices, ring_step(): return lax.ppermute(block, 'seq', route)  73.5 us
    pallas_call x2, Pallas kernels, cache_part(): pl.pallas_call(functools.partial(cache_kernel, slots), grid_spec=pltpu.Pr...  44.1 us
    ppermute x2, waiting for transfers between devices, exchange(): lax.ppermute(value.astype(jnp.bfloat16), 'seq', self.swap)  36 us
    pallas_call x4, Pallas kernels, project(): pl.pallas_call(functools.partial(project_kernel, len(pieces), turned), gr...  36 us
    ppermute x8, waiting for transfers between devices, step(): self.got = lax.ppermute(self.value, self.axis, route)  25.5 us
    pallas_call x2, Pallas kernels, finish_part(): pl.pallas_call(functools.partial(finish_kernel, slots), grid_spec=pltpu.P...  22.7 us
    unnamed x98, local copies, waits for them, and re-layouts  16.2 us
  transfers between devices with their start and end apart: 74, of which 34 were waited for; matrix products, arithmetic and copies ran while one was open for 19% of the time, Pallas kernels for 20%

profile of v14, /device:TPU:0, one launch (start us, length us, event | category | flops | bytes accessed | tf_op | source)
XLA Modules:
  0.0 519.8 jit_solution(1879696505122047415)
XLA Ops:
  3.7 4.6 reshape.124
  8.3 5.6 %copy.40 = f32[8,16,64,64]{2,1,3,0:T(8,128)} copy(f32[8,16,64,64]{3,2,1,0:T(8,128)} %reshape.124) | data formatting | bytes 4194304 | tf_op jit(solution)/shard_map/reshape | solution.py:696
  17.4 10.3 %copy.52 = bf16[256,8,2,1024]{3,1,2,0:T(8,128)(2,1)} copy(bf16[256,8,2,1024]{3,2,1,0:T(2,128)(2,1)} %bitcast.103) | data formatting | bytes 16777216
  30.8 11.6 %enter_mixer.1 = (f32[512,2048]{1,0:T(8,128)}, f32[512,128]{1,0:T(8,128)}, f32[512,16]{1,0:T(8,128)}) custom-call(bf16[512,4096]{1,0:T(8,128)(2,1)} %bitcast.64, f32[1,2048]{1,0:T(1,128)} %bitcast.126, bf16[2048,128]{1,0:T(8,128)(2,1)} %bc_ref.1, bf16[2048,16]{1,0:T(8,128)(2,1)} %copy.41.dt_ref, f32[1,16]{1,0:T(1,128)} %bitcast.127, bf16[2048,2048]{1,0:T(8,128)(2,1)} %bitcast.104), custom_call_target="tpu_custom_call" | custom-call | flops 4294967296 | bytes 14680064 | tf_op jit(solution)/shard_map/enter_mixer/pallas_call | solution.py:231
  50.1 9.6 %inside_block.1 = (f32[512,1024]{1,0:T(8,128)}, f32[8,64,1024]{2,1,0:T(8,128)}, f32[8,1,1024]{2,1,0:T(1,128)}) custom-call(f32[512,2048]{1,0:T(8,128)} %get-tuple-element.166.inner_ref.gate_ref, f32[512,128]{1,0:T(8,128)} %get-tuple-element.167.map_ref, f32[8,64,16]{2,1,0:T(8,128)} %bitcast.107, f32[8,64,16]{2,1,0:T(8,128)} %bitcast.111, ...), custom_call_target="tpu_custom_call" | custom-call | flops 402653184 | bytes 8388608 | tf_op jit(solution)/shard_map/inside_block/pallas_call | solution.py:309
  65.4 11.8 %collective-permute-done.10 = f32[8,1,1024]{2,1,0:T(1,128)S(1)} collective-permute-done((f32[8,1,1024]{2,1,0:T(1,128)}, f32[8,1,1024]{2,1,0:T(1,128)S(1)}, u32[]{:S(2)}, u32[]{:S(2)}) %collective-permute-start.10) | collective-permute-done | bytes 32800 | tf_op jit(solution)/shard_map/ppermute | solution.py:578
  82.7 28.2 %collective-permute-done.11 = bf16[8,64,512]{2,1,0:T(8,128)(2,1)S(1)} collective-permute-done((bf16[8,64,512]{2,1,0:T(8,128)(2,1)S(1)}, bf16[8,64,512]{2,1,0:T(8,128)(2,1)S(1)}, u32[]{:S(2)}, u32[]{:S(2)}) %collective-permute-start.11) | collective-permute-done | bytes 524320 | tf_op jit(solution)/shard_map/ppermute | solution.py:589
  118.0 14.1 %collective-permute-done.6.refs_14_ = bf16[512,1024]{1,0:T(8,128)(2,1)} collective-permute-done((bf16[512,1024]{1,0:T(8,128)(2,1)}, bf16[512,1024]{1,0:T(8,128)(2,1)}, u32[]{:S(2)}, u32[]{:S(2)}) %collective-permute-start.6) | collective-permute-done | bytes 1048608 | tf_op jit(solution)/shard_map/ppermute | solution.py:36
  141.7 7.4 %collective-permute-done.12.refs_16_ = bf16[256,1024]{1,0:T(8,128)(2,1)S(1)} collective-permute-done((bf16[256,1024]{1,0:T(8,128)(2,1)S(1)}, bf16[256,1024]{1,0:T(8,128)(2,1)S(1)}, u32[]{:S(2)}, u32[]{:S(2)}) %collective-permute-start.12) | collective-permute-done | bytes 524320 | tf_op jit(solution)/shard_map/ppermute | solution.py:36
  150.9 10.4 %project.4 = bf16[512,1024]{1,0:T(8,128)(2,1)} custom-call(s32[8]{0:T(128)} %fusion.21.places_ref.place_ref, bf16[512,4096]{1,0:T(8,128)(2,1)} %bitcast.65, bf16[512,4096]{1,0:T(8,128)(2,1)} %bitcast.66, bf16[512,4096]{1,0:T(8,128)(2,1)} %bitcast.67, bf16[512,4096]{1,0:T(8,128)(2,1)} %bitcast.68, bf16[512,4096]{1,0:T(8,128)(2,1)} %bitcast.69, ...), custom_call_target="tpu_custom_call" | custom-call | flops 4294967296 | bytes 12582912 | tf_op jit(solution)/shard_map/project/pallas_call | solution.py:169
  161.4 7.8 %collective-permute-done.15.refs_14_ = bf16[512,1024]{1,0:T(8,128)(2,1)S(1)} collective-permute-done((bf16[512,1024]{1,0:T(8,128)(2,1)}, bf16[512,1024]{1,0:T(8,128)(2,1)S(1)}, u32[]{:S(2)}, u32[]{:S(2)}) %collective-permute-start.15) | collective-permute-done | bytes 1048608 | tf_op jit(solution)/shard_map/ppermute | solution.py:36
  176.7 7.5 %collective-permute-done.17.refs_16_ = bf16[256,1024]{1,0:T(8,128)(2,1)S(1)} collective-permute-done((bf16[256,1024]{1,0:T(8,128)(2,1)S(1)}, bf16[256,1024]{1,0:T(8,128)(2,1)S(1)}, u32[]{:S(2)}, u32[]{:S(2)}) %collective-permute-start.17) | collective-permute-done | bytes 524320 | tf_op jit(solution)/shard_map/ppermute | solution.py:36
  189.8 10.4 %project.5 = bf16[512,1024]{1,0:T(8,128)(2,1)} custom-call(s32[8]{0:T(128)} %fusion.21.places_ref.place_ref, bf16[512,4096]{1,0:T(8,128)(2,1)} %bitcast.78, bf16[512,4096]{1,0:T(8,128)(2,1)} %bitcast.75, bf16[512,4096]{1,0:T(8,128)(2,1)} %bitcast.76, bf16[512,4096]{1,0:T(8,128)(2,1)} %bitcast.77, bf16[512,4096]{1,0:T(8,128)(2,1)} %bitcast.74, ...), custom_call_target="tpu_custom_call" | custom-call | flops 4294967296 | bytes 12582912 | tf_op jit(solution)/shard_map/project/pallas_call | solution.py:169
  209.8 7.3 %collective-permute-start.27 = (bf16[4,64,1024]{2,1,0:T(8,128)(2,1)}, bf16[4,64,1024]{2,1,0:T(8,128)(2,1)}, u32[]{:S(2)}, u32[]{:S(2)}) collective-permute-start(bf16[4,64,1024]{2,1,0:T(8,128)(2,1)} %collective-permute-done.22.refs_1_), channel_id=1, source_target_pairs={{0,8},{8,16},{16,24},{24,28},{28,20},{20,12},{12,4},{4,0},{1,9},{9... | collective-permute-start | bytes 1572872 | tf_op jit(solution)/shard_map/ppermute | solution.py:36
  222.5 7.8 %collective-permute-done.29 = bf16[8,64,512]{2,1,0:T(8,128)(2,1)S(1)} collective-permute-done((bf16[8,64,512]{2,1,0:T(8,128)(2,1)S(1)}, bf16[8,64,512]{2,1,0:T(8,128)(2,1)S(1)}, u32[]{:S(2)}, u32[]{:S(2)}) %collective-permute-start.29) | collective-permute-done | bytes 524320 | tf_op jit(solution)/shard_map/ppermute | solution.py:589
  232.2 9.4 %collective-permute-done.27.refs_3_ = bf16[4,64,1024]{2,1,0:T(8,128)(2,1)} collective-permute-done((bf16[4,64,1024]{2,1,0:T(8,128)(2,1)}, bf16[4,64,1024]{2,1,0:T(8,128)(2,1)}, u32[]{:S(2)}, u32[]{:S(2)}) %collective-permute-start.27) | collective-permute-done | bytes 524320 | tf_op jit(solution)/shard_map/ppermute | solution.py:36
  243.7 8.9 %leave_mixer.1 = (bf16[512,1024]{1,0:T(8,128)(2,1)}, f32[512,128]{1,0:T(8,128)}, f32[8,64,1024]{2,1,0:T(8,128)}) custom-call(f32[8,64,1024]{2,1,0:T(8,128)} %pad_maximum_fusion.entry_ref, f32[512,128]{1,0:T(8,128)} %get-tuple-element.167.map_ref, f32[8,64,16]{2,1,0:T(8,128)} %bitcast.108, f32[512,1024]{1,0:T(8,128)} %get-tuple-element.168.read_ref, ...), custom_call_target="tpu_custom_call" | custom-call | flops 67108864 | bytes 12582912 | tf_op jit(solution)/shard_map/leave_mixer/pallas_call | solution.py:362
  255.0 7.4 %collective-permute-done.32.refs_5_ = bf16[4,64,1024]{2,1,0:T(8,128)(2,1)S(1)} collective-permute-done((bf16[4,64,1024]{2,1,0:T(8,128)(2,1)}, bf16[4,64,1024]{2,1,0:T(8,128)(2,1)S(1)}, u32[]{:S(2)}, u32[]{:S(2)}) %collective-permute-start.32) | collective-permute-done | bytes 524320 | tf_op jit(solution)/shard_map/ppermute | solution.py:36
  272.6 22.0 %cache_part.2 = (bf16[4,512,1024]{2,1,0:T(8,128)(2,1)}, bf16[4,1024,512]{2,1,0:T(8,128)(2,1)}, f32[4,8,512]{2,1,0:T(8,128)}, f32[4,8,512]{2,1,0:T(8,128)}) custom-call(s32[1]{0:T(128)} %bitcast.1.first_ref, s32[8]{0:T(128)} %fusion.21.places_ref.place_ref, s32[4]{0:T(128)} %get-tuple-element.330.live_ref, bf16[4,64,1024]{2,1,0:T(8,128)(2,1)} %bitcast.117, ...), custom_call_target="tpu_custom_call" | custom-call | flops 4294967296 | bytes 20971520 | tf_op jit(solution)/shard_map/cache_part/pallas_call | solution.py:448
  298.6 22.1 %cache_part.3 = (bf16[4,512,1024]{2,1,0:T(8,128)(2,1)}, bf16[4,1024,512]{2,1,0:T(8,128)(2,1)}, f32[4,8,512]{2,1,0:T(8,128)}, f32[4,8,512]{2,1,0:T(8,128)}) custom-call(s32[1]{0:T(128)} %bitcast.1.first_ref, s32[8]{0:T(128)} %fusion.21.places_ref.place_ref, s32[4]{0:T(128)} %get-tuple-element.329.live_ref, bf16[4,64,1024]{2,1,0:T(8,128)(2,1)} %bitcast.114, ...), custom_call_target="tpu_custom_call" | custom-call | flops 4294967296 | bytes 20971520 | tf_op jit(solution)/shard_map/cache_part/pallas_call | solution.py:448
  333.2 5.5 %copy.45 = f32[8,16,64,64]{3,2,1,0:T(8,128)} copy(f32[8,16,64,64]{2,1,3,0:T(8,128)} %bitcast.99) | data formatting | bytes 4194304 | tf_op jit(solution)/shard_map/transpose | solution.py:778
  338.7 4.8 reshape.134
  343.4 8.3 %project.6.refs_10_ = f32[512,1024]{1,0:T(8,128)} custom-call(s32[8]{0:T(128)} %fusion.21.places_ref.place_ref, bf16[512,4096]{1,0:T(8,128)(2,1)} %bitcast.83, bf16[512,4096]{1,0:T(8,128)(2,1)} %bitcast.84, bf16[512,4096]{1,0:T(8,128)(2,1)} %bitcast.85, bf16[512,4096]{1,0:T(8,128)(2,1)} %bitcast.86, bf16[512,4096]{1,0:T(8,128)(2,1)} %bitcast.87, ...), custom_call_target="tpu_custom_call" | custom-call | flops 2684354560 | bytes 12582912 | tf_op jit(solution)/shard_map/project/pallas_call | solution.py:169
  354.1 6.6 %convolution_multiply_fusion = f32[512,2048]{1,0:T(8,128)} fusion(bf16[512,1024]{1,0:T(8,128)(2,1)S(1)} %copy-done.44, bf16[1024,2048]{1,0:T(8,128)(2,1)} %param.35, f32[512]{0:T(512)S(1)} %bitcast.125), kind=kOutput, calls=%fused_computation | convolution fusion | flops 2148532224 | bytes 9439232 | tf_op jit(solution)/shard_map/dot_general | solution.py:771
  364.1 10.0 %collective-permute-done.50 = f32[8,8,512]{2,1,0:T(8,128)S(1)} collective-permute-done((f32[8,8,512]{2,1,0:T(8,128)S(1)}, f32[8,8,512]{2,1,0:T(8,128)S(1)}, u32[]{:S(2)}, u32[]{:S(2)}) %collective-permute-start.50) | collective-permute-done | bytes 131104 | tf_op jit(solution)/shard_map/ppermute | solution.py:96
  376.4 6.8 %project.7 = bf16[512,1024]{1,0:T(8,128)(2,1)} custom-call(s32[8]{0:T(128)} %fusion.21.places_ref.place_ref, bf16[512,4096]{1,0:T(8,128)(2,1)} %bitcast.88, bf16[512,4096]{1,0:T(8,128)(2,1)} %bitcast.89, bf16[512,4096]{1,0:T(8,128)(2,1)} %bitcast.90, bf16[512,4096]{1,0:T(8,128)(2,1)} %bitcast.91, bf16[512,1024]{1,0:T(8,128)(2,1)} %copy-done.8, ...), custom_call_target="tpu_custom_call" | custom-call | flops 1610612736 | bytes 12582912 | tf_op jit(solution)/shard_map/project/pallas_call | solution.py:169
  383.2 11.3 %finish_part.2 = (f32[4,8,512]{2,1,0:T(8,128)}, bf16[4,64,1024]{2,1,0:T(8,128)(2,1)}, bf16[4,64,1024]{2,1,0:T(8,128)(2,1)}, bf16[4,64,1024]{2,1,0:T(8,128)(2,1)}...) custom-call(s32[1]{0:T(128)} %bitcast.1.first_ref, ...), custom_call_target="tpu_custom_call" | custom-call | flops 536870912 | bytes 12582912 | tf_op jit(solution)/shard_map/finish_part/pallas_call | solution.py:510
  396.2 11.4 %finish_part.3 = (f32[4,8,512]{2,1,0:T(8,128)}, bf16[4,64,1024]{2,1,0:T(8,128)(2,1)}, bf16[4,64,1024]{2,1,0:T(8,128)(2,1)}, bf16[4,64,1024]{2,1,0:T(8,128)(2,1)}...) custom-call(s32[1]{0:T(128)} %bitcast.1.first_ref, ...), custom_call_target="tpu_custom_call" | custom-call | flops 536870912 | bytes 12582912 | tf_op jit(solution)/shard_map/finish_part/pallas_call | solution.py:510
  429.1 10.1 %collective-permute-done.64 = bf16[4,64,1024]{2,1,0:T(8,128)(2,1)S(1)} collective-permute-done((bf16[4,64,1024]{2,1,0:T(8,128)(2,1)S(1)}, bf16[4,64,1024]{2,1,0:T(8,128)(2,1)S(1)}, u32[]{:S(2)}, u32[]{:S(2)}) %collective-permute-start.64) | collective-permute-done | bytes 524320 | tf_op jit(solution)/shard_map/ppermute | solution.py:36
  442.3 4.6 collective-permute-done.53
  457.0 12.1 %collective-permute-done.65 = f32[8,8,512]{2,1,0:T(8,128)S(1)} collective-permute-done((f32[8,8,512]{2,1,0:T(8,128)S(1)}, f32[8,8,512]{2,1,0:T(8,128)S(1)}, u32[]{:S(2)}, u32[]{:S(2)}) %collective-permute-start.65) | collective-permute-done | bytes 131104 | tf_op jit(solution)/shard_map/ppermute | solution.py:96
  511.4 5.3 %collective-permute-done.67 = bf16[256,512]{1,0:T(8,128)(2,1)} collective-permute-done((bf16[256,512]{1,0:T(8,128)(2,1)}, bf16[256,512]{1,0:T(8,128)(2,1)}, u32[]{:S(2)}, u32[]{:S(2)}) %collective-permute-start.67) | collective-permute-done | bytes 262176 | tf_op jit(solution)/shard_map/ppermute | solution.py:557
  (330 shorter events, 196.4 us)
Async XLA Ops:
  0.6 45.6 %collective-permute-start = (bf16[512,1024]{1,0:T(8,128)(2,1)}, bf16[512,1024]{1,0:T(8,128)(2,1)}, u32[]{:S(2)}, u32[]{:S(2)}) collective-permute-start(bf16[512,1024]{1,0:T(8,128)(2,1)} %refs_9_.4), channel_id=1, source_target_pairs={{0,8},{8,16},{16,24},{24,28},{28,20},{20,12},{12,4},{4,0},{1,9},{9... | collective-permute-start | bytes 3145736 | tf_op jit(solution)/shard_map/ppermute | solution.py:36
  3.7 42.6 %collective-permute-start.1 = (bf16[512,1024]{1,0:T(8,128)(2,1)}, bf16[512,1024]{1,0:T(8,128)(2,1)}, u32[]{:S(2)}, u32[]{:S(2)}) collective-permute-start(bf16[512,1024]{1,0:T(8,128)(2,1)} %refs_9_.4), channel_id=1, source_target_pairs={{0,4},{8,0},{16,8},{24,16},{28,24},{20,28},{12,20},{4,12},{1,5},{9... | collective-permute-start | bytes 3145736 | tf_op jit(solution)/shard_map/ppermute | solution.py:36
  27.7 34.0 %collective-permute-start.4 = (bf16[512,1024]{1,0:T(8,128)(2,1)}, bf16[512,1024]{1,0:T(8,128)(2,1)}, u32[]{:S(2)}, u32[]{:S(2)}) collective-permute-start(bf16[512,1024]{1,0:T(8,128)(2,1)} %refs_9_.5), channel_id=1, source_target_pairs={{0,8},{8,16},{16,24},{24,28},{28,20},{20,12},{12,4},{4,0},{1,9},{9... | collective-permute-start | bytes 3145736 | tf_op jit(solution)/shard_map/ppermute | solution.py:36
  29.8 32.0 %collective-permute-start.5 = (bf16[512,1024]{1,0:T(8,128)(2,1)}, bf16[512,1024]{1,0:T(8,128)(2,1)}, u32[]{:S(2)}, u32[]{:S(2)}) collective-permute-start(bf16[512,1024]{1,0:T(8,128)(2,1)} %refs_9_.5), channel_id=1, source_target_pairs={{0,4},{8,0},{16,8},{24,16},{28,24},{20,28},{12,20},{4,12},{1,5},{9... | collective-permute-start | bytes 3145736 | tf_op jit(solution)/shard_map/ppermute | solution.py:36
  46.3 33.9 %collective-permute-start.2 = (bf16[512,1024]{1,0:T(8,128)(2,1)}, bf16[512,1024]{1,0:T(8,128)(2,1)}, u32[]{:S(2)}, u32[]{:S(2)}) collective-permute-start(bf16[512,1024]{1,0:T(8,128)(2,1)} %collective-permute-done.refs_10_), channel_id=1, source_target_pairs={{0,8},{8,16},{16,24},{24,28},{28,20},{20,12},{12,4},{4,0},{1,9},{9... | collective-permute-start | bytes 3145736 | tf_op jit(solution)/shard_map/ppermute | solution.py:36
  48.3 31.9 %collective-permute-start.3 = (bf16[512,1024]{1,0:T(8,128)(2,1)}, bf16[512,1024]{1,0:T(8,128)(2,1)}, u32[]{:S(2)}, u32[]{:S(2)}) collective-permute-start(bf16[512,1024]{1,0:T(8,128)(2,1)} %collective-permute-done.1.refs_11_), channel_id=1, source_target_pairs={{0,4},{8,0},{16,8},{24,16},{28,24},{20,28},{12,20},{4,12},{1,5},{9... | collective-permute-start | bytes 3145736 | tf_op jit(solution)/shard_map/ppermute | solution.py:36
  61.7 52.0 %collective-permute-start.8 = (bf16[512,1024]{1,0:T(8,128)(2,1)}, bf16[512,1024]{1,0:T(8,128)(2,1)}, u32[]{:S(2)}, u32[]{:S(2)}) collective-permute-start(bf16[512,1024]{1,0:T(8,128)(2,1)} %collective-permute-done.4.refs_10_), channel_id=1, source_target_pairs={{0,8},{8,16},{16,24},{24,28},{28,20},{20,12},{12,4},{4,0},{1,9},{9... | collective-permute-start | bytes 3145736 | tf_op jit(solution)/shard_map/ppermute | solution.py:36
  63.3 50.4 %collective-permute-start.9 = (bf16[512,1024]{1,0:T(8,128)(2,1)}, bf16[512,1024]{1,0:T(8,128)(2,1)}, u32[]{:S(2)}, u32[]{:S(2)}) collective-permute-start(bf16[512,1024]{1,0:T(8,128)(2,1)} %collective-permute-done.5.refs_11_), channel_id=1, source_target_pairs={{0,4},{8,0},{16,8},{24,16},{28,24},{20,28},{12,20},{4,12},{1,5},{9... | collective-permute-start | bytes 3145736 | tf_op jit(solution)/shard_map/ppermute | solution.py:36
  77.2 33.7 %collective-permute-start.11 = (bf16[8,64,512]{2,1,0:T(8,128)(2,1)S(1)}, bf16[8,64,512]{2,1,0:T(8,128)(2,1)S(1)}, u32[]{:S(2)}, u32[]{:S(2)}) collective-permute-start(bf16[8,64,512]{2,1,0:T(8,128)(2,1)S(1)} %select_convert_fusion.1), channel_id=1, source_target_pairs={{0,4},{4,0},{8,12},{12,8},{16,20},{20,16},{24,28},{28,24},{1,5},{5... | collective-permute-start | bytes 1572872 | tf_op jit(solution)/shard_map/ppermute | solution.py:589
  80.2 51.9 %collective-permute-start.6 = (bf16[512,1024]{1,0:T(8,128)(2,1)}, bf16[512,1024]{1,0:T(8,128)(2,1)}, u32[]{:S(2)}, u32[]{:S(2)}) collective-permute-start(bf16[512,1024]{1,0:T(8,128)(2,1)} %collective-permute-done.2.refs_12_), channel_id=1, source_target_pairs={{0,8},{8,16},{16,24},{24,28},{28,20},{20,12},{12,4},{4,0},{1,9},{9... | collective-permute-start | bytes 3145736 | tf_op jit(solution)/shard_map/ppermute | solution.py:36
  80.2 52.9 %collective-permute-start.7 = (bf16[512,1024]{1,0:T(8,128)(2,1)}, bf16[512,1024]{1,0:T(8,128)(2,1)}, u32[]{:S(2)}, u32[]{:S(2)}) collective-permute-start(bf16[512,1024]{1,0:T(8,128)(2,1)} %collective-permute-done.3.refs_13_), channel_id=1, source_target_pairs={{0,4},{8,0},{16,8},{24,16},{28,24},{20,28},{12,20},{4,12},{1,5},{9... | collective-permute-start | bytes 3145736 | tf_op jit(solution)/shard_map/ppermute | solution.py:36
  114.8 25.7 %collective-permute-start.14 = (bf16[8,64,512]{2,1,0:T(8,128)(2,1)}, bf16[8,64,512]{2,1,0:T(8,128)(2,1)}, u32[]{:S(2)}, u32[]{:S(2)}) collective-permute-start(bf16[8,64,512]{2,1,0:T(8,128)(2,1)} %add_convert_fusion.10), channel_id=1, source_target_pairs={{0,8},{4,12},{1,9},{5,13},{2,10},{6,14},{3,11},{7,15}} | collective-permute-start | bytes 1572872 | tf_op jit(solution)/shard_map/ppermute | solution.py:604
  137.3 31.9 %collective-permute-start.15 = (bf16[512,1024]{1,0:T(8,128)(2,1)}, bf16[512,1024]{1,0:T(8,128)(2,1)S(1)}, u32[]{:S(2)}, u32[]{:S(2)}) collective-permute-start(bf16[512,1024]{1,0:T(8,128)(2,1)} %collective-permute-done.8.refs_12_), channel_id=1, source_target_pairs={{0,8},{8,16},{16,24},{24,28},{28,20},{20,12},{12,4},{4,0},{1,9},{9... | collective-permute-start | bytes 3145736 | tf_op jit(solution)/shard_map/ppermute | solution.py:36
  137.3 31.9 %collective-permute-start.16 = (bf16[512,1024]{1,0:T(8,128)(2,1)}, bf16[512,1024]{1,0:T(8,128)(2,1)S(1)}, u32[]{:S(2)}, u32[]{:S(2)}) collective-permute-start(bf16[512,1024]{1,0:T(8,128)(2,1)} %collective-permute-done.9.refs_13_), channel_id=1, source_target_pairs={{0,4},{8,0},{16,8},{24,16},{28,24},{20,28},{12,20},{4,12},{1,5},{9... | collective-permute-start | bytes 3145736 | tf_op jit(solution)/shard_map/ppermute | solution.py:36
  149.5 23.6 %collective-permute-start.19 = (bf16[8,64,512]{2,1,0:T(8,128)(2,1)S(1)}, bf16[8,64,512]{2,1,0:T(8,128)(2,1)}, u32[]{:S(2)}, u32[]{:S(2)}) collective-permute-start(bf16[8,64,512]{2,1,0:T(8,128)(2,1)S(1)} %add_convert_fusion.9), channel_id=1, source_target_pairs={{8,16},{12,20},{9,17},{13,21},{10,18},{14,22},{11,19},{15,23}} | collective-permute-start | bytes 1572872 | tf_op jit(solution)/shard_map/ppermute | solution.py:604
  174.6 25.6 %collective-permute-start.20 = (bf16[4,64,1024]{2,1,0:T(8,128)(2,1)S(1)}, bf16[4,64,1024]{2,1,0:T(8,128)(2,1)}, u32[]{:S(2)}, u32[]{:S(2)}) collective-permute-start(bf16[4,64,1024]{2,1,0:T(8,128)(2,1)S(1)} %bitcast.115), channel_id=1, source_target_pairs={{0,8},{8,16},{16,24},{24,28},{28,20},{20,12},{12,4},{4,0},{1,9},{9... | collective-permute-start | bytes 1572872 | tf_op jit(solution)/shard_map/ppermute | solution.py:36
  176.7 23.6 %collective-permute-start.21 = (bf16[4,64,1024]{2,1,0:T(8,128)(2,1)S(1)}, bf16[4,64,1024]{2,1,0:T(8,128)(2,1)}, u32[]{:S(2)}, u32[]{:S(2)}) collective-permute-start(bf16[4,64,1024]{2,1,0:T(8,128)(2,1)S(1)} %bitcast.116), channel_id=1, source_target_pairs={{0,4},{8,0},{16,8},{24,16},{28,24},{20,28},{12,20},{4,12},{1,5},{9... | collective-permute-start | bytes 1572872 | tf_op jit(solution)/shard_map/ppermute | solution.py:36
  209.8 31.7 %collective-permute-start.27 = (bf16[4,64,1024]{2,1,0:T(8,128)(2,1)}, bf16[4,64,1024]{2,1,0:T(8,128)(2,1)}, u32[]{:S(2)}, u32[]{:S(2)}) collective-permute-start(bf16[4,64,1024]{2,1,0:T(8,128)(2,1)} %collective-permute-done.22.refs_1_), channel_id=1, source_target_pairs={{0,8},{8,16},{16,24},{24,28},{28,20},{20,12},{12,4},{4,0},{1,9},{9... | collective-permute-start | bytes 1572872 | tf_op jit(solution)/shard_map/ppermute | solution.py:36
  217.1 24.5 %collective-permute-start.28 = (bf16[4,64,1024]{2,1,0:T(8,128)(2,1)}, bf16[4,64,1024]{2,1,0:T(8,128)(2,1)}, u32[]{:S(2)}, u32[]{:S(2)}) collective-permute-start(bf16[4,64,1024]{2,1,0:T(8,128)(2,1)} %collective-permute-done.23.refs_2_), channel_id=1, source_target_pairs={{0,4},{8,0},{16,8},{24,16},{28,24},{20,28},{12,20},{4,12},{1,5},{9... | collective-permute-start | bytes 1572872 | tf_op jit(solution)/shard_map/ppermute | solution.py:36
  219.1 33.6 %collective-permute-start.30 = (bf16[4,64,1024]{2,1,0:T(8,128)(2,1)}, bf16[4,64,1024]{2,1,0:T(8,128)(2,1)S(1)}, u32[]{:S(2)}, u32[]{:S(2)}) collective-permute-start(bf16[4,64,1024]{2,1,0:T(8,128)(2,1)} %collective-permute-done.25.refs_3_), channel_id=1, source_target_pairs={{0,8},{8,16},{16,24},{24,28},{28,20},{20,12},{12,4},{4,0},{1,9},{9... | collective-permute-start | bytes 1572872 | tf_op jit(solution)/shard_map/ppermute | solution.py:36
  222.5 30.2 %collective-permute-start.31 = (bf16[4,64,1024]{2,1,0:T(8,128)(2,1)}, bf16[4,64,1024]{2,1,0:T(8,128)(2,1)S(1)}, u32[]{:S(2)}, u32[]{:S(2)}) collective-permute-start(bf16[4,64,1024]{2,1,0:T(8,128)(2,1)} %collective-permute-done.26.refs_4_), channel_id=1, source_target_pairs={{0,4},{8,0},{16,8},{24,16},{28,24},{20,28},{12,20},{4,12},{1,5},{9... | collective-permute-start | bytes 1572872 | tf_op jit(solution)/shard_map/ppermute | solution.py:36
  266.8 28.9 %collective-permute-start.38 = (bf16[512,1024]{1,0:T(8,128)(2,1)S(1)}, bf16[512,1024]{1,0:T(8,128)(2,1)S(1)}, u32[]{:S(2)}, u32[]{:S(2)}) collective-permute-start(bf16[512,1024]{1,0:T(8,128)(2,1)S(1)} %copy-done.16), channel_id=1, source_target_pairs={{0,8},{8,16},{16,24},{24,28},{28,20},{20,12},{12,4},{4,0},{1,9},{9... | collective-permute-start | bytes 3145736 | tf_op jit(solution)/shard_map/ppermute | solution.py:36
  266.8 28.9 %collective-permute-start.39 = (bf16[512,1024]{1,0:T(8,128)(2,1)S(1)}, bf16[512,1024]{1,0:T(8,128)(2,1)S(1)}, u32[]{:S(2)}, u32[]{:S(2)}) collective-permute-start(bf16[512,1024]{1,0:T(8,128)(2,1)S(1)} %copy-done.16), channel_id=1, source_target_pairs={{0,4},{8,0},{16,8},{24,16},{28,24},{20,28},{12,20},{4,12},{1,5},{9... | collective-permute-start | bytes 3145736 | tf_op jit(solution)/shard_map/ppermute | solution.py:36
  270.3 25.3 %collective-permute-start.36 = (bf16[2,64,1024]{2,1,0:T(8,128)(2,1)S(1)}, bf16[2,64,1024]{2,1,0:T(8,128)(2,1)S(1)}, u32[]{:S(2)}, u32[]{:S(2)}) collective-permute-start(bf16[2,64,1024]{2,1,0:T(8,128)(2,1)S(1)} %slice.207), channel_id=1, source_target_pairs={{0,8},{8,16},{16,24},{24,28},{28,20},{20,12},{12,4},{4,0},{1,9},{9... | collective-permute-start | bytes 786440 | tf_op jit(solution)/shard_map/ppermute | solution.py:36
  270.6 25.1 %collective-permute-start.37 = (bf16[2,64,1024]{2,1,0:T(8,128)(2,1)S(1)}, bf16[2,64,1024]{2,1,0:T(8,128)(2,1)S(1)}, u32[]{:S(2)}, u32[]{:S(2)}) collective-permute-start(bf16[2,64,1024]{2,1,0:T(8,128)(2,1)S(1)} %slice.208), channel_id=1, source_target_pairs={{0,4},{8,0},{16,8},{24,16},{28,24},{20,28},{12,20},{4,12},{1,5},{9... | collective-permute-start | bytes 786440 | tf_op jit(solution)/shard_map/ppermute | solution.py:36
  295.7 25.1 %collective-permute-start.40 = (bf16[512,1024]{1,0:T(8,128)(2,1)S(1)}, bf16[512,1024]{1,0:T(8,128)(2,1)}, u32[]{:S(2)}, u32[]{:S(2)}) collective-permute-start(bf16[512,1024]{1,0:T(8,128)(2,1)S(1)} %collective-permute-done.38.refs_6_), channel_id=1, source_target_pairs={{0,8},{8,16},{16,24},{24,28},{28,20},{20,12},{12,4},{4,0},{1,9},{9... | collective-permute-start | bytes 3145736 | tf_op jit(solution)/shard_map/ppermute | solution.py:36
  296.1 24.6 %collective-permute-start.41 = (bf16[512,1024]{1,0:T(8,128)(2,1)S(1)}, bf16[512,1024]{1,0:T(8,128)(2,1)S(1)}, u32[]{:S(2)}, u32[]{:S(2)}) collective-permute-start(bf16[512,1024]{1,0:T(8,128)(2,1)S(1)} %collective-permute-done.39.refs_7_), channel_id=1, source_target_pairs={{0,4},{8,0},{16,8},{24,16},{28,24},{20,28},{12,20},{4,12},{1,5},{9... | collective-permute-start | bytes 3145736 | tf_op jit(solution)/shard_map/ppermute | solution.py:36
  320.8 31.1 %collective-permute-start.42 = (bf16[512,1024]{1,0:T(8,128)(2,1)}, bf16[512,1024]{1,0:T(8,128)(2,1)S(1)}, u32[]{:S(2)}, u32[]{:S(2)}) collective-permute-start(bf16[512,1024]{1,0:T(8,128)(2,1)} %collective-permute-done.40.refs_8_), channel_id=1, source_target_pairs={{0,8},{8,16},{16,24},{24,28},{28,20},{20,12},{12,4},{4,0},{1,9},{9... | collective-permute-start | bytes 3145736 | tf_op jit(solution)/shard_map/ppermute | solution.py:36
  321.2 30.7 %collective-permute-start.43 = (bf16[512,1024]{1,0:T(8,128)(2,1)S(1)}, bf16[512,1024]{1,0:T(8,128)(2,1)S(1)}, u32[]{:S(2)}, u32[]{:S(2)}) collective-permute-start(bf16[512,1024]{1,0:T(8,128)(2,1)S(1)} %collective-permute-done.41.refs_9_), channel_id=1, source_target_pairs={{0,4},{8,0},{16,8},{24,16},{28,24},{20,28},{12,20},{4,12},{1,5},{9... | collective-permute-start | bytes 3145736 | tf_op jit(solution)/shard_map/ppermute | solution.py:36
  324.4 27.4 %collective-permute-start.45 = (f32[1,512]{1,0:T(1,128)S(1)}, f32[1,512]{1,0:T(1,128)S(1)}, u32[]{:S(2)}, u32[]{:S(2)}) collective-permute-start(f32[1,512]{1,0:T(1,128)S(1)} %add.222), channel_id=1, source_target_pairs={{0,2},{1,3},{2,0},{3,1},{4,6},{5,7},{6,4},{7,5},{8,10},{9,11},{10,... | collective-permute-start | bytes 6152 | tf_op jit(solution)/shard_map/ppermute | solution.py:96
  326.7 25.1 %collective-permute-start.48 = (f32[8,8,512]{2,1,0:T(8,128)S(1)}, f32[8,8,512]{2,1,0:T(8,128)S(1)}, u32[]{:S(2)}, u32[]{:S(2)}) collective-permute-start(f32[8,8,512]{2,1,0:T(8,128)S(1)} %constant_dynamic-update-slice_fusion), channel_id=1, source_target_pairs={{0,4},{4,0},{8,12},{12,8},{16,20},{20,16},{24,28},{28,24},{1,5},{5... | collective-permute-start | bytes 393224 | tf_op jit(solution)/shard_map/ppermute | solution.py:96
  429.0 23.7 %collective-permute-start.62 = (f32[8,8,512]{2,1,0:T(8,128)S(1)}, f32[8,8,512]{2,1,0:T(8,128)S(1)}, u32[]{:S(2)}, u32[]{:S(2)}) collective-permute-start(f32[8,8,512]{2,1,0:T(8,128)S(1)} %add.234), channel_id=1, source_target_pairs={{0,8},{4,12},{8,0},{12,4},{16,24},{20,28},{24,16},{28,20},{1,9},{5... | collective-permute-start | bytes 393224 | tf_op jit(solution)/shard_map/ppermute | solution.py:96
  (88 other events, 1488.7 us)
